TPU v7x, 128 devices: a whole 4x4x4 slice. The times are simulated.
128 devices in a mesh: row: 16 (over x, z), col: 8 (over y, core).
Axes of the slice: x: 4, y: 4, z: 4, core: 2. Of those that a mesh axis runs over, the one named last changes fastest.
Arguments:
- layer_input: bfloat16 [1536, 8192], P(None, 'row'), may hold values from -6 to 6
- output_grad: bfloat16 [1536, 29568], P(None, 'col'), may hold values from -0.15625 to 0.15625
- sketch: bfloat16 [29568, 576], P('col'), may hold values from -6 to 6
- first_moment: float32 [512, 29568], P('row', 'col'), may hold values from -6 to 6
- second_moment: float32 [512, 29568], P('row', 'col'), may hold values from 0.001 to 0.01
Outputs:
- update: float32 [8192, 29568], P('row', 'col')
- new_first: float32 [512, 29568], P('row', 'col')
- new_second: float32 [512, 29568], P('row', 'col')
All inputs are finite; a program needn't handle non-finite values.
Results may differ from a plain program's by a relative error of at most 0.023.
Values may be sent and summed in bfloat16 or wider, within the bound.
No kernel may reach another device: no remote copies, remote signals or barrier semaphores. Data moves between devices by JAX's collectives and lax.ppermute only.
A program may use at most 128 MiB of HBM per device.

v0:
```python
import jax
import jax.numpy as jnp
from jax import lax
from jax.sharding import PartitionSpec as P

RANK = 512
ADAM_STEP = 10


beta_one = 0.9
beta_two = 0.999
adam_epsilon = 1e-08


def local(layer_input, output_grad, sketch, first_moment, second_moment):
    grad_tile = jnp.einsum(
        "td,tf->df", layer_input, output_grad, preferred_element_type=jnp.float32
    ).astype(jnp.bfloat16)
    sketched = lax.psum(jnp.dot(grad_tile, sketch, preferred_element_type=jnp.float32), "col")
    gram_local = jnp.dot(
        sketched.T, sketched, precision=lax.Precision.HIGHEST, preferred_element_type=jnp.float32
    )
    gram = lax.psum(gram_local, "row")
    factor_low = jnp.linalg.cholesky(gram)
    basis = lax.linalg.triangular_solve(
        factor_low, sketched, left_side=False, lower=True, transpose_a=True
    )
    projector = basis[:, :RANK].astype(jnp.bfloat16)
    owned = first_moment.shape[0]
    full_term = jnp.einsum("dr,df->rf", projector, grad_tile, preferred_element_type=jnp.float32)
    summed = lax.psum(full_term.astype(jnp.bfloat16), "row").astype(jnp.float32)
    projected = lax.dynamic_slice_in_dim(summed, lax.axis_index("row") * owned, owned, 0)
    new_first = beta_one * first_moment + (1.0 - beta_one) * projected
    new_second = beta_two * second_moment + (1.0 - beta_two) * projected * projected
    first_hat = new_first / (1.0 - beta_one**ADAM_STEP)
    second_hat = new_second / (1.0 - beta_two**ADAM_STEP)
    normalized = (first_hat / (jnp.sqrt(second_hat) + adam_epsilon)).astype(jnp.bfloat16)
    update = jnp.dot(
        projector,
        lax.all_gather(normalized, "row", axis=0, tiled=True),
        preferred_element_type=jnp.float32,
    )
    return (update, new_first, new_second)


def solution(mesh):
    placed = (P(None, "row"), P(None, "col"), P("col", None), P("row", "col"), P("row", "col"))
    return jax.shard_map(
        local,
        mesh=mesh,
        in_specs=placed,
        out_specs=(P("row", "col"), P("row", "col"), P("row", "col")),
        check_vma=False,
    )
```

profile of v0, /device:TPU:1, one launch (start us, length us, event | category | flops | bytes accessed | tf_op | source)
XLA Modules:
  0.0 542.1 jit_solution(2305106965878618376)
XLA Ops:
  7.2 1.4 copy-done
  8.6 9.0 %convolution_convert_fusion = bf16[512,3696]{0,1:T(8,128)(2,1)S(1)} fusion(bf16[1536,3696]{0,1:T(8,128)(2,1)} %param.6, bf16[1536,512]{1,0:T(8,128)(2,1)S(1)} %copy-done), kind=kOutput, calls=%fused_computation.2 | convolution fusion | flops 5815197696 | bytes 16711680 | tf_op jit(solution)/shard_map/td,tf->df/dot_general | solution.py:16
  17.6 1.9 copy-done.9
  19.5 3.4 fusion.46
  23.0 64.2 %all-reduce.7.cloned.1.call-done = f32[512,576]{0,1:T(8,128)} async-done(((f32[512,576]{0,1:T(8,128)}), f32[512,576]{0,1:T(8,128)}) %all-reduce.7.cloned.1.call-update) | async-done | bytes 1179664 | tf_op jit(solution)/shard_map/psum | solution.py:19
  87.2 5.7 %fusion.45 = f32[576,576]{0,1:T(8,128)} fusion(f32[512,576]{0,1:T(8,128)} %all-reduce.7.cloned.1.call-done), kind=kOutput, calls=%fused_computation.97 | convolution fusion | flops 2038431744 | bytes 2506752 | tf_op jit(solution)/shard_map/dot_general | solution.py:20
  93.8 87.6 %all-reduce.9.cloned.1.call-done = f32[576,576]{0,1:T(8,128)} async-done(((f32[576,576]{0,1:T(8,128)}), f32[576,576]{0,1:T(8,128)}) %all-reduce.9.cloned.1.call-update) | async-done | bytes 1327120 | tf_op jit(solution)/shard_map/psum | solution.py:23
  181.4 3.1 copy.9
  184.5 1.5 fusion
  186.1 1.1 copy-done.3
  187.2 11.7 %cholesky.134 = f32[128,128]{1,0:T(8,128)S(1)} custom-call(f32[128,128]{1,0:T(8,128)S(1)} %cholesky.346), custom_call_target="Cholesky" | custom-call | tf_op jit(solution)/shard_map/jit(cholesky)/cholesky | solution.py:24
  198.9 9.8 %custom-call.38 = f32[1,128,128]{1,2,0:T(8,128)S(1)} custom-call(f32[1,128,128]{2,1,0:T(8,128)S(1)} %get-tuple-element.34), custom_call_target="InvertDiagBlocksLowerTriangular" | custom-call | tf_op jit(solution)/shard_map/jit(cholesky)/cholesky | solution.py:24
  208.9 1.3 constant_dynamic-update-slice_fusion.3
  210.2 1.3 convolution_subtract_fusion.3
  212.1 13.2 %cholesky.274 = f32[128,128]{1,0:T(8,128)} custom-call(f32[128,128]{1,0:T(8,128)} %cholesky.350), custom_call_target="Cholesky" | custom-call | tf_op jit(solution)/shard_map/jit(cholesky)/cholesky | solution.py:24
  225.3 1.5 select_reduce_fusion.2
  226.8 11.5 %custom-call.39 = f32[1,128,128]{1,2,0:T(8,128)} custom-call(f32[1,128,128]{2,1,0:T(8,128)} %get-tuple-element.31), custom_call_target="InvertDiagBlocksLowerTriangular" | custom-call | tf_op jit(solution)/shard_map/jit(cholesky)/cholesky | solution.py:24
  238.2 1.1 convolution_dynamic-update-slice_fusion
  239.3 1.3 convolution_subtract_fusion.4
  240.7 12.3 %cholesky.295 = f32[128,128]{1,0:T(8,128)} custom-call(f32[128,128]{1,0:T(8,128)S(1)} %cholesky.355), custom_call_target="Cholesky" | custom-call | tf_op jit(solution)/shard_map/jit(cholesky)/cholesky | solution.py:24
  253.0 0.9 select_reduce_fusion.1
  253.9 0.7 compare_reduce_fusion.2
  254.6 10.4 %custom-call.40 = f32[1,128,128]{1,2,0:T(8,128)} custom-call(f32[1,128,128]{2,1,0:T(8,128)S(1)} %get-tuple-element.28), custom_call_target="InvertDiagBlocksLowerTriangular" | custom-call | tf_op jit(solution)/shard_map/jit(cholesky)/cholesky | solution.py:24
  265.0 1.1 convolution_dynamic-update-slice_fusion.1
  266.1 1.3 convolution_subtract_fusion.5
  267.4 12.1 %cholesky.314 = f32[128,128]{1,0:T(8,128)S(1)} custom-call(f32[128,128]{1,0:T(8,128)S(1)} %cholesky.360), custom_call_target="Cholesky" | custom-call | tf_op jit(solution)/shard_map/jit(cholesky)/cholesky | solution.py:24
  279.5 0.7 compare_reduce_fusion.1
  280.2 9.8 %custom-call.41 = f32[1,128,128]{1,2,0:T(8,128)S(1)} custom-call(f32[1,128,128]{2,1,0:T(8,128)S(1)} %get-tuple-element.25), custom_call_target="InvertDiagBlocksLowerTriangular" | custom-call | tf_op jit(solution)/shard_map/jit(cholesky)/cholesky | solution.py:24
  290.3 1.0 convolution_subtract_fusion.6
  291.3 5.8 %cholesky.334 = f32[64,64]{1,0:T(8,128)S(1)} custom-call(f32[64,64]{1,0:T(8,128)S(1)} %convolution_subtract_fusion.6), custom_call_target="Cholesky" | custom-call | tf_op jit(solution)/shard_map/jit(cholesky)/cholesky | solution.py:24
  297.2 0.7 compare_reduce_fusion
  297.9 0.6 compare_reduce_fusion.3
  301.8 1.1 copy-done.4
  302.9 11.6 %while.1 = (s32[]{:T(128)}, f32[576,576]{1,0:T(8,128)}, s32[4,2]{0,1:T(2,128)S(1)}, f32[4,128,128]{2,1,0:T(8,128)S(1)}, s32[]{:T(128)}) while((s32[]{:T(128)}, f32[576,576]{1,0:T(8,128)}, s32[4,2]{0,1:T(2,128)S(1)}, f32[4,128,128]{2,1,0:T(8,128)S(1)}, s32[]{:T(128)}) %tuple.49), condition=%wide.while_cond, body=%wide.while_body.sunk | while | flops 2 | bytes 131189 | solution.py:25
  303.5 2.3 bitcast_dynamic-update-slice_fusion.2
  306.4 2.3 bitcast_dynamic-update-slice_fusion.2
  309.3 2.3 bitcast_dynamic-update-slice_fusion.2
  312.2 2.3 bitcast_dynamic-update-slice_fusion.2
  314.7 49.1 %custom-call.42 = f32[5,128,128]{1,2,0:T(8,128)S(1)} custom-call(f32[5,128,128]{2,1,0:T(8,128)S(1)} %pad_maximum_fusion.1), custom_call_target="InvertDiagBlocksLowerTriangular" | custom-call | tf_op jit(solution)/shard_map/triangular_solve | solution.py:25
  363.8 1.4 fusion.44
  365.2 1.2 convolution_subtract_fusion.1
  366.9 1.5 convolution_subtract_fusion
  368.8 1.6 convolution_subtract_fusion.2
  370.8 4.1 convolution_convert_fusion.1
  375.2 100.2 %all-reduce.11.cloned.1.call-done = bf16[512,3696]{1,0:T(8,128)(2,1)} async-done(((bf16[512,3696]{1,0:T(8,128)(2,1)}), bf16[512,3696]{1,0:T(8,128)(2,1)}) %all-reduce.11.cloned.1.call-update) | async-done | bytes 3784720 | tf_op jit(solution)/shard_map/psum | solution.py:31
  475.4 2.1 divide_convert_fusion
  477.6 50.5 %all-gather.2.cloned.1.call-done = bf16[512,3696]{1,0:T(8,128)(2,1)} async-done(((bf16[32,3696]{1,0:T(8,128)(2,1)}), bf16[512,3696]{1,0:T(8,128)(2,1)}) %all-gather.2.cloned.1.call-update) | async-done | bytes 3784720 | tf_op jit(solution)/shard_map/all_gather | solution.py:40
  528.0 7.4 %fusion.24 = f32[512,3696]{0,1:T(8,128)} fusion(bf16[512,3696]{1,0:T(8,128)(2,1)} %all-gather.2.cloned.1.call-done, bf16[512,128]{0,1:T(8,128)(2,1)S(1)} %convolution_convert_fusion.2, bf16[512,128]{0,1:T(8,128)(2,1)S(1)} %get-tuple-element.39, bf16[512,128]{0,1:T(8,128)(2,1)S(1)} %get-tuple-element.41, bf16[512,128]{0,1:T(8,128)(2,1)S(1)} %get-tuple-element.43), kind=kOutput, calls=%fused_computation.47 | convolution fusion | flops 1939865600 | bytes 11878400 | tf_op jit(solution)/shard_map/dot_general | solution.py:38
  (55 shorter events, 6.1 us)
Async XLA Ops:
  7.2 1.4 copy-start
  7.2 80.0 %all-reduce.7.cloned.1.call-start = ((), (), s32[]{:S(2)}) async-start(), calls=%async_computation | async-start | bytes 2359296 | tf_op jit(solution)/shard_map/psum | solution.py:19
  8.6 10.9 %copy-start.8 = (bf16[3696,576]{0,1:T(8,128)(2,1)S(1)}, bf16[3696,576]{0,1:T(8,128)(2,1)}, u32[]{:S(2)}) copy-start(bf16[3696,576]{0,1:T(8,128)(2,1)} %param.7) | copy-start | bytes 12773380
  17.6 1.9 copy-start.9
  23.0 158.5 %all-reduce.9.cloned.1.call-start = ((), (), s32[]{:S(2)}) async-start(), calls=%async_computation.1 | async-start | bytes 2949120 | tf_op jit(solution)/shard_map/psum | solution.py:23
  92.9 382.5 %all-reduce.11.cloned.1.call-start = ((), (), s32[]{:S(2)}) async-start(), calls=%async_computation.2 | async-start | bytes 7602176 | tf_op jit(solution)/shard_map/psum | solution.py:31
  181.4 3.1 copy-start.2
  186.1 1.1 copy-start.3
  301.7 12.9 %copy-start.7 = (f32[128,64]{1,0:T(8,128)S(1)}, f32[128,64]{1,0:T(8,128)}, u32[]{:S(2)}) copy-start(f32[128,64]{1,0:T(8,128)} %pad_convert_fusion) | copy-start | bytes 98308
  301.8 1.1 copy-start.4
  301.8 63.4 %copy-start.1 = (f32[512,576]{0,1:T(8,128)S(1)}, f32[512,576]{0,1:T(8,128)}, u32[]{:S(2)}) copy-start(f32[512,576]{0,1:T(8,128)} %all-reduce.7.cloned.1.call-done) | copy-start | bytes 3538948
  366.9 3.9 copy-start.10
  374.9 100.5 %copy-start.5 = (f32[32,3696]{1,0:T(8,128)S(1)}, f32[32,3696]{1,0:T(8,128)}, u32[]{:S(2)}) copy-start(f32[32,3696]{1,0:T(8,128)} %param.8) | copy-start | bytes 1419268
  374.9 100.5 %copy-start.6 = (f32[32,3696]{1,0:T(8,128)S(1)}, f32[32,3696]{1,0:T(8,128)}, u32[]{:S(2)}) copy-start(f32[32,3696]{1,0:T(8,128)} %param.9) | copy-start | bytes 1419268
  375.0 153.1 %all-gather.2.cloned.1.call-start = ((), (), s32[]{:S(2)}) async-start(), calls=%async_computation.3 | async-start | bytes 4038656 | tf_op jit(solution)/shard_map/all_gather | solution.py:40
Sparse Core Ops, SparseCore 0:
  23.1 64.0 all-reduce.6
  93.1 88.3 all-reduce.8
  375.1 100.2 all-reduce.10
  478.3 49.7 all-gather.1
where the time goes:
time: 548 us; the launch traced here: 542 us
  waiting for transfers between devices  303 us (55%)
  other arithmetic  155 us (28%)
  matrix products  45.2 us (8%)
  local copies, waits for them, and re-layouts  20.9 us (4%)
  between operations  17.4 us (3%)
    another operation x18, other arithmetic, local(): factor_low = jnp.linalg.cholesky(gram)  102 us
    psum x1, waiting for transfers between devices, local(): summed = lax.psum(full_term.astype(jnp.bfloat16), 'row').astype(jnp.float32)  100 us
    psum x1, waiting for transfers between devices, local(): gram = lax.psum(gram_local, 'row')  87.6 us
    psum x1, waiting for transfers between devices, local(): lax.psum(jnp.dot(grad_tile, sketch, preferred_element_type=jnp.float32),...  64.2 us
    all_gather x1, waiting for transfers between devices, local(): lax.all_gather(normalized, 'row', axis=0, tiled=True)  50.5 us
    another operation x7, other arithmetic, local(): lax.linalg.triangular_solve(factor_low, sketched, left_side=False, lower=...  50 us
    another operation x12, local copies, waits for them, and re-layouts  11.6 us
  transfers between devices with their start and end apart: 4, of which 4 were waited for; matrix products, arithmetic and copies ran while one was open for 0% of the time, Pallas kernels for 0%

commit v1 on v0

v1 whole, which is shorter than its diff:
```python
import jax
import jax.numpy as jnp
from jax import lax
from jax.experimental import pallas as pl
from jax.experimental.pallas import tpu as pltpu
from jax.sharding import PartitionSpec as P

RANK = 512
ADAM_STEP = 10
BLOCK = 128
TILE = 640

beta_one = 0.9
beta_two = 0.999
adam_epsilon = 1e-08

f32 = jnp.float32
bf16 = jnp.bfloat16
HIGHEST = lax.Precision.HIGHEST

EXTENT = {"x": 4, "z": 4, "y": 4, "core": 2}
HOME = {"x": ("row", 4), "z": ("row", 1), "y": ("col", 2), "core": ("col", 1)}


def place(sub):
    axis, stride = HOME[sub]
    return lax.axis_index(axis) // stride % EXTENT[sub]


def shift(value, sub, by):
    axis, stride = HOME[sub]
    n = EXTENT[sub]
    pairs = []
    for i in range(16 if axis == "row" else 8):
        at = i // stride % n
        pairs.append((i, i + ((at + by) % n - at) * stride))
    return lax.ppermute(value, axis, pairs)


def scatter_sum(value, sub):
    n, me = EXTENT[sub], place(sub)
    pick = lambda k: lax.dynamic_index_in_dim(value, (me + k) % n, 0, keepdims=False)
    got = [shift(pick(k), sub, k) for k in range(1, n)]
    total = pick(0)
    for term in got:
        total = total + term
    return total


def gather(value, sub):
    n, me = EXTENT[sub], place(sub)
    got = [value] + [shift(value, sub, k) for k in range(1, n)]
    out = jnp.zeros((n,) + value.shape, value.dtype)
    for k in range(n):
        out = lax.dynamic_update_index_in_dim(out, got[k], (me - k) % n, 0)
    return out


def full_sum(value, sub):
    total = value
    for k in range(1, EXTENT[sub]):
        total = total + shift(value, sub, k)
    return total


def lane_of(value, k):
    return jnp.take_along_axis(value, jnp.full(value.shape, k, jnp.int32), axis=1)


def invert_block(rows, lane, sub):
    scale = [None] * len(rows)
    for k in range(len(rows) * 8):
        g, r = divmod(k, 8)
        column = lane_of(rows[g], k)
        row = jnp.broadcast_to(rows[g][r : r + 1], (8, BLOCK))
        pivot = jnp.broadcast_to(column[r : r + 1], (8, BLOCK))
        inverse = 1.0 / pivot
        unit = jnp.where(lane == k, 1.0, row)
        for h in range(g, len(rows)):
            factor = (column if h == g else lane_of(rows[h], k)) * inverse
            reduced = jnp.where(lane == k, 0.0, rows[h]) - factor * unit
            if h == g:
                rows[g] = jnp.where(sub > r, reduced, jnp.where(sub == r, unit, rows[g]))
            else:
                rows[h] = reduced
        root = lax.rsqrt(pivot)
        scale[g] = root if scale[g] is None else jnp.where(sub == r, root, scale[g])
    return [a * b for a, b in zip(rows, scale)]


def factor_kernel(gram_ref, out_ref, work):
    size, padded = gram_ref.shape[0], work.shape[0]
    work[...] = jnp.zeros_like(work)
    work[:size, :size] = gram_ref[...]
    lane = lax.broadcasted_iota(jnp.int32, (8, BLOCK), 1)
    sub = lax.broadcasted_iota(jnp.int32, (8, BLOCK), 0)
    row_in = lax.broadcasted_iota(jnp.int32, (BLOCK, BLOCK), 0)
    lane_in = lax.broadcasted_iota(jnp.int32, (BLOCK, BLOCK), 1)
    if padded > size:
        last = pl.ds(padded - BLOCK, BLOCK)
        spare = (row_in == lane_in) & (row_in >= size - (padded - BLOCK))
        work[last, last] = jnp.where(spare, 1.0, work[last, last])
    lanes = lax.broadcasted_iota(jnp.int32, (BLOCK, padded), 1)

    def step(b, carry):
        o = pl.multiple_of(b * BLOCK, BLOCK)
        here = pl.ds(o, BLOCK)
        rows = [work[pl.ds(pl.multiple_of(o + 8 * h, 8), 8), here] for h in range(BLOCK // 8)]
        inverse = jnp.concatenate(invert_block(rows, lane, sub), axis=0)
        inverse = jnp.where(row_in >= lane_in, inverse, 0.0)
        panel = work[here, :]
        work[:, here] = jnp.zeros((padded, BLOCK), f32)
        solved = jnp.dot(inverse, panel, precision=HIGHEST, preferred_element_type=f32)
        work[here, :] = solved
        work[here, here] = inverse
        later = jnp.where(lanes >= o + BLOCK, solved, 0.0)
        work[...] -= lax.dot_general(
            later, work[here, :], (((0,), (0,)), ((), ())), precision=HIGHEST, preferred_element_type=f32
        )
        return carry

    lax.fori_loop(0, padded // BLOCK, step, 0)
    row_at = lax.broadcasted_iota(jnp.int32, (padded, padded), 0)
    lane_at = lax.broadcasted_iota(jnp.int32, (padded, padded), 1)
    out_ref[...] = jnp.where(row_at >= lane_at, work[...], 0.0)[:size, :size]


def inverse_factor(gram):
    size = gram.shape[0]
    padded = pl.cdiv(size, BLOCK) * BLOCK
    return pl.pallas_call(
        factor_kernel,
        out_shape=jax.ShapeDtypeStruct((size, size), f32),
        in_specs=[pl.BlockSpec(memory_space=pltpu.VMEM)],
        out_specs=pl.BlockSpec(memory_space=pltpu.VMEM),
        scratch_shapes=[pltpu.VMEM((padded, padded), f32)],
        compiler_params=pltpu.CompilerParams(vmem_limit_bytes=32 << 20),
        cost_estimate=pl.CostEstimate(flops=12 * size**3, bytes_accessed=8 * size**2, transcendentals=0),
        name="inverse_factor",
    )(gram)


def moments(first, second, projected):
    new_first = beta_one * first + (1.0 - beta_one) * projected
    new_second = beta_two * second + (1.0 - beta_two) * projected * projected
    return new_first, new_second


def step_kernel(
    at_ref, mixed_ref, projector_ref, grad_ref, first_ref, second_ref, own_first_ref, own_second_ref,
    update_ref, new_first_ref, new_second_ref, projected_ref,
):
    projected_ref[...] = jnp.dot(mixed_ref[...], grad_ref[...], preferred_element_type=f32)
    new_first, new_second = moments(
        first_ref[...].astype(f32), second_ref[...].astype(f32), projected_ref[...]
    )
    first_hat = new_first / (1.0 - beta_one**ADAM_STEP)
    second_hat = new_second / (1.0 - beta_two**ADAM_STEP)
    normalized = (first_hat / (jnp.sqrt(second_hat) + adam_epsilon)).astype(bf16)
    update_ref[...] = jnp.dot(projector_ref[...], normalized, preferred_element_type=f32)
    owned = own_first_ref.shape[0]
    mine = projected_ref[pl.ds(pl.multiple_of(at_ref[0] * owned, owned), owned), :]
    new_first_ref[...], new_second_ref[...] = moments(own_first_ref[...], own_second_ref[...], mine)


def adam_step(at, mixed, projector, output_grad, first, second, own_first, own_second):
    tokens, width = output_grad.shape
    features, rank = projector.shape
    owned = own_first.shape[0]
    whole = lambda shape: pl.BlockSpec(shape, lambda i, at: (0, 0))
    strip = lambda rows: pl.BlockSpec((rows, TILE), lambda i, at: (0, i))
    return pl.pallas_call(
        step_kernel,
        out_shape=(
            jax.ShapeDtypeStruct((features, width), f32),
            jax.ShapeDtypeStruct((owned, width), f32),
            jax.ShapeDtypeStruct((owned, width), f32),
        ),
        grid_spec=pltpu.PrefetchScalarGridSpec(
            num_scalar_prefetch=1,
            grid=(pl.cdiv(width, TILE),),
            in_specs=[whole((rank, tokens)), whole((features, rank)), strip(tokens)]
            + [strip(rank), strip(rank), strip(owned), strip(owned)],
            out_specs=[strip(features), strip(owned), strip(owned)],
            scratch_shapes=[pltpu.VMEM((rank, TILE), f32)],
        ),
        compiler_params=pltpu.CompilerParams(vmem_limit_bytes=48 << 20),
        cost_estimate=pl.CostEstimate(
            flops=2 * rank * width * (tokens + features),
            bytes_accessed=width * (2 * tokens + 4 * rank + 4 * features + 16 * owned),
            transcendentals=rank * width,
        ),
        name="adam_step",
    )(at, mixed, projector, output_grad, first, second, own_first, own_second)


def two_parts(value):
    high = value.astype(bf16)
    return high, (value - high.astype(f32)).astype(bf16)


def local(layer_input, output_grad, sketch, first_moment, second_moment):
    tokens, features = layer_input.shape
    columns = sketch.shape[1]
    first_rows = lax.all_gather(first_moment.astype(bf16), "row", axis=0, tiled=True)
    second_rows = lax.all_gather(second_moment.astype(bf16), "row", axis=0, tiled=True)

    token_sketch = jnp.dot(output_grad, sketch, preferred_element_type=f32)
    turned = lambda part: lax.dot_general(
        part, layer_input, (((0,), (0,)), ((), ())), preferred_element_type=f32
    )
    high, low = two_parts(token_sketch)
    partial = turned(high) + turned(low)
    half = scatter_sum(partial.reshape(2, columns // 2, features), "core")
    owned_rows = scatter_sum(half.reshape(4, columns // 8, features), "y")
    sketched = gather(gather(owned_rows, "y").reshape(columns // 2, features), "core")
    sketched = sketched.reshape(columns, features)

    gram_rows = lax.dot_general(
        owned_rows, sketched, (((1,), (1,)), ((), ())), precision=HIGHEST, preferred_element_type=f32
    )
    gram_rows = full_sum(full_sum(gram_rows, "x"), "z")
    gram = gather(gather(gram_rows, "y").reshape(columns // 2, columns), "core").reshape(columns, columns)

    share = tokens // 128
    own_tokens = lax.dynamic_index_in_dim(
        layer_input.reshape(16, 8, share, features), lax.axis_index("col"), 1, keepdims=False
    ).reshape(tokens // 8, features)
    sketched_high, rest = two_parts(sketched)
    times = lambda part: lax.dot_general(
        own_tokens, part, (((1,), (1,)), ((), ())), preferred_element_type=f32
    )
    mixed = times(sketched_high) + times(rest)
    mixed = scatter_sum(mixed.reshape(4, 4 * share, columns), "x")
    mixed = scatter_sum(mixed.reshape(4, share, columns), "z")
    mixed = lax.all_gather(mixed, ("row", "col"), axis=0, tiled=True)

    inverse = inverse_factor(gram)
    basis = lax.dot_general(
        sketched, inverse, (((0,), (1,)), ((), ())), precision=HIGHEST, preferred_element_type=f32
    )
    projector = basis[:, :RANK].astype(bf16)
    turned_mixed = lax.dot_general(
        inverse[:RANK], mixed, (((1,), (1,)), ((), ())), precision=HIGHEST, preferred_element_type=f32
    ).astype(bf16)
    at = lax.axis_index("row").astype(jnp.int32).reshape(1)
    return adam_step(
        at, turned_mixed, projector, output_grad, first_rows, second_rows, first_moment, second_moment
    )


def solution(mesh):
    placed = (P(None, "row"), P(None, "col"), P("col", None), P("row", "col"), P("row", "col"))
    return jax.shard_map(
        local,
        mesh=mesh,
        in_specs=placed,
        out_specs=(P("row", "col"), P("row", "col"), P("row", "col")),
        check_vma=False,
    )
```

time: 548 us -> 283 us (0.52)
  waiting for transfers between devices: 303 us -> 75.7 us
  other arithmetic: 155 us -> 4.58 us
  Pallas kernels: 0 us -> 81.9 us
  starting transfers between devices: 0.51 us -> 38 us
  local copies, waits for them, and re-layouts: 20.9 us -> 36.7 us
  matrix products: 45.2 us -> 31.2 us
    psum x3 -> x0, waiting for transfers between devices: 252 us -> none  [the longest x1 100 us: local(): summed = lax.psum(full_term.astype(jnp.bfloat16), 'row').astype(jnp.float32)]
    another operation x25 -> x0, other arithmetic: 152 us -> none  [the longest x18 102 us: local(): factor_low = jnp.linalg.cholesky(gram)]
    pallas_call x0 -> x2, Pallas kernels: none -> 81.9 us  [the longest x1 63.8 us: inverse_factor(): pl.pallas_call(factor_kernel, out_shape=jax.ShapeDtypeStruct((size, size)...]
    ppermute x0 -> x24, waiting for transfers between devices: none -> 39.6 us  [shift(): return lax.ppermute(value, axis, pairs)]
    ppermute x0 -> x24, starting transfers between devices: none -> 37.7 us  [shift(): return lax.ppermute(value, axis, pairs)]
    unnamed x22 -> x16, local copies, waits for them, and re-layouts: 5.48 us -> 23.8 us
    another operation x15 -> x0, matrix products: 15.5 us -> none  [the longest x8 8.61 us: local(): factor_low = jnp.linalg.cholesky(gram)]
    all_gather x1 -> x3, waiting for transfers between devices: 50.5 us -> 36.1 us  [the longest x1 36.1 us: local(): lax.all_gather(second_moment.astype(bf16), 'row', axis=0, tiled=True)]
  transfers between devices with their start and end apart: 4 -> 27, of which waited for: 4 -> 18; matrix products, arithmetic and copies ran while one was open for 0% -> 15% of each run, Pallas kernels for 0% -> 23%
where the time goes in v1:
time: 283 us; the launch traced here: 282 us
  Pallas kernels  81.9 us (29%)
  waiting for transfers between devices  75.7 us (27%)
  starting transfers between devices  38 us (13%)
  local copies, waits for them, and re-layouts  36.7 us (13%)
  matrix products  31.2 us (11%)
  between operations  14.1 us (5%)
  other arithmetic  4.58 us (2%)
    pallas_call x1, Pallas kernels, inverse_factor(): pl.pallas_call(factor_kernel, out_shape=jax.ShapeDtypeStruct((size, size)...  63.8 us
    ppermute x24, waiting for transfers between devices, shift(): return lax.ppermute(value, axis, pairs)  39.6 us
    ppermute x24, starting transfers between devices, shift(): return lax.ppermute(value, axis, pairs)  37.7 us
    all_gather x1, waiting for transfers between devices, local(): lax.all_gather(second_moment.astype(bf16), 'row', axis=0, tiled=True)  36.1 us
    unnamed x16, local copies, waits for them, and re-layouts  23.8 us
    pallas_call x1, Pallas kernels, adam_step(): pl.pallas_call(step_kernel, out_shape=(jax.ShapeDtypeStruct((features, wi...  18.1 us
    dot_general x1, matrix products, local(): token_sketch = jnp.dot(output_grad, sketch, preferred_element_type=f32)  11.2 us
    dot_general x1, matrix products, local(): lax.dot_general(inverse[:RANK], mixed, (((1,), (1,)), ((), ())), precisio...  9.53 us
  transfers between devices with their start and end apart: 27, of which 18 were waited for; matrix products, arithmetic and copies ran while one was open for 15% of the time, Pallas kernels for 23%

profile of v1, /device:TPU:1, one launch (start us, length us, event | category | flops | bytes accessed | tf_op | source)
XLA Modules:
  0.0 282.2 jit_solution(10617635848095602845)
XLA Ops:
  7.2 11.2 %fusion.15 = f32[1536,576]{0,1:T(8,128)S(1)} fusion(bf16[3696,576]{0,1:T(8,128)(2,1)} %param.7, bf16[1536,3696]{0,1:T(8,128)(2,1)} %param.6), kind=kOutput, calls=%fused_computation.49 | convolution fusion | flops 6539968512 | bytes 19150848 | tf_op jit(solution)/shard_map/dot_general | solution.py:208
  18.5 1.1 fusion
  19.6 1.1 convolution_add_fusion
  20.8 1.5 collective-permute-start
  22.3 1.8 collective-permute-done
  24.0 1.2 bitcast_add_fusion
  25.2 1.4 collective-permute-start.1
  26.7 1.5 collective-permute-start.3
  28.2 1.6 collective-permute-start.2
  29.8 2.1 collective-permute-done.1
  31.9 4.2 %collective-permute-done.2 = f32[72,512]{1,0:T(8,128)S(1)} collective-permute-done((f32[72,512]{1,0:T(8,128)S(1)}, f32[72,512]{1,0:T(8,128)S(1)}, u32[]{:S(2)}, u32[]{:S(2)}) %collective-permute-start.2) | collective-permute-done | bytes 147488 | tf_op jit(solution)/shard_map/ppermute | solution.py:37
  36.8 2.1 collective-permute-start.6
  38.9 2.5 collective-permute-done.4
  41.5 3.3 %collective-permute-done.5 = f32[72,512]{1,0:T(8,128)S(1)} collective-permute-done((f32[72,512]{1,0:T(8,128)S(1)}, f32[72,512]{1,0:T(8,128)S(1)}, u32[]{:S(2)}, u32[]{:S(2)}) %collective-permute-start.5) | collective-permute-done | bytes 147488 | tf_op jit(solution)/shard_map/ppermute | solution.py:37
  44.8 2.6 collective-permute-start.7
  47.5 1.5 reshape.51
  51.3 1.3 collective-permute-start.18
  52.6 1.5 collective-permute-start.20
  54.0 1.5 collective-permute-start.19
  55.5 1.8 collective-permute-done.18
  58.6 2.4 collective-permute-done.19
  61.1 1.0 fusion.7
  62.2 1.7 collective-permute-start.21
  63.9 2.2 collective-permute-start.23
  66.1 1.2 collective-permute-start.22
  67.4 3.0 %collective-permute-done.22 = f32[12,576]{1,0:T(8,128)S(1)} collective-permute-done((f32[12,576]{1,0:T(8,128)S(1)}, f32[12,576]{1,0:T(8,128)S(1)}, u32[]{:S(2)}, u32[]{:S(2)}) %collective-permute-start.22) | collective-permute-done | bytes 27680 | tf_op jit(solution)/shard_map/ppermute | solution.py:37
  72.9 1.2 fusion.12
  74.1 1.2 collective-permute-start.10
  75.3 1.5 collective-permute-start.9
  76.8 1.8 collective-permute-done.10
  78.5 2.8 collective-permute-done.9
  81.3 1.9 collective-permute-done.8
  83.2 1.8 collective-permute-start.13
  85.7 3.9 %collective-permute-done.13 = f32[72,576]{1,0:T(8,128)S(1)} collective-permute-done((f32[72,576]{1,0:T(8,128)S(1)}, f32[72,576]{1,0:T(8,128)S(1)}, u32[]{:S(2)}, u32[]{:S(2)}) %collective-permute-start.13) | collective-permute-done | bytes 165920 | tf_op jit(solution)/shard_map/ppermute | solution.py:37
  89.6 1.4 collective-permute-done.12
  91.1 1.7 collective-permute-done.11
  93.6 3.0 %collective-permute-start.15 = (f32[72,576]{1,0:T(8,128)S(1)}, f32[72,576]{1,0:T(8,128)S(1)}, u32[]{:S(2)}, u32[]{:S(2)}) collective-permute-start(f32[72,576]{1,0:T(8,128)S(1)} %get-tuple-element.13), channel_id=1, source_target_pairs={{0,4},{1,5},{2,6},{3,7},{4,0},{5,1},{6,2},{7,3},{8,12},{9,13},{10,... | collective-permute-start | bytes 497672 | tf_op jit(solution)/shard_map/ppermute | solution.py:37
  96.6 2.2 collective-permute-done.14
  98.9 2.6 collective-permute-done.15
  101.6 7.9 %collective-permute-start.17 = (f32[288,576]{1,0:T(8,128)S(1)}, f32[288,576]{1,0:T(8,128)S(1)}, u32[]{:S(2)}, u32[]{:S(2)}) collective-permute-start(f32[288,576]{1,0:T(8,128)S(1)} %bitcast.99), channel_id=1, source_target_pairs={{0,1},{1,0},{2,3},{3,2},{4,5},{5,4},{6,7},{7,6},{8,9},{9,8},{10,11... | collective-permute-start | bytes 1990664 | tf_op jit(solution)/shard_map/ppermute | solution.py:37
  109.5 14.9 %copy.12.grad_ref = bf16[1536,3696]{1,0:T(8,128)(2,1)} copy(bf16[1536,3696]{0,1:T(8,128)(2,1)} %param.6) | data formatting | bytes 22708224 | tf_op args[1]
  124.6 63.8 %inverse_factor.1 = f32[576,576]{1,0:T(8,128)S(1)} custom-call(f32[576,576]{1,0:T(8,128)S(1)} %bitcast.94), custom_call_target="tpu_custom_call" | custom-call | flops 2293235712 | bytes 2654208 | tf_op jit(solution)/shard_map/inverse_factor/pallas_call | solution.py:131
  188.5 6.3 %fusion.14 = bf16[512,576]{1,0:T(8,128)(2,1)S(1)} fusion(f32[576,512]{1,0:T(8,128)S(1)} %bitcast.96, f32[576,576]{1,0:T(8,128)S(1)} %inverse_factor.1), kind=kOutput, calls=%fused_computation.48 | convolution fusion | flops 2038431744 | bytes 3096576 | tf_op jit(solution)/shard_map/dot_general | solution.py:239
  195.6 5.5 %reshape.56 = f32[1536,576]{1,0:T(8,128)} reshape(f32[128,12,576]{2,1,0:T(8,128)} %all-gather.9.cloned.1.call-done) | data formatting | bytes 7077888
  201.1 9.5 %convolution_convert_fusion.mixed_ref = bf16[512,1536]{1,0:T(8,128)(2,1)S(1)} fusion(f32[1536,576]{1,0:T(8,128)} %reshape.56, f32[576,576]{1,0:T(8,128)S(1)} %inverse_factor.1), kind=kOutput, calls=%fused_computation.1 | convolution fusion | flops 5436604416 | bytes 6422528 | tf_op jit(solution)/shard_map/dot_general | solution.py:243
  210.7 36.1 %all-gather.7.cloned.1.call-done.second_ref = bf16[512,3696]{1,0:T(8,128)(2,1)} async-done(((bf16[32,3696]{1,0:T(8,128)(2,1)}), bf16[512,3696]{1,0:T(8,128)(2,1)}) %all-gather.7.cloned.1.call-update) | async-done | bytes 3784720 | tf_op jit(solution)/shard_map/all_gather | solution.py:206
  248.9 18.1 %adam_step.1 = (f32[512,3696]{1,0:T(8,128)}, f32[32,3696]{1,0:T(8,128)}, f32[32,3696]{1,0:T(8,128)}) custom-call(s32[1]{0:T(128)} %bitcast.at_ref, bf16[512,1536]{1,0:T(8,128)(2,1)S(1)} %convolution_convert_fusion.mixed_ref, bf16[512,512]{1,0:T(8,128)(2,1)S(1)} %copy-done, bf16[1536,3696]{1,0:T(8,128)(2,1)} %copy.12.grad_ref, ...), custom_call_target="tpu_custom_call" | custom-call | flops 7751073792 | bytes 28385280 | tf_op jit(solution)/shard_map/adam_step/pallas_call | solution.py:172
  267.0 8.7 %copy.13 = f32[512,3696]{0,1:T(8,128)} copy(f32[512,3696]{1,0:T(8,128)} %get-tuple-element.9) | data formatting | bytes 15138816 | tf_op jit(solution)/shard_map/adam_step/pallas_call | solution.py:172
  (68 shorter events, 11.6 us)
Async XLA Ops:
  7.2 188.4 %all-gather.9.cloned.1.call-start = ((), (), s32[]{:S(2)}) async-start(), calls=%async_computation.2 | async-start | bytes 5283840 | tf_op jit(solution)/shard_map/all_gather | solution.py:236
  7.2 11.2 %copy-start.4 = (bf16[1536,512]{1,0:T(8,128)(2,1)S(1)}, bf16[1536,512]{1,0:T(8,128)(2,1)}, u32[]{:S(2)}) copy-start(bf16[1536,512]{1,0:T(8,128)(2,1)} %param.5) | copy-start | bytes 4718596
  20.8 3.3 %collective-permute-start = (f32[288,512]{1,0:T(8,128)S(1)}, f32[288,512]{1,0:T(8,128)}, u32[]{:S(2)}, u32[]{:S(2)}) collective-permute-start(f32[288,512]{1,0:T(8,128)S(1)} %dynamic-slice_bitcast_fusion), channel_id=1, source_target_pairs={{0,1},{1,0},{2,3},{3,2},{4,5},{5,4},{6,7},{7,6},{8,9},{9,8},{10,11... | collective-permute-start | bytes 1769480 | tf_op jit(solution)/shard_map/ppermute | solution.py:37
  25.2 6.6 %collective-permute-start.1 = (f32[72,512]{1,0:T(8,128)S(1)}, f32[72,512]{1,0:T(8,128)S(1)}, u32[]{:S(2)}, u32[]{:S(2)}) collective-permute-start(f32[72,512]{1,0:T(8,128)S(1)} %get-tuple-element.18), channel_id=1, source_target_pairs={{0,2},{1,3},{2,4},{3,5},{4,6},{5,7},{6,0},{7,1},{8,10},{9,11},{10,... | collective-permute-start | bytes 442376 | tf_op jit(solution)/shard_map/ppermute | solution.py:37
  26.7 5.2 %collective-permute-start.3 = (f32[72,512]{1,0:T(8,128)S(1)}, f32[72,512]{1,0:T(8,128)S(1)}, u32[]{:S(2)}, u32[]{:S(2)}) collective-permute-start(f32[72,512]{1,0:T(8,128)S(1)} %get-tuple-element.19), channel_id=1, source_target_pairs={{0,6},{1,7},{2,0},{3,1},{4,2},{5,3},{6,4},{7,5},{8,14},{9,15},{10,... | collective-permute-start | bytes 442376 | tf_op jit(solution)/shard_map/ppermute | solution.py:37
  28.2 7.9 %collective-permute-start.2 = (f32[72,512]{1,0:T(8,128)S(1)}, f32[72,512]{1,0:T(8,128)S(1)}, u32[]{:S(2)}, u32[]{:S(2)}) collective-permute-start(f32[72,512]{1,0:T(8,128)S(1)} %get-tuple-element.20), channel_id=1, source_target_pairs={{0,4},{1,5},{2,6},{3,7},{4,0},{5,1},{6,2},{7,3},{8,12},{9,13},{10,... | collective-permute-start | bytes 442376 | tf_op jit(solution)/shard_map/ppermute | solution.py:37
  36.2 5.3 %collective-permute-start.4 = (f32[72,512]{1,0:T(8,128)S(1)}, f32[72,512]{1,0:T(8,128)S(1)}, u32[]{:S(2)}, u32[]{:S(2)}) collective-permute-start(f32[72,512]{1,0:T(8,128)S(1)} %get-tuple-element.17), channel_id=1, source_target_pairs={{0,2},{1,3},{2,4},{3,5},{4,6},{5,7},{6,0},{7,1},{8,10},{9,11},{10,... | collective-permute-start | bytes 442376 | tf_op jit(solution)/shard_map/ppermute | solution.py:37
  36.8 8.0 %collective-permute-start.6 = (f32[72,512]{1,0:T(8,128)S(1)}, f32[72,512]{1,0:T(8,128)S(1)}, u32[]{:S(2)}, u32[]{:S(2)}) collective-permute-start(f32[72,512]{1,0:T(8,128)S(1)} %get-tuple-element.17), channel_id=1, source_target_pairs={{0,6},{1,7},{2,0},{3,1},{4,2},{5,3},{6,4},{7,5},{8,14},{9,15},{10,... | collective-permute-start | bytes 442376 | tf_op jit(solution)/shard_map/ppermute | solution.py:37
  38.9 5.9 %collective-permute-start.5 = (f32[72,512]{1,0:T(8,128)S(1)}, f32[72,512]{1,0:T(8,128)S(1)}, u32[]{:S(2)}, u32[]{:S(2)}) collective-permute-start(f32[72,512]{1,0:T(8,128)S(1)} %get-tuple-element.17), channel_id=1, source_target_pairs={{0,4},{1,5},{2,6},{3,7},{4,0},{5,1},{6,2},{7,3},{8,12},{9,13},{10,... | collective-permute-start | bytes 442376 | tf_op jit(solution)/shard_map/ppermute | solution.py:37
  44.8 5.4 %collective-permute-start.7 = (f32[288,512]{1,0:T(8,128)S(1)}, f32[288,512]{1,0:T(8,128)S(1)}, u32[]{:S(2)}, u32[]{:S(2)}) collective-permute-start(f32[288,512]{1,0:T(8,128)S(1)} %bitcast.101), channel_id=1, source_target_pairs={{0,1},{1,0},{2,3},{3,2},{4,5},{5,4},{6,7},{7,6},{8,9},{9,8},{10,11... | collective-permute-start | bytes 1769480 | tf_op jit(solution)/shard_map/ppermute | solution.py:37
  51.2 19.9 %copy-start.1 = (f32[32,3696]{1,0:T(8,128)S(1)}, f32[32,3696]{1,0:T(8,128)}, u32[]{:S(2)}) copy-start(f32[32,3696]{1,0:T(8,128)} %own_first_ref.1) | copy-start | bytes 1419268
  51.2 20.9 %copy-start.2 = (f32[32,3696]{1,0:T(8,128)S(1)}, f32[32,3696]{1,0:T(8,128)}, u32[]{:S(2)}) copy-start(f32[32,3696]{1,0:T(8,128)} %own_second_ref.1) | copy-start | bytes 1419268
  51.3 6.1 %collective-permute-start.18 = (f32[48,576]{1,0:T(8,128)S(1)}, f32[48,576]{1,0:T(8,128)S(1)}, u32[]{:S(2)}, u32[]{:S(2)}) collective-permute-start(f32[48,576]{1,0:T(8,128)S(1)} %get-tuple-element.21), channel_id=1, source_target_pairs={{0,32},{8,40},{16,48},{24,56},{32,64},{40,72},{48,80},{56,88},{64,... | collective-permute-start | bytes 331784 | tf_op jit(solution)/shard_map/ppermute | solution.py:37
  52.6 4.8 %collective-permute-start.20 = (f32[48,576]{1,0:T(8,128)S(1)}, f32[48,576]{1,0:T(8,128)S(1)}, u32[]{:S(2)}, u32[]{:S(2)}) collective-permute-start(f32[48,576]{1,0:T(8,128)S(1)} %get-tuple-element.22), channel_id=1, source_target_pairs={{0,96},{8,104},{16,112},{24,120},{32,0},{40,8},{48,16},{56,24},{64... | collective-permute-start | bytes 331784 | tf_op jit(solution)/shard_map/ppermute | solution.py:37
  54.0 7.0 %collective-permute-start.19 = (f32[48,576]{1,0:T(8,128)S(1)}, f32[48,576]{1,0:T(8,128)}, u32[]{:S(2)}, u32[]{:S(2)}) collective-permute-start(f32[48,576]{1,0:T(8,128)S(1)} %get-tuple-element.23), channel_id=1, source_target_pairs={{0,64},{8,72},{16,80},{24,88},{32,96},{40,104},{48,112},{56,120},{... | collective-permute-start | bytes 331784 | tf_op jit(solution)/shard_map/ppermute | solution.py:37
  57.3 0.6 copy-start.5
  58.0 0.6 copy-start.6
  62.2 5.2 %collective-permute-start.21 = (f32[12,576]{1,0:T(8,128)S(1)}, f32[12,576]{1,0:T(8,128)S(1)}, u32[]{:S(2)}, u32[]{:S(2)}) collective-permute-start(f32[12,576]{1,0:T(8,128)S(1)} %get-tuple-element.24), channel_id=1, source_target_pairs={{0,8},{8,16},{16,24},{24,0},{32,40},{40,48},{48,56},{56,32},{64,72... | collective-permute-start | bytes 82952 | tf_op jit(solution)/shard_map/ppermute | solution.py:37
  63.9 3.5 %collective-permute-start.23 = (f32[12,576]{1,0:T(8,128)S(1)}, f32[12,576]{1,0:T(8,128)S(1)}, u32[]{:S(2)}, u32[]{:S(2)}) collective-permute-start(f32[12,576]{1,0:T(8,128)S(1)} %get-tuple-element.25), channel_id=1, source_target_pairs={{0,24},{8,0},{16,8},{24,16},{32,56},{40,32},{48,40},{56,48},{64,88... | collective-permute-start | bytes 82952 | tf_op jit(solution)/shard_map/ppermute | solution.py:37
  66.1 4.4 %collective-permute-start.22 = (f32[12,576]{1,0:T(8,128)S(1)}, f32[12,576]{1,0:T(8,128)S(1)}, u32[]{:S(2)}, u32[]{:S(2)}) collective-permute-start(f32[12,576]{1,0:T(8,128)S(1)} %get-tuple-element.26), channel_id=1, source_target_pairs={{0,16},{8,24},{16,0},{24,8},{32,48},{40,56},{48,32},{56,40},{64,80... | collective-permute-start | bytes 82952 | tf_op jit(solution)/shard_map/ppermute | solution.py:37
  71.1 139.6 %all-gather.5.cloned.1.call-start = ((), (), s32[]{:S(2)}) async-start(), calls=%async_computation | async-start | bytes 4038656 | tf_op jit(solution)/shard_map/all_gather | solution.py:205
  71.9 174.9 %all-gather.7.cloned.1.call-start = ((), (), s32[]{:S(2)}) async-start(), calls=%async_computation.1 | async-start | bytes 4038656 | tf_op jit(solution)/shard_map/all_gather | solution.py:206
  74.1 4.5 %collective-permute-start.10 = (f32[72,576]{1,0:T(8,128)S(1)}, f32[72,576]{1,0:T(8,128)S(1)}, u32[]{:S(2)}, u32[]{:S(2)}) collective-permute-start(f32[72,576]{1,0:T(8,128)S(1)} %fusion.12), channel_id=1, source_target_pairs={{0,96},{8,104},{16,112},{24,120},{32,0},{40,8},{48,16},{56,24},{64... | collective-permute-start | bytes 497672 | tf_op jit(solution)/shard_map/ppermute | solution.py:37
  75.3 6.0 %collective-permute-start.9 = (f32[72,576]{1,0:T(8,128)S(1)}, f32[72,576]{1,0:T(8,128)S(1)}, u32[]{:S(2)}, u32[]{:S(2)}) collective-permute-start(f32[72,576]{1,0:T(8,128)S(1)} %fusion.12), channel_id=1, source_target_pairs={{0,64},{8,72},{16,80},{24,88},{32,96},{40,104},{48,112},{56,120},{... | collective-permute-start | bytes 497672 | tf_op jit(solution)/shard_map/ppermute | solution.py:37
  76.8 6.4 %collective-permute-start.8 = (f32[72,576]{1,0:T(8,128)S(1)}, f32[72,576]{1,0:T(8,128)S(1)}, u32[]{:S(2)}, u32[]{:S(2)}) collective-permute-start(f32[72,576]{1,0:T(8,128)S(1)} %fusion.12), channel_id=1, source_target_pairs={{0,32},{8,40},{16,48},{24,56},{32,64},{40,72},{48,80},{56,88},{64,... | collective-permute-start | bytes 497672 | tf_op jit(solution)/shard_map/ppermute | solution.py:37
  83.2 6.4 %collective-permute-start.13 = (f32[72,576]{1,0:T(8,128)S(1)}, f32[72,576]{1,0:T(8,128)S(1)}, u32[]{:S(2)}, u32[]{:S(2)}) collective-permute-start(f32[72,576]{1,0:T(8,128)S(1)} %add_add_fusion.1), channel_id=1, source_target_pairs={{0,24},{8,0},{16,8},{24,16},{32,56},{40,32},{48,40},{56,48},{64,88... | collective-permute-start | bytes 497672 | tf_op jit(solution)/shard_map/ppermute | solution.py:37
  85.0 6.0 %collective-permute-start.12 = (f32[72,576]{1,0:T(8,128)S(1)}, f32[72,576]{1,0:T(8,128)S(1)}, u32[]{:S(2)}, u32[]{:S(2)}) collective-permute-start(f32[72,576]{1,0:T(8,128)S(1)} %add_add_fusion.1), channel_id=1, source_target_pairs={{0,16},{8,24},{16,0},{24,8},{32,48},{40,56},{48,32},{56,40},{64,80... | collective-permute-start | bytes 497672 | tf_op jit(solution)/shard_map/ppermute | solution.py:37
  85.0 7.7 %collective-permute-start.11 = (f32[72,576]{1,0:T(8,128)S(1)}, f32[72,576]{1,0:T(8,128)S(1)}, u32[]{:S(2)}, u32[]{:S(2)}) collective-permute-start(f32[72,576]{1,0:T(8,128)S(1)} %add_add_fusion.1), channel_id=1, source_target_pairs={{0,8},{8,16},{16,24},{24,0},{32,40},{40,48},{48,56},{56,32},{64,72... | collective-permute-start | bytes 497672 | tf_op jit(solution)/shard_map/ppermute | solution.py:37
  92.9 6.0 %collective-permute-start.14 = (f32[72,576]{1,0:T(8,128)S(1)}, f32[72,576]{1,0:T(8,128)S(1)}, u32[]{:S(2)}, u32[]{:S(2)}) collective-permute-start(f32[72,576]{1,0:T(8,128)S(1)} %get-tuple-element.13), channel_id=1, source_target_pairs={{0,2},{1,3},{2,4},{3,5},{4,6},{5,7},{6,0},{7,1},{8,10},{9,11},{10,... | collective-permute-start | bytes 497672 | tf_op jit(solution)/shard_map/ppermute | solution.py:37
  93.6 7.9 %collective-permute-start.15 = (f32[72,576]{1,0:T(8,128)S(1)}, f32[72,576]{1,0:T(8,128)S(1)}, u32[]{:S(2)}, u32[]{:S(2)}) collective-permute-start(f32[72,576]{1,0:T(8,128)S(1)} %get-tuple-element.13), channel_id=1, source_target_pairs={{0,4},{1,5},{2,6},{3,7},{4,0},{5,1},{6,2},{7,3},{8,12},{9,13},{10,... | collective-permute-start | bytes 497672 | tf_op jit(solution)/shard_map/ppermute | solution.py:37
  96.6 4.9 %collective-permute-start.16 = (f32[72,576]{1,0:T(8,128)S(1)}, f32[72,576]{1,0:T(8,128)S(1)}, u32[]{:S(2)}, u32[]{:S(2)}) collective-permute-start(f32[72,576]{1,0:T(8,128)S(1)} %get-tuple-element.13), channel_id=1, source_target_pairs={{0,6},{1,7},{2,0},{3,1},{4,2},{5,3},{6,4},{7,5},{8,14},{9,15},{10,... | collective-permute-start | bytes 497672 | tf_op jit(solution)/shard_map/ppermute | solution.py:37
  101.6 23.0 %collective-permute-start.17 = (f32[288,576]{1,0:T(8,128)S(1)}, f32[288,576]{1,0:T(8,128)S(1)}, u32[]{:S(2)}, u32[]{:S(2)}) collective-permute-start(f32[288,576]{1,0:T(8,128)S(1)} %bitcast.99), channel_id=1, source_target_pairs={{0,1},{1,0},{2,3},{3,2},{4,5},{5,4},{6,7},{7,6},{8,9},{9,8},{10,11... | collective-permute-start | bytes 1990664 | tf_op jit(solution)/shard_map/ppermute | solution.py:37
  246.8 1.0 copy-start
  247.8 1.0 copy-start.3
Sparse Core Ops, SparseCore 0:
  71.2 71.8 all-gather.8
  145.8 48.1 all-gather.4
  196.8 49.9 all-gather.6

commit v2 on v1

--- a/solution.py
+++ b/solution.py
@@ -9,6 +9,8 @@
 ADAM_STEP = 10
 BLOCK = 128
 TILE = 640
+TOKEN_TILE = 256
+MIX_TILE = 384
 
 beta_one = 0.9
 beta_two = 0.999
@@ -140,6 +142,80 @@
     )(gram)
 
 
+def two_parts(value):
+    high = value.astype(bf16)
+    return high, (value - high.astype(f32)).astype(bf16)
+
+
+def sketch_kernel(sketch_ref, grad_ref, input_ref, out_ref):
+    token_sketch = jnp.dot(sketch_ref[...], grad_ref[...], preferred_element_type=f32)
+    high, low = two_parts(token_sketch)
+    values = input_ref[...]
+    term = jnp.dot(high, values, preferred_element_type=f32) + jnp.dot(low, values, preferred_element_type=f32)
+
+    @pl.when(pl.program_id(0) == 0)
+    def _():
+        out_ref[...] = term
+
+    @pl.when(pl.program_id(0) > 0)
+    def _():
+        out_ref[...] += term
+
+
+def sketched_term(sketch_turned, grad_turned, layer_input):
+    columns, width = sketch_turned.shape
+    tokens, features = layer_input.shape
+    return pl.pallas_call(
+        sketch_kernel,
+        out_shape=jax.ShapeDtypeStruct((columns, features), f32),
+        grid=(tokens // TOKEN_TILE,),
+        in_specs=[
+            pl.BlockSpec((columns, width), lambda i: (0, 0)),
+            pl.BlockSpec((width, TOKEN_TILE), lambda i: (0, i)),
+            pl.BlockSpec((TOKEN_TILE, features), lambda i: (i, 0)),
+        ],
+        out_specs=pl.BlockSpec((columns, features), lambda i: (0, 0)),
+        compiler_params=pltpu.CompilerParams(vmem_limit_bytes=48 << 20),
+        cost_estimate=pl.CostEstimate(
+            flops=2 * columns * tokens * (width + 2 * features),
+            bytes_accessed=2 * width * (columns + tokens) + 2 * tokens * features + 4 * columns * features,
+            transcendentals=0,
+        ),
+        name="sketched_term",
+    )(sketch_turned, grad_turned, layer_input)
+
+
+def mix_kernel(inverse_ref, mixed_ref, out_ref):
+    values = jnp.concatenate([mixed_ref[i] for i in range(mixed_ref.shape[0])], axis=0)
+    high, low = two_parts(values)
+    inverse_high, inverse_low = two_parts(inverse_ref[...])
+    times = lambda a, b: lax.dot_general(a, b, (((1,), (1,)), ((), ())), preferred_element_type=f32)
+    total = times(inverse_high, low) + times(inverse_low, high) + times(inverse_high, high)
+    out_ref[...] = total.astype(out_ref.dtype)
+
+
+def mixed_tokens(inverse, mixed):
+    blocks, share, columns = mixed.shape
+    group = MIX_TILE // share
+    return pl.pallas_call(
+        mix_kernel,
+        out_shape=jax.ShapeDtypeStruct((RANK, blocks * share), bf16),
+        grid=(blocks // group,),
+        in_specs=[
+            pl.BlockSpec((RANK, columns), lambda i: (0, 0)),
+            pl.BlockSpec((group, share, columns), lambda i: (i, 0, 0)),
+        ],
+        out_specs=pl.BlockSpec((RANK, MIX_TILE), lambda i: (0, i)),
+        compiler_params=pltpu.CompilerParams(vmem_limit_bytes=48 << 20),
+        cost_estimate=pl.CostEstimate(
+            flops=6 * RANK * columns * blocks * share,
+            bytes_accessed=4 * blocks * share * columns + 2 * RANK * blocks * share,
+            transcendentals=0,
+        ),
+        name="mixed_tokens",
+    )(inverse, mixed)
+
+
 def moments(first, second, projected):
     new_first = beta_one * first + (1.0 - beta_one) * projected
     new_second = beta_two * second + (1.0 - beta_two) * projected * projected
@@ -147,41 +223,52 @@
 
 
 def step_kernel(
-    at_ref, mixed_ref, projector_ref, grad_ref, first_ref, second_ref, own_first_ref, own_second_ref,
+    at_ref, mixed_ref, projector_ref, grad_ref, gathered_ref, own_first_ref, own_second_ref,
     update_ref, new_first_ref, new_second_ref, projected_ref,
 ):
-    projected_ref[...] = jnp.dot(mixed_ref[...], grad_ref[...], preferred_element_type=f32)
-    new_first, new_second = moments(
-        first_ref[...].astype(f32), second_ref[...].astype(f32), projected_ref[...]
-    )
+    projected_ref[...] = lax.dot_general(
+        mixed_ref[...], grad_ref[...], (((1,), (1,)), ((), ())), preferred_element_type=f32
+    )
+    owned = own_first_ref.shape[0]
+    first = gathered_ref[:, :owned, :].reshape(projected_ref.shape).astype(f32)
+    second = gathered_ref[:, owned:, :].reshape(projected_ref.shape).astype(f32)
+    new_first, new_second = moments(first, second, projected_ref[...])
     first_hat = new_first / (1.0 - beta_one**ADAM_STEP)
     second_hat = new_second / (1.0 - beta_two**ADAM_STEP)
     normalized = (first_hat / (jnp.sqrt(second_hat) + adam_epsilon)).astype(bf16)
-    update_ref[...] = jnp.dot(projector_ref[...], normalized, preferred_element_type=f32)
-    owned = own_first_ref.shape[0]
+    update_ref[...] = lax.dot_general(
+        normalized, projector_ref[...], (((0,), (0,)), ((), ())), preferred_element_type=f32
+    )
     mine = projected_ref[pl.ds(pl.multiple_of(at_ref[0] * owned, owned), owned), :]
     new_first_ref[...], new_second_ref[...] = moments(own_first_ref[...], own_second_ref[...], mine)
 
 
-def adam_step(at, mixed, projector, output_grad, first, second, own_first, own_second):
-    tokens, width = output_grad.shape
-    features, rank = projector.shape
+def adam_step(at, mixed, projector, grad_turned, gathered, own_first, own_second):
+    width, tokens = grad_turned.shape
+    rank, features = projector.shape
     owned = own_first.shape[0]
     whole = lambda shape: pl.BlockSpec(shape, lambda i, at: (0, 0))
     strip = lambda rows: pl.BlockSpec((rows, TILE), lambda i, at: (0, i))
+    turned = lambda columns: pl.BlockSpec((TILE, columns), lambda i, at: (i, 0))
     return pl.pallas_call(
         step_kernel,
         out_shape=(
-            jax.ShapeDtypeStruct((features, width), f32),
+            jax.ShapeDtypeStruct((width, features), f32),
             jax.ShapeDtypeStruct((owned, width), f32),
             jax.ShapeDtypeStruct((owned, width), f32),
         ),
         grid_spec=pltpu.PrefetchScalarGridSpec(
             num_scalar_prefetch=1,
             grid=(pl.cdiv(width, TILE),),
-            in_specs=[whole((rank, tokens)), whole((features, rank)), strip(tokens)]
-            + [strip(rank), strip(rank), strip(owned), strip(owned)],
-            out_specs=[strip(features), strip(owned), strip(owned)],
+            in_specs=[
+                whole((rank, tokens)),
+                whole((rank, features)),
+                turned(tokens),
+                pl.BlockSpec((rank // owned, 2 * owned, TILE), lambda i, at: (0, 0, i)),
+                strip(owned),
+                strip(owned),
+            ],
+            out_specs=[turned(features), strip(owned), strip(owned)],
             scratch_shapes=[pltpu.VMEM((rank, TILE), f32)],
         ),
         compiler_params=pltpu.CompilerParams(vmem_limit_bytes=48 << 20),
@@ -191,62 +278,56 @@
             transcendentals=rank * width,
         ),
         name="adam_step",
-    )(at, mixed, projector, output_grad, first, second, own_first, own_second)
-
-
-def two_parts(value):
-    high = value.astype(bf16)
-    return high, (value - high.astype(f32)).astype(bf16)
+    )(at, mixed, projector, grad_turned, gathered, own_first, own_second)
 
 
 def local(layer_input, output_grad, sketch, first_moment, second_moment):
     tokens, features = layer_input.shape
     columns = sketch.shape[1]
-    first_rows = lax.all_gather(first_moment.astype(bf16), "row", axis=0, tiled=True)
-    second_rows = lax.all_gather(second_moment.astype(bf16), "row", axis=0, tiled=True)
-
-    token_sketch = jnp.dot(output_grad, sketch, preferred_element_type=f32)
-    turned = lambda part: lax.dot_general(
-        part, layer_input, (((0,), (0,)), ((), ())), preferred_element_type=f32
-    )
-    high, low = two_parts(token_sketch)
-    partial = turned(high) + turned(low)
+    own = columns // 8
+    share = tokens // 128
+    grad_turned = output_grad.T
+    both = jnp.concatenate([first_moment.astype(bf16), second_moment.astype(bf16)], axis=0)
+    gathered = lax.all_gather(both, "row", axis=0, tiled=False)
+
+    partial = sketched_term(sketch.T, grad_turned, layer_input)
     half = scatter_sum(partial.reshape(2, columns // 2, features), "core")
-    owned_rows = scatter_sum(half.reshape(4, columns // 8, features), "y")
+    owned_rows = scatter_sum(half.reshape(4, own, features), "y")
     sketched = gather(gather(owned_rows, "y").reshape(columns // 2, features), "core")
     sketched = sketched.reshape(columns, features)
 
-    gram_rows = lax.dot_general(
-        owned_rows, sketched, (((1,), (1,)), ((), ())), precision=HIGHEST, preferred_element_type=f32
-    )
-    gram_rows = full_sum(full_sum(gram_rows, "x"), "z")
-    gram = gather(gather(gram_rows, "y").reshape(columns // 2, columns), "core").reshape(columns, columns)
-
-    share = tokens // 128
     own_tokens = lax.dynamic_index_in_dim(
-        layer_input.reshape(16, 8, share, features), lax.axis_index("col"), 1, keepdims=False
-    ).reshape(tokens // 8, features)
-    sketched_high, rest = two_parts(sketched)
-    times = lambda part: lax.dot_general(
-        own_tokens, part, (((1,), (1,)), ((), ())), preferred_element_type=f32
-    )
-    mixed = times(sketched_high) + times(rest)
-    mixed = scatter_sum(mixed.reshape(4, 4 * share, columns), "x")
-    mixed = scatter_sum(mixed.reshape(4, share, columns), "z")
-    mixed = lax.all_gather(mixed, ("row", "col"), axis=0, tiled=True)
-
-    inverse = inverse_factor(gram)
-    basis = lax.dot_general(
-        sketched, inverse, (((0,), (1,)), ((), ())), precision=HIGHEST, preferred_element_type=f32
-    )
-    projector = basis[:, :RANK].astype(bf16)
-    turned_mixed = lax.dot_general(
-        inverse[:RANK], mixed, (((1,), (1,)), ((), ())), precision=HIGHEST, preferred_element_type=f32
-    ).astype(bf16)
+        layer_input.reshape(4, 4, 8, share, features), lax.axis_index("col"), 2, keepdims=False
+    ).reshape(4, 4 * share, features)
+    left = jnp.concatenate(
+        [jnp.broadcast_to(owned_rows, (4, own, features)), own_tokens.astype(f32)], axis=1
+    )
+    both_terms = lax.dot_general(
+        left.reshape(4 * (own + 4 * share), features), sketched, (((1,), (1,)), ((), ())),
+        precision=HIGHEST, preferred_element_type=f32,
+    )
+    both_terms = scatter_sum(both_terms.reshape(4, own + 4 * share, columns), "x")
+    both_terms = jnp.concatenate(
+        [
+            jnp.broadcast_to(both_terms[:own], (4, own, columns)),
+            both_terms[own:].reshape(4, share, columns),
+        ],
+        axis=1,
+    )
+    both_terms = scatter_sum(both_terms, "z")
+    mixed, gathered = lax.optimization_barrier((both_terms[own:], gathered))
+    mixed = lax.all_gather(mixed, ("row", "col"), axis=0, tiled=False).reshape(128, share, columns)
+    gram = gather(gather(both_terms[:own], "y").reshape(columns // 2, columns), "core")
+
+    inverse = inverse_factor(gram.reshape(columns, columns))
+    basis = jnp.dot(inverse, sketched, precision=lax.Precision.HIGH, preferred_element_type=f32)
+    projector = basis[:RANK].astype(bf16)
+    turned_mixed = mixed_tokens(inverse, mixed)
     at = lax.axis_index("row").astype(jnp.int32).reshape(1)
-    return adam_step(
-        at, turned_mixed, projector, output_grad, first_rows, second_rows, first_moment, second_moment
-    )
+    update, new_first, new_second = adam_step(
+        at, turned_mixed, projector, grad_turned, gathered, first_moment, second_moment
+    )
+    return update.T, new_first, new_second
 
 
 def solution(mesh):

time: 283 us -> 219 us (0.77)
  local copies, waits for them, and re-layouts: 36.7 us -> 3.94 us
  matrix products: 31.2 us -> 3.63 us
  Pallas kernels: 81.9 us -> 106 us
  waiting for transfers between devices: 75.7 us -> 57.4 us
  starting transfers between devices: 38 us -> 26.9 us
    all_gather x3 -> x2, waiting for transfers between devices: 36.1 us -> 0.02 us  [the longest x1 0.02 us: local(): lax.all_gather(mixed, ('row', 'col'), axis=0, tiled=False)]
    dot_general x8 -> x2, matrix products: 31.2 us -> 3.63 us  [the longest x1 2.06 us: local(): lax.dot_general(left.reshape(4 * (own + 4 * share), features), sketched,...]
    pallas_call x1 -> x3, Pallas kernels: 18.1 us -> 42.6 us  [the longest x1 19 us: adam_step(): pl.pallas_call(step_kernel, out_shape=(jax.ShapeDtypeStruct((width, featu...]
    unnamed x16 -> x6, local copies, waits for them, and re-layouts: 23.8 us -> 0.02 us
    ppermute x24 -> x18, waiting for transfers between devices: 39.6 us -> 57.4 us  [shift(): return lax.ppermute(value, axis, pairs)]
    ppermute x24 -> x18, starting transfers between devices: 37.7 us -> 26.8 us  [shift(): return lax.ppermute(value, axis, pairs)]
    pallas_call x1 -> x0, local copies, waits for them, and re-layouts: 8.72 us -> none  [adam_step(): pl.pallas_call(step_kernel, out_shape=(jax.ShapeDtypeStruct((features, wi...]
  transfers between devices with their start and end apart: 27 -> 20, of which waited for: 18 -> 11; matrix products, arithmetic and copies ran while one was open for 15% -> 5% of each run, Pallas kernels for 23% -> 37%
where the time goes in v2:
time: 219 us
  Pallas kernels  106 us (48%)
  waiting for transfers between devices  57.4 us (26%)
  starting transfers between devices  26.9 us (12%)
  between operations  14.4 us (7%)
  other arithmetic  6.58 us (3%)
  local copies, waits for them, and re-layouts  3.94 us (2%)
  matrix products  3.63 us (2%)
    pallas_call x1, Pallas kernels, inverse_factor(): pl.pallas_call(factor_kernel, out_shape=jax.ShapeDtypeStruct((size, size)...  63.6 us
    ppermute x18, waiting for transfers between devices, shift(): return lax.ppermute(value, axis, pairs)  57.4 us
    ppermute x18, starting transfers between devices, shift(): return lax.ppermute(value, axis, pairs)  26.8 us
    pallas_call x1, Pallas kernels, adam_step(): pl.pallas_call(step_kernel, out_shape=(jax.ShapeDtypeStruct((width, featu...  19 us
    pallas_call x1, Pallas kernels, sketched_term(): pl.pallas_call(sketch_kernel, out_shape=jax.ShapeDtypeStruct((columns, fe...  16.7 us
    pallas_call x1, Pallas kernels, mixed_tokens(): pl.pallas_call(mix_kernel, out_shape=jax.ShapeDtypeStruct((RANK, blocks *...  6.85 us
  transfers between devices with their start and end apart: 20, of which 11 were waited for; matrix products, arithmetic and copies ran while one was open for 5% of the time, Pallas kernels for 37%

profile of v2, /device:TPU:1, one launch (start us, length us, event | category | flops | bytes accessed | tf_op | source)
XLA Modules:
  0.0 219.1 jit_solution(12598105602083292355)
XLA Ops:
  7.2 1.2 convert_element_type.15
  8.4 1.1 convert_element_type.16
  9.4 0.8 pad_maximum_fusion
  10.4 16.7 %sketched_term.1 = f32[576,512]{1,0:T(8,128)S(1)} custom-call(bf16[576,3696]{1,0:T(8,128)(2,1)} %bitcast.105, bf16[3696,1536]{1,0:T(8,128)(2,1)} %bitcast.102, bf16[1536,512]{1,0:T(8,128)(2,1)S(1)} %copy-done), custom_call_target="tpu_custom_call" | custom-call | flops 8351907840 | bytes 18364416 | tf_op jit(solution)/shard_map/sketched_term/pallas_call | solution.py:168
  27.2 1.5 collective-permute-start
  28.7 1.8 collective-permute-done
  30.4 1.2 bitcast_add_fusion
  31.7 1.4 collective-permute-start.1
  33.1 1.5 collective-permute-start.3
  34.6 1.6 collective-permute-start.2
  36.2 2.2 %collective-permute-done.1 = f32[72,512]{1,0:T(8,128)S(1)} collective-permute-done((f32[72,512]{1,0:T(8,128)S(1)}, f32[72,512]{1,0:T(8,128)S(1)}, u32[]{:S(2)}, u32[]{:S(2)}) %collective-permute-start.1) | collective-permute-done | bytes 147488 | tf_op jit(solution)/shard_map/ppermute | solution.py:39
  38.4 4.1 %collective-permute-done.2 = f32[72,512]{1,0:T(8,128)S(1)} collective-permute-done((f32[72,512]{1,0:T(8,128)S(1)}, f32[72,512]{1,0:T(8,128)S(1)}, u32[]{:S(2)}, u32[]{:S(2)}) %collective-permute-start.2) | collective-permute-done | bytes 147488 | tf_op jit(solution)/shard_map/ppermute | solution.py:39
  42.6 0.6 collective-permute-start.4
  43.2 1.5 collective-permute-start.5
  44.7 1.0 collective-permute-start.6
  45.8 4.4 %collective-permute-done.4 = f32[72,512]{1,0:T(8,128)S(1)} collective-permute-done((f32[72,512]{1,0:T(8,128)S(1)}, f32[72,512]{1,0:T(8,128)S(1)}, u32[]{:S(2)}, u32[]{:S(2)}) %collective-permute-start.4) | collective-permute-done | bytes 147488 | tf_op jit(solution)/shard_map/ppermute | solution.py:39
  50.3 1.4 collective-permute-done.6
  51.7 2.3 %collective-permute-start.7 = (f32[288,512]{1,0:T(8,128)S(1)}, f32[288,512]{1,0:T(8,128)S(1)}, u32[]{:S(2)}, u32[]{:S(2)}) collective-permute-start(f32[288,512]{1,0:T(8,128)S(1)} %bitcast.96), channel_id=1, source_target_pairs={{0,1},{1,0},{2,3},{3,2},{4,5},{5,4},{6,7},{7,6},{8,9},{9,8},{10,11... | collective-permute-start | bytes 1769480 | tf_op jit(solution)/shard_map/ppermute | solution.py:39
  54.0 1.5 reshape.46
  55.5 1.0 dynamic-slice_convert_fusion
  56.5 0.3 copy.14
  56.9 0.1 broadcast_in_dim.61
  57.2 2.1 fusion
  59.4 1.3 collective-permute-start.8
  60.7 1.5 collective-permute-start.10
  62.1 1.5 collective-permute-start.9
  63.7 12.2 %collective-permute-done.8 = f32[120,576]{0,1:T(8,128)} collective-permute-done((f32[120,576]{0,1:T(8,128)S(1)}, f32[120,576]{0,1:T(8,128)}, u32[]{:S(2)}, u32[]{:S(2)}) %collective-permute-start.8) | collective-permute-done | bytes 276512 | tf_op jit(solution)/shard_map/ppermute | solution.py:39
  75.9 13.6 %collective-permute-done.9 = f32[120,576]{0,1:T(8,128)} collective-permute-done((f32[120,576]{0,1:T(8,128)S(1)}, f32[120,576]{0,1:T(8,128)}, u32[]{:S(2)}, u32[]{:S(2)}) %collective-permute-start.9) | collective-permute-done | bytes 276512 | tf_op jit(solution)/shard_map/ppermute | solution.py:39
  89.5 1.2 fusion.5
  90.7 0.1 slice.22
  90.9 0.2 copy.16
  91.0 0.1 copy.17
  91.3 1.7 collective-permute-start.11
  93.0 3.3 %collective-permute-start.12 = (f32[84,576]{1,0:T(8,128)S(1)}, f32[84,576]{1,0:T(8,128)S(1)}, u32[]{:S(2)}, u32[]{:S(2)}) collective-permute-start(f32[84,576]{1,0:T(8,128)S(1)} %get-tuple-element.19), channel_id=1, source_target_pairs={{0,16},{8,24},{16,0},{24,8},{32,48},{40,56},{48,32},{56,40},{64,80... | collective-permute-start | bytes 580616 | tf_op jit(solution)/shard_map/ppermute | solution.py:39
  96.3 0.8 collective-permute-start.13
  97.1 2.9 %collective-permute-done.11 = f32[84,576]{1,0:T(8,128)S(1)} collective-permute-done((f32[84,576]{1,0:T(8,128)S(1)}, f32[84,576]{1,0:T(8,128)S(1)}, u32[]{:S(2)}, u32[]{:S(2)}) %collective-permute-start.11) | collective-permute-done | bytes 193568 | tf_op jit(solution)/shard_map/ppermute | solution.py:39
  100.0 5.7 %collective-permute-done.12 = f32[84,576]{1,0:T(8,128)S(1)} collective-permute-done((f32[84,576]{1,0:T(8,128)S(1)}, f32[84,576]{1,0:T(8,128)S(1)}, u32[]{:S(2)}, u32[]{:S(2)}) %collective-permute-start.12) | collective-permute-done | bytes 193568 | tf_op jit(solution)/shard_map/ppermute | solution.py:39
  105.8 0.6 slice.24
  106.4 1.1 collective-permute-start.15
  107.5 1.9 collective-permute-start.14
  109.5 0.7 collective-permute-start.16
  110.3 7.3 %collective-permute-done.14 = f32[72,576]{1,0:T(8,128)S(1)} collective-permute-done((f32[72,576]{1,0:T(8,128)S(1)}, f32[72,576]{1,0:T(8,128)S(1)}, u32[]{:S(2)}, u32[]{:S(2)}) %collective-permute-start.14) | collective-permute-done | bytes 165920 | tf_op jit(solution)/shard_map/ppermute | solution.py:39
  117.7 1.5 collective-permute-start.17
  119.4 1.7 collective-permute-done.17
  121.1 63.6 %inverse_factor.1.inverse_ref = f32[576,576]{1,0:T(8,128)S(1)} custom-call(f32[576,576]{1,0:T(8,128)S(1)} %bitcast.88), custom_call_target="tpu_custom_call" | custom-call | flops 2293235712 | bytes 2654208 | tf_op jit(solution)/shard_map/inverse_factor/pallas_call | solution.py:133
  184.7 1.6 fusion.21
  186.4 6.9 %mixed_tokens.1.mixed_ref = bf16[512,1536]{1,0:T(8,128)(2,1)S(1)} custom-call(f32[576,576]{1,0:T(8,128)S(1)} %inverse_factor.1.inverse_ref, f32[128,12,576]{2,1,0:T(8,128)} %all-gather.8.cloned.1.call-done.mixed_ref), custom_call_target="tpu_custom_call" | custom-call | flops 2717908992 | bytes 5111808 | tf_op jit(solution)/shard_map/mixed_tokens/pallas_call | solution.py:200
  193.2 19.0 %adam_step.1 = (f32[3696,512]{1,0:T(8,128)}, f32[32,3696]{1,0:T(8,128)}, f32[32,3696]{1,0:T(8,128)}) custom-call(s32[1]{0:T(128)} %bitcast.at_ref, bf16[512,1536]{1,0:T(8,128)(2,1)S(1)} %mixed_tokens.1.mixed_ref, bf16[512,512]{1,0:T(8,128)(2,1)S(1)} %slice.28.projector_ref, bf16[3696,1536]{1,0:T(8,128)(2,1)} %bitcast.103, bf16[16,64,3696]{2,1,0:T(8,128)(2,1)} %bitcast.104, ...), custom_call_target="tpu_custom_call" | custom-call | flops 7751073792 | bytes 28385280 | tf_op jit(solution)/shard_map/adam_step/pallas_call | solution.py:253
  (45 shorter events, 1.4 us)
Async XLA Ops:
  7.2 3.2 %copy-start = (bf16[1536,512]{1,0:T(8,128)(2,1)S(1)}, bf16[1536,512]{1,0:T(8,128)(2,1)}, u32[]{:S(2)}) copy-start(bf16[1536,512]{1,0:T(8,128)(2,1)} %input_ref.1) | copy-start | bytes 4718596
  7.2 99.2 %all-gather.6.cloned.1.call-start = ((), (), s32[]{:S(2)}) async-start(), calls=%async_computation | async-start | bytes 8077312 | tf_op jit(solution)/shard_map/all_gather | solution.py:291
  10.3 176.1 %all-gather.8.cloned.1.call-start = ((), (), s32[]{:S(2)}) async-start(), calls=%async_computation.1 | async-start | bytes 5283840 | tf_op jit(solution)/shard_map/all_gather | solution.py:319
  27.2 3.3 %collective-permute-start = (f32[288,512]{1,0:T(8,128)S(1)}, f32[288,512]{1,0:T(8,128)}, u32[]{:S(2)}, u32[]{:S(2)}) collective-permute-start(f32[288,512]{1,0:T(8,128)S(1)} %dynamic-slice_bitcast_fusion), channel_id=1, source_target_pairs={{0,1},{1,0},{2,3},{3,2},{4,5},{5,4},{6,7},{7,6},{8,9},{9,8},{10,11... | collective-permute-start | bytes 1769480 | tf_op jit(solution)/shard_map/ppermute | solution.py:39
  31.7 6.8 %collective-permute-start.1 = (f32[72,512]{1,0:T(8,128)S(1)}, f32[72,512]{1,0:T(8,128)S(1)}, u32[]{:S(2)}, u32[]{:S(2)}) collective-permute-start(f32[72,512]{1,0:T(8,128)S(1)} %get-tuple-element.21), channel_id=1, source_target_pairs={{0,2},{1,3},{2,4},{3,5},{4,6},{5,7},{6,0},{7,1},{8,10},{9,11},{10,... | collective-permute-start | bytes 442376 | tf_op jit(solution)/shard_map/ppermute | solution.py:39
  33.1 5.3 %collective-permute-start.3 = (f32[72,512]{1,0:T(8,128)S(1)}, f32[72,512]{1,0:T(8,128)S(1)}, u32[]{:S(2)}, u32[]{:S(2)}) collective-permute-start(f32[72,512]{1,0:T(8,128)S(1)} %get-tuple-element.22), channel_id=1, source_target_pairs={{0,6},{1,7},{2,0},{3,1},{4,2},{5,3},{6,4},{7,5},{8,14},{9,15},{10,... | collective-permute-start | bytes 442376 | tf_op jit(solution)/shard_map/ppermute | solution.py:39
  34.6 7.9 %collective-permute-start.2 = (f32[72,512]{1,0:T(8,128)S(1)}, f32[72,512]{1,0:T(8,128)S(1)}, u32[]{:S(2)}, u32[]{:S(2)}) collective-permute-start(f32[72,512]{1,0:T(8,128)S(1)} %get-tuple-element.23), channel_id=1, source_target_pairs={{0,4},{1,5},{2,6},{3,7},{4,0},{5,1},{6,2},{7,3},{8,12},{9,13},{10,... | collective-permute-start | bytes 442376 | tf_op jit(solution)/shard_map/ppermute | solution.py:39
  42.6 7.6 %collective-permute-start.4 = (f32[72,512]{1,0:T(8,128)S(1)}, f32[72,512]{1,0:T(8,128)S(1)}, u32[]{:S(2)}, u32[]{:S(2)}) collective-permute-start(f32[72,512]{1,0:T(8,128)S(1)} %get-tuple-element.14), channel_id=1, source_target_pairs={{0,2},{1,3},{2,4},{3,5},{4,6},{5,7},{6,0},{7,1},{8,10},{9,11},{10,... | collective-permute-start | bytes 442376 | tf_op jit(solution)/shard_map/ppermute | solution.py:39
  43.2 7.0 %collective-permute-start.5 = (f32[72,512]{1,0:T(8,128)S(1)}, f32[72,512]{1,0:T(8,128)S(1)}, u32[]{:S(2)}, u32[]{:S(2)}) collective-permute-start(f32[72,512]{1,0:T(8,128)S(1)} %get-tuple-element.14), channel_id=1, source_target_pairs={{0,4},{1,5},{2,6},{3,7},{4,0},{5,1},{6,2},{7,3},{8,12},{9,13},{10,... | collective-permute-start | bytes 442376 | tf_op jit(solution)/shard_map/ppermute | solution.py:39
  44.7 6.9 %collective-permute-start.6 = (f32[72,512]{1,0:T(8,128)S(1)}, f32[72,512]{1,0:T(8,128)S(1)}, u32[]{:S(2)}, u32[]{:S(2)}) collective-permute-start(f32[72,512]{1,0:T(8,128)S(1)} %get-tuple-element.14), channel_id=1, source_target_pairs={{0,6},{1,7},{2,0},{3,1},{4,2},{5,3},{6,4},{7,5},{8,14},{9,15},{10,... | collective-permute-start | bytes 442376 | tf_op jit(solution)/shard_map/ppermute | solution.py:39
  51.7 5.4 %collective-permute-start.7 = (f32[288,512]{1,0:T(8,128)S(1)}, f32[288,512]{1,0:T(8,128)S(1)}, u32[]{:S(2)}, u32[]{:S(2)}) collective-permute-start(f32[288,512]{1,0:T(8,128)S(1)} %bitcast.96), channel_id=1, source_target_pairs={{0,1},{1,0},{2,3},{3,2},{4,5},{5,4},{6,7},{7,6},{8,9},{9,8},{10,11... | collective-permute-start | bytes 1769480 | tf_op jit(solution)/shard_map/ppermute | solution.py:39
  59.4 16.5 %collective-permute-start.8 = (f32[120,576]{0,1:T(8,128)S(1)}, f32[120,576]{0,1:T(8,128)}, u32[]{:S(2)}, u32[]{:S(2)}) collective-permute-start(f32[120,576]{0,1:T(8,128)S(1)} %get-tuple-element.15), channel_id=1, source_target_pairs={{0,32},{8,40},{16,48},{24,56},{32,64},{40,72},{48,80},{56,88},{64,... | collective-permute-start | bytes 829448 | tf_op jit(solution)/shard_map/ppermute | solution.py:39
  60.7 15.2 %collective-permute-start.10 = (f32[120,576]{0,1:T(8,128)S(1)}, f32[120,576]{0,1:T(8,128)}, u32[]{:S(2)}, u32[]{:S(2)}) collective-permute-start(f32[120,576]{0,1:T(8,128)S(1)} %get-tuple-element.16), channel_id=1, source_target_pairs={{0,96},{8,104},{16,112},{24,120},{32,0},{40,8},{48,16},{56,24},{64... | collective-permute-start | bytes 829448 | tf_op jit(solution)/shard_map/ppermute | solution.py:39
  62.1 27.4 %collective-permute-start.9 = (f32[120,576]{0,1:T(8,128)S(1)}, f32[120,576]{0,1:T(8,128)}, u32[]{:S(2)}, u32[]{:S(2)}) collective-permute-start(f32[120,576]{0,1:T(8,128)S(1)} %get-tuple-element.17), channel_id=1, source_target_pairs={{0,64},{8,72},{16,80},{24,88},{32,96},{40,104},{48,112},{56,120},{... | collective-permute-start | bytes 829448 | tf_op jit(solution)/shard_map/ppermute | solution.py:39
  91.3 8.7 %collective-permute-start.11 = (f32[84,576]{1,0:T(8,128)S(1)}, f32[84,576]{1,0:T(8,128)S(1)}, u32[]{:S(2)}, u32[]{:S(2)}) collective-permute-start(f32[84,576]{1,0:T(8,128)S(1)} %get-tuple-element.18), channel_id=1, source_target_pairs={{0,8},{8,16},{16,24},{24,0},{32,40},{40,48},{48,56},{56,32},{64,72... | collective-permute-start | bytes 580616 | tf_op jit(solution)/shard_map/ppermute | solution.py:39
  93.0 12.7 %collective-permute-start.12 = (f32[84,576]{1,0:T(8,128)S(1)}, f32[84,576]{1,0:T(8,128)S(1)}, u32[]{:S(2)}, u32[]{:S(2)}) collective-permute-start(f32[84,576]{1,0:T(8,128)S(1)} %get-tuple-element.19), channel_id=1, source_target_pairs={{0,16},{8,24},{16,0},{24,8},{32,48},{40,56},{48,32},{56,40},{64,80... | collective-permute-start | bytes 580616 | tf_op jit(solution)/shard_map/ppermute | solution.py:39
  96.3 9.4 %collective-permute-start.13 = (f32[84,576]{1,0:T(8,128)S(1)}, f32[84,576]{1,0:T(8,128)S(1)}, u32[]{:S(2)}, u32[]{:S(2)}) collective-permute-start(f32[84,576]{1,0:T(8,128)S(1)} %get-tuple-element.20), channel_id=1, source_target_pairs={{0,24},{8,0},{16,8},{24,16},{32,56},{40,32},{48,40},{56,48},{64,88... | collective-permute-start | bytes 580616 | tf_op jit(solution)/shard_map/ppermute | solution.py:39
  106.4 11.2 %collective-permute-start.15 = (f32[72,576]{1,0:T(8,128)S(1)}, f32[72,576]{1,0:T(8,128)S(1)}, u32[]{:S(2)}, u32[]{:S(2)}) collective-permute-start(f32[72,576]{1,0:T(8,128)S(1)} %slice.23), channel_id=1, source_target_pairs={{0,4},{1,5},{2,6},{3,7},{4,0},{5,1},{6,2},{7,3},{8,12},{9,13},{10,... | collective-permute-start | bytes 497672 | tf_op jit(solution)/shard_map/ppermute | solution.py:39
  107.5 10.1 %collective-permute-start.14 = (f32[72,576]{1,0:T(8,128)S(1)}, f32[72,576]{1,0:T(8,128)S(1)}, u32[]{:S(2)}, u32[]{:S(2)}) collective-permute-start(f32[72,576]{1,0:T(8,128)S(1)} %slice.23), channel_id=1, source_target_pairs={{0,2},{1,3},{2,4},{3,5},{4,6},{5,7},{6,0},{7,1},{8,10},{9,11},{10,... | collective-permute-start | bytes 497672 | tf_op jit(solution)/shard_map/ppermute | solution.py:39
  109.5 8.2 %collective-permute-start.16 = (f32[72,576]{1,0:T(8,128)S(1)}, f32[72,576]{1,0:T(8,128)S(1)}, u32[]{:S(2)}, u32[]{:S(2)}) collective-permute-start(f32[72,576]{1,0:T(8,128)S(1)} %slice.23), channel_id=1, source_target_pairs={{0,6},{1,7},{2,0},{3,1},{4,2},{5,3},{6,4},{7,5},{8,14},{9,15},{10,... | collective-permute-start | bytes 497672 | tf_op jit(solution)/shard_map/ppermute | solution.py:39
  117.7 3.3 %collective-permute-start.17 = (f32[288,576]{1,0:T(8,128)S(1)}, f32[288,576]{1,0:T(8,128)S(1)}, u32[]{:S(2)}, u32[]{:S(2)}) collective-permute-start(f32[288,576]{1,0:T(8,128)S(1)} %bitcast.93), channel_id=1, source_target_pairs={{0,1},{1,0},{2,3},{3,2},{4,5},{5,4},{6,7},{7,6},{8,9},{9,8},{10,11... | collective-permute-start | bytes 1990664 | tf_op jit(solution)/shard_map/ppermute | solution.py:39
  186.3 6.9 %copy-start.1 = (f32[32,3696]{1,0:T(8,128)S(1)}, f32[32,3696]{1,0:T(8,128)}, u32[]{:S(2)}) copy-start(f32[32,3696]{1,0:T(8,128)} %own_second_ref.1) | copy-start | bytes 1419268
  186.3 6.9 %copy-start.2 = (f32[32,3696]{1,0:T(8,128)S(1)}, f32[32,3696]{1,0:T(8,128)}, u32[]{:S(2)}) copy-start(f32[32,3696]{1,0:T(8,128)} %own_first_ref.1) | copy-start | bytes 1419268
Sparse Core Ops, SparseCore 0:
  10.8 83.0 all-gather.5
  106.5 69.5 all-gather.7

commit v3 on v2

--- a/solution.py
+++ b/solution.py
@@ -8,9 +8,9 @@
 RANK = 512
 ADAM_STEP = 10
 BLOCK = 128
-TILE = 640
-TOKEN_TILE = 256
-MIX_TILE = 384
+TILE = 1024
+MIX_TILE = 768
+PART, STEP = 24, 16
 
 beta_one = 0.9
 beta_two = 0.999
@@ -69,24 +69,44 @@
     return jnp.take_along_axis(value, jnp.full(value.shape, k, jnp.int32), axis=1)
 
 
+def row_of(value, k):
+    return jnp.broadcast_to(value[k : k + 1], value.shape)
+
+
+def reciprocal(value):
+    guess = pl.reciprocal(value, approx=True)
+    guess = guess * (2.0 - value * guess)
+    return guess * (2.0 - value * guess)
+
+
 def invert_block(rows, lane, sub):
-    scale = [None] * len(rows)
-    for k in range(len(rows) * 8):
-        g, r = divmod(k, 8)
-        column = lane_of(rows[g], k)
-        row = jnp.broadcast_to(rows[g][r : r + 1], (8, BLOCK))
-        pivot = jnp.broadcast_to(column[r : r + 1], (8, BLOCK))
-        inverse = 1.0 / pivot
-        unit = jnp.where(lane == k, 1.0, row)
-        for h in range(g, len(rows)):
-            factor = (column if h == g else lane_of(rows[h], k)) * inverse
-            reduced = jnp.where(lane == k, 0.0, rows[h]) - factor * unit
-            if h == g:
-                rows[g] = jnp.where(sub > r, reduced, jnp.where(sub == r, unit, rows[g]))
-            else:
-                rows[h] = reduced
-        root = lax.rsqrt(pivot)
-        scale[g] = root if scale[g] is None else jnp.where(sub == r, root, scale[g])
+    rows, scale = list(rows), []
+    for g in range(len(rows)):
+        group = (lane >= 8 * g) & (lane < 8 * g + 8)
+        column = [lane_of(rows[g], 8 * g + m) for m in range(8)]
+        now = jnp.where(group, jnp.where(lane == 8 * g + sub, 1.0, 0.0), rows[g])
+        units, inverses, tops, diagonal = [], [], {}, None
+        for k in range(8):
+            pivot = row_of(column[k], k)
+            inverses.append(reciprocal(pivot))
+            units.append(row_of(now, k))
+            factor = jnp.where(sub > k, column[k] * inverses[k], 0.0)
+            for m in range(k + 1, 8):
+                tops[k, m] = row_of(column[m], k)
+                column[m] = column[m] - factor * tops[k, m]
+            now = now - factor * units[k]
+            diagonal = pivot if k == 0 else jnp.where(sub == k, pivot, diagonal)
+        rows[g] = now
+        scale.append(lax.rsqrt(diagonal))
+        for h in range(g + 1, len(rows)):
+            column = [lane_of(rows[h], 8 * g + m) for m in range(8)]
+            now = jnp.where(group, 0.0, rows[h])
+            for k in range(8):
+                factor = column[k] * inverses[k]
+                for m in range(k + 1, 8):
+                    column[m] = column[m] - factor * tops[k, m]
+                now = now - factor * units[k]
+            rows[h] = now
     return [a * b for a, b in zip(rows, scale)]
 
 
@@ -96,20 +116,19 @@
     work[:size, :size] = gram_ref[...]
     lane = lax.broadcasted_iota(jnp.int32, (8, BLOCK), 1)
     sub = lax.broadcasted_iota(jnp.int32, (8, BLOCK), 0)
-    row_in = lax.broadcasted_iota(jnp.int32, (BLOCK, BLOCK), 0)
-    lane_in = lax.broadcasted_iota(jnp.int32, (BLOCK, BLOCK), 1)
-    if padded > size:
-        last = pl.ds(padded - BLOCK, BLOCK)
-        spare = (row_in == lane_in) & (row_in >= size - (padded - BLOCK))
-        work[last, last] = jnp.where(spare, 1.0, work[last, last])
     lanes = lax.broadcasted_iota(jnp.int32, (BLOCK, padded), 1)
+
+    def diagonal_inverse(o, n):
+        rows = [work[pl.ds(pl.multiple_of(o + 8 * h, 8), 8), pl.ds(o, BLOCK)] for h in range(n // 8)]
+        inverse = jnp.concatenate(invert_block(rows, lane, sub), axis=0)
+        row_in = lax.broadcasted_iota(jnp.int32, (n, BLOCK), 0)
+        lane_in = lax.broadcasted_iota(jnp.int32, (n, BLOCK), 1)
+        return jnp.where(row_in >= lane_in, inverse, 0.0)
 
     def step(b, carry):
         o = pl.multiple_of(b * BLOCK, BLOCK)
         here = pl.ds(o, BLOCK)
-        rows = [work[pl.ds(pl.multiple_of(o + 8 * h, 8), 8), here] for h in range(BLOCK // 8)]
-        inverse = jnp.concatenate(invert_block(rows, lane, sub), axis=0)
-        inverse = jnp.where(row_in >= lane_in, inverse, 0.0)
+        inverse = diagonal_inverse(o, BLOCK)
         panel = work[here, :]
         work[:, here] = jnp.zeros((padded, BLOCK), f32)
         solved = jnp.dot(inverse, panel, precision=HIGHEST, preferred_element_type=f32)
@@ -121,7 +140,14 @@
         )
         return carry
 
-    lax.fori_loop(0, padded // BLOCK, step, 0)
+    lax.fori_loop(0, size // BLOCK, step, 0)
+    o, n = size // BLOCK * BLOCK, size % BLOCK
+    if n:
+        inverse = diagonal_inverse(o, n)
+        work[o:size, :] = jnp.dot(
+            inverse[:, :n], work[o:size, :], precision=HIGHEST, preferred_element_type=f32
+        )
+        work[o:size, o:] = inverse
     row_at = lax.broadcasted_iota(jnp.int32, (padded, padded), 0)
     lane_at = lax.broadcasted_iota(jnp.int32, (padded, padded), 1)
     out_ref[...] = jnp.where(row_at >= lane_at, work[...], 0.0)[:size, :size]
@@ -147,47 +173,30 @@
     return high, (value - high.astype(f32)).astype(bf16)
 
 
-def sketch_kernel(sketch_ref, grad_ref, input_ref, out_ref):
-    token_sketch = jnp.dot(sketch_ref[...], grad_ref[...], preferred_element_type=f32)
+def pack_kernel(first_ref, second_ref, out_ref):
+    owned = first_ref.shape[0]
+    out_ref[:owned, :] = first_ref[...].astype(out_ref.dtype)
+    out_ref[owned:, :] = second_ref[...].astype(out_ref.dtype)
+
+
+def pack(first, second):
+    owned, width = first.shape
+    return pl.pallas_call(
+        pack_kernel,
+        out_shape=jax.ShapeDtypeStruct((2 * owned, width), bf16),
+        name="pack",
+    )(first, second)
+
+
+def sketched_term(sketch_turned, grad_turned, layer_input):
+    token_sketch = jnp.dot(sketch_turned, grad_turned, preferred_element_type=f32)
     high, low = two_parts(token_sketch)
-    values = input_ref[...]
-    term = jnp.dot(high, values, preferred_element_type=f32) + jnp.dot(low, values, preferred_element_type=f32)
-
-    @pl.when(pl.program_id(0) == 0)
-    def _():
-        out_ref[...] = term
-
-    @pl.when(pl.program_id(0) > 0)
-    def _():
-        out_ref[...] += term
-
-
-def sketched_term(sketch_turned, grad_turned, layer_input):
-    columns, width = sketch_turned.shape
-    tokens, features = layer_input.shape
-    return pl.pallas_call(
-        sketch_kernel,
-        out_shape=jax.ShapeDtypeStruct((columns, features), f32),
-        grid=(tokens // TOKEN_TILE,),
-        in_specs=[
-            pl.BlockSpec((columns, width), lambda i: (0, 0)),
-            pl.BlockSpec((width, TOKEN_TILE), lambda i: (0, i)),
-            pl.BlockSpec((TOKEN_TILE, features), lambda i: (i, 0)),
-        ],
-        out_specs=pl.BlockSpec((columns, features), lambda i: (0, 0)),
-        compiler_params=pltpu.CompilerParams(vmem_limit_bytes=48 << 20),
-        cost_estimate=pl.CostEstimate(
-            flops=2 * columns * tokens * (width + 2 * features),
-            bytes_accessed=2 * width * (columns + tokens) + 2 * tokens * features + 4 * columns * features,
-            transcendentals=0,
-        ),
-        name="sketched_term",
-    )(sketch_turned, grad_turned, layer_input)
+    times = lambda part: jnp.dot(part, layer_input, preferred_element_type=f32)
+    return times(high) + times(low)
 
 
 def mix_kernel(inverse_ref, mixed_ref, out_ref):
-    values = jnp.concatenate([mixed_ref[i] for i in range(mixed_ref.shape[0])], axis=0)
-    high, low = two_parts(values)
+    high, low = two_parts(mixed_ref[...])
     inverse_high, inverse_low = two_parts(inverse_ref[...])
     times = lambda a, b: lax.dot_general(a, b, (((1,), (1,)), ((), ())), preferred_element_type=f32)
     total = times(inverse_high, low) + times(inverse_low, high) + times(inverse_high, high)
@@ -195,21 +204,20 @@
 
 
 def mixed_tokens(inverse, mixed):
-    blocks, share, columns = mixed.shape
-    group = MIX_TILE // share
+    tokens, columns = mixed.shape
     return pl.pallas_call(
         mix_kernel,
-        out_shape=jax.ShapeDtypeStruct((RANK, blocks * share), bf16),
-        grid=(blocks // group,),
+        out_shape=jax.ShapeDtypeStruct((RANK, tokens), bf16),
+        grid=(tokens // MIX_TILE,),
         in_specs=[
             pl.BlockSpec((RANK, columns), lambda i: (0, 0)),
-            pl.BlockSpec((group, share, columns), lambda i: (i, 0, 0)),
+            pl.BlockSpec((MIX_TILE, columns), lambda i: (i, 0)),
         ],
         out_specs=pl.BlockSpec((RANK, MIX_TILE), lambda i: (0, i)),
         compiler_params=pltpu.CompilerParams(vmem_limit_bytes=48 << 20),
         cost_estimate=pl.CostEstimate(
-            flops=6 * RANK * columns * blocks * share,
-            bytes_accessed=4 * blocks * share * columns + 2 * RANK * blocks * share,
+            flops=6 * RANK * columns * tokens,
+            bytes_accessed=4 * tokens * columns + 2 * RANK * tokens,
             transcendentals=0,
         ),
         name="mixed_tokens",
@@ -233,9 +241,9 @@
     first = gathered_ref[:, :owned, :].reshape(projected_ref.shape).astype(f32)
     second = gathered_ref[:, owned:, :].reshape(projected_ref.shape).astype(f32)
     new_first, new_second = moments(first, second, projected_ref[...])
-    first_hat = new_first / (1.0 - beta_one**ADAM_STEP)
-    second_hat = new_second / (1.0 - beta_two**ADAM_STEP)
-    normalized = (first_hat / (jnp.sqrt(second_hat) + adam_epsilon)).astype(bf16)
+    root = (1.0 - beta_two**ADAM_STEP) ** 0.5
+    below = jnp.sqrt(new_second) + adam_epsilon * root
+    normalized = (new_first * (root / (1.0 - beta_one**ADAM_STEP)) * pl.reciprocal(below)).astype(bf16)
     update_ref[...] = lax.dot_general(
         normalized, projector_ref[...], (((0,), (0,)), ((), ())), preferred_element_type=f32
     )
@@ -287,8 +295,7 @@
     own = columns // 8
     share = tokens // 128
     grad_turned = output_grad.T
-    both = jnp.concatenate([first_moment.astype(bf16), second_moment.astype(bf16)], axis=0)
-    gathered = lax.all_gather(both, "row", axis=0, tiled=False)
+    gathered = lax.all_gather(pack(first_moment, second_moment), "row", axis=0, tiled=False)
 
     partial = sketched_term(sketch.T, grad_turned, layer_input)
     half = scatter_sum(partial.reshape(2, columns // 2, features), "core")
@@ -299,25 +306,26 @@
     own_tokens = lax.dynamic_index_in_dim(
         layer_input.reshape(4, 4, 8, share, features), lax.axis_index("col"), 2, keepdims=False
     ).reshape(4, 4 * share, features)
-    left = jnp.concatenate(
-        [jnp.broadcast_to(owned_rows, (4, own, features)), own_tokens.astype(f32)], axis=1
-    )
-    both_terms = lax.dot_general(
-        left.reshape(4 * (own + 4 * share), features), sketched, (((1,), (1,)), ((), ())),
+    left = [[owned_rows[k * STEP : k * STEP + PART], own_tokens[k].astype(f32)] for k in range(4)]
+    terms = lax.dot_general(
+        jnp.concatenate(sum(left, []), axis=0), sketched, (((1,), (1,)), ((), ())),
         precision=HIGHEST, preferred_element_type=f32,
     )
-    both_terms = scatter_sum(both_terms.reshape(4, own + 4 * share, columns), "x")
-    both_terms = jnp.concatenate(
+    terms = scatter_sum(terms.reshape(4, PART + 4 * share, columns), "x")
+    terms = jnp.concatenate(
         [
-            jnp.broadcast_to(both_terms[:own], (4, own, columns)),
-            both_terms[own:].reshape(4, share, columns),
+            jnp.broadcast_to(terms[:PART], (4, PART, columns)),
+            terms[PART:].reshape(4, share, columns),
         ],
         axis=1,
     )
-    both_terms = scatter_sum(both_terms, "z")
-    mixed, gathered = lax.optimization_barrier((both_terms[own:], gathered))
-    mixed = lax.all_gather(mixed, ("row", "col"), axis=0, tiled=False).reshape(128, share, columns)
-    gram = gather(gather(both_terms[:own], "y").reshape(columns // 2, columns), "core")
+    terms = scatter_sum(terms, "z")
+    mixed = gather(gather(terms[PART:], "core"), "y").reshape(8 * share, columns)
+    mixed, gathered = lax.optimization_barrier((mixed, gathered))
+    mixed = lax.all_gather(mixed, "row", axis=0, tiled=True)
+    gram = gather(terms[:PART], "x")
+    gram = jnp.concatenate([gram[0, :STEP], gram[1, :STEP], gram[2, :STEP], gram[3]], axis=0)
+    gram = gather(gather(gram, "y").reshape(columns // 2, columns), "core")
 
     inverse = inverse_factor(gram.reshape(columns, columns))
     basis = jnp.dot(inverse, sketched, precision=lax.Precision.HIGH, preferred_element_type=f32)

time: 219 us -> 179 us (0.82)
  Pallas kernels: 106 us -> 51.7 us
  matrix products: 3.63 us -> 16.6 us
  starting transfers between devices: 26.9 us -> 34.4 us
  other arithmetic: 6.58 us -> 2.36 us
    pallas_call x1, Pallas kernels: 63.6 us -> 27.5 us  [inverse_factor(): pl.pallas_call(factor_kernel, out_shape=jax.ShapeDtypeStruct((size, size)...]
    pallas_call x2, Pallas kernels: 23.6 us -> 7.76 us  [the longest x1 5.77 us: mixed_tokens(): pl.pallas_call(mix_kernel, out_shape=jax.ShapeDtypeStruct((RANK, tokens),...]
    dot_general x1 -> x4, matrix products: 2.06 us -> 15 us  [the longest x1 11.2 us: sketched_term(): jnp.dot(sketch_turned, grad_turned, preferred_element_type=f32)]
    ppermute x18 -> x25, starting transfers between devices: 26.8 us -> 34.3 us  [shift(): return lax.ppermute(value, axis, pairs)]
    pallas_call x1, Pallas kernels: 19 us -> 16.4 us  [adam_step(): pl.pallas_call(step_kernel, out_shape=(jax.ShapeDtypeStruct((width, featu...]
    convert_element_type x3 -> x1, other arithmetic: 3.21 us -> 1 us  [local(): own_tokens[k].astype(f32)]
    ppermute x18 -> x25, waiting for transfers between devices: 57.4 us -> 55.3 us  [shift(): return lax.ppermute(value, axis, pairs)]
  transfers between devices with their start and end apart: 20 -> 27, of which waited for: 11 -> 14; matrix products, arithmetic and copies ran while one was open for 5% -> 12% of each run, Pallas kernels for 37% -> 15%
where the time goes in v3:
time: 179 us
  waiting for transfers between devices  55.4 us (31%)
  Pallas kernels  51.7 us (29%)
  starting transfers between devices  34.4 us (19%)
  matrix products  16.6 us (9%)
  between operations  14.7 us (8%)
  local copies, waits for them, and re-layouts  3.38 us (2%)
  other arithmetic  2.36 us (1%)
    ppermute x25, waiting for transfers between devices, shift(): return lax.ppermute(value, axis, pairs)  55.3 us
    ppermute x25, starting transfers between devices, shift(): return lax.ppermute(value, axis, pairs)  34.3 us
    pallas_call x1, Pallas kernels, inverse_factor(): pl.pallas_call(factor_kernel, out_shape=jax.ShapeDtypeStruct((size, size)...  27.5 us
    pallas_call x1, Pallas kernels, adam_step(): pl.pallas_call(step_kernel, out_shape=(jax.ShapeDtypeStruct((width, featu...  16.4 us
    dot_general x1, matrix products, sketched_term(): jnp.dot(sketch_turned, grad_turned, preferred_element_type=f32)  11.2 us
    pallas_call x1, Pallas kernels, mixed_tokens(): pl.pallas_call(mix_kernel, out_shape=jax.ShapeDtypeStruct((RANK, tokens),...  5.77 us
  transfers between devices with their start and end apart: 27, of which 14 were waited for; matrix products, arithmetic and copies ran while one was open for 12% of the time, Pallas kernels for 15%

profile of v3, /device:TPU:1, one launch (start us, length us, event | category | flops | bytes accessed | tf_op | source)
XLA Modules:
  0.0 178.5 jit_solution(12745949831374294371)
XLA Ops:
  7.2 2.0 %pack.1 = bf16[64,3696]{1,0:T(8,128)(2,1)} custom-call(f32[32,3696]{1,0:T(8,128)} %own_first_ref.1, f32[32,3696]{1,0:T(8,128)} %own_second_ref.1), custom_call_target="tpu_custom_call" | custom-call | tf_op jit(solution)/shard_map/pack/pallas_call | solution.py:184
  9.3 11.2 %fusion.19 = f32[576,1536]{1,0:T(8,128)S(1)} fusion(bf16[3696,576]{0,1:T(8,128)(2,1)} %param.7, bf16[1536,3696]{0,1:T(8,128)(2,1)} %param.6), kind=kOutput, calls=%fused_computation.78 | convolution fusion | flops 6539968512 | bytes 19150848 | tf_op jit(solution)/shard_map/dot_general | solution.py:192
  20.5 1.1 fusion
  21.6 1.1 convolution_add_fusion
  22.8 1.5 collective-permute-start
  24.3 1.8 collective-permute-done
  26.1 1.2 bitcast_add_fusion
  27.3 1.4 collective-permute-start.1
  28.7 1.5 collective-permute-start.3
  30.3 1.6 collective-permute-start.2
  31.8 1.5 reshape.61
  33.3 1.0 dynamic-slice_convert_fusion
  34.5 3.6 %collective-permute-done.2 = f32[72,512]{1,0:T(8,128)S(1)} collective-permute-done((f32[72,512]{1,0:T(8,128)S(1)}, f32[72,512]{1,0:T(8,128)S(1)}, u32[]{:S(2)}, u32[]{:S(2)}) %collective-permute-start.2) | collective-permute-done | bytes 147488 | tf_op jit(solution)/shard_map/ppermute | solution.py:39
  38.3 1.5 collective-permute-start.4
  39.8 1.4 collective-permute-start.6
  41.3 7.1 %collective-permute-done.4 = f32[72,512]{1,0:T(8,128)S(1)} collective-permute-done((f32[72,512]{1,0:T(8,128)S(1)}, f32[72,512]{1,0:T(8,128)S(1)}, u32[]{:S(2)}, u32[]{:S(2)}) %collective-permute-start.4) | collective-permute-done | bytes 147488 | tf_op jit(solution)/shard_map/ppermute | solution.py:39
  48.5 0.9 collective-permute-start.7
  49.6 1.4 collective-permute-done.7
  51.1 1.6 fusion.20
  52.7 1.3 collective-permute-start.8
  54.0 1.4 collective-permute-start.10
  55.5 1.6 collective-permute-start.9
  57.0 7.4 %collective-permute-done.8 = f32[72,576]{1,0:T(8,128)S(1)} collective-permute-done((f32[72,576]{1,0:T(8,128)S(1)}, f32[72,576]{1,0:T(8,128)S(1)}, u32[]{:S(2)}, u32[]{:S(2)}) %collective-permute-start.8) | collective-permute-done | bytes 165920 | tf_op jit(solution)/shard_map/ppermute | solution.py:39
  64.4 8.8 %collective-permute-done.9 = f32[72,576]{1,0:T(8,128)S(1)} collective-permute-done((f32[72,576]{1,0:T(8,128)S(1)}, f32[72,576]{1,0:T(8,128)S(1)}, u32[]{:S(2)}, u32[]{:S(2)}) %collective-permute-start.9) | collective-permute-done | bytes 165920 | tf_op jit(solution)/shard_map/ppermute | solution.py:39
  73.4 1.7 collective-permute-start.11
  75.1 3.3 %collective-permute-start.12 = (f32[36,576]{1,0:T(8,128)S(1)}, f32[36,576]{1,0:T(8,128)S(1)}, u32[]{:S(2)}, u32[]{:S(2)}) collective-permute-start(f32[36,576]{1,0:T(8,128)S(1)} %get-tuple-element.26), channel_id=1, source_target_pairs={{0,16},{8,24},{16,0},{24,8},{32,48},{40,56},{48,32},{56,40},{64,80... | collective-permute-start | bytes 248840 | tf_op jit(solution)/shard_map/ppermute | solution.py:39
  78.4 0.7 collective-permute-start.13
  79.1 1.6 collective-permute-done.11
  80.7 4.2 %collective-permute-done.12 = f32[36,576]{1,0:T(8,128)S(1)} collective-permute-done((f32[36,576]{1,0:T(8,128)S(1)}, f32[36,576]{1,0:T(8,128)S(1)}, u32[]{:S(2)}, u32[]{:S(2)}) %collective-permute-start.12) | collective-permute-done | bytes 82976 | tf_op jit(solution)/shard_map/ppermute | solution.py:39
  85.4 1.7 collective-permute-start.21
  87.1 0.9 collective-permute-done.21
  88.0 3.2 %collective-permute-start.24 = (f32[2,12,576]{2,1,0:T(8,128)S(1)}, f32[2,12,576]{2,1,0:T(8,128)S(1)}, u32[]{:S(2)}, u32[]{:S(2)}) collective-permute-start(f32[2,12,576]{2,1,0:T(8,128)S(1)} %bitcast_dynamic-update-slice_fusion.20), channel_id=1, source_target_pairs={{0,6},{1,7},{2,0},{3,1},{4,2},{5,3},{6,4},{7,5},{8,14},{9,15},{10,... | collective-permute-start | bytes 165896 | tf_op jit(solution)/shard_map/ppermute | solution.py:39
  91.5 0.7 collective-permute-start.22
  92.3 6.2 %collective-permute-done.22 = f32[2,12,576]{2,1,0:T(8,128)S(1)} collective-permute-done((f32[2,12,576]{2,1,0:T(8,128)S(1)}, f32[2,12,576]{2,1,0:T(8,128)S(1)}, u32[]{:S(2)}, u32[]{:S(2)}) %collective-permute-start.22) | collective-permute-done | bytes 55328 | tf_op jit(solution)/shard_map/ppermute | solution.py:39
  98.6 0.7 reshape.67
  99.4 0.7 collective-permute-start.15
  100.2 0.8 collective-permute-start.14
  100.9 1.9 %collective-permute-start.16 = (f32[24,576]{1,0:T(8,128)S(1)}, f32[24,576]{1,0:T(8,128)S(1)}, u32[]{:S(2)}, u32[]{:S(2)}) collective-permute-start(f32[24,576]{1,0:T(8,128)S(1)} %slice.79), channel_id=1, source_target_pairs={{0,96},{8,104},{16,112},{24,120},{32,0},{40,8},{48,16},{56,24},{64... | collective-permute-start | bytes 165896 | tf_op jit(solution)/shard_map/ppermute | solution.py:39
  102.9 2.2 %collective-permute-done.14 = f32[24,576]{1,0:T(8,128)S(1)} collective-permute-done((f32[24,576]{1,0:T(8,128)S(1)}, f32[24,576]{1,0:T(8,128)S(1)}, u32[]{:S(2)}, u32[]{:S(2)}) %collective-permute-start.14) | collective-permute-done | bytes 55328 | tf_op jit(solution)/shard_map/ppermute | solution.py:39
  105.3 0.5 collective-permute-start.18
  105.7 2.2 %collective-permute-start.19 = (f32[72,576]{1,0:T(8,128)S(1)}, f32[72,576]{1,0:T(8,128)S(1)}, u32[]{:S(2)}, u32[]{:S(2)}) collective-permute-start(f32[72,576]{1,0:T(8,128)S(1)} %pad_maximum_fusion), channel_id=1, source_target_pairs={{0,6},{1,7},{2,0},{3,1},{4,2},{5,3},{6,4},{7,5},{8,14},{9,15},{10,... | collective-permute-start | bytes 497672 | tf_op jit(solution)/shard_map/ppermute | solution.py:39
  108.0 8.1 %collective-permute-done.17 = f32[72,576]{1,0:T(8,128)S(1)} collective-permute-done((f32[72,576]{1,0:T(8,128)S(1)}, f32[72,576]{1,0:T(8,128)S(1)}, u32[]{:S(2)}, u32[]{:S(2)}) %collective-permute-start.17) | collective-permute-done | bytes 165920 | tf_op jit(solution)/shard_map/ppermute | solution.py:39
  116.2 2.2 %collective-permute-start.20 = (f32[288,576]{1,0:T(8,128)S(1)}, f32[288,576]{1,0:T(8,128)S(1)}, u32[]{:S(2)}, u32[]{:S(2)}) collective-permute-start(f32[288,576]{1,0:T(8,128)S(1)} %bitcast.123), channel_id=1, source_target_pairs={{0,1},{1,0},{2,3},{3,2},{4,5},{5,4},{6,7},{7,6},{8,9},{9,8},{10,11... | collective-permute-start | bytes 1990664 | tf_op jit(solution)/shard_map/ppermute | solution.py:39
  118.6 1.7 collective-permute-done.20
  120.3 27.5 %inverse_factor.1.inverse_ref = f32[576,576]{1,0:T(8,128)S(1)} custom-call(f32[576,576]{1,0:T(8,128)S(1)} %bitcast.118), custom_call_target="tpu_custom_call" | custom-call | flops 2293235712 | bytes 2654208 | tf_op jit(solution)/shard_map/inverse_factor/pallas_call | solution.py:159
  147.8 1.6 fusion.21
  149.5 5.8 %mixed_tokens.1.mixed_ref = bf16[512,1536]{1,0:T(8,128)(2,1)S(1)} custom-call(f32[576,576]{1,0:T(8,128)S(1)} %inverse_factor.1.inverse_ref, f32[1536,576]{1,0:T(8,128)} %all-gather.4.cloned.1.call-done.mixed_ref), custom_call_target="tpu_custom_call" | custom-call | flops 2717908992 | bytes 5111808 | tf_op jit(solution)/shard_map/mixed_tokens/pallas_call | solution.py:208
  155.3 16.4 %adam_step.1 = (f32[3696,512]{1,0:T(8,128)}, f32[32,3696]{1,0:T(8,128)}, f32[32,3696]{1,0:T(8,128)}) custom-call(s32[1]{0:T(128)} %bitcast.at_ref, bf16[512,1536]{1,0:T(8,128)(2,1)S(1)} %mixed_tokens.1.mixed_ref, bf16[512,512]{1,0:T(8,128)(2,1)S(1)} %slice.97.projector_ref, bf16[3696,1536]{1,0:T(8,128)(2,1)} %bitcast.130, bf16[16,64,3696]{2,1,0:T(8,128)(2,1)} %bitcast.131, ...), custom_call_target="tpu_custom_call" | custom-call | flops 7751073792 | bytes 28385280 | tf_op jit(solution)/shard_map/adam_step/pallas_call | solution.py:261
  (84 shorter events, 2.4 us)
Async XLA Ops:
  7.2 92.2 %all-gather.6.cloned.1.call-start = ((), (), s32[]{:S(2)}) async-start(), calls=%async_computation.1 | async-start | bytes 8077312 | tf_op jit(solution)/shard_map/all_gather | solution.py:298
  9.2 140.3 %all-gather.4.cloned.1.call-start = ((), (), s32[]{:S(2)}) async-start(), calls=%async_computation | async-start | bytes 4177920 | tf_op jit(solution)/shard_map/all_gather | solution.py:325
  9.3 11.2 %copy-start.2 = (bf16[1536,512]{1,0:T(8,128)(2,1)S(1)}, bf16[1536,512]{1,0:T(8,128)(2,1)}, u32[]{:S(2)}) copy-start(bf16[1536,512]{1,0:T(8,128)(2,1)} %param.5) | copy-start | bytes 4718596
  22.8 3.3 %collective-permute-start = (f32[288,512]{1,0:T(8,128)S(1)}, f32[288,512]{1,0:T(8,128)}, u32[]{:S(2)}, u32[]{:S(2)}) collective-permute-start(f32[288,512]{1,0:T(8,128)S(1)} %dynamic-slice_bitcast_fusion), channel_id=1, source_target_pairs={{0,1},{1,0},{2,3},{3,2},{4,5},{5,4},{6,7},{7,6},{8,9},{9,8},{10,11... | collective-permute-start | bytes 1769480 | tf_op jit(solution)/shard_map/ppermute | solution.py:39
  27.3 7.2 %collective-permute-start.1 = (f32[72,512]{1,0:T(8,128)S(1)}, f32[72,512]{1,0:T(8,128)S(1)}, u32[]{:S(2)}, u32[]{:S(2)}) collective-permute-start(f32[72,512]{1,0:T(8,128)S(1)} %get-tuple-element.22), channel_id=1, source_target_pairs={{0,2},{1,3},{2,4},{3,5},{4,6},{5,7},{6,0},{7,1},{8,10},{9,11},{10,... | collective-permute-start | bytes 442376 | tf_op jit(solution)/shard_map/ppermute | solution.py:39
  28.7 5.7 %collective-permute-start.3 = (f32[72,512]{1,0:T(8,128)S(1)}, f32[72,512]{1,0:T(8,128)S(1)}, u32[]{:S(2)}, u32[]{:S(2)}) collective-permute-start(f32[72,512]{1,0:T(8,128)S(1)} %get-tuple-element.23), channel_id=1, source_target_pairs={{0,6},{1,7},{2,0},{3,1},{4,2},{5,3},{6,4},{7,5},{8,14},{9,15},{10,... | collective-permute-start | bytes 442376 | tf_op jit(solution)/shard_map/ppermute | solution.py:39
  30.3 7.9 %collective-permute-start.2 = (f32[72,512]{1,0:T(8,128)S(1)}, f32[72,512]{1,0:T(8,128)S(1)}, u32[]{:S(2)}, u32[]{:S(2)}) collective-permute-start(f32[72,512]{1,0:T(8,128)S(1)} %get-tuple-element.24), channel_id=1, source_target_pairs={{0,4},{1,5},{2,6},{3,7},{4,0},{5,1},{6,2},{7,3},{8,12},{9,13},{10,... | collective-permute-start | bytes 442376 | tf_op jit(solution)/shard_map/ppermute | solution.py:39
  38.2 10.1 %collective-permute-start.5 = (f32[72,512]{1,0:T(8,128)S(1)}, f32[72,512]{1,0:T(8,128)S(1)}, u32[]{:S(2)}, u32[]{:S(2)}) collective-permute-start(f32[72,512]{1,0:T(8,128)S(1)} %get-tuple-element.14), channel_id=1, source_target_pairs={{0,4},{1,5},{2,6},{3,7},{4,0},{5,1},{6,2},{7,3},{8,12},{9,13},{10,... | collective-permute-start | bytes 442376 | tf_op jit(solution)/shard_map/ppermute | solution.py:39
  38.3 10.0 %collective-permute-start.4 = (f32[72,512]{1,0:T(8,128)S(1)}, f32[72,512]{1,0:T(8,128)S(1)}, u32[]{:S(2)}, u32[]{:S(2)}) collective-permute-start(f32[72,512]{1,0:T(8,128)S(1)} %get-tuple-element.14), channel_id=1, source_target_pairs={{0,2},{1,3},{2,4},{3,5},{4,6},{5,7},{6,0},{7,1},{8,10},{9,11},{10,... | collective-permute-start | bytes 442376 | tf_op jit(solution)/shard_map/ppermute | solution.py:39
  39.8 8.6 %collective-permute-start.6 = (f32[72,512]{1,0:T(8,128)S(1)}, f32[72,512]{1,0:T(8,128)S(1)}, u32[]{:S(2)}, u32[]{:S(2)}) collective-permute-start(f32[72,512]{1,0:T(8,128)S(1)} %get-tuple-element.14), channel_id=1, source_target_pairs={{0,6},{1,7},{2,0},{3,1},{4,2},{5,3},{6,4},{7,5},{8,14},{9,15},{10,... | collective-permute-start | bytes 442376 | tf_op jit(solution)/shard_map/ppermute | solution.py:39
  48.5 2.6 %collective-permute-start.7 = (f32[288,512]{1,0:T(8,128)S(1)}, f32[288,512]{1,0:T(8,128)S(1)}, u32[]{:S(2)}, u32[]{:S(2)}) collective-permute-start(f32[288,512]{1,0:T(8,128)S(1)} %bitcast.125), channel_id=1, source_target_pairs={{0,1},{1,0},{2,3},{3,2},{4,5},{5,4},{6,7},{7,6},{8,9},{9,8},{10,11... | collective-permute-start | bytes 1769480 | tf_op jit(solution)/shard_map/ppermute | solution.py:39
  52.7 11.7 %collective-permute-start.8 = (f32[72,576]{1,0:T(8,128)S(1)}, f32[72,576]{1,0:T(8,128)S(1)}, u32[]{:S(2)}, u32[]{:S(2)}) collective-permute-start(f32[72,576]{1,0:T(8,128)S(1)} %get-tuple-element.19), channel_id=1, source_target_pairs={{0,32},{8,40},{16,48},{24,56},{32,64},{40,72},{48,80},{56,88},{64,... | collective-permute-start | bytes 497672 | tf_op jit(solution)/shard_map/ppermute | solution.py:39
  54.0 10.4 %collective-permute-start.10 = (f32[72,576]{1,0:T(8,128)S(1)}, f32[72,576]{1,0:T(8,128)S(1)}, u32[]{:S(2)}, u32[]{:S(2)}) collective-permute-start(f32[72,576]{1,0:T(8,128)S(1)} %get-tuple-element.20), channel_id=1, source_target_pairs={{0,96},{8,104},{16,112},{24,120},{32,0},{40,8},{48,16},{56,24},{64... | collective-permute-start | bytes 497672 | tf_op jit(solution)/shard_map/ppermute | solution.py:39
  55.5 17.8 %collective-permute-start.9 = (f32[72,576]{1,0:T(8,128)S(1)}, f32[72,576]{1,0:T(8,128)S(1)}, u32[]{:S(2)}, u32[]{:S(2)}) collective-permute-start(f32[72,576]{1,0:T(8,128)S(1)} %get-tuple-element.21), channel_id=1, source_target_pairs={{0,64},{8,72},{16,80},{24,88},{32,96},{40,104},{48,112},{56,120},{... | collective-permute-start | bytes 497672 | tf_op jit(solution)/shard_map/ppermute | solution.py:39
  73.4 7.3 %collective-permute-start.11 = (f32[36,576]{1,0:T(8,128)S(1)}, f32[36,576]{1,0:T(8,128)S(1)}, u32[]{:S(2)}, u32[]{:S(2)}) collective-permute-start(f32[36,576]{1,0:T(8,128)S(1)} %get-tuple-element.25), channel_id=1, source_target_pairs={{0,8},{8,16},{16,24},{24,0},{32,40},{40,48},{48,56},{56,32},{64,72... | collective-permute-start | bytes 248840 | tf_op jit(solution)/shard_map/ppermute | solution.py:39
  75.1 9.9 %collective-permute-start.12 = (f32[36,576]{1,0:T(8,128)S(1)}, f32[36,576]{1,0:T(8,128)S(1)}, u32[]{:S(2)}, u32[]{:S(2)}) collective-permute-start(f32[36,576]{1,0:T(8,128)S(1)} %get-tuple-element.26), channel_id=1, source_target_pairs={{0,16},{8,24},{16,0},{24,8},{32,48},{40,56},{48,32},{56,40},{64,80... | collective-permute-start | bytes 248840 | tf_op jit(solution)/shard_map/ppermute | solution.py:39
  78.4 7.0 %collective-permute-start.13 = (f32[36,576]{1,0:T(8,128)S(1)}, f32[36,576]{1,0:T(8,128)S(1)}, u32[]{:S(2)}, u32[]{:S(2)}) collective-permute-start(f32[36,576]{1,0:T(8,128)S(1)} %get-tuple-element.27), channel_id=1, source_target_pairs={{0,24},{8,0},{16,8},{24,16},{32,56},{40,32},{48,40},{56,48},{64,88... | collective-permute-start | bytes 248840 | tf_op jit(solution)/shard_map/ppermute | solution.py:39
  85.4 2.6 %collective-permute-start.21 = (f32[12,576]{1,0:T(8,128)S(1)}, f32[12,576]{1,0:T(8,128)S(1)}, u32[]{:S(2)}, u32[]{:S(2)}) collective-permute-start(f32[12,576]{1,0:T(8,128)S(1)} %slice.84), channel_id=1, source_target_pairs={{0,1},{1,0},{2,3},{3,2},{4,5},{5,4},{6,7},{7,6},{8,9},{9,8},{10,11... | collective-permute-start | bytes 82952 | tf_op jit(solution)/shard_map/ppermute | solution.py:39
  88.0 10.6 %collective-permute-start.24 = (f32[2,12,576]{2,1,0:T(8,128)S(1)}, f32[2,12,576]{2,1,0:T(8,128)S(1)}, u32[]{:S(2)}, u32[]{:S(2)}) collective-permute-start(f32[2,12,576]{2,1,0:T(8,128)S(1)} %bitcast_dynamic-update-slice_fusion.20), channel_id=1, source_target_pairs={{0,6},{1,7},{2,0},{3,1},{4,2},{5,3},{6,4},{7,5},{8,14},{9,15},{10,... | collective-permute-start | bytes 165896 | tf_op jit(solution)/shard_map/ppermute | solution.py:39
  91.2 7.3 %collective-permute-start.23 = (f32[2,12,576]{2,1,0:T(8,128)S(1)}, f32[2,12,576]{2,1,0:T(8,128)S(1)}, u32[]{:S(2)}, u32[]{:S(2)}) collective-permute-start(f32[2,12,576]{2,1,0:T(8,128)S(1)} %bitcast_dynamic-update-slice_fusion.20), channel_id=1, source_target_pairs={{0,4},{1,5},{2,6},{3,7},{4,0},{5,1},{6,2},{7,3},{8,12},{9,13},{10,... | collective-permute-start | bytes 165896 | tf_op jit(solution)/shard_map/ppermute | solution.py:39
  91.5 7.0 %collective-permute-start.22 = (f32[2,12,576]{2,1,0:T(8,128)S(1)}, f32[2,12,576]{2,1,0:T(8,128)S(1)}, u32[]{:S(2)}, u32[]{:S(2)}) collective-permute-start(f32[2,12,576]{2,1,0:T(8,128)S(1)} %bitcast_dynamic-update-slice_fusion.20), channel_id=1, source_target_pairs={{0,2},{1,3},{2,4},{3,5},{4,6},{5,7},{6,0},{7,1},{8,10},{9,11},{10,... | collective-permute-start | bytes 165896 | tf_op jit(solution)/shard_map/ppermute | solution.py:39
  99.4 5.6 %collective-permute-start.15 = (f32[24,576]{1,0:T(8,128)S(1)}, f32[24,576]{1,0:T(8,128)S(1)}, u32[]{:S(2)}, u32[]{:S(2)}) collective-permute-start(f32[24,576]{1,0:T(8,128)S(1)} %slice.79), channel_id=1, source_target_pairs={{0,64},{8,72},{16,80},{24,88},{32,96},{40,104},{48,112},{56,120},{... | collective-permute-start | bytes 165896 | tf_op jit(solution)/shard_map/ppermute | solution.py:39
  100.2 4.9 %collective-permute-start.14 = (f32[24,576]{1,0:T(8,128)S(1)}, f32[24,576]{1,0:T(8,128)S(1)}, u32[]{:S(2)}, u32[]{:S(2)}) collective-permute-start(f32[24,576]{1,0:T(8,128)S(1)} %slice.79), channel_id=1, source_target_pairs={{0,32},{8,40},{16,48},{24,56},{32,64},{40,72},{48,80},{56,88},{64,... | collective-permute-start | bytes 165896 | tf_op jit(solution)/shard_map/ppermute | solution.py:39
  100.9 4.2 %collective-permute-start.16 = (f32[24,576]{1,0:T(8,128)S(1)}, f32[24,576]{1,0:T(8,128)S(1)}, u32[]{:S(2)}, u32[]{:S(2)}) collective-permute-start(f32[24,576]{1,0:T(8,128)S(1)} %slice.79), channel_id=1, source_target_pairs={{0,96},{8,104},{16,112},{24,120},{32,0},{40,8},{48,16},{56,24},{64... | collective-permute-start | bytes 165896 | tf_op jit(solution)/shard_map/ppermute | solution.py:39
  105.2 10.9 %collective-permute-start.17 = (f32[72,576]{1,0:T(8,128)S(1)}, f32[72,576]{1,0:T(8,128)S(1)}, u32[]{:S(2)}, u32[]{:S(2)}) collective-permute-start(f32[72,576]{1,0:T(8,128)S(1)} %pad_maximum_fusion), channel_id=1, source_target_pairs={{0,2},{1,3},{2,4},{3,5},{4,6},{5,7},{6,0},{7,1},{8,10},{9,11},{10,... | collective-permute-start | bytes 497672 | tf_op jit(solution)/shard_map/ppermute | solution.py:39
  105.3 10.9 %collective-permute-start.18 = (f32[72,576]{1,0:T(8,128)S(1)}, f32[72,576]{1,0:T(8,128)S(1)}, u32[]{:S(2)}, u32[]{:S(2)}) collective-permute-start(f32[72,576]{1,0:T(8,128)S(1)} %pad_maximum_fusion), channel_id=1, source_target_pairs={{0,4},{1,5},{2,6},{3,7},{4,0},{5,1},{6,2},{7,3},{8,12},{9,13},{10,... | collective-permute-start | bytes 497672 | tf_op jit(solution)/shard_map/ppermute | solution.py:39
  105.7 10.4 %collective-permute-start.19 = (f32[72,576]{1,0:T(8,128)S(1)}, f32[72,576]{1,0:T(8,128)S(1)}, u32[]{:S(2)}, u32[]{:S(2)}) collective-permute-start(f32[72,576]{1,0:T(8,128)S(1)} %pad_maximum_fusion), channel_id=1, source_target_pairs={{0,6},{1,7},{2,0},{3,1},{4,2},{5,3},{6,4},{7,5},{8,14},{9,15},{10,... | collective-permute-start | bytes 497672 | tf_op jit(solution)/shard_map/ppermute | solution.py:39
  116.2 4.1 %collective-permute-start.20 = (f32[288,576]{1,0:T(8,128)S(1)}, f32[288,576]{1,0:T(8,128)S(1)}, u32[]{:S(2)}, u32[]{:S(2)}) collective-permute-start(f32[288,576]{1,0:T(8,128)S(1)} %bitcast.123), channel_id=1, source_target_pairs={{0,1},{1,0},{2,3},{3,2},{4,5},{5,4},{6,7},{7,6},{8,9},{9,8},{10,11... | collective-permute-start | bytes 1990664 | tf_op jit(solution)/shard_map/ppermute | solution.py:39
  149.5 5.8 %copy-start = (f32[32,3696]{1,0:T(8,128)S(1)}, f32[32,3696]{1,0:T(8,128)}, u32[]{:S(2)}) copy-start(f32[32,3696]{1,0:T(8,128)} %own_first_ref.1) | copy-start | bytes 1419268
  149.5 5.8 %copy-start.1 = (f32[32,3696]{1,0:T(8,128)S(1)}, f32[32,3696]{1,0:T(8,128)}, u32[]{:S(2)}) copy-start(f32[32,3696]{1,0:T(8,128)} %own_second_ref.1) | copy-start | bytes 1419268
Sparse Core Ops, SparseCore 0:
  10.8 78.3 all-gather.5
  99.5 46.3 all-gather.3

commit v4 on v3

--- a/solution.py
+++ b/solution.py
@@ -8,8 +8,9 @@
 RANK = 512
 ADAM_STEP = 10
 BLOCK = 128
-TILE = 1024
-MIX_TILE = 768
+TILE = 512
+MIX_TILE = 512
+STEP_VMEM = 30 << 20
 PART, STEP = 24, 16
 
 beta_one = 0.9
@@ -39,13 +40,13 @@
     return lax.ppermute(value, axis, pairs)
 
 
-def scatter_sum(value, sub):
+def scatter_sum(value, sub, wire=f32):
     n, me = EXTENT[sub], place(sub)
     pick = lambda k: lax.dynamic_index_in_dim(value, (me + k) % n, 0, keepdims=False)
-    got = [shift(pick(k), sub, k) for k in range(1, n)]
+    got = [shift(pick(k).astype(wire), sub, k) for k in range(1, n)]
     total = pick(0)
     for term in got:
-        total = total + term
+        total = total + term.astype(value.dtype)
     return total
 
 
@@ -56,13 +57,6 @@
     for k in range(n):
         out = lax.dynamic_update_index_in_dim(out, got[k], (me - k) % n, 0)
     return out
-
-
-def full_sum(value, sub):
-    total = value
-    for k in range(1, EXTENT[sub]):
-        total = total + shift(value, sub, k)
-    return total
 
 
 def lane_of(value, k):
@@ -190,38 +184,10 @@
 
 def sketched_term(sketch_turned, grad_turned, layer_input):
     token_sketch = jnp.dot(sketch_turned, grad_turned, preferred_element_type=f32)
-    high, low = two_parts(token_sketch)
+    rounded = lax.reduce_precision(token_sketch, 8, 7)
+    high, low = rounded.astype(bf16), (token_sketch - rounded).astype(bf16)
     times = lambda part: jnp.dot(part, layer_input, preferred_element_type=f32)
     return times(high) + times(low)
-
-
-def mix_kernel(inverse_ref, mixed_ref, out_ref):
-    high, low = two_parts(mixed_ref[...])
-    inverse_high, inverse_low = two_parts(inverse_ref[...])
-    times = lambda a, b: lax.dot_general(a, b, (((1,), (1,)), ((), ())), preferred_element_type=f32)
-    total = times(inverse_high, low) + times(inverse_low, high) + times(inverse_high, high)
-    out_ref[...] = total.astype(out_ref.dtype)
-
-
-def mixed_tokens(inverse, mixed):
-    tokens, columns = mixed.shape
-    return pl.pallas_call(
-        mix_kernel,
-        out_shape=jax.ShapeDtypeStruct((RANK, tokens), bf16),
-        grid=(tokens // MIX_TILE,),
-        in_specs=[
-            pl.BlockSpec((RANK, columns), lambda i: (0, 0)),
-            pl.BlockSpec((MIX_TILE, columns), lambda i: (i, 0)),
-        ],
-        out_specs=pl.BlockSpec((RANK, MIX_TILE), lambda i: (0, i)),
-        compiler_params=pltpu.CompilerParams(vmem_limit_bytes=48 << 20),
-        cost_estimate=pl.CostEstimate(
-            flops=6 * RANK * columns * tokens,
-            bytes_accessed=4 * tokens * columns + 2 * RANK * tokens,
-            transcendentals=0,
-        ),
-        name="mixed_tokens",
-    )(inverse, mixed)
 
 
 def moments(first, second, projected):
@@ -231,11 +197,27 @@
 
 
 def step_kernel(
-    at_ref, mixed_ref, projector_ref, grad_ref, gathered_ref, own_first_ref, own_second_ref,
-    update_ref, new_first_ref, new_second_ref, projected_ref,
+    at_ref, inverse_ref, sketched_ref, mixed_ref, grad_ref, gathered_ref, own_first_ref, own_second_ref,
+    update_ref, new_first_ref, new_second_ref, projector_ref, turned_ref, projected_ref,
 ):
+    @pl.when(pl.program_id(0) == 0)
+    def _():
+        high, low = two_parts(inverse_ref[...])
+        values = sketched_ref[...]
+        projector_ref[...] = (
+            jnp.dot(low, values, preferred_element_type=f32)
+            + jnp.dot(high, values, preferred_element_type=f32)
+        ).astype(bf16)
+        times = lambda a, b: lax.dot_general(a, b, (((1,), (1,)), ((), ())), preferred_element_type=f32)
+        for o in range(0, mixed_ref.shape[0], MIX_TILE):
+            here = pl.ds(o, MIX_TILE)
+            mixed_high, mixed_low = two_parts(mixed_ref[here, :])
+            turned_ref[:, here] = (
+                times(high, mixed_low) + times(low, mixed_high) + times(high, mixed_high)
+            ).astype(bf16)
+
     projected_ref[...] = lax.dot_general(
-        mixed_ref[...], grad_ref[...], (((1,), (1,)), ((), ())), preferred_element_type=f32
+        turned_ref[...], grad_ref[...], (((1,), (1,)), ((), ())), preferred_element_type=f32
     )
     owned = own_first_ref.shape[0]
     first = gathered_ref[:, :owned, :].reshape(projected_ref.shape).astype(f32)
@@ -251,13 +233,13 @@
     new_first_ref[...], new_second_ref[...] = moments(own_first_ref[...], own_second_ref[...], mine)
 
 
-def adam_step(at, mixed, projector, grad_turned, gathered, own_first, own_second):
+def adam_step(at, inverse, sketched, mixed, grad_turned, gathered, own_first, own_second):
     width, tokens = grad_turned.shape
-    rank, features = projector.shape
+    columns, features = sketched.shape
     owned = own_first.shape[0]
-    whole = lambda shape: pl.BlockSpec(shape, lambda i, at: (0, 0))
+    whole = lambda shape: pl.BlockSpec(shape, lambda i, at: (0, 0), pipeline_mode=pl.Buffered(1))
     strip = lambda rows: pl.BlockSpec((rows, TILE), lambda i, at: (0, i))
-    turned = lambda columns: pl.BlockSpec((TILE, columns), lambda i, at: (i, 0))
+    turned = lambda across: pl.BlockSpec((TILE, across), lambda i, at: (i, 0))
     return pl.pallas_call(
         step_kernel,
         out_shape=(
@@ -269,24 +251,29 @@
             num_scalar_prefetch=1,
             grid=(pl.cdiv(width, TILE),),
             in_specs=[
-                whole((rank, tokens)),
-                whole((rank, features)),
+                whole((RANK, columns)),
+                whole((columns, features)),
+                whole((tokens, columns)),
                 turned(tokens),
-                pl.BlockSpec((rank // owned, 2 * owned, TILE), lambda i, at: (0, 0, i)),
+                pl.BlockSpec((RANK // owned, 2 * owned, TILE), lambda i, at: (0, 0, i)),
                 strip(owned),
                 strip(owned),
             ],
             out_specs=[turned(features), strip(owned), strip(owned)],
-            scratch_shapes=[pltpu.VMEM((rank, TILE), f32)],
+            scratch_shapes=[
+                pltpu.VMEM((RANK, features), bf16),
+                pltpu.VMEM((RANK, tokens), bf16),
+                pltpu.VMEM((RANK, TILE), f32),
+            ],
         ),
-        compiler_params=pltpu.CompilerParams(vmem_limit_bytes=48 << 20),
+        compiler_params=pltpu.CompilerParams(vmem_limit_bytes=STEP_VMEM),
         cost_estimate=pl.CostEstimate(
-            flops=2 * rank * width * (tokens + features),
-            bytes_accessed=width * (2 * tokens + 4 * rank + 4 * features + 16 * owned),
-            transcendentals=rank * width,
+            flops=2 * RANK * width * (tokens + features) + 6 * RANK * columns * tokens,
+            bytes_accessed=width * (2 * tokens + 4 * RANK + 4 * features + 16 * owned) + 4 * tokens * columns,
+            transcendentals=RANK * width,
         ),
         name="adam_step",
-    )(at, mixed, projector, grad_turned, gathered, own_first, own_second)
+    )(at, inverse, sketched, mixed, grad_turned, gathered, own_first, own_second)
 
 
 def local(layer_input, output_grad, sketch, first_moment, second_moment):
@@ -298,18 +285,18 @@
     gathered = lax.all_gather(pack(first_moment, second_moment), "row", axis=0, tiled=False)
 
     partial = sketched_term(sketch.T, grad_turned, layer_input)
-    half = scatter_sum(partial.reshape(2, columns // 2, features), "core")
-    owned_rows = scatter_sum(half.reshape(4, own, features), "y")
+    half = scatter_sum(partial.reshape(2, columns // 2, features), "core", bf16)
+    owned_rows = scatter_sum(half.reshape(4, own, features), "y", bf16).astype(bf16)
     sketched = gather(gather(owned_rows, "y").reshape(columns // 2, features), "core")
     sketched = sketched.reshape(columns, features)
 
     own_tokens = lax.dynamic_index_in_dim(
         layer_input.reshape(4, 4, 8, share, features), lax.axis_index("col"), 2, keepdims=False
     ).reshape(4, 4 * share, features)
-    left = [[owned_rows[k * STEP : k * STEP + PART], own_tokens[k].astype(f32)] for k in range(4)]
+    left = [[owned_rows[k * STEP : k * STEP + PART], own_tokens[k]] for k in range(4)]
     terms = lax.dot_general(
         jnp.concatenate(sum(left, []), axis=0), sketched, (((1,), (1,)), ((), ())),
-        precision=HIGHEST, preferred_element_type=f32,
+        preferred_element_type=f32,
     )
     terms = scatter_sum(terms.reshape(4, PART + 4 * share, columns), "x")
     terms = jnp.concatenate(
@@ -328,12 +315,9 @@
     gram = gather(gather(gram, "y").reshape(columns // 2, columns), "core")
 
     inverse = inverse_factor(gram.reshape(columns, columns))
-    basis = jnp.dot(inverse, sketched, precision=lax.Precision.HIGH, preferred_element_type=f32)
-    projector = basis[:RANK].astype(bf16)
-    turned_mixed = mixed_tokens(inverse, mixed)
     at = lax.axis_index("row").astype(jnp.int32).reshape(1)
     update, new_first, new_second = adam_step(
-        at, turned_mixed, projector, grad_turned, gathered, first_moment, second_moment
+        at, inverse, sketched, mixed, grad_turned, gathered, first_moment, second_moment
     )
     return update.T, new_first, new_second
 

time: 179 us -> 177 us (0.989)
  waiting for transfers between devices: 55.4 us -> 46.4 us
  local copies, waits for them, and re-layouts: 3.38 us -> 9.36 us
  starting transfers between devices: 34.4 us -> 40.1 us
  matrix products: 16.6 us -> 13.9 us
  other arithmetic: 2.36 us -> 0.29 us
    ppermute x25, waiting for transfers between devices: 55.3 us -> 46.3 us  [shift(): return lax.ppermute(value, axis, pairs)]
    pallas_call x1, Pallas kernels: 16.4 us -> 22.8 us  [adam_step(): pl.pallas_call(step_kernel, out_shape=(jax.ShapeDtypeStruct((width, featu...]
    pallas_call x1 -> x0, Pallas kernels: 5.77 us -> none  [mixed_tokens(): pl.pallas_call(mix_kernel, out_shape=jax.ShapeDtypeStruct((RANK, tokens),...]
    ppermute x25, starting transfers between devices: 34.3 us -> 40.1 us  [shift(): return lax.ppermute(value, axis, pairs)]
    unnamed x13 -> x17, local copies, waits for them, and re-layouts: 0.07 us -> 5.31 us
  transfers between devices with their start and end apart: 27 -> 27, of which waited for: 14 -> 15; matrix products, arithmetic and copies ran while one was open for 12% -> 10% of each run, Pallas kernels for 15% -> 16%
where the time goes in v4:
time: 177 us
  Pallas kernels  52.3 us (30%)
  waiting for transfers between devices  46.4 us (26%)
  starting transfers between devices  40.1 us (23%)
  between operations  14.7 us (8%)
  matrix products  13.9 us (8%)
  local copies, waits for them, and re-layouts  9.36 us (5%)
    ppermute x25, waiting for transfers between devices, shift(): return lax.ppermute(value, axis, pairs)  46.3 us
    ppermute x25, starting transfers between devices, shift(): return lax.ppermute(value, axis, pairs)  40.1 us
    pallas_call x1, Pallas kernels, inverse_factor(): pl.pallas_call(factor_kernel, out_shape=jax.ShapeDtypeStruct((size, size)...  27.5 us
    pallas_call x1, Pallas kernels, adam_step(): pl.pallas_call(step_kernel, out_shape=(jax.ShapeDtypeStruct((width, featu...  22.8 us
    dot_general x1, matrix products, sketched_term(): jnp.dot(sketch_turned, grad_turned, preferred_element_type=f32)  11.2 us
    unnamed x17, local copies, waits for them, and re-layouts  5.31 us
  transfers between devices with their start and end apart: 27, of which 15 were waited for; matrix products, arithmetic and copies ran while one was open for 10% of the time, Pallas kernels for 16%

profile of v4, /device:TPU:1, one launch (start us, length us, event | category | flops | bytes accessed | tf_op | source)
XLA Modules:
  0.0 177.0 jit_solution(3770941749918329263)
XLA Ops:
  7.2 2.0 %pack.1 = bf16[64,3696]{1,0:T(8,128)(2,1)} custom-call(f32[32,3696]{1,0:T(8,128)} %own_first_ref.1, f32[32,3696]{1,0:T(8,128)} %own_second_ref.1), custom_call_target="tpu_custom_call" | custom-call | tf_op jit(solution)/shard_map/pack/pallas_call | solution.py:178
  9.3 11.2 %fusion.26 = f32[576,1536]{1,0:T(8,128)S(1)} fusion(bf16[3696,576]{0,1:T(8,128)(2,1)} %param.7, bf16[1536,3696]{0,1:T(8,128)(2,1)} %param.6), kind=kOutput, calls=%fused_computation.83 | convolution fusion | flops 6539968512 | bytes 19150848 | tf_op jit(solution)/shard_map/dot_general | solution.py:186
  20.5 1.1 fusion.1
  21.7 1.1 fusion.4
  22.8 1.5 collective-permute-start
  24.3 1.5 reshape.57
  26.0 1.4 collective-permute-start.1
  27.4 1.5 collective-permute-start.3
  28.9 1.6 collective-permute-start.2
  30.5 1.0 constant_dynamic-slice_fusion.3
  31.6 2.0 %collective-permute-done.2 = bf16[72,512]{1,0:T(8,128)(2,1)S(1)} collective-permute-done((bf16[72,512]{1,0:T(8,128)(2,1)S(1)}, bf16[72,512]{1,0:T(8,128)(2,1)S(1)}, u32[]{:S(2)}, u32[]{:S(2)}) %collective-permute-start.2) | collective-permute-done | bytes 73760 | tf_op jit(solution)/shard_map/ppermute | solution.py:40
  33.7 1.6 collective-permute-start.5
  35.4 0.4 collective-permute-start.4
  35.8 2.3 %collective-permute-start.6 = (bf16[72,512]{1,0:T(8,128)(2,1)S(1)}, bf16[72,512]{1,0:T(8,128)(2,1)S(1)}, u32[]{:S(2)}, u32[]{:S(2)}) collective-permute-start(bf16[72,512]{1,0:T(8,128)(2,1)S(1)} %get-tuple-element.14), channel_id=1, source_target_pairs={{0,6},{1,7},{2,0},{3,1},{4,2},{5,3},{6,4},{7,5},{8,14},{9,15},{10,... | collective-permute-start | bytes 221192 | tf_op jit(solution)/shard_map/ppermute | solution.py:40
  38.1 1.7 collective-permute-done.4
  40.1 3.3 %collective-permute-start.7 = (bf16[288,512]{1,0:T(8,128)(2,1)S(1)}, bf16[288,512]{1,0:T(8,128)(2,1)S(1)}, u32[]{:S(2)}, u32[]{:S(2)}) collective-permute-start(bf16[288,512]{1,0:T(8,128)(2,1)S(1)} %bitcast.128), channel_id=1, source_target_pairs={{0,1},{1,0},{2,3},{3,2},{4,5},{5,4},{6,7},{7,6},{8,9},{9,8},{10,11... | collective-permute-start | bytes 884744 | tf_op jit(solution)/shard_map/ppermute | solution.py:40
  43.5 1.1 collective-permute-done.7
  44.6 0.4 fusion.27
  45.1 1.3 collective-permute-start.8
  46.4 1.5 collective-permute-start.10
  47.8 1.5 collective-permute-start.9
  49.4 4.7 %collective-permute-done.8 = f32[72,576]{1,0:T(8,128)S(1)} collective-permute-done((f32[72,576]{1,0:T(8,128)S(1)}, f32[72,576]{1,0:T(8,128)S(1)}, u32[]{:S(2)}, u32[]{:S(2)}) %collective-permute-start.8) | collective-permute-done | bytes 165920 | tf_op jit(solution)/shard_map/ppermute | solution.py:40
  54.1 2.3 %collective-permute-done.10 = f32[72,576]{1,0:T(8,128)S(1)} collective-permute-done((f32[72,576]{1,0:T(8,128)S(1)}, f32[72,576]{1,0:T(8,128)S(1)}, u32[]{:S(2)}, u32[]{:S(2)}) %collective-permute-start.10) | collective-permute-done | bytes 165920 | tf_op jit(solution)/shard_map/ppermute | solution.py:40
  56.3 7.5 %collective-permute-done.9 = f32[72,576]{1,0:T(8,128)S(1)} collective-permute-done((f32[72,576]{1,0:T(8,128)S(1)}, f32[72,576]{1,0:T(8,128)S(1)}, u32[]{:S(2)}, u32[]{:S(2)}) %collective-permute-start.9) | collective-permute-done | bytes 165920 | tf_op jit(solution)/shard_map/ppermute | solution.py:40
  64.0 2.8 %collective-permute-start.11 = (f32[36,576]{1,0:T(8,128)S(1)}, f32[36,576]{1,0:T(8,128)S(1)}, u32[]{:S(2)}, u32[]{:S(2)}) collective-permute-start(f32[36,576]{1,0:T(8,128)S(1)} %get-tuple-element.25), channel_id=1, source_target_pairs={{0,8},{8,16},{16,24},{24,0},{32,40},{40,48},{48,56},{56,32},{64,72... | collective-permute-start | bytes 248840 | tf_op jit(solution)/shard_map/ppermute | solution.py:40
  66.8 3.8 %collective-permute-start.12 = (f32[36,576]{1,0:T(8,128)S(1)}, f32[36,576]{1,0:T(8,128)S(1)}, u32[]{:S(2)}, u32[]{:S(2)}) collective-permute-start(f32[36,576]{1,0:T(8,128)S(1)} %get-tuple-element.26), channel_id=1, source_target_pairs={{0,16},{8,24},{16,0},{24,8},{32,48},{40,56},{48,32},{56,40},{64,80... | collective-permute-start | bytes 248840 | tf_op jit(solution)/shard_map/ppermute | solution.py:40
  70.6 1.0 collective-permute-start.13
  71.6 1.3 collective-permute-done.11
  73.0 6.0 %collective-permute-done.12 = f32[36,576]{1,0:T(8,128)S(1)} collective-permute-done((f32[36,576]{1,0:T(8,128)S(1)}, f32[36,576]{1,0:T(8,128)S(1)}, u32[]{:S(2)}, u32[]{:S(2)}) %collective-permute-start.12) | collective-permute-done | bytes 82976 | tf_op jit(solution)/shard_map/ppermute | solution.py:40
  79.3 2.2 %collective-permute-start.21 = (f32[12,576]{1,0:T(8,128)S(1)}, f32[12,576]{1,0:T(8,128)S(1)}, u32[]{:S(2)}, u32[]{:S(2)}) collective-permute-start(f32[12,576]{1,0:T(8,128)S(1)} %slice.79), channel_id=1, source_target_pairs={{0,1},{1,0},{2,3},{3,2},{4,5},{5,4},{6,7},{7,6},{8,9},{9,8},{10,11... | collective-permute-start | bytes 82952 | tf_op jit(solution)/shard_map/ppermute | solution.py:40
  81.5 0.9 collective-permute-done.21
  82.4 2.9 %collective-permute-start.24 = (f32[2,12,576]{2,1,0:T(8,128)S(1)}, f32[2,12,576]{2,1,0:T(8,128)S(1)}, u32[]{:S(2)}, u32[]{:S(2)}) collective-permute-start(f32[2,12,576]{2,1,0:T(8,128)S(1)} %bitcast_dynamic-update-slice_fusion.20), channel_id=1, source_target_pairs={{0,6},{1,7},{2,0},{3,1},{4,2},{5,3},{6,4},{7,5},{8,14},{9,15},{10,... | collective-permute-start | bytes 165896 | tf_op jit(solution)/shard_map/ppermute | solution.py:40
  85.3 0.7 collective-permute-start.22
  86.0 6.3 %collective-permute-done.22 = f32[2,12,576]{2,1,0:T(8,128)S(1)} collective-permute-done((f32[2,12,576]{2,1,0:T(8,128)S(1)}, f32[2,12,576]{2,1,0:T(8,128)S(1)}, u32[]{:S(2)}, u32[]{:S(2)}) %collective-permute-start.22) | collective-permute-done | bytes 55328 | tf_op jit(solution)/shard_map/ppermute | solution.py:40
  92.4 0.7 reshape.63
  93.2 1.3 collective-permute-start.15
  94.5 1.4 collective-permute-start.14
  96.0 1.3 collective-permute-start.16
  97.2 2.2 %collective-permute-done.14 = f32[24,576]{1,0:T(8,128)S(1)} collective-permute-done((f32[24,576]{1,0:T(8,128)S(1)}, f32[24,576]{1,0:T(8,128)S(1)}, u32[]{:S(2)}, u32[]{:S(2)}) %collective-permute-start.14) | collective-permute-done | bytes 55328 | tf_op jit(solution)/shard_map/ppermute | solution.py:40
  99.7 1.1 collective-permute-start.18
  100.8 1.6 collective-permute-start.19
  102.4 8.1 %collective-permute-done.17 = f32[72,576]{1,0:T(8,128)S(1)} collective-permute-done((f32[72,576]{1,0:T(8,128)S(1)}, f32[72,576]{1,0:T(8,128)S(1)}, u32[]{:S(2)}, u32[]{:S(2)}) %collective-permute-start.17) | collective-permute-done | bytes 165920 | tf_op jit(solution)/shard_map/ppermute | solution.py:40
  110.6 2.0 %collective-permute-start.20 = (f32[288,576]{1,0:T(8,128)S(1)}, f32[288,576]{1,0:T(8,128)S(1)}, u32[]{:S(2)}, u32[]{:S(2)}) collective-permute-start(f32[288,576]{1,0:T(8,128)S(1)} %bitcast.124), channel_id=1, source_target_pairs={{0,1},{1,0},{2,3},{3,2},{4,5},{5,4},{6,7},{7,6},{8,9},{9,8},{10,11... | collective-permute-start | bytes 1990664 | tf_op jit(solution)/shard_map/ppermute | solution.py:40
  112.8 1.7 collective-permute-done.20
  114.5 27.5 %inverse_factor.1.inverse_ref = f32[576,576]{1,0:T(8,128)S(1)} custom-call(f32[576,576]{1,0:T(8,128)S(1)} %bitcast.120), custom_call_target="tpu_custom_call" | custom-call | flops 2293235712 | bytes 2654208 | tf_op jit(solution)/shard_map/inverse_factor/pallas_call | solution.py:153
  142.1 3.1 %copy-done.2 = bf16[1024,3696]{1,0:T(8,128)(2,1)S(1)} copy-done((bf16[1024,3696]{1,0:T(8,128)(2,1)S(1)}, bf16[1024,3696]{1,0:T(8,128)(2,1)}, u32[]{:S(2)}) %copy-start.2) | copy-done | bytes 7569432
  145.3 2.1 %copy-done.3 = f32[1536,576]{1,0:T(8,128)S(1)} copy-done((f32[1536,576]{1,0:T(8,128)S(1)}, f32[1536,576]{1,0:T(8,128)}, u32[]{:S(2)}) %copy-start.3) | copy-done | bytes 3538968
  147.4 22.8 %adam_step.1 = (f32[3696,512]{1,0:T(8,128)}, f32[32,3696]{1,0:T(8,128)}, f32[32,3696]{1,0:T(8,128)}) custom-call(s32[1]{0:T(128)} %bitcast.at_ref, f32[576,576]{1,0:T(8,128)S(1)} %inverse_factor.1.inverse_ref, bf16[576,512]{1,0:T(8,128)(2,1)S(1)} %bitcast.119, f32[1536,576]{1,0:T(8,128)S(1)} %copy-done.3, bf16[3696,1536]{1,0:T(8,128)(2,1)} %bitcast.131, ...), custom_call_target="tpu_custom_call" | custom-call | flops 10468982784 | bytes 31924224 | tf_op jit(solution)/shard_map/adam_step/pallas_call | solution.py:243
  (85 shorter events, 2.0 us)
Async XLA Ops:
  7.2 85.9 %all-gather.6.cloned.1.call-start = ((), (), s32[]{:S(2)}) async-start(), calls=%async_computation.1 | async-start | bytes 8077312 | tf_op jit(solution)/shard_map/all_gather | solution.py:285
  9.2 132.9 %all-gather.4.cloned.1.call-start = ((), (), s32[]{:S(2)}) async-start(), calls=%async_computation | async-start | bytes 4177920 | tf_op jit(solution)/shard_map/all_gather | solution.py:312
  9.3 11.2 %copy-start.4 = (bf16[1536,512]{1,0:T(8,128)(2,1)S(1)}, bf16[1536,512]{1,0:T(8,128)(2,1)}, u32[]{:S(2)}) copy-start(bf16[1536,512]{1,0:T(8,128)(2,1)} %param.5) | copy-start | bytes 4718596
  22.8 3.0 %collective-permute-start = (bf16[288,512]{1,0:T(8,128)(2,1)S(1)}, bf16[288,512]{1,0:T(8,128)(2,1)S(1)}, u32[]{:S(2)}, u32[]{:S(2)}) collective-permute-start(bf16[288,512]{1,0:T(8,128)(2,1)S(1)} %fusion.5), channel_id=1, source_target_pairs={{0,1},{1,0},{2,3},{3,2},{4,5},{5,4},{6,7},{7,6},{8,9},{9,8},{10,11... | collective-permute-start | bytes 884744 | tf_op jit(solution)/shard_map/ppermute | solution.py:40
  26.0 5.6 %collective-permute-start.1 = (bf16[72,512]{1,0:T(8,128)(2,1)S(1)}, bf16[72,512]{1,0:T(8,128)(2,1)S(1)}, u32[]{:S(2)}, u32[]{:S(2)}) collective-permute-start(bf16[72,512]{1,0:T(8,128)(2,1)S(1)} %get-tuple-element.22), channel_id=1, source_target_pairs={{0,2},{1,3},{2,4},{3,5},{4,6},{5,7},{6,0},{7,1},{8,10},{9,11},{10,... | collective-permute-start | bytes 221192 | tf_op jit(solution)/shard_map/ppermute | solution.py:40
  27.4 4.2 %collective-permute-start.3 = (bf16[72,512]{1,0:T(8,128)(2,1)S(1)}, bf16[72,512]{1,0:T(8,128)(2,1)S(1)}, u32[]{:S(2)}, u32[]{:S(2)}) collective-permute-start(bf16[72,512]{1,0:T(8,128)(2,1)S(1)} %get-tuple-element.23), channel_id=1, source_target_pairs={{0,6},{1,7},{2,0},{3,1},{4,2},{5,3},{6,4},{7,5},{8,14},{9,15},{10,... | collective-permute-start | bytes 221192 | tf_op jit(solution)/shard_map/ppermute | solution.py:40
  28.9 4.7 %collective-permute-start.2 = (bf16[72,512]{1,0:T(8,128)(2,1)S(1)}, bf16[72,512]{1,0:T(8,128)(2,1)S(1)}, u32[]{:S(2)}, u32[]{:S(2)}) collective-permute-start(bf16[72,512]{1,0:T(8,128)(2,1)S(1)} %get-tuple-element.24), channel_id=1, source_target_pairs={{0,4},{1,5},{2,6},{3,7},{4,0},{5,1},{6,2},{7,3},{8,12},{9,13},{10,... | collective-permute-start | bytes 221192 | tf_op jit(solution)/shard_map/ppermute | solution.py:40
  33.7 6.1 %collective-permute-start.5 = (bf16[72,512]{1,0:T(8,128)(2,1)S(1)}, bf16[72,512]{1,0:T(8,128)(2,1)S(1)}, u32[]{:S(2)}, u32[]{:S(2)}) collective-permute-start(bf16[72,512]{1,0:T(8,128)(2,1)S(1)} %get-tuple-element.14), channel_id=1, source_target_pairs={{0,4},{1,5},{2,6},{3,7},{4,0},{5,1},{6,2},{7,3},{8,12},{9,13},{10,... | collective-permute-start | bytes 221192 | tf_op jit(solution)/shard_map/ppermute | solution.py:40
  35.4 4.4 %collective-permute-start.4 = (bf16[72,512]{1,0:T(8,128)(2,1)S(1)}, bf16[72,512]{1,0:T(8,128)(2,1)S(1)}, u32[]{:S(2)}, u32[]{:S(2)}) collective-permute-start(bf16[72,512]{1,0:T(8,128)(2,1)S(1)} %get-tuple-element.14), channel_id=1, source_target_pairs={{0,2},{1,3},{2,4},{3,5},{4,6},{5,7},{6,0},{7,1},{8,10},{9,11},{10,... | collective-permute-start | bytes 221192 | tf_op jit(solution)/shard_map/ppermute | solution.py:40
  35.8 4.3 %collective-permute-start.6 = (bf16[72,512]{1,0:T(8,128)(2,1)S(1)}, bf16[72,512]{1,0:T(8,128)(2,1)S(1)}, u32[]{:S(2)}, u32[]{:S(2)}) collective-permute-start(bf16[72,512]{1,0:T(8,128)(2,1)S(1)} %get-tuple-element.14), channel_id=1, source_target_pairs={{0,6},{1,7},{2,0},{3,1},{4,2},{5,3},{6,4},{7,5},{8,14},{9,15},{10,... | collective-permute-start | bytes 221192 | tf_op jit(solution)/shard_map/ppermute | solution.py:40
  40.1 4.5 %collective-permute-start.7 = (bf16[288,512]{1,0:T(8,128)(2,1)S(1)}, bf16[288,512]{1,0:T(8,128)(2,1)S(1)}, u32[]{:S(2)}, u32[]{:S(2)}) collective-permute-start(bf16[288,512]{1,0:T(8,128)(2,1)S(1)} %bitcast.128), channel_id=1, source_target_pairs={{0,1},{1,0},{2,3},{3,2},{4,5},{5,4},{6,7},{7,6},{8,9},{9,8},{10,11... | collective-permute-start | bytes 884744 | tf_op jit(solution)/shard_map/ppermute | solution.py:40
  45.1 9.0 %collective-permute-start.8 = (f32[72,576]{1,0:T(8,128)S(1)}, f32[72,576]{1,0:T(8,128)S(1)}, u32[]{:S(2)}, u32[]{:S(2)}) collective-permute-start(f32[72,576]{1,0:T(8,128)S(1)} %get-tuple-element.19), channel_id=1, source_target_pairs={{0,32},{8,40},{16,48},{24,56},{32,64},{40,72},{48,80},{56,88},{64,... | collective-permute-start | bytes 497672 | tf_op jit(solution)/shard_map/ppermute | solution.py:40
  46.4 9.9 %collective-permute-start.10 = (f32[72,576]{1,0:T(8,128)S(1)}, f32[72,576]{1,0:T(8,128)S(1)}, u32[]{:S(2)}, u32[]{:S(2)}) collective-permute-start(f32[72,576]{1,0:T(8,128)S(1)} %get-tuple-element.20), channel_id=1, source_target_pairs={{0,96},{8,104},{16,112},{24,120},{32,0},{40,8},{48,16},{56,24},{64... | collective-permute-start | bytes 497672 | tf_op jit(solution)/shard_map/ppermute | solution.py:40
  47.8 16.0 %collective-permute-start.9 = (f32[72,576]{1,0:T(8,128)S(1)}, f32[72,576]{1,0:T(8,128)S(1)}, u32[]{:S(2)}, u32[]{:S(2)}) collective-permute-start(f32[72,576]{1,0:T(8,128)S(1)} %get-tuple-element.21), channel_id=1, source_target_pairs={{0,64},{8,72},{16,80},{24,88},{32,96},{40,104},{48,112},{56,120},{... | collective-permute-start | bytes 497672 | tf_op jit(solution)/shard_map/ppermute | solution.py:40
  64.0 9.0 %collective-permute-start.11 = (f32[36,576]{1,0:T(8,128)S(1)}, f32[36,576]{1,0:T(8,128)S(1)}, u32[]{:S(2)}, u32[]{:S(2)}) collective-permute-start(f32[36,576]{1,0:T(8,128)S(1)} %get-tuple-element.25), channel_id=1, source_target_pairs={{0,8},{8,16},{16,24},{24,0},{32,40},{40,48},{48,56},{56,32},{64,72... | collective-permute-start | bytes 248840 | tf_op jit(solution)/shard_map/ppermute | solution.py:40
  66.8 12.1 %collective-permute-start.12 = (f32[36,576]{1,0:T(8,128)S(1)}, f32[36,576]{1,0:T(8,128)S(1)}, u32[]{:S(2)}, u32[]{:S(2)}) collective-permute-start(f32[36,576]{1,0:T(8,128)S(1)} %get-tuple-element.26), channel_id=1, source_target_pairs={{0,16},{8,24},{16,0},{24,8},{32,48},{40,56},{48,32},{56,40},{64,80... | collective-permute-start | bytes 248840 | tf_op jit(solution)/shard_map/ppermute | solution.py:40
  70.6 8.6 %collective-permute-start.13 = (f32[36,576]{1,0:T(8,128)S(1)}, f32[36,576]{1,0:T(8,128)S(1)}, u32[]{:S(2)}, u32[]{:S(2)}) collective-permute-start(f32[36,576]{1,0:T(8,128)S(1)} %get-tuple-element.27), channel_id=1, source_target_pairs={{0,24},{8,0},{16,8},{24,16},{32,56},{40,32},{48,40},{56,48},{64,88... | collective-permute-start | bytes 248840 | tf_op jit(solution)/shard_map/ppermute | solution.py:40
  79.3 3.1 %collective-permute-start.21 = (f32[12,576]{1,0:T(8,128)S(1)}, f32[12,576]{1,0:T(8,128)S(1)}, u32[]{:S(2)}, u32[]{:S(2)}) collective-permute-start(f32[12,576]{1,0:T(8,128)S(1)} %slice.79), channel_id=1, source_target_pairs={{0,1},{1,0},{2,3},{3,2},{4,5},{5,4},{6,7},{7,6},{8,9},{9,8},{10,11... | collective-permute-start | bytes 82952 | tf_op jit(solution)/shard_map/ppermute | solution.py:40
  82.4 10.0 %collective-permute-start.24 = (f32[2,12,576]{2,1,0:T(8,128)S(1)}, f32[2,12,576]{2,1,0:T(8,128)S(1)}, u32[]{:S(2)}, u32[]{:S(2)}) collective-permute-start(f32[2,12,576]{2,1,0:T(8,128)S(1)} %bitcast_dynamic-update-slice_fusion.20), channel_id=1, source_target_pairs={{0,6},{1,7},{2,0},{3,1},{4,2},{5,3},{6,4},{7,5},{8,14},{9,15},{10,... | collective-permute-start | bytes 165896 | tf_op jit(solution)/shard_map/ppermute | solution.py:40
  85.3 7.0 %collective-permute-start.23 = (f32[2,12,576]{2,1,0:T(8,128)S(1)}, f32[2,12,576]{2,1,0:T(8,128)S(1)}, u32[]{:S(2)}, u32[]{:S(2)}) collective-permute-start(f32[2,12,576]{2,1,0:T(8,128)S(1)} %bitcast_dynamic-update-slice_fusion.20), channel_id=1, source_target_pairs={{0,4},{1,5},{2,6},{3,7},{4,0},{5,1},{6,2},{7,3},{8,12},{9,13},{10,... | collective-permute-start | bytes 165896 | tf_op jit(solution)/shard_map/ppermute | solution.py:40
  85.3 7.0 %collective-permute-start.22 = (f32[2,12,576]{2,1,0:T(8,128)S(1)}, f32[2,12,576]{2,1,0:T(8,128)S(1)}, u32[]{:S(2)}, u32[]{:S(2)}) collective-permute-start(f32[2,12,576]{2,1,0:T(8,128)S(1)} %bitcast_dynamic-update-slice_fusion.20), channel_id=1, source_target_pairs={{0,2},{1,3},{2,4},{3,5},{4,6},{5,7},{6,0},{7,1},{8,10},{9,11},{10,... | collective-permute-start | bytes 165896 | tf_op jit(solution)/shard_map/ppermute | solution.py:40
  93.2 6.3 %collective-permute-start.15 = (f32[24,576]{1,0:T(8,128)S(1)}, f32[24,576]{1,0:T(8,128)S(1)}, u32[]{:S(2)}, u32[]{:S(2)}) collective-permute-start(f32[24,576]{1,0:T(8,128)S(1)} %slice.74), channel_id=1, source_target_pairs={{0,64},{8,72},{16,80},{24,88},{32,96},{40,104},{48,112},{56,120},{... | collective-permute-start | bytes 165896 | tf_op jit(solution)/shard_map/ppermute | solution.py:40
  94.5 4.9 %collective-permute-start.14 = (f32[24,576]{1,0:T(8,128)S(1)}, f32[24,576]{1,0:T(8,128)S(1)}, u32[]{:S(2)}, u32[]{:S(2)}) collective-permute-start(f32[24,576]{1,0:T(8,128)S(1)} %slice.74), channel_id=1, source_target_pairs={{0,32},{8,40},{16,48},{24,56},{32,64},{40,72},{48,80},{56,88},{64,... | collective-permute-start | bytes 165896 | tf_op jit(solution)/shard_map/ppermute | solution.py:40
  96.0 3.5 %collective-permute-start.16 = (f32[24,576]{1,0:T(8,128)S(1)}, f32[24,576]{1,0:T(8,128)S(1)}, u32[]{:S(2)}, u32[]{:S(2)}) collective-permute-start(f32[24,576]{1,0:T(8,128)S(1)} %slice.74), channel_id=1, source_target_pairs={{0,96},{8,104},{16,112},{24,120},{32,0},{40,8},{48,16},{56,24},{64... | collective-permute-start | bytes 165896 | tf_op jit(solution)/shard_map/ppermute | solution.py:40
  99.6 10.9 %collective-permute-start.17 = (f32[72,576]{1,0:T(8,128)S(1)}, f32[72,576]{1,0:T(8,128)S(1)}, u32[]{:S(2)}, u32[]{:S(2)}) collective-permute-start(f32[72,576]{1,0:T(8,128)S(1)} %pad_maximum_fusion), channel_id=1, source_target_pairs={{0,2},{1,3},{2,4},{3,5},{4,6},{5,7},{6,0},{7,1},{8,10},{9,11},{10,... | collective-permute-start | bytes 497672 | tf_op jit(solution)/shard_map/ppermute | solution.py:40
  99.7 10.9 %collective-permute-start.18 = (f32[72,576]{1,0:T(8,128)S(1)}, f32[72,576]{1,0:T(8,128)S(1)}, u32[]{:S(2)}, u32[]{:S(2)}) collective-permute-start(f32[72,576]{1,0:T(8,128)S(1)} %pad_maximum_fusion), channel_id=1, source_target_pairs={{0,4},{1,5},{2,6},{3,7},{4,0},{5,1},{6,2},{7,3},{8,12},{9,13},{10,... | collective-permute-start | bytes 497672 | tf_op jit(solution)/shard_map/ppermute | solution.py:40
  100.8 9.8 %collective-permute-start.19 = (f32[72,576]{1,0:T(8,128)S(1)}, f32[72,576]{1,0:T(8,128)S(1)}, u32[]{:S(2)}, u32[]{:S(2)}) collective-permute-start(f32[72,576]{1,0:T(8,128)S(1)} %pad_maximum_fusion), channel_id=1, source_target_pairs={{0,6},{1,7},{2,0},{3,1},{4,2},{5,3},{6,4},{7,5},{8,14},{9,15},{10,... | collective-permute-start | bytes 497672 | tf_op jit(solution)/shard_map/ppermute | solution.py:40
  110.6 3.8 %collective-permute-start.20 = (f32[288,576]{1,0:T(8,128)S(1)}, f32[288,576]{1,0:T(8,128)S(1)}, u32[]{:S(2)}, u32[]{:S(2)}) collective-permute-start(f32[288,576]{1,0:T(8,128)S(1)} %bitcast.124), channel_id=1, source_target_pairs={{0,1},{1,0},{2,3},{3,2},{4,5},{5,4},{6,7},{7,6},{8,9},{9,8},{10,11... | collective-permute-start | bytes 1990664 | tf_op jit(solution)/shard_map/ppermute | solution.py:40
  114.5 27.6 %copy-start = (f32[32,3696]{1,0:T(8,128)S(1)}, f32[32,3696]{1,0:T(8,128)}, u32[]{:S(2)}) copy-start(f32[32,3696]{1,0:T(8,128)} %own_first_ref.1) | copy-start | bytes 1419268
  114.5 27.6 %copy-start.1 = (f32[32,3696]{1,0:T(8,128)S(1)}, f32[32,3696]{1,0:T(8,128)}, u32[]{:S(2)}) copy-start(f32[32,3696]{1,0:T(8,128)} %own_second_ref.1) | copy-start | bytes 1419268
  142.1 3.2 %copy-start.2 = (bf16[1024,3696]{1,0:T(8,128)(2,1)S(1)}, bf16[1024,3696]{1,0:T(8,128)(2,1)}, u32[]{:S(2)}) copy-start(bf16[1024,3696]{1,0:T(8,128)(2,1)} %all-gather.6.cloned.1.call-done) | copy-start | bytes 22708228
  145.3 2.1 %copy-start.3 = (f32[1536,576]{1,0:T(8,128)S(1)}, f32[1536,576]{1,0:T(8,128)}, u32[]{:S(2)}) copy-start(f32[1536,576]{1,0:T(8,128)} %all-gather.4.cloned.1.call-done.mixed_ref) | copy-start | bytes 10616836
Sparse Core Ops, SparseCore 0:
  10.8 77.1 all-gather.5
  93.3 48.6 all-gather.3

commit v5 on v4

--- a/solution.py
+++ b/solution.py
@@ -8,9 +8,9 @@
 RANK = 512
 ADAM_STEP = 10
 BLOCK = 128
-TILE = 512
+TILE = 1024
 MIX_TILE = 512
-STEP_VMEM = 30 << 20
+STEP_VMEM = 50 << 20
 PART, STEP = 24, 16
 
 beta_one = 0.9
@@ -156,8 +156,8 @@
         in_specs=[pl.BlockSpec(memory_space=pltpu.VMEM)],
         out_specs=pl.BlockSpec(memory_space=pltpu.VMEM),
         scratch_shapes=[pltpu.VMEM((padded, padded), f32)],
-        compiler_params=pltpu.CompilerParams(vmem_limit_bytes=32 << 20),
-        cost_estimate=pl.CostEstimate(flops=12 * size**3, bytes_accessed=8 * size**2, transcendentals=0),
+        compiler_params=pltpu.CompilerParams(vmem_limit_bytes=16 << 20),
+        cost_estimate=pl.CostEstimate(flops=160 * size**3, bytes_accessed=8 * size**2, transcendentals=0),
         name="inverse_factor",
     )(gram)
 
@@ -198,48 +198,74 @@
 
 def step_kernel(
     at_ref, inverse_ref, sketched_ref, mixed_ref, grad_ref, gathered_ref, own_first_ref, own_second_ref,
-    update_ref, new_first_ref, new_second_ref, projector_ref, turned_ref, projected_ref,
+    update_ref, new_first_ref, new_second_ref,
+    projector, turned, projected, ready, mixed, grad, gathered, arrived, sent,
 ):
-    @pl.when(pl.program_id(0) == 0)
-    def _():
-        high, low = two_parts(inverse_ref[...])
-        values = sketched_ref[...]
-        projector_ref[...] = (
-            jnp.dot(low, values, preferred_element_type=f32)
-            + jnp.dot(high, values, preferred_element_type=f32)
+    width, owned = grad_ref.shape[0], own_first_ref.shape[0]
+    tiles = [(o, min(TILE, width - o)) for o in range(0, width, TILE)]
+    fetch_mixed = pltpu.make_async_copy(mixed_ref, mixed, arrived.at[0])
+    fetch_gathered = pltpu.make_async_copy(gathered_ref, gathered, arrived.at[1])
+    fetch_grad = [
+        pltpu.make_async_copy(grad_ref.at[pl.ds(o, n)], grad.at[pl.ds(o, n)], arrived.at[2 + i])
+        for i, (o, n) in enumerate(tiles)
+    ]
+    fetch_mixed.start()
+
+    high, low = two_parts(inverse_ref[:RANK, :])
+    values = sketched_ref[...]
+    projector[...] = (
+        jnp.dot(low, values, preferred_element_type=f32) + jnp.dot(high, values, preferred_element_type=f32)
+    ).astype(bf16)
+    times = lambda a, b: lax.dot_general(a, b, (((1,), (1,)), ((), ())), preferred_element_type=f32)
+    fetch_mixed.wait()
+    fetch_grad[0].start()
+    fetch_gathered.start()
+    for o in range(0, mixed.shape[0], MIX_TILE):
+        here = pl.ds(o, MIX_TILE)
+        mixed_high, mixed_low = two_parts(mixed[here, :])
+        turned[:, here] = (
+            times(high, mixed_low) + times(low, mixed_high) + times(high, mixed_high)
         ).astype(bf16)
-        times = lambda a, b: lax.dot_general(a, b, (((1,), (1,)), ((), ())), preferred_element_type=f32)
-        for o in range(0, mixed_ref.shape[0], MIX_TILE):
-            here = pl.ds(o, MIX_TILE)
-            mixed_high, mixed_low = two_parts(mixed_ref[here, :])
-            turned_ref[:, here] = (
-                times(high, mixed_low) + times(low, mixed_high) + times(high, mixed_high)
-            ).astype(bf16)
-
-    projected_ref[...] = lax.dot_general(
-        turned_ref[...], grad_ref[...], (((1,), (1,)), ((), ())), preferred_element_type=f32
-    )
-    owned = own_first_ref.shape[0]
-    first = gathered_ref[:, :owned, :].reshape(projected_ref.shape).astype(f32)
-    second = gathered_ref[:, owned:, :].reshape(projected_ref.shape).astype(f32)
-    new_first, new_second = moments(first, second, projected_ref[...])
-    root = (1.0 - beta_two**ADAM_STEP) ** 0.5
-    below = jnp.sqrt(new_second) + adam_epsilon * root
-    normalized = (new_first * (root / (1.0 - beta_one**ADAM_STEP)) * pl.reciprocal(below)).astype(bf16)
-    update_ref[...] = lax.dot_general(
-        normalized, projector_ref[...], (((0,), (0,)), ((), ())), preferred_element_type=f32
-    )
-    mine = projected_ref[pl.ds(pl.multiple_of(at_ref[0] * owned, owned), owned), :]
-    new_first_ref[...], new_second_ref[...] = moments(own_first_ref[...], own_second_ref[...], mine)
+
+    mine = pl.ds(pl.multiple_of(at_ref[0] * owned, owned), owned)
+    send = [
+        pltpu.make_async_copy(ready.at[i % 2, :n], update_ref.at[pl.ds(o, n)], sent.at[i % 2])
+        for i, (o, n) in enumerate(tiles)
+    ]
+    for i, (o, n) in enumerate(tiles):
+        here = pl.ds(o, n)
+        fetch_grad[i].wait()
+        if i + 1 < len(tiles):
+            fetch_grad[i + 1].start()
+        projected[:, :n] = times(turned[...], grad[here, :])
+        if i == 0:
+            fetch_gathered.wait()
+        first = gathered[:, :owned, here].reshape(RANK, n).astype(f32)
+        second = gathered[:, owned:, here].reshape(RANK, n).astype(f32)
+        new_first, new_second = moments(first, second, projected[:, :n])
+        root = (1.0 - beta_two**ADAM_STEP) ** 0.5
+        below = new_second * lax.rsqrt(new_second) + adam_epsilon * root
+        scaled = new_first * (root / (1.0 - beta_one**ADAM_STEP))
+        normalized = (scaled * pltpu.reciprocal(below)).astype(bf16)
+        if i >= 2:
+            send[i - 2].wait()
+        ready[i % 2, :n] = lax.dot_general(
+            normalized, projector[...], (((0,), (0,)), ((), ())), preferred_element_type=f32
+        )
+        send[i].start()
+        new_first_ref[:, here], new_second_ref[:, here] = moments(
+            own_first_ref[:, here], own_second_ref[:, here], projected[mine, :n]
+        )
+    for copy in send[-2:]:
+        copy.wait()
 
 
 def adam_step(at, inverse, sketched, mixed, grad_turned, gathered, own_first, own_second):
     width, tokens = grad_turned.shape
     columns, features = sketched.shape
     owned = own_first.shape[0]
-    whole = lambda shape: pl.BlockSpec(shape, lambda i, at: (0, 0), pipeline_mode=pl.Buffered(1))
-    strip = lambda rows: pl.BlockSpec((rows, TILE), lambda i, at: (0, i))
-    turned = lambda across: pl.BlockSpec((TILE, across), lambda i, at: (i, 0))
+    inside = pl.BlockSpec(memory_space=pltpu.VMEM)
+    outside = pl.BlockSpec(memory_space=pl.ANY)
     return pl.pallas_call(
         step_kernel,
         out_shape=(
@@ -247,25 +273,20 @@
             jax.ShapeDtypeStruct((owned, width), f32),
             jax.ShapeDtypeStruct((owned, width), f32),
         ),
-        grid_spec=pltpu.PrefetchScalarGridSpec(
-            num_scalar_prefetch=1,
-            grid=(pl.cdiv(width, TILE),),
-            in_specs=[
-                whole((RANK, columns)),
-                whole((columns, features)),
-                whole((tokens, columns)),
-                turned(tokens),
-                pl.BlockSpec((RANK // owned, 2 * owned, TILE), lambda i, at: (0, 0, i)),
-                strip(owned),
-                strip(owned),
-            ],
-            out_specs=[turned(features), strip(owned), strip(owned)],
-            scratch_shapes=[
-                pltpu.VMEM((RANK, features), bf16),
-                pltpu.VMEM((RANK, tokens), bf16),
-                pltpu.VMEM((RANK, TILE), f32),
-            ],
-        ),
+        in_specs=[pl.BlockSpec(memory_space=pltpu.SMEM), inside, inside]
+        + [outside, outside, outside, inside, inside],
+        out_specs=(outside, inside, inside),
+        scratch_shapes=[
+            pltpu.VMEM((RANK, features), bf16),
+            pltpu.VMEM((RANK, tokens), bf16),
+            pltpu.VMEM((RANK, TILE), f32),
+            pltpu.VMEM((2, TILE, features), f32),
+            pltpu.VMEM(mixed.shape, f32),
+            pltpu.VMEM(grad_turned.shape, bf16),
+            pltpu.VMEM(gathered.shape, bf16),
+            pltpu.SemaphoreType.DMA((2 + pl.cdiv(width, TILE),)),
+            pltpu.SemaphoreType.DMA((2,)),
+        ],
         compiler_params=pltpu.CompilerParams(vmem_limit_bytes=STEP_VMEM),
         cost_estimate=pl.CostEstimate(
             flops=2 * RANK * width * (tokens + features) + 6 * RANK * columns * tokens,

time: 177 us -> 170 us (0.960)
  local copies, waits for them, and re-layouts: 9.36 us -> 4.1 us
    unnamed x17 -> x13, local copies, waits for them, and re-layouts: 5.31 us -> 0.05 us
  transfers between devices with their start and end apart: 27 -> 27, of which waited for: 15 -> 15; matrix products, arithmetic and copies ran while one was open for 10% -> 11% of each run, Pallas kernels for 16% -> 16%
where the time goes in v5:
time: 170 us
  Pallas kernels  50.8 us (30%)
  waiting for transfers between devices  46.4 us (27%)
  starting transfers between devices  40.1 us (24%)
  between operations  14.7 us (9%)
  matrix products  13.9 us (8%)
  local copies, waits for them, and re-layouts  4.1 us (2%)
    ppermute x25, waiting for transfers between devices, shift(): return lax.ppermute(value, axis, pairs)  46.3 us
    ppermute x25, starting transfers between devices, shift(): return lax.ppermute(value, axis, pairs)  40.1 us
    pallas_call x1, Pallas kernels, inverse_factor(): pl.pallas_call(factor_kernel, out_shape=jax.ShapeDtypeStruct((size, size)...  27.7 us
    pallas_call x1, Pallas kernels, adam_step(): pl.pallas_call(step_kernel, out_shape=(jax.ShapeDtypeStruct((width, featu...  21.1 us
    dot_general x1, matrix products, sketched_term(): jnp.dot(sketch_turned, grad_turned, preferred_element_type=f32)  11.2 us
  transfers between devices with their start and end apart: 27, of which 15 were waited for; matrix products, arithmetic and copies ran while one was open for 11% of the time, Pallas kernels for 16%

profile of v5, /device:TPU:1, one launch (start us, length us, event | category | flops | bytes accessed | tf_op | source)
XLA Modules:
  0.0 170.3 jit_solution(16300412329469769839)
XLA Ops:
  7.2 2.0 %pack.1 = bf16[64,3696]{1,0:T(8,128)(2,1)} custom-call(f32[32,3696]{1,0:T(8,128)} %own_first_ref.1, f32[32,3696]{1,0:T(8,128)} %own_second_ref.1), custom_call_target="tpu_custom_call" | custom-call | tf_op jit(solution)/shard_map/pack/pallas_call | solution.py:178
  9.3 11.2 %fusion.26 = f32[576,1536]{1,0:T(8,128)S(1)} fusion(bf16[3696,576]{0,1:T(8,128)(2,1)} %param.7, bf16[1536,3696]{0,1:T(8,128)(2,1)} %param.6), kind=kOutput, calls=%fused_computation.83 | convolution fusion | flops 6539968512 | bytes 19150848 | tf_op jit(solution)/shard_map/dot_general | solution.py:186
  20.5 1.1 fusion.1
  21.7 1.1 fusion.4
  22.8 1.5 collective-permute-start
  24.3 1.5 reshape.57
  26.0 1.4 collective-permute-start.1
  27.4 1.5 collective-permute-start.3
  28.9 1.6 collective-permute-start.2
  30.5 1.0 constant_dynamic-slice_fusion.3
  31.6 2.0 %collective-permute-done.2 = bf16[72,512]{1,0:T(8,128)(2,1)S(1)} collective-permute-done((bf16[72,512]{1,0:T(8,128)(2,1)S(1)}, bf16[72,512]{1,0:T(8,128)(2,1)S(1)}, u32[]{:S(2)}, u32[]{:S(2)}) %collective-permute-start.2) | collective-permute-done | bytes 73760 | tf_op jit(solution)/shard_map/ppermute | solution.py:40
  33.7 1.6 collective-permute-start.5
  35.4 0.4 collective-permute-start.4
  35.8 2.3 %collective-permute-start.6 = (bf16[72,512]{1,0:T(8,128)(2,1)S(1)}, bf16[72,512]{1,0:T(8,128)(2,1)S(1)}, u32[]{:S(2)}, u32[]{:S(2)}) collective-permute-start(bf16[72,512]{1,0:T(8,128)(2,1)S(1)} %get-tuple-element.14), channel_id=1, source_target_pairs={{0,6},{1,7},{2,0},{3,1},{4,2},{5,3},{6,4},{7,5},{8,14},{9,15},{10,... | collective-permute-start | bytes 221192 | tf_op jit(solution)/shard_map/ppermute | solution.py:40
  38.1 1.7 collective-permute-done.4
  39.8 0.2 collective-permute-done.6
  40.1 3.3 %collective-permute-start.7 = (bf16[288,512]{1,0:T(8,128)(2,1)S(1)}, bf16[288,512]{1,0:T(8,128)(2,1)S(1)}, u32[]{:S(2)}, u32[]{:S(2)}) collective-permute-start(bf16[288,512]{1,0:T(8,128)(2,1)S(1)} %bitcast.127), channel_id=1, source_target_pairs={{0,1},{1,0},{2,3},{3,2},{4,5},{5,4},{6,7},{7,6},{8,9},{9,8},{10,11... | collective-permute-start | bytes 884744 | tf_op jit(solution)/shard_map/ppermute | solution.py:40
  43.5 1.1 collective-permute-done.7
  44.6 0.4 fusion.27
  45.1 1.3 collective-permute-start.8
  46.4 1.5 collective-permute-start.10
  47.8 1.5 collective-permute-start.9
  49.4 4.7 %collective-permute-done.8 = f32[72,576]{1,0:T(8,128)S(1)} collective-permute-done((f32[72,576]{1,0:T(8,128)S(1)}, f32[72,576]{1,0:T(8,128)S(1)}, u32[]{:S(2)}, u32[]{:S(2)}) %collective-permute-start.8) | collective-permute-done | bytes 165920 | tf_op jit(solution)/shard_map/ppermute | solution.py:40
  54.1 2.3 %collective-permute-done.10 = f32[72,576]{1,0:T(8,128)S(1)} collective-permute-done((f32[72,576]{1,0:T(8,128)S(1)}, f32[72,576]{1,0:T(8,128)S(1)}, u32[]{:S(2)}, u32[]{:S(2)}) %collective-permute-start.10) | collective-permute-done | bytes 165920 | tf_op jit(solution)/shard_map/ppermute | solution.py:40
  56.3 7.5 %collective-permute-done.9 = f32[72,576]{1,0:T(8,128)S(1)} collective-permute-done((f32[72,576]{1,0:T(8,128)S(1)}, f32[72,576]{1,0:T(8,128)S(1)}, u32[]{:S(2)}, u32[]{:S(2)}) %collective-permute-start.9) | collective-permute-done | bytes 165920 | tf_op jit(solution)/shard_map/ppermute | solution.py:40
  64.0 2.8 %collective-permute-start.11 = (f32[36,576]{1,0:T(8,128)S(1)}, f32[36,576]{1,0:T(8,128)S(1)}, u32[]{:S(2)}, u32[]{:S(2)}) collective-permute-start(f32[36,576]{1,0:T(8,128)S(1)} %get-tuple-element.25), channel_id=1, source_target_pairs={{0,8},{8,16},{16,24},{24,0},{32,40},{40,48},{48,56},{56,32},{64,72... | collective-permute-start | bytes 248840 | tf_op jit(solution)/shard_map/ppermute | solution.py:40
  66.8 3.8 %collective-permute-start.12 = (f32[36,576]{1,0:T(8,128)S(1)}, f32[36,576]{1,0:T(8,128)S(1)}, u32[]{:S(2)}, u32[]{:S(2)}) collective-permute-start(f32[36,576]{1,0:T(8,128)S(1)} %get-tuple-element.26), channel_id=1, source_target_pairs={{0,16},{8,24},{16,0},{24,8},{32,48},{40,56},{48,32},{56,40},{64,80... | collective-permute-start | bytes 248840 | tf_op jit(solution)/shard_map/ppermute | solution.py:40
  70.6 1.0 collective-permute-start.13
  71.6 1.3 collective-permute-done.11
  73.0 6.0 %collective-permute-done.12 = f32[36,576]{1,0:T(8,128)S(1)} collective-permute-done((f32[36,576]{1,0:T(8,128)S(1)}, f32[36,576]{1,0:T(8,128)S(1)}, u32[]{:S(2)}, u32[]{:S(2)}) %collective-permute-start.12) | collective-permute-done | bytes 82976 | tf_op jit(solution)/shard_map/ppermute | solution.py:40
  78.9 0.3 collective-permute-done.13
  79.3 2.2 %collective-permute-start.21 = (f32[12,576]{1,0:T(8,128)S(1)}, f32[12,576]{1,0:T(8,128)S(1)}, u32[]{:S(2)}, u32[]{:S(2)}) collective-permute-start(f32[12,576]{1,0:T(8,128)S(1)} %slice.79), channel_id=1, source_target_pairs={{0,1},{1,0},{2,3},{3,2},{4,5},{5,4},{6,7},{7,6},{8,9},{9,8},{10,11... | collective-permute-start | bytes 82952 | tf_op jit(solution)/shard_map/ppermute | solution.py:40
  81.5 0.9 collective-permute-done.21
  82.4 2.9 %collective-permute-start.24 = (f32[2,12,576]{2,1,0:T(8,128)S(1)}, f32[2,12,576]{2,1,0:T(8,128)S(1)}, u32[]{:S(2)}, u32[]{:S(2)}) collective-permute-start(f32[2,12,576]{2,1,0:T(8,128)S(1)} %bitcast_dynamic-update-slice_fusion.20), channel_id=1, source_target_pairs={{0,6},{1,7},{2,0},{3,1},{4,2},{5,3},{6,4},{7,5},{8,14},{9,15},{10,... | collective-permute-start | bytes 165896 | tf_op jit(solution)/shard_map/ppermute | solution.py:40
  85.3 0.7 collective-permute-start.22
  86.0 6.3 %collective-permute-done.22 = f32[2,12,576]{2,1,0:T(8,128)S(1)} collective-permute-done((f32[2,12,576]{2,1,0:T(8,128)S(1)}, f32[2,12,576]{2,1,0:T(8,128)S(1)}, u32[]{:S(2)}, u32[]{:S(2)}) %collective-permute-start.22) | collective-permute-done | bytes 55328 | tf_op jit(solution)/shard_map/ppermute | solution.py:40
  92.4 0.7 reshape.63
  93.2 1.3 collective-permute-start.15
  94.5 1.4 collective-permute-start.14
  96.0 1.3 collective-permute-start.16
  97.2 2.2 %collective-permute-done.14 = f32[24,576]{1,0:T(8,128)S(1)} collective-permute-done((f32[24,576]{1,0:T(8,128)S(1)}, f32[24,576]{1,0:T(8,128)S(1)}, u32[]{:S(2)}, u32[]{:S(2)}) %collective-permute-start.14) | collective-permute-done | bytes 55328 | tf_op jit(solution)/shard_map/ppermute | solution.py:40
  99.7 1.1 collective-permute-start.18
  100.8 1.6 collective-permute-start.19
  102.4 8.1 %collective-permute-done.17 = f32[72,576]{1,0:T(8,128)S(1)} collective-permute-done((f32[72,576]{1,0:T(8,128)S(1)}, f32[72,576]{1,0:T(8,128)S(1)}, u32[]{:S(2)}, u32[]{:S(2)}) %collective-permute-start.17) | collective-permute-done | bytes 165920 | tf_op jit(solution)/shard_map/ppermute | solution.py:40
  110.6 2.0 %collective-permute-start.20 = (f32[288,576]{1,0:T(8,128)S(1)}, f32[288,576]{1,0:T(8,128)S(1)}, u32[]{:S(2)}, u32[]{:S(2)}) collective-permute-start(f32[288,576]{1,0:T(8,128)S(1)} %bitcast.123), channel_id=1, source_target_pairs={{0,1},{1,0},{2,3},{3,2},{4,5},{5,4},{6,7},{7,6},{8,9},{9,8},{10,11... | collective-permute-start | bytes 1990664 | tf_op jit(solution)/shard_map/ppermute | solution.py:40
  112.8 1.7 collective-permute-done.20
  114.5 27.7 %inverse_factor.1.inverse_ref = f32[576,576]{1,0:T(8,128)S(1)} custom-call(f32[576,576]{1,0:T(8,128)S(1)} %bitcast.120), custom_call_target="tpu_custom_call" | custom-call | flops 30576476160 | bytes 2654208 | tf_op jit(solution)/shard_map/inverse_factor/pallas_call | solution.py:153
  142.3 21.1 %adam_step.1 = (f32[3696,512]{1,0:T(8,128)}, f32[32,3696]{1,0:T(8,128)}, f32[32,3696]{1,0:T(8,128)}) custom-call(s32[1]{0:T(128)} %bitcast.at_ref, f32[576,576]{1,0:T(8,128)S(1)} %inverse_factor.1.inverse_ref, bf16[576,512]{1,0:T(8,128)(2,1)S(1)} %bitcast.119, f32[1536,576]{1,0:T(8,128)} %all-gather.4.cloned.1.call-done.mixed_ref, ...), custom_call_target="tpu_custom_call" | custom-call | flops 10468982784 | bytes 31924224 | tf_op jit(solution)/shard_map/adam_step/pallas_call | solution.py:269
  (81 shorter events, 1.5 us)
Async XLA Ops:
  7.2 85.9 %all-gather.6.cloned.1.call-start = ((), (), s32[]{:S(2)}) async-start(), calls=%async_computation.1 | async-start | bytes 8077312 | tf_op jit(solution)/shard_map/all_gather | solution.py:306
  9.2 133.1 %all-gather.4.cloned.1.call-start = ((), (), s32[]{:S(2)}) async-start(), calls=%async_computation | async-start | bytes 4177920 | tf_op jit(solution)/shard_map/all_gather | solution.py:333
  9.3 11.2 %copy-start.2 = (bf16[1536,512]{1,0:T(8,128)(2,1)S(1)}, bf16[1536,512]{1,0:T(8,128)(2,1)}, u32[]{:S(2)}) copy-start(bf16[1536,512]{1,0:T(8,128)(2,1)} %param.5) | copy-start | bytes 4718596
  22.8 3.0 %collective-permute-start = (bf16[288,512]{1,0:T(8,128)(2,1)S(1)}, bf16[288,512]{1,0:T(8,128)(2,1)S(1)}, u32[]{:S(2)}, u32[]{:S(2)}) collective-permute-start(bf16[288,512]{1,0:T(8,128)(2,1)S(1)} %fusion.5), channel_id=1, source_target_pairs={{0,1},{1,0},{2,3},{3,2},{4,5},{5,4},{6,7},{7,6},{8,9},{9,8},{10,11... | collective-permute-start | bytes 884744 | tf_op jit(solution)/shard_map/ppermute | solution.py:40
  26.0 5.6 %collective-permute-start.1 = (bf16[72,512]{1,0:T(8,128)(2,1)S(1)}, bf16[72,512]{1,0:T(8,128)(2,1)S(1)}, u32[]{:S(2)}, u32[]{:S(2)}) collective-permute-start(bf16[72,512]{1,0:T(8,128)(2,1)S(1)} %get-tuple-element.22), channel_id=1, source_target_pairs={{0,2},{1,3},{2,4},{3,5},{4,6},{5,7},{6,0},{7,1},{8,10},{9,11},{10,... | collective-permute-start | bytes 221192 | tf_op jit(solution)/shard_map/ppermute | solution.py:40
  27.4 4.2 %collective-permute-start.3 = (bf16[72,512]{1,0:T(8,128)(2,1)S(1)}, bf16[72,512]{1,0:T(8,128)(2,1)S(1)}, u32[]{:S(2)}, u32[]{:S(2)}) collective-permute-start(bf16[72,512]{1,0:T(8,128)(2,1)S(1)} %get-tuple-element.23), channel_id=1, source_target_pairs={{0,6},{1,7},{2,0},{3,1},{4,2},{5,3},{6,4},{7,5},{8,14},{9,15},{10,... | collective-permute-start | bytes 221192 | tf_op jit(solution)/shard_map/ppermute | solution.py:40
  28.9 4.7 %collective-permute-start.2 = (bf16[72,512]{1,0:T(8,128)(2,1)S(1)}, bf16[72,512]{1,0:T(8,128)(2,1)S(1)}, u32[]{:S(2)}, u32[]{:S(2)}) collective-permute-start(bf16[72,512]{1,0:T(8,128)(2,1)S(1)} %get-tuple-element.24), channel_id=1, source_target_pairs={{0,4},{1,5},{2,6},{3,7},{4,0},{5,1},{6,2},{7,3},{8,12},{9,13},{10,... | collective-permute-start | bytes 221192 | tf_op jit(solution)/shard_map/ppermute | solution.py:40
  33.7 6.1 %collective-permute-start.5 = (bf16[72,512]{1,0:T(8,128)(2,1)S(1)}, bf16[72,512]{1,0:T(8,128)(2,1)S(1)}, u32[]{:S(2)}, u32[]{:S(2)}) collective-permute-start(bf16[72,512]{1,0:T(8,128)(2,1)S(1)} %get-tuple-element.14), channel_id=1, source_target_pairs={{0,4},{1,5},{2,6},{3,7},{4,0},{5,1},{6,2},{7,3},{8,12},{9,13},{10,... | collective-permute-start | bytes 221192 | tf_op jit(solution)/shard_map/ppermute | solution.py:40
  35.4 4.4 %collective-permute-start.4 = (bf16[72,512]{1,0:T(8,128)(2,1)S(1)}, bf16[72,512]{1,0:T(8,128)(2,1)S(1)}, u32[]{:S(2)}, u32[]{:S(2)}) collective-permute-start(bf16[72,512]{1,0:T(8,128)(2,1)S(1)} %get-tuple-element.14), channel_id=1, source_target_pairs={{0,2},{1,3},{2,4},{3,5},{4,6},{5,7},{6,0},{7,1},{8,10},{9,11},{10,... | collective-permute-start | bytes 221192 | tf_op jit(solution)/shard_map/ppermute | solution.py:40
  35.8 4.3 %collective-permute-start.6 = (bf16[72,512]{1,0:T(8,128)(2,1)S(1)}, bf16[72,512]{1,0:T(8,128)(2,1)S(1)}, u32[]{:S(2)}, u32[]{:S(2)}) collective-permute-start(bf16[72,512]{1,0:T(8,128)(2,1)S(1)} %get-tuple-element.14), channel_id=1, source_target_pairs={{0,6},{1,7},{2,0},{3,1},{4,2},{5,3},{6,4},{7,5},{8,14},{9,15},{10,... | collective-permute-start | bytes 221192 | tf_op jit(solution)/shard_map/ppermute | solution.py:40
  40.1 4.5 %collective-permute-start.7 = (bf16[288,512]{1,0:T(8,128)(2,1)S(1)}, bf16[288,512]{1,0:T(8,128)(2,1)S(1)}, u32[]{:S(2)}, u32[]{:S(2)}) collective-permute-start(bf16[288,512]{1,0:T(8,128)(2,1)S(1)} %bitcast.127), channel_id=1, source_target_pairs={{0,1},{1,0},{2,3},{3,2},{4,5},{5,4},{6,7},{7,6},{8,9},{9,8},{10,11... | collective-permute-start | bytes 884744 | tf_op jit(solution)/shard_map/ppermute | solution.py:40
  45.1 9.0 %collective-permute-start.8 = (f32[72,576]{1,0:T(8,128)S(1)}, f32[72,576]{1,0:T(8,128)S(1)}, u32[]{:S(2)}, u32[]{:S(2)}) collective-permute-start(f32[72,576]{1,0:T(8,128)S(1)} %get-tuple-element.19), channel_id=1, source_target_pairs={{0,32},{8,40},{16,48},{24,56},{32,64},{40,72},{48,80},{56,88},{64,... | collective-permute-start | bytes 497672 | tf_op jit(solution)/shard_map/ppermute | solution.py:40
  46.4 9.9 %collective-permute-start.10 = (f32[72,576]{1,0:T(8,128)S(1)}, f32[72,576]{1,0:T(8,128)S(1)}, u32[]{:S(2)}, u32[]{:S(2)}) collective-permute-start(f32[72,576]{1,0:T(8,128)S(1)} %get-tuple-element.20), channel_id=1, source_target_pairs={{0,96},{8,104},{16,112},{24,120},{32,0},{40,8},{48,16},{56,24},{64... | collective-permute-start | bytes 497672 | tf_op jit(solution)/shard_map/ppermute | solution.py:40
  47.8 16.0 %collective-permute-start.9 = (f32[72,576]{1,0:T(8,128)S(1)}, f32[72,576]{1,0:T(8,128)S(1)}, u32[]{:S(2)}, u32[]{:S(2)}) collective-permute-start(f32[72,576]{1,0:T(8,128)S(1)} %get-tuple-element.21), channel_id=1, source_target_pairs={{0,64},{8,72},{16,80},{24,88},{32,96},{40,104},{48,112},{56,120},{... | collective-permute-start | bytes 497672 | tf_op jit(solution)/shard_map/ppermute | solution.py:40
  64.0 9.0 %collective-permute-start.11 = (f32[36,576]{1,0:T(8,128)S(1)}, f32[36,576]{1,0:T(8,128)S(1)}, u32[]{:S(2)}, u32[]{:S(2)}) collective-permute-start(f32[36,576]{1,0:T(8,128)S(1)} %get-tuple-element.25), channel_id=1, source_target_pairs={{0,8},{8,16},{16,24},{24,0},{32,40},{40,48},{48,56},{56,32},{64,72... | collective-permute-start | bytes 248840 | tf_op jit(solution)/shard_map/ppermute | solution.py:40
  66.8 12.1 %collective-permute-start.12 = (f32[36,576]{1,0:T(8,128)S(1)}, f32[36,576]{1,0:T(8,128)S(1)}, u32[]{:S(2)}, u32[]{:S(2)}) collective-permute-start(f32[36,576]{1,0:T(8,128)S(1)} %get-tuple-element.26), channel_id=1, source_target_pairs={{0,16},{8,24},{16,0},{24,8},{32,48},{40,56},{48,32},{56,40},{64,80... | collective-permute-start | bytes 248840 | tf_op jit(solution)/shard_map/ppermute | solution.py:40
  70.6 8.6 %collective-permute-start.13 = (f32[36,576]{1,0:T(8,128)S(1)}, f32[36,576]{1,0:T(8,128)S(1)}, u32[]{:S(2)}, u32[]{:S(2)}) collective-permute-start(f32[36,576]{1,0:T(8,128)S(1)} %get-tuple-element.27), channel_id=1, source_target_pairs={{0,24},{8,0},{16,8},{24,16},{32,56},{40,32},{48,40},{56,48},{64,88... | collective-permute-start | bytes 248840 | tf_op jit(solution)/shard_map/ppermute | solution.py:40
  79.3 3.1 %collective-permute-start.21 = (f32[12,576]{1,0:T(8,128)S(1)}, f32[12,576]{1,0:T(8,128)S(1)}, u32[]{:S(2)}, u32[]{:S(2)}) collective-permute-start(f32[12,576]{1,0:T(8,128)S(1)} %slice.79), channel_id=1, source_target_pairs={{0,1},{1,0},{2,3},{3,2},{4,5},{5,4},{6,7},{7,6},{8,9},{9,8},{10,11... | collective-permute-start | bytes 82952 | tf_op jit(solution)/shard_map/ppermute | solution.py:40
  82.4 10.0 %collective-permute-start.24 = (f32[2,12,576]{2,1,0:T(8,128)S(1)}, f32[2,12,576]{2,1,0:T(8,128)S(1)}, u32[]{:S(2)}, u32[]{:S(2)}) collective-permute-start(f32[2,12,576]{2,1,0:T(8,128)S(1)} %bitcast_dynamic-update-slice_fusion.20), channel_id=1, source_target_pairs={{0,6},{1,7},{2,0},{3,1},{4,2},{5,3},{6,4},{7,5},{8,14},{9,15},{10,... | collective-permute-start | bytes 165896 | tf_op jit(solution)/shard_map/ppermute | solution.py:40
  85.3 7.0 %collective-permute-start.23 = (f32[2,12,576]{2,1,0:T(8,128)S(1)}, f32[2,12,576]{2,1,0:T(8,128)S(1)}, u32[]{:S(2)}, u32[]{:S(2)}) collective-permute-start(f32[2,12,576]{2,1,0:T(8,128)S(1)} %bitcast_dynamic-update-slice_fusion.20), channel_id=1, source_target_pairs={{0,4},{1,5},{2,6},{3,7},{4,0},{5,1},{6,2},{7,3},{8,12},{9,13},{10,... | collective-permute-start | bytes 165896 | tf_op jit(solution)/shard_map/ppermute | solution.py:40
  85.3 7.0 %collective-permute-start.22 = (f32[2,12,576]{2,1,0:T(8,128)S(1)}, f32[2,12,576]{2,1,0:T(8,128)S(1)}, u32[]{:S(2)}, u32[]{:S(2)}) collective-permute-start(f32[2,12,576]{2,1,0:T(8,128)S(1)} %bitcast_dynamic-update-slice_fusion.20), channel_id=1, source_target_pairs={{0,2},{1,3},{2,4},{3,5},{4,6},{5,7},{6,0},{7,1},{8,10},{9,11},{10,... | collective-permute-start | bytes 165896 | tf_op jit(solution)/shard_map/ppermute | solution.py:40
  93.2 6.3 %collective-permute-start.15 = (f32[24,576]{1,0:T(8,128)S(1)}, f32[24,576]{1,0:T(8,128)S(1)}, u32[]{:S(2)}, u32[]{:S(2)}) collective-permute-start(f32[24,576]{1,0:T(8,128)S(1)} %slice.74), channel_id=1, source_target_pairs={{0,64},{8,72},{16,80},{24,88},{32,96},{40,104},{48,112},{56,120},{... | collective-permute-start | bytes 165896 | tf_op jit(solution)/shard_map/ppermute | solution.py:40
  94.5 4.9 %collective-permute-start.14 = (f32[24,576]{1,0:T(8,128)S(1)}, f32[24,576]{1,0:T(8,128)S(1)}, u32[]{:S(2)}, u32[]{:S(2)}) collective-permute-start(f32[24,576]{1,0:T(8,128)S(1)} %slice.74), channel_id=1, source_target_pairs={{0,32},{8,40},{16,48},{24,56},{32,64},{40,72},{48,80},{56,88},{64,... | collective-permute-start | bytes 165896 | tf_op jit(solution)/shard_map/ppermute | solution.py:40
  96.0 3.5 %collective-permute-start.16 = (f32[24,576]{1,0:T(8,128)S(1)}, f32[24,576]{1,0:T(8,128)S(1)}, u32[]{:S(2)}, u32[]{:S(2)}) collective-permute-start(f32[24,576]{1,0:T(8,128)S(1)} %slice.74), channel_id=1, source_target_pairs={{0,96},{8,104},{16,112},{24,120},{32,0},{40,8},{48,16},{56,24},{64... | collective-permute-start | bytes 165896 | tf_op jit(solution)/shard_map/ppermute | solution.py:40
  99.6 10.9 %collective-permute-start.17 = (f32[72,576]{1,0:T(8,128)S(1)}, f32[72,576]{1,0:T(8,128)S(1)}, u32[]{:S(2)}, u32[]{:S(2)}) collective-permute-start(f32[72,576]{1,0:T(8,128)S(1)} %pad_maximum_fusion), channel_id=1, source_target_pairs={{0,2},{1,3},{2,4},{3,5},{4,6},{5,7},{6,0},{7,1},{8,10},{9,11},{10,... | collective-permute-start | bytes 497672 | tf_op jit(solution)/shard_map/ppermute | solution.py:40
  99.7 10.9 %collective-permute-start.18 = (f32[72,576]{1,0:T(8,128)S(1)}, f32[72,576]{1,0:T(8,128)S(1)}, u32[]{:S(2)}, u32[]{:S(2)}) collective-permute-start(f32[72,576]{1,0:T(8,128)S(1)} %pad_maximum_fusion), channel_id=1, source_target_pairs={{0,4},{1,5},{2,6},{3,7},{4,0},{5,1},{6,2},{7,3},{8,12},{9,13},{10,... | collective-permute-start | bytes 497672 | tf_op jit(solution)/shard_map/ppermute | solution.py:40
  100.8 9.8 %collective-permute-start.19 = (f32[72,576]{1,0:T(8,128)S(1)}, f32[72,576]{1,0:T(8,128)S(1)}, u32[]{:S(2)}, u32[]{:S(2)}) collective-permute-start(f32[72,576]{1,0:T(8,128)S(1)} %pad_maximum_fusion), channel_id=1, source_target_pairs={{0,6},{1,7},{2,0},{3,1},{4,2},{5,3},{6,4},{7,5},{8,14},{9,15},{10,... | collective-permute-start | bytes 497672 | tf_op jit(solution)/shard_map/ppermute | solution.py:40
  110.6 3.8 %collective-permute-start.20 = (f32[288,576]{1,0:T(8,128)S(1)}, f32[288,576]{1,0:T(8,128)S(1)}, u32[]{:S(2)}, u32[]{:S(2)}) collective-permute-start(f32[288,576]{1,0:T(8,128)S(1)} %bitcast.123), channel_id=1, source_target_pairs={{0,1},{1,0},{2,3},{3,2},{4,5},{5,4},{6,7},{7,6},{8,9},{9,8},{10,11... | collective-permute-start | bytes 1990664 | tf_op jit(solution)/shard_map/ppermute | solution.py:40
  114.5 27.8 %copy-start = (f32[32,3696]{1,0:T(8,128)S(1)}, f32[32,3696]{1,0:T(8,128)}, u32[]{:S(2)}) copy-start(f32[32,3696]{1,0:T(8,128)} %own_first_ref.1) | copy-start | bytes 1419268
  114.5 27.8 %copy-start.1 = (f32[32,3696]{1,0:T(8,128)S(1)}, f32[32,3696]{1,0:T(8,128)}, u32[]{:S(2)}) copy-start(f32[32,3696]{1,0:T(8,128)} %own_second_ref.1) | copy-start | bytes 1419268
Sparse Core Ops, SparseCore 0:
  10.8 77.1 all-gather.5
  93.3 48.6 all-gather.3

commit v6 on v5

--- a/solution.py
+++ b/solution.py
@@ -11,7 +11,7 @@
 TILE = 1024
 MIX_TILE = 512
 STEP_VMEM = 50 << 20
-PART, STEP = 24, 16
+PART = 40
 
 beta_one = 0.9
 beta_two = 0.999
@@ -57,6 +57,44 @@
     for k in range(n):
         out = lax.dynamic_update_index_in_dim(out, got[k], (me - k) % n, 0)
     return out
+
+
+def swap(value, sub, turn):
+    axis, stride = HOME[sub]
+    pairs = []
+    for i in range(16 if axis == "row" else 8):
+        at = i // stride % 4
+        pairs.append((i, i + ((at ^ turn) - at) * stride))
+    return lax.ppermute(value, axis, pairs)
+
+
+def halving_sum(value, sub):
+    me = place(sub)
+    pick = lambda k: lax.dynamic_index_in_dim(value, k, 0, keepdims=False)
+    kept = jnp.stack([pick(me), pick(3 - me)])
+    kept = kept + swap(jnp.stack([pick(me ^ 1), pick(3 - (me ^ 1))]), sub, 1)
+    return kept[0] + swap(kept[1], sub, 3)
+
+
+def doubling_gather(value, sub):
+    me = place(sub)
+    near = jnp.stack([value, swap(value, sub, 3)])
+    far = swap(near, sub, 1)
+    out = jnp.zeros((4,) + value.shape, value.dtype)
+    for k, piece in ((me, near[0]), (3 - me, near[1]), (me ^ 1, far[0]), (3 - (me ^ 1), far[1])):
+        out = lax.dynamic_update_index_in_dim(out, piece, k, 0)
+    return out
+
+
+def row_total(rows):
+    upper = (place("x") == 1) | (place("x") == 2)
+    lo, hi = rows[:PART], rows[-PART:]
+    part = jnp.where(upper, hi, lo) + swap(jnp.where(upper, lo, hi), "x", 1)
+    for sub, turn in (("x", 3), ("z", 1), ("z", 3)):
+        part = part + swap(part, sub, turn)
+    other = swap(part, "x", 1)
+    lo, hi = jnp.where(upper, other, part), jnp.where(upper, part, other)
+    return jnp.concatenate([lo, hi[2 * PART - rows.shape[0] :]], axis=0)
 
 
 def lane_of(value, k):
@@ -211,8 +249,8 @@
     ]
     fetch_mixed.start()
 
-    high, low = two_parts(inverse_ref[:RANK, :])
-    values = sketched_ref[...]
+    high, low = two_parts(inverse_ref[:RANK, :RANK])
+    values = sketched_ref[:RANK, :]
     projector[...] = (
         jnp.dot(low, values, preferred_element_type=f32) + jnp.dot(high, values, preferred_element_type=f32)
     ).astype(bf16)
@@ -262,7 +300,7 @@
 
 def adam_step(at, inverse, sketched, mixed, grad_turned, gathered, own_first, own_second):
     width, tokens = grad_turned.shape
-    columns, features = sketched.shape
+    features = sketched.shape[1]
     owned = own_first.shape[0]
     inside = pl.BlockSpec(memory_space=pltpu.VMEM)
     outside = pl.BlockSpec(memory_space=pl.ANY)
@@ -289,8 +327,8 @@
         ],
         compiler_params=pltpu.CompilerParams(vmem_limit_bytes=STEP_VMEM),
         cost_estimate=pl.CostEstimate(
-            flops=2 * RANK * width * (tokens + features) + 6 * RANK * columns * tokens,
-            bytes_accessed=width * (2 * tokens + 4 * RANK + 4 * features + 16 * owned) + 4 * tokens * columns,
+            flops=2 * RANK * width * (tokens + features) + 6 * RANK * RANK * tokens,
+            bytes_accessed=width * (2 * tokens + 4 * RANK + 4 * features + 16 * owned) + 4 * tokens * RANK,
             transcendentals=RANK * width,
         ),
         name="adam_step",
@@ -312,27 +350,17 @@
     sketched = sketched.reshape(columns, features)
 
     own_tokens = lax.dynamic_index_in_dim(
-        layer_input.reshape(4, 4, 8, share, features), lax.axis_index("col"), 2, keepdims=False
-    ).reshape(4, 4 * share, features)
-    left = [[owned_rows[k * STEP : k * STEP + PART], own_tokens[k]] for k in range(4)]
-    terms = lax.dot_general(
-        jnp.concatenate(sum(left, []), axis=0), sketched, (((1,), (1,)), ((), ())),
-        preferred_element_type=f32,
-    )
-    terms = scatter_sum(terms.reshape(4, PART + 4 * share, columns), "x")
-    terms = jnp.concatenate(
-        [
-            jnp.broadcast_to(terms[:PART], (4, PART, columns)),
-            terms[PART:].reshape(4, share, columns),
-        ],
-        axis=1,
-    )
-    terms = scatter_sum(terms, "z")
-    mixed = gather(gather(terms[PART:], "core"), "y").reshape(8 * share, columns)
+        layer_input.reshape(16, 8, share, features), lax.axis_index("col"), 1, keepdims=False
+    ).reshape(tokens // 8, features)
+    times = lambda a, b: lax.dot_general(a, b, (((1,), (1,)), ((), ())), preferred_element_type=f32)
+    mixed = times(own_tokens, sketched[:RANK])
+    mixed = halving_sum(mixed.reshape(4, 4 * share, RANK), "x")
+    mixed = halving_sum(mixed.reshape(4, share, RANK), "z")
+    mixed = doubling_gather(gather(mixed, "core"), "y").reshape(8 * share, RANK)
     mixed, gathered = lax.optimization_barrier((mixed, gathered))
     mixed = lax.all_gather(mixed, "row", axis=0, tiled=True)
-    gram = gather(terms[:PART], "x")
-    gram = jnp.concatenate([gram[0, :STEP], gram[1, :STEP], gram[2, :STEP], gram[3]], axis=0)
+
+    gram = row_total(times(owned_rows, sketched))
     gram = gather(gather(gram, "y").reshape(columns // 2, columns), "core")
 
     inverse = inverse_factor(gram.reshape(columns, columns))

time: 170 us -> 182 us (1.071)
  waiting for transfers between devices: 46.4 us -> 58.1 us
    ppermute x0 -> x11, waiting for transfers between devices: none -> 41.1 us  [swap(): return lax.ppermute(value, axis, pairs)]
    ppermute x25 -> x13, waiting for transfers between devices: 46.3 us -> 16.9 us  [shift(): return lax.ppermute(value, axis, pairs)]
    ppermute x0 -> x11, starting transfers between devices: none -> 14.8 us  [swap(): return lax.ppermute(value, axis, pairs)]
    ppermute x25 -> x13, starting transfers between devices: 40.1 us -> 26.3 us  [shift(): return lax.ppermute(value, axis, pairs)]
  transfers between devices with their start and end apart: 27 -> 26, of which waited for: 15 -> 19; matrix products, arithmetic and copies ran while one was open for 11% -> 11% of each run, Pallas kernels for 16% -> 15%
where the time goes in v6:
time: 182 us
  waiting for transfers between devices  58.1 us (32%)
  Pallas kernels  49 us (27%)
  starting transfers between devices  41.2 us (23%)
  between operations  14.5 us (8%)
  matrix products  14.1 us (8%)
  local copies, waits for them, and re-layouts  3.99 us (2%)
    ppermute x11, waiting for transfers between devices, swap(): return lax.ppermute(value, axis, pairs)  41.1 us
    pallas_call x1, Pallas kernels, inverse_factor(): pl.pallas_call(factor_kernel, out_shape=jax.ShapeDtypeStruct((size, size)...  27.5 us
    ppermute x13, starting transfers between devices, shift(): return lax.ppermute(value, axis, pairs)  26.3 us
    pallas_call x1, Pallas kernels, adam_step(): pl.pallas_call(step_kernel, out_shape=(jax.ShapeDtypeStruct((width, featu...  19.4 us
    ppermute x13, waiting for transfers between devices, shift(): return lax.ppermute(value, axis, pairs)  16.9 us
    ppermute x11, starting transfers between devices, swap(): return lax.ppermute(value, axis, pairs)  14.8 us
    dot_general x1, matrix products, sketched_term(): jnp.dot(sketch_turned, grad_turned, preferred_element_type=f32)  11.2 us
  transfers between devices with their start and end apart: 26, of which 19 were waited for; matrix products, arithmetic and copies ran while one was open for 11% of the time, Pallas kernels for 15%

profile of v6, /device:TPU:1, one launch (start us, length us, event | category | flops | bytes accessed | tf_op | source)
XLA Modules:
  0.0 182.1 jit_solution(1030457166382123359)
XLA Ops:
  7.2 2.0 %pack.1 = bf16[64,3696]{1,0:T(8,128)(2,1)} custom-call(f32[32,3696]{1,0:T(8,128)} %own_first_ref.1, f32[32,3696]{1,0:T(8,128)} %own_second_ref.1), custom_call_target="tpu_custom_call" | custom-call | tf_op jit(solution)/shard_map/pack/pallas_call | solution.py:216
  9.3 11.2 %fusion.17 = f32[576,1536]{1,0:T(8,128)S(1)} fusion(bf16[3696,576]{0,1:T(8,128)(2,1)} %param.7, bf16[1536,3696]{0,1:T(8,128)(2,1)} %param.6), kind=kOutput, calls=%fused_computation.64 | convolution fusion | flops 6539968512 | bytes 19150848 | tf_op jit(solution)/shard_map/dot_general | solution.py:224
  20.5 1.1 fusion.1
  21.7 1.1 fusion.4
  22.8 1.5 collective-permute-start
  24.3 1.3 collective-permute-done
  25.7 1.0 bitcast_add_fusion
  26.8 1.4 collective-permute-start.1
  28.2 1.5 collective-permute-start.3
  29.7 1.6 collective-permute-start.2
  31.3 0.5 collective-permute-done.1
  31.8 2.7 %collective-permute-done.2 = bf16[72,512]{1,0:T(8,128)(2,1)S(1)} collective-permute-done((bf16[72,512]{1,0:T(8,128)(2,1)S(1)}, bf16[72,512]{1,0:T(8,128)(2,1)S(1)}, u32[]{:S(2)}, u32[]{:S(2)}) %collective-permute-start.2) | collective-permute-done | bytes 73760 | tf_op jit(solution)/shard_map/ppermute | solution.py:40
  34.6 0.6 collective-permute-start.4
  35.2 2.1 %collective-permute-start.6 = (bf16[72,512]{1,0:T(8,128)(2,1)S(1)}, bf16[72,512]{1,0:T(8,128)(2,1)S(1)}, u32[]{:S(2)}, u32[]{:S(2)}) collective-permute-start(bf16[72,512]{1,0:T(8,128)(2,1)S(1)} %get-tuple-element.16), channel_id=1, source_target_pairs={{0,6},{1,7},{2,0},{3,1},{4,2},{5,3},{6,4},{7,5},{8,14},{9,15},{10,... | collective-permute-start | bytes 221192 | tf_op jit(solution)/shard_map/ppermute | solution.py:40
  37.3 0.4 collective-permute-start.5
  37.7 1.8 collective-permute-done.4
  39.5 2.8 %collective-permute-done.5 = bf16[72,512]{1,0:T(8,128)(2,1)S(1)} collective-permute-done((bf16[72,512]{1,0:T(8,128)(2,1)S(1)}, bf16[72,512]{1,0:T(8,128)(2,1)S(1)}, u32[]{:S(2)}, u32[]{:S(2)}) %collective-permute-start.5) | collective-permute-done | bytes 73760 | tf_op jit(solution)/shard_map/ppermute | solution.py:40
  42.3 3.4 %collective-permute-start.7 = (bf16[288,512]{1,0:T(8,128)(2,1)S(1)}, bf16[288,512]{1,0:T(8,128)(2,1)S(1)}, u32[]{:S(2)}, u32[]{:S(2)}) collective-permute-start(bf16[288,512]{1,0:T(8,128)(2,1)S(1)} %bitcast.96), channel_id=1, source_target_pairs={{0,1},{1,0},{2,3},{3,2},{4,5},{5,4},{6,7},{7,6},{8,9},{9,8},{10,11... | collective-permute-start | bytes 884744 | tf_op jit(solution)/shard_map/ppermute | solution.py:40
  45.7 1.5 reshape.54
  47.2 1.0 constant_dynamic-slice_fusion.8
  48.4 0.3 fusion.5
  48.8 1.4 collective-permute-start.17
  50.2 9.7 %collective-permute-done.17 = f32[2,48,512]{2,1,0:T(8,128)S(1)} collective-permute-done((f32[2,48,512]{2,1,0:T(8,128)S(1)}, f32[2,48,512]{2,1,0:T(8,128)S(1)}, u32[]{:S(2)}, u32[]{:S(2)}) %collective-permute-start.17) | collective-permute-done | bytes 196640 | tf_op jit(solution)/shard_map/ppermute | solution.py:68
  60.0 2.6 %collective-permute-start.18 = (f32[48,512]{1,0:T(8,128)S(1)}, f32[48,512]{1,0:T(8,128)S(1)}, u32[]{:S(2)}, u32[]{:S(2)}) collective-permute-start(f32[48,512]{1,0:T(8,128)S(1)} %slice_bitcast_fusion.2), channel_id=1, source_target_pairs={{0,96},{8,104},{16,112},{24,120},{32,64},{40,72},{48,80},{56,88},{... | collective-permute-start | bytes 294920 | tf_op jit(solution)/shard_map/ppermute | solution.py:68
  62.6 5.2 %collective-permute-done.18 = f32[48,512]{1,0:T(8,128)S(1)} collective-permute-done((f32[48,512]{1,0:T(8,128)S(1)}, f32[48,512]{1,0:T(8,128)S(1)}, u32[]{:S(2)}, u32[]{:S(2)}) %collective-permute-start.18) | collective-permute-done | bytes 98336 | tf_op jit(solution)/shard_map/ppermute | solution.py:68
  67.9 1.8 collective-permute-start.19
  69.7 3.5 %collective-permute-done.19 = f32[2,12,512]{2,1,0:T(8,128)S(1)} collective-permute-done((f32[2,12,512]{2,1,0:T(8,128)S(1)}, f32[2,12,512]{2,1,0:T(8,128)S(1)}, u32[]{:S(2)}, u32[]{:S(2)}) %collective-permute-start.19) | collective-permute-done | bytes 49184 | tf_op jit(solution)/shard_map/ppermute | solution.py:68
  73.3 3.4 %collective-permute-start.20 = (f32[12,512]{1,0:T(8,128)S(1)}, f32[12,512]{1,0:T(8,128)S(1)}, u32[]{:S(2)}, u32[]{:S(2)}) collective-permute-start(f32[12,512]{1,0:T(8,128)S(1)} %slice_bitcast_fusion.4), channel_id=1, source_target_pairs={{0,24},{8,16},{16,8},{24,0},{32,56},{40,48},{48,40},{56,32},{64,88... | collective-permute-start | bytes 73736 | tf_op jit(solution)/shard_map/ppermute | solution.py:68
  77.0 2.1 %collective-permute-done.20 = f32[12,512]{1,0:T(8,128)S(1)} collective-permute-done((f32[12,512]{1,0:T(8,128)S(1)}, f32[12,512]{1,0:T(8,128)S(1)}, u32[]{:S(2)}, u32[]{:S(2)}) %collective-permute-start.20) | collective-permute-done | bytes 24608 | tf_op jit(solution)/shard_map/ppermute | solution.py:68
  79.1 2.9 %collective-permute-start.21 = (f32[12,512]{1,0:T(8,128)S(1)}, f32[12,512]{1,0:T(8,128)S(1)}, u32[]{:S(2)}, u32[]{:S(2)}) collective-permute-start(f32[12,512]{1,0:T(8,128)S(1)} %get-tuple-element.14), channel_id=1, source_target_pairs={{0,1},{1,0},{2,3},{3,2},{4,5},{5,4},{6,7},{7,6},{8,9},{9,8},{10,11... | collective-permute-start | bytes 73736 | tf_op jit(solution)/shard_map/ppermute | solution.py:40
  82.1 0.8 collective-permute-done.21
  83.1 4.1 %collective-permute-done.22 = f32[2,12,512]{2,1,0:T(8,128)S(1)} collective-permute-done((f32[2,12,512]{2,1,0:T(8,128)S(1)}, f32[2,12,512]{2,1,0:T(8,128)S(1)}, u32[]{:S(2)}, u32[]{:S(2)}) %collective-permute-start.22) | collective-permute-done | bytes 49184 | tf_op jit(solution)/shard_map/ppermute | solution.py:68
  87.4 3.8 %collective-permute-done.23 = f32[2,2,12,512]{3,2,1,0:T(8,128)S(1)} collective-permute-done((f32[2,2,12,512]{3,2,1,0:T(8,128)S(1)}, f32[2,2,12,512]{3,2,1,0:T(8,128)S(1)}, u32[]{:S(2)}, u32[]{:S(2)}) %collective-permute-start.23) | collective-permute-done | bytes 98336 | tf_op jit(solution)/shard_map/ppermute | solution.py:68
  91.2 0.7 reshape.56
  91.9 2.5 %collective-permute-start.9 = (f32[40,576]{1,0:T(8,128)S(1)}, f32[40,576]{1,0:T(8,128)S(1)}, u32[]{:S(2)}, u32[]{:S(2)}) collective-permute-start(f32[40,576]{1,0:T(8,128)S(1)} %select_add_fusion), channel_id=1, source_target_pairs={{0,96},{8,104},{16,112},{24,120},{32,64},{40,72},{48,80},{56,88},{... | collective-permute-start | bytes 276488 | tf_op jit(solution)/shard_map/ppermute | solution.py:68
  94.5 2.3 %collective-permute-done.9 = f32[40,576]{1,0:T(8,128)S(1)} collective-permute-done((f32[40,576]{1,0:T(8,128)S(1)}, f32[40,576]{1,0:T(8,128)S(1)}, u32[]{:S(2)}, u32[]{:S(2)}) %collective-permute-start.9) | collective-permute-done | bytes 92192 | tf_op jit(solution)/shard_map/ppermute | solution.py:68
  96.9 3.5 %collective-permute-done.10 = f32[40,576]{1,0:T(8,128)S(1)} collective-permute-done((f32[40,576]{1,0:T(8,128)S(1)}, f32[40,576]{1,0:T(8,128)S(1)}, u32[]{:S(2)}, u32[]{:S(2)}) %collective-permute-start.10) | collective-permute-done | bytes 92192 | tf_op jit(solution)/shard_map/ppermute | solution.py:68
  100.4 2.4 %collective-permute-start.11 = (f32[40,576]{1,0:T(8,128)S(1)}, f32[40,576]{1,0:T(8,128)S(1)}, u32[]{:S(2)}, u32[]{:S(2)}) collective-permute-start(f32[40,576]{1,0:T(8,128)S(1)} %add.250), channel_id=1, source_target_pairs={{0,24},{8,16},{16,8},{24,0},{32,56},{40,48},{48,40},{56,32},{64,88... | collective-permute-start | bytes 276488 | tf_op jit(solution)/shard_map/ppermute | solution.py:68
  102.7 2.7 %collective-permute-done.11 = f32[40,576]{1,0:T(8,128)S(1)} collective-permute-done((f32[40,576]{1,0:T(8,128)S(1)}, f32[40,576]{1,0:T(8,128)S(1)}, u32[]{:S(2)}, u32[]{:S(2)}) %collective-permute-start.11) | collective-permute-done | bytes 92192 | tf_op jit(solution)/shard_map/ppermute | solution.py:68
  105.7 4.1 %collective-permute-done.12 = f32[40,576]{1,0:T(8,128)S(1)} collective-permute-done((f32[40,576]{1,0:T(8,128)S(1)}, f32[40,576]{1,0:T(8,128)S(1)}, u32[]{:S(2)}, u32[]{:S(2)}) %collective-permute-start.12) | collective-permute-done | bytes 92192 | tf_op jit(solution)/shard_map/ppermute | solution.py:68
  110.0 1.7 collective-permute-start.14
  111.7 1.0 collective-permute-start.15
  112.7 4.8 %collective-permute-done.13 = f32[72,576]{1,0:T(8,128)S(1)} collective-permute-done((f32[72,576]{1,0:T(8,128)S(1)}, f32[72,576]{1,0:T(8,128)S(1)}, u32[]{:S(2)}, u32[]{:S(2)}) %collective-permute-start.13) | collective-permute-done | bytes 165920 | tf_op jit(solution)/shard_map/ppermute | solution.py:40
  117.6 0.6 collective-permute-done.15
  118.2 8.1 %collective-permute-start.16 = (f32[288,576]{1,0:T(8,128)S(1)}, f32[288,576]{1,0:T(8,128)S(1)}, u32[]{:S(2)}, u32[]{:S(2)}) collective-permute-start(f32[288,576]{1,0:T(8,128)S(1)} %bitcast.92), channel_id=1, source_target_pairs={{0,1},{1,0},{2,3},{3,2},{4,5},{5,4},{6,7},{7,6},{8,9},{9,8},{10,11... | collective-permute-start | bytes 1990664 | tf_op jit(solution)/shard_map/ppermute | solution.py:40
  126.5 1.7 collective-permute-done.16
  128.2 27.5 %inverse_factor.1.inverse_ref = f32[576,576]{1,0:T(8,128)S(1)} custom-call(f32[576,576]{1,0:T(8,128)S(1)} %bitcast.89), custom_call_target="tpu_custom_call" | custom-call | flops 30576476160 | bytes 2654208 | tf_op jit(solution)/shard_map/inverse_factor/pallas_call | solution.py:191
  155.8 19.4 %adam_step.1 = (f32[3696,512]{1,0:T(8,128)}, f32[32,3696]{1,0:T(8,128)}, f32[32,3696]{1,0:T(8,128)}) custom-call(s32[1]{0:T(128)} %bitcast.at_ref, f32[576,576]{1,0:T(8,128)S(1)} %inverse_factor.1.inverse_ref, bf16[576,512]{1,0:T(8,128)(2,1)S(1)} %bitcast.88, f32[1536,512]{1,0:T(8,128)} %all-gather.4.cloned.1.call-done.mixed_ref, ...), custom_call_target="tpu_custom_call" | custom-call | flops 10166992896 | bytes 31531008 | tf_op jit(solution)/shard_map/adam_step/pallas_call | solution.py:307
  (70 shorter events, 2.2 us)
Async XLA Ops:
  7.2 84.7 %all-gather.6.cloned.1.call-start = ((), (), s32[]{:S(2)}) async-start(), calls=%async_computation.1 | async-start | bytes 8077312 | tf_op jit(solution)/shard_map/all_gather | solution.py:344
  9.2 146.6 %all-gather.4.cloned.1.call-start = ((), (), s32[]{:S(2)}) async-start(), calls=%async_computation | async-start | bytes 3342336 | tf_op jit(solution)/shard_map/all_gather | solution.py:361
  9.3 11.2 %copy-start.2 = (bf16[1536,512]{1,0:T(8,128)(2,1)S(1)}, bf16[1536,512]{1,0:T(8,128)(2,1)}, u32[]{:S(2)}) copy-start(bf16[1536,512]{1,0:T(8,128)(2,1)} %param.5) | copy-start | bytes 4718596
  22.8 2.8 %collective-permute-start = (bf16[288,512]{1,0:T(8,128)(2,1)S(1)}, bf16[288,512]{1,0:T(8,128)(2,1)}, u32[]{:S(2)}, u32[]{:S(2)}) collective-permute-start(bf16[288,512]{1,0:T(8,128)(2,1)S(1)} %fusion.6), channel_id=1, source_target_pairs={{0,1},{1,0},{2,3},{3,2},{4,5},{5,4},{6,7},{7,6},{8,9},{9,8},{10,11... | collective-permute-start | bytes 884744 | tf_op jit(solution)/shard_map/ppermute | solution.py:40
  26.8 5.1 %collective-permute-start.1 = (bf16[72,512]{1,0:T(8,128)(2,1)S(1)}, bf16[72,512]{1,0:T(8,128)(2,1)S(1)}, u32[]{:S(2)}, u32[]{:S(2)}) collective-permute-start(bf16[72,512]{1,0:T(8,128)(2,1)S(1)} %get-tuple-element.17), channel_id=1, source_target_pairs={{0,2},{1,3},{2,4},{3,5},{4,6},{5,7},{6,0},{7,1},{8,10},{9,11},{10,... | collective-permute-start | bytes 221192 | tf_op jit(solution)/shard_map/ppermute | solution.py:40
  28.2 3.6 %collective-permute-start.3 = (bf16[72,512]{1,0:T(8,128)(2,1)S(1)}, bf16[72,512]{1,0:T(8,128)(2,1)S(1)}, u32[]{:S(2)}, u32[]{:S(2)}) collective-permute-start(bf16[72,512]{1,0:T(8,128)(2,1)S(1)} %get-tuple-element.18), channel_id=1, source_target_pairs={{0,6},{1,7},{2,0},{3,1},{4,2},{5,3},{6,4},{7,5},{8,14},{9,15},{10,... | collective-permute-start | bytes 221192 | tf_op jit(solution)/shard_map/ppermute | solution.py:40
  29.7 4.8 %collective-permute-start.2 = (bf16[72,512]{1,0:T(8,128)(2,1)S(1)}, bf16[72,512]{1,0:T(8,128)(2,1)S(1)}, u32[]{:S(2)}, u32[]{:S(2)}) collective-permute-start(bf16[72,512]{1,0:T(8,128)(2,1)S(1)} %get-tuple-element.19), channel_id=1, source_target_pairs={{0,4},{1,5},{2,6},{3,7},{4,0},{5,1},{6,2},{7,3},{8,12},{9,13},{10,... | collective-permute-start | bytes 221192 | tf_op jit(solution)/shard_map/ppermute | solution.py:40
  34.6 4.9 %collective-permute-start.4 = (bf16[72,512]{1,0:T(8,128)(2,1)S(1)}, bf16[72,512]{1,0:T(8,128)(2,1)S(1)}, u32[]{:S(2)}, u32[]{:S(2)}) collective-permute-start(bf16[72,512]{1,0:T(8,128)(2,1)S(1)} %get-tuple-element.16), channel_id=1, source_target_pairs={{0,2},{1,3},{2,4},{3,5},{4,6},{5,7},{6,0},{7,1},{8,10},{9,11},{10,... | collective-permute-start | bytes 221192 | tf_op jit(solution)/shard_map/ppermute | solution.py:40
  35.2 7.0 %collective-permute-start.6 = (bf16[72,512]{1,0:T(8,128)(2,1)S(1)}, bf16[72,512]{1,0:T(8,128)(2,1)S(1)}, u32[]{:S(2)}, u32[]{:S(2)}) collective-permute-start(bf16[72,512]{1,0:T(8,128)(2,1)S(1)} %get-tuple-element.16), channel_id=1, source_target_pairs={{0,6},{1,7},{2,0},{3,1},{4,2},{5,3},{6,4},{7,5},{8,14},{9,15},{10,... | collective-permute-start | bytes 221192 | tf_op jit(solution)/shard_map/ppermute | solution.py:40
  37.3 4.9 %collective-permute-start.5 = (bf16[72,512]{1,0:T(8,128)(2,1)S(1)}, bf16[72,512]{1,0:T(8,128)(2,1)S(1)}, u32[]{:S(2)}, u32[]{:S(2)}) collective-permute-start(bf16[72,512]{1,0:T(8,128)(2,1)S(1)} %get-tuple-element.16), channel_id=1, source_target_pairs={{0,4},{1,5},{2,6},{3,7},{4,0},{5,1},{6,2},{7,3},{8,12},{9,13},{10,... | collective-permute-start | bytes 221192 | tf_op jit(solution)/shard_map/ppermute | solution.py:40
  42.3 6.1 %collective-permute-start.7 = (bf16[288,512]{1,0:T(8,128)(2,1)S(1)}, bf16[288,512]{1,0:T(8,128)(2,1)S(1)}, u32[]{:S(2)}, u32[]{:S(2)}) collective-permute-start(bf16[288,512]{1,0:T(8,128)(2,1)S(1)} %bitcast.96), channel_id=1, source_target_pairs={{0,1},{1,0},{2,3},{3,2},{4,5},{5,4},{6,7},{7,6},{8,9},{9,8},{10,11... | collective-permute-start | bytes 884744 | tf_op jit(solution)/shard_map/ppermute | solution.py:40
  48.8 11.1 %collective-permute-start.17 = (f32[2,48,512]{2,1,0:T(8,128)S(1)}, f32[2,48,512]{2,1,0:T(8,128)S(1)}, u32[]{:S(2)}, u32[]{:S(2)}) collective-permute-start(f32[2,48,512]{2,1,0:T(8,128)S(1)} %pad_maximum_fusion), channel_id=1, source_target_pairs={{0,32},{8,40},{16,48},{24,56},{32,0},{40,8},{48,16},{56,24},{64,96... | collective-permute-start | bytes 589832 | tf_op jit(solution)/shard_map/ppermute | solution.py:68
  60.0 7.9 %collective-permute-start.18 = (f32[48,512]{1,0:T(8,128)S(1)}, f32[48,512]{1,0:T(8,128)S(1)}, u32[]{:S(2)}, u32[]{:S(2)}) collective-permute-start(f32[48,512]{1,0:T(8,128)S(1)} %slice_bitcast_fusion.2), channel_id=1, source_target_pairs={{0,96},{8,104},{16,112},{24,120},{32,64},{40,72},{48,80},{56,88},{... | collective-permute-start | bytes 294920 | tf_op jit(solution)/shard_map/ppermute | solution.py:68
  67.9 5.3 %collective-permute-start.19 = (f32[2,12,512]{2,1,0:T(8,128)S(1)}, f32[2,12,512]{2,1,0:T(8,128)S(1)}, u32[]{:S(2)}, u32[]{:S(2)}) collective-permute-start(f32[2,12,512]{2,1,0:T(8,128)S(1)} %pad_maximum_fusion.3), channel_id=1, source_target_pairs={{0,8},{8,0},{16,24},{24,16},{32,40},{40,32},{48,56},{56,48},{64,72... | collective-permute-start | bytes 147464 | tf_op jit(solution)/shard_map/ppermute | solution.py:68
  73.3 5.8 %collective-permute-start.20 = (f32[12,512]{1,0:T(8,128)S(1)}, f32[12,512]{1,0:T(8,128)S(1)}, u32[]{:S(2)}, u32[]{:S(2)}) collective-permute-start(f32[12,512]{1,0:T(8,128)S(1)} %slice_bitcast_fusion.4), channel_id=1, source_target_pairs={{0,24},{8,16},{16,8},{24,0},{32,56},{40,48},{48,40},{56,32},{64,88... | collective-permute-start | bytes 73736 | tf_op jit(solution)/shard_map/ppermute | solution.py:68
  79.1 3.8 %collective-permute-start.21 = (f32[12,512]{1,0:T(8,128)S(1)}, f32[12,512]{1,0:T(8,128)S(1)}, u32[]{:S(2)}, u32[]{:S(2)}) collective-permute-start(f32[12,512]{1,0:T(8,128)S(1)} %get-tuple-element.14), channel_id=1, source_target_pairs={{0,1},{1,0},{2,3},{3,2},{4,5},{5,4},{6,7},{7,6},{8,9},{9,8},{10,11... | collective-permute-start | bytes 73736 | tf_op jit(solution)/shard_map/ppermute | solution.py:40
  82.1 9.9 %collective-permute-start.8 = (f32[40,576]{1,0:T(8,128)S(1)}, f32[40,576]{1,0:T(8,128)S(1)}, u32[]{:S(2)}, u32[]{:S(2)}) collective-permute-start(f32[40,576]{1,0:T(8,128)S(1)} %slice_select_fusion), channel_id=1, source_target_pairs={{0,32},{8,40},{16,48},{24,56},{32,0},{40,8},{48,16},{56,24},{64,96... | collective-permute-start | bytes 276488 | tf_op jit(solution)/shard_map/ppermute | solution.py:68
  82.9 4.3 %collective-permute-start.22 = (f32[2,12,512]{2,1,0:T(8,128)S(1)}, f32[2,12,512]{2,1,0:T(8,128)S(1)}, u32[]{:S(2)}, u32[]{:S(2)}) collective-permute-start(f32[2,12,512]{2,1,0:T(8,128)S(1)} %bitcast_dynamic-update-slice_fusion.12), channel_id=1, source_target_pairs={{0,6},{1,7},{2,4},{3,5},{4,2},{5,3},{6,0},{7,1},{8,14},{9,15},{10,... | collective-permute-start | bytes 147464 | tf_op jit(solution)/shard_map/ppermute | solution.py:68
  87.2 3.9 %collective-permute-start.23 = (f32[2,2,12,512]{3,2,1,0:T(8,128)S(1)}, f32[2,2,12,512]{3,2,1,0:T(8,128)S(1)}, u32[]{:S(2)}, u32[]{:S(2)}) collective-permute-start(f32[2,2,12,512]{3,2,1,0:T(8,128)S(1)} %pad_maximum_fusion.2), channel_id=1, source_target_pairs={{0,2},{1,3},{2,0},{3,1},{4,6},{5,7},{6,4},{7,5},{8,10},{9,11},{10,... | collective-permute-start | bytes 294920 | tf_op jit(solution)/shard_map/ppermute | solution.py:68
  91.9 4.8 %collective-permute-start.9 = (f32[40,576]{1,0:T(8,128)S(1)}, f32[40,576]{1,0:T(8,128)S(1)}, u32[]{:S(2)}, u32[]{:S(2)}) collective-permute-start(f32[40,576]{1,0:T(8,128)S(1)} %select_add_fusion), channel_id=1, source_target_pairs={{0,96},{8,104},{16,112},{24,120},{32,64},{40,72},{48,80},{56,88},{... | collective-permute-start | bytes 276488 | tf_op jit(solution)/shard_map/ppermute | solution.py:68
  96.8 3.6 %collective-permute-start.10 = (f32[40,576]{1,0:T(8,128)S(1)}, f32[40,576]{1,0:T(8,128)S(1)}, u32[]{:S(2)}, u32[]{:S(2)}) collective-permute-start(f32[40,576]{1,0:T(8,128)S(1)} %add.249), channel_id=1, source_target_pairs={{0,8},{8,0},{16,24},{24,16},{32,40},{40,32},{48,56},{56,48},{64,72... | collective-permute-start | bytes 276488 | tf_op jit(solution)/shard_map/ppermute | solution.py:68
  100.4 5.1 %collective-permute-start.11 = (f32[40,576]{1,0:T(8,128)S(1)}, f32[40,576]{1,0:T(8,128)S(1)}, u32[]{:S(2)}, u32[]{:S(2)}) collective-permute-start(f32[40,576]{1,0:T(8,128)S(1)} %add.250), channel_id=1, source_target_pairs={{0,24},{8,16},{16,8},{24,0},{32,56},{40,48},{48,40},{56,32},{64,88... | collective-permute-start | bytes 276488 | tf_op jit(solution)/shard_map/ppermute | solution.py:68
  105.5 4.4 %collective-permute-start.12 = (f32[40,576]{1,0:T(8,128)S(1)}, f32[40,576]{1,0:T(8,128)S(1)}, u32[]{:S(2)}, u32[]{:S(2)}) collective-permute-start(f32[40,576]{1,0:T(8,128)S(1)} %add.251), channel_id=1, source_target_pairs={{0,32},{8,40},{16,48},{24,56},{32,0},{40,8},{48,16},{56,24},{64,96... | collective-permute-start | bytes 276488 | tf_op jit(solution)/shard_map/ppermute | solution.py:68
  109.9 7.6 %collective-permute-start.13 = (f32[72,576]{1,0:T(8,128)S(1)}, f32[72,576]{1,0:T(8,128)S(1)}, u32[]{:S(2)}, u32[]{:S(2)}) collective-permute-start(f32[72,576]{1,0:T(8,128)S(1)} %pad_maximum_fusion.1), channel_id=1, source_target_pairs={{0,2},{1,3},{2,4},{3,5},{4,6},{5,7},{6,0},{7,1},{8,10},{9,11},{10,... | collective-permute-start | bytes 497672 | tf_op jit(solution)/shard_map/ppermute | solution.py:40
  110.0 7.6 %collective-permute-start.14 = (f32[72,576]{1,0:T(8,128)S(1)}, f32[72,576]{1,0:T(8,128)S(1)}, u32[]{:S(2)}, u32[]{:S(2)}) collective-permute-start(f32[72,576]{1,0:T(8,128)S(1)} %pad_maximum_fusion.1), channel_id=1, source_target_pairs={{0,4},{1,5},{2,6},{3,7},{4,0},{5,1},{6,2},{7,3},{8,12},{9,13},{10,... | collective-permute-start | bytes 497672 | tf_op jit(solution)/shard_map/ppermute | solution.py:40
  111.7 6.5 %collective-permute-start.15 = (f32[72,576]{1,0:T(8,128)S(1)}, f32[72,576]{1,0:T(8,128)S(1)}, u32[]{:S(2)}, u32[]{:S(2)}) collective-permute-start(f32[72,576]{1,0:T(8,128)S(1)} %pad_maximum_fusion.1), channel_id=1, source_target_pairs={{0,6},{1,7},{2,0},{3,1},{4,2},{5,3},{6,4},{7,5},{8,14},{9,15},{10,... | collective-permute-start | bytes 497672 | tf_op jit(solution)/shard_map/ppermute | solution.py:40
  118.2 10.0 %collective-permute-start.16 = (f32[288,576]{1,0:T(8,128)S(1)}, f32[288,576]{1,0:T(8,128)S(1)}, u32[]{:S(2)}, u32[]{:S(2)}) collective-permute-start(f32[288,576]{1,0:T(8,128)S(1)} %bitcast.92), channel_id=1, source_target_pairs={{0,1},{1,0},{2,3},{3,2},{4,5},{5,4},{6,7},{7,6},{8,9},{9,8},{10,11... | collective-permute-start | bytes 1990664 | tf_op jit(solution)/shard_map/ppermute | solution.py:40
  128.2 27.6 %copy-start = (f32[32,3696]{1,0:T(8,128)S(1)}, f32[32,3696]{1,0:T(8,128)}, u32[]{:S(2)}) copy-start(f32[32,3696]{1,0:T(8,128)} %own_first_ref.1) | copy-start | bytes 1419268
  128.2 27.6 %copy-start.1 = (f32[32,3696]{1,0:T(8,128)S(1)}, f32[32,3696]{1,0:T(8,128)}, u32[]{:S(2)}) copy-start(f32[32,3696]{1,0:T(8,128)} %own_second_ref.1) | copy-start | bytes 1419268
Sparse Core Ops, SparseCore 0:
  10.8 73.4 all-gather.5
  92.0 48.7 all-gather.3

commit v7 on v5

--- a/solution.py
+++ b/solution.py
@@ -11,7 +11,6 @@
 TILE = 1024
 MIX_TILE = 512
 STEP_VMEM = 50 << 20
-PART, STEP = 24, 16
 
 beta_one = 0.9
 beta_two = 0.999
@@ -211,8 +210,8 @@
     ]
     fetch_mixed.start()
 
-    high, low = two_parts(inverse_ref[:RANK, :])
-    values = sketched_ref[...]
+    high, low = two_parts(inverse_ref[:RANK, :RANK])
+    values = sketched_ref[:RANK, :]
     projector[...] = (
         jnp.dot(low, values, preferred_element_type=f32) + jnp.dot(high, values, preferred_element_type=f32)
     ).astype(bf16)
@@ -262,7 +261,7 @@
 
 def adam_step(at, inverse, sketched, mixed, grad_turned, gathered, own_first, own_second):
     width, tokens = grad_turned.shape
-    columns, features = sketched.shape
+    features = sketched.shape[1]
     owned = own_first.shape[0]
     inside = pl.BlockSpec(memory_space=pltpu.VMEM)
     outside = pl.BlockSpec(memory_space=pl.ANY)
@@ -289,8 +288,8 @@
         ],
         compiler_params=pltpu.CompilerParams(vmem_limit_bytes=STEP_VMEM),
         cost_estimate=pl.CostEstimate(
-            flops=2 * RANK * width * (tokens + features) + 6 * RANK * columns * tokens,
-            bytes_accessed=width * (2 * tokens + 4 * RANK + 4 * features + 16 * owned) + 4 * tokens * columns,
+            flops=2 * RANK * width * (tokens + features) + 6 * RANK * RANK * tokens,
+            bytes_accessed=width * (2 * tokens + 4 * RANK + 4 * features + 16 * owned) + 4 * tokens * RANK,
             transcendentals=RANK * width,
         ),
         name="adam_step",
@@ -312,27 +311,24 @@
     sketched = sketched.reshape(columns, features)
 
     own_tokens = lax.dynamic_index_in_dim(
-        layer_input.reshape(4, 4, 8, share, features), lax.axis_index("col"), 2, keepdims=False
-    ).reshape(4, 4 * share, features)
-    left = [[owned_rows[k * STEP : k * STEP + PART], own_tokens[k]] for k in range(4)]
+        layer_input.reshape(16, 8, share, features), lax.axis_index("col"), 1, keepdims=False
+    )
+    chunks = [owned_rows[8 * (i % (own // 8)) : 8 * (i % (own // 8)) + 8] for i in range(16)]
+    left = jnp.concatenate([jnp.stack(chunks), own_tokens], axis=1)
     terms = lax.dot_general(
-        jnp.concatenate(sum(left, []), axis=0), sketched, (((1,), (1,)), ((), ())),
+        left.reshape(16 * (8 + share), features), sketched, (((1,), (1,)), ((), ())),
         preferred_element_type=f32,
     )
-    terms = scatter_sum(terms.reshape(4, PART + 4 * share, columns), "x")
-    terms = jnp.concatenate(
-        [
-            jnp.broadcast_to(terms[:PART], (4, PART, columns)),
-            terms[PART:].reshape(4, share, columns),
-        ],
-        axis=1,
-    )
-    terms = scatter_sum(terms, "z")
-    mixed = gather(gather(terms[PART:], "core"), "y").reshape(8 * share, columns)
+    terms = lax.all_to_all(terms.reshape(16, 8 + share, columns), "row", 0, 0, tiled=False)
+    terms = terms.sum(axis=0)
+
+    mixed = gather(terms[8:, :RANK], "core")
+    gram = gather(terms[:8], "z")
+    mixed, gram = lax.optimization_barrier((mixed, gram))
+    mixed = gather(mixed, "y").reshape(8 * share, RANK)
+    gram = gather(gram.reshape(32, columns), "x").reshape(128, columns)[:own]
     mixed, gathered = lax.optimization_barrier((mixed, gathered))
     mixed = lax.all_gather(mixed, "row", axis=0, tiled=True)
-    gram = gather(terms[:PART], "x")
-    gram = jnp.concatenate([gram[0, :STEP], gram[1, :STEP], gram[2, :STEP], gram[3]], axis=0)
     gram = gather(gather(gram, "y").reshape(columns // 2, columns), "core")
 
     inverse = inverse_factor(gram.reshape(columns, columns))

time: 170 us -> 171 us (level)
  starting transfers between devices: 40.1 us -> 42.1 us
    ppermute x25 -> x22, waiting for transfers between devices: 46.3 us -> 22.8 us  [shift(): return lax.ppermute(value, axis, pairs)]
    all_to_all x0 -> x1, waiting for transfers between devices: none -> 23.1 us  [local(): lax.all_to_all(terms.reshape(16, 8 + share, columns), 'row', 0, 0, tiled=...]
    all_to_all x0 -> x1, starting transfers between devices: none -> 7.6 us  [local(): lax.all_to_all(terms.reshape(16, 8 + share, columns), 'row', 0, 0, tiled=...]
    ppermute x25 -> x22, starting transfers between devices: 40.1 us -> 34.5 us  [shift(): return lax.ppermute(value, axis, pairs)]
  transfers between devices with their start and end apart: 27 -> 25, of which waited for: 15 -> 10; matrix products, arithmetic and copies ran while one was open for 11% -> 11% of each run, Pallas kernels for 16% -> 16%
where the time goes in v7:
time: 171 us
  Pallas kernels  49.2 us (29%)
  waiting for transfers between devices  46 us (27%)
  starting transfers between devices  42.1 us (25%)
  matrix products  14.9 us (9%)
  between operations  14.8 us (9%)
  local copies, waits for them, and re-layouts  4 us (2%)
    ppermute x22, starting transfers between devices, shift(): return lax.ppermute(value, axis, pairs)  34.5 us
    pallas_call x1, Pallas kernels, inverse_factor(): pl.pallas_call(factor_kernel, out_shape=jax.ShapeDtypeStruct((size, size)...  27.7 us
    all_to_all x1, waiting for transfers between devices, local(): lax.all_to_all(terms.reshape(16, 8 + share, columns), 'row', 0, 0, tiled=...  23.1 us
    ppermute x22, waiting for transfers between devices, shift(): return lax.ppermute(value, axis, pairs)  22.8 us
    pallas_call x1, Pallas kernels, adam_step(): pl.pallas_call(step_kernel, out_shape=(jax.ShapeDtypeStruct((width, featu...  19.4 us
    dot_general x1, matrix products, sketched_term(): jnp.dot(sketch_turned, grad_turned, preferred_element_type=f32)  11.2 us
    all_to_all x1, starting transfers between devices, local(): lax.all_to_all(terms.reshape(16, 8 + share, columns), 'row', 0, 0, tiled=...  7.6 us
  transfers between devices with their start and end apart: 25, of which 10 were waited for; matrix products, arithmetic and copies ran while one was open for 11% of the time, Pallas kernels for 16%

profile of v7, /device:TPU:1, one launch (start us, length us, event | category | flops | bytes accessed | tf_op | source)
XLA Modules:
  0.0 171.2 jit_solution(8725690222997785439)
XLA Ops:
  7.2 0.0 all-gather.6.cloned.1.call-start
  7.2 2.0 %pack.1 = bf16[64,3696]{1,0:T(8,128)(2,1)} custom-call(f32[32,3696]{1,0:T(8,128)} %own_first_ref.1, f32[32,3696]{1,0:T(8,128)} %own_second_ref.1), custom_call_target="tpu_custom_call" | custom-call | tf_op jit(solution)/shard_map/pack/pallas_call | solution.py:177
  9.3 11.2 %fusion.18 = f32[576,1536]{1,0:T(8,128)S(1)} fusion(bf16[3696,576]{0,1:T(8,128)(2,1)} %param.7, bf16[1536,3696]{0,1:T(8,128)(2,1)} %param.6), kind=kOutput, calls=%fused_computation.76 | convolution fusion | flops 6539968512 | bytes 19150848 | tf_op jit(solution)/shard_map/dot_general | solution.py:185
  20.5 1.1 fusion.1
  21.6 1.1 fusion.4
  22.8 1.5 collective-permute-start
  24.3 1.5 reshape.53
  25.8 0.1 bitcast_add_fusion
  25.9 1.4 collective-permute-start.1
  27.4 1.5 collective-permute-start.3
  28.9 1.6 collective-permute-start.2
  30.4 1.0 dynamic-slice_bitcast_fusion
  31.4 2.1 %collective-permute-done.2 = bf16[72,512]{1,0:T(8,128)(2,1)S(1)} collective-permute-done((bf16[72,512]{1,0:T(8,128)(2,1)S(1)}, bf16[72,512]{1,0:T(8,128)(2,1)S(1)}, u32[]{:S(2)}, u32[]{:S(2)}) %collective-permute-start.2) | collective-permute-done | bytes 73760 | tf_op jit(solution)/shard_map/ppermute | solution.py:39
  33.7 1.5 collective-permute-start.6
  35.1 1.2 collective-permute-start.5
  36.4 4.3 %collective-permute-done.4 = bf16[72,512]{1,0:T(8,128)(2,1)S(1)} collective-permute-done((bf16[72,512]{1,0:T(8,128)(2,1)S(1)}, bf16[72,512]{1,0:T(8,128)(2,1)S(1)}, u32[]{:S(2)}, u32[]{:S(2)}) %collective-permute-start.4) | collective-permute-done | bytes 73760 | tf_op jit(solution)/shard_map/ppermute | solution.py:39
  40.8 3.4 %collective-permute-start.7 = (bf16[288,512]{1,0:T(8,128)(2,1)S(1)}, bf16[288,512]{1,0:T(8,128)(2,1)S(1)}, u32[]{:S(2)}, u32[]{:S(2)}) collective-permute-start(bf16[288,512]{1,0:T(8,128)(2,1)S(1)} %bitcast.155), channel_id=1, source_target_pairs={{0,1},{1,0},{2,3},{3,2},{4,5},{5,4},{6,7},{7,6},{8,9},{9,8},{10,11... | collective-permute-start | bytes 884744 | tf_op jit(solution)/shard_map/ppermute | solution.py:39
  44.2 1.1 collective-permute-done.7
  45.4 1.5 fusion.5
  46.8 7.6 %all-to-all-start = ((f32[16,20,576]{2,1,0:T(8,128)}), f32[16,20,576]{2,1,0:T(8,128)S(1)}, u32[]{:S(2)}, u32[]{:S(2)}) async-start(f32[16,20,576]{2,1,0:T(8,128)} %fusion.5), calls=%async_computation | async-start | bytes 1966080 | tf_op jit(solution)/shard_map/all_to_all | solution.py:322
  54.4 0.0 all-gather.4.cloned.1.call-start
  54.6 23.1 %all-to-all-done = f32[16,20,576]{2,1,0:T(8,128)S(1)} async-done(((f32[16,20,576]{2,1,0:T(8,128)}), f32[16,20,576]{2,1,0:T(8,128)S(1)}, u32[]{:S(2)}, u32[]{:S(2)}) %all-to-all-start) | async-done | bytes 737312 | tf_op jit(solution)/shard_map/all_to_all | solution.py:322
  77.7 0.1 reduce_sum.9
  77.8 4.5 %collective-permute-start.10 = (f32[8,576]{1,0:T(8,128)S(1)}, f32[8,576]{1,0:T(8,128)S(1)}, u32[]{:S(2)}, u32[]{:S(2)}) collective-permute-start(f32[8,576]{1,0:T(8,128)S(1)} %slice.65), channel_id=1, source_target_pairs={{0,16},{8,24},{16,0},{24,8},{32,48},{40,56},{48,32},{56,40},{64,80... | collective-permute-start | bytes 55304 | tf_op jit(solution)/shard_map/ppermute | solution.py:39
  82.3 0.3 collective-permute-start.9
  82.6 2.4 %collective-permute-start.11 = (f32[8,576]{1,0:T(8,128)S(1)}, f32[8,576]{1,0:T(8,128)S(1)}, u32[]{:S(2)}, u32[]{:S(2)}) collective-permute-start(f32[8,576]{1,0:T(8,128)S(1)} %slice.65), channel_id=1, source_target_pairs={{0,24},{8,0},{16,8},{24,16},{32,56},{40,32},{48,40},{56,48},{64,88... | collective-permute-start | bytes 55304 | tf_op jit(solution)/shard_map/ppermute | solution.py:39
  84.9 2.3 %collective-permute-start.8 = (f32[12,512]{1,0:T(8,128)S(1)}, f32[12,512]{1,0:T(8,128)S(1)}, u32[]{:S(2)}, u32[]{:S(2)}) collective-permute-start(f32[12,512]{1,0:T(8,128)S(1)} %slice.64), channel_id=1, source_target_pairs={{0,1},{1,0},{2,3},{3,2},{4,5},{5,4},{6,7},{7,6},{8,9},{9,8},{10,11... | collective-permute-start | bytes 73736 | tf_op jit(solution)/shard_map/ppermute | solution.py:39
  87.4 0.7 collective-permute-done.8
  88.2 0.3 collective-permute-start.21
  88.5 0.7 collective-permute-start.20
  89.2 0.8 collective-permute-start.19
  90.0 3.8 %collective-permute-done.19 = f32[2,12,512]{2,1,0:T(8,128)S(1)} collective-permute-done((f32[2,12,512]{2,1,0:T(8,128)S(1)}, f32[2,12,512]{2,1,0:T(8,128)S(1)}, u32[]{:S(2)}, u32[]{:S(2)}) %collective-permute-start.19) | collective-permute-done | bytes 49184 | tf_op jit(solution)/shard_map/ppermute | solution.py:39
  93.9 0.7 reshape.60
  94.7 0.8 collective-permute-start.14
  95.5 1.2 collective-permute-start.13
  96.7 0.8 collective-permute-start.12
  97.5 3.7 %collective-permute-done.12 = f32[32,576]{1,0:T(8,128)S(1)} collective-permute-done((f32[32,576]{1,0:T(8,128)S(1)}, f32[32,576]{1,0:T(8,128)S(1)}, u32[]{:S(2)}, u32[]{:S(2)}) %collective-permute-start.12) | collective-permute-done | bytes 73760 | tf_op jit(solution)/shard_map/ppermute | solution.py:39
  101.3 3.4 %collective-permute-start.16 = (f32[72,576]{1,0:T(8,128)S(1)}, f32[72,576]{1,0:T(8,128)S(1)}, u32[]{:S(2)}, u32[]{:S(2)}) collective-permute-start(f32[72,576]{1,0:T(8,128)S(1)} %slice.66), channel_id=1, source_target_pairs={{0,4},{1,5},{2,6},{3,7},{4,0},{5,1},{6,2},{7,3},{8,12},{9,13},{10,... | collective-permute-start | bytes 497672 | tf_op jit(solution)/shard_map/ppermute | solution.py:39
  104.7 2.7 %collective-permute-start.17 = (f32[72,576]{1,0:T(8,128)S(1)}, f32[72,576]{1,0:T(8,128)S(1)}, u32[]{:S(2)}, u32[]{:S(2)}) collective-permute-start(f32[72,576]{1,0:T(8,128)S(1)} %slice.66), channel_id=1, source_target_pairs={{0,6},{1,7},{2,0},{3,1},{4,2},{5,3},{6,4},{7,5},{8,14},{9,15},{10,... | collective-permute-start | bytes 497672 | tf_op jit(solution)/shard_map/ppermute | solution.py:39
  107.5 5.3 %collective-permute-done.15 = f32[72,576]{1,0:T(8,128)S(1)} collective-permute-done((f32[72,576]{1,0:T(8,128)S(1)}, f32[72,576]{1,0:T(8,128)S(1)}, u32[]{:S(2)}, u32[]{:S(2)}) %collective-permute-start.15) | collective-permute-done | bytes 165920 | tf_op jit(solution)/shard_map/ppermute | solution.py:39
  112.8 0.1 collective-permute-done.17
  112.9 2.3 %collective-permute-start.18 = (f32[288,576]{1,0:T(8,128)S(1)}, f32[288,576]{1,0:T(8,128)S(1)}, u32[]{:S(2)}, u32[]{:S(2)}) collective-permute-start(f32[288,576]{1,0:T(8,128)S(1)} %bitcast.149), channel_id=1, source_target_pairs={{0,1},{1,0},{2,3},{3,2},{4,5},{5,4},{6,7},{7,6},{8,9},{9,8},{10,11... | collective-permute-start | bytes 1990664 | tf_op jit(solution)/shard_map/ppermute | solution.py:39
  115.1 0.1 broadcast_in_dim.110
  115.2 0.1 bitcast_dynamic-update-slice_fusion.1
  115.3 1.7 collective-permute-done.18
  117.0 0.1 bitcast_dynamic-update-slice_fusion
  117.1 27.7 %inverse_factor.1.inverse_ref = f32[576,576]{1,0:T(8,128)S(1)} custom-call(f32[576,576]{1,0:T(8,128)S(1)} %bitcast.146), custom_call_target="tpu_custom_call" | custom-call | flops 30576476160 | bytes 2654208 | tf_op jit(solution)/shard_map/inverse_factor/pallas_call | solution.py:152
  144.9 19.4 %adam_step.1 = (f32[3696,512]{1,0:T(8,128)}, f32[32,3696]{1,0:T(8,128)}, f32[32,3696]{1,0:T(8,128)}) custom-call(s32[1]{0:T(128)} %bitcast.at_ref, f32[576,576]{1,0:T(8,128)S(1)} %inverse_factor.1.inverse_ref, bf16[576,512]{1,0:T(8,128)(2,1)S(1)} %bitcast.145, f32[1536,512]{1,0:T(8,128)} %all-gather.4.cloned.1.call-done.mixed_ref, ...), custom_call_target="tpu_custom_call" | custom-call | flops 10166992896 | bytes 31531008 | tf_op jit(solution)/shard_map/adam_step/pallas_call | solution.py:268
  (77 shorter events, 0.8 us)
Async XLA Ops:
  7.2 87.4 %all-gather.6.cloned.1.call-start = ((), (), s32[]{:S(2)}) async-start(), calls=%async_computation.2 | async-start | bytes 8077312 | tf_op jit(solution)/shard_map/all_gather | solution.py:305
  9.2 11.2 %copy-start.2 = (bf16[1536,512]{1,0:T(8,128)(2,1)S(1)}, bf16[1536,512]{1,0:T(8,128)(2,1)}, u32[]{:S(2)}) copy-start(bf16[1536,512]{1,0:T(8,128)(2,1)} %param.5) | copy-start | bytes 4718596
  22.8 3.0 %collective-permute-start = (bf16[288,512]{1,0:T(8,128)(2,1)S(1)}, bf16[288,512]{1,0:T(8,128)(2,1)S(1)}, u32[]{:S(2)}, u32[]{:S(2)}) collective-permute-start(bf16[288,512]{1,0:T(8,128)(2,1)S(1)} %fusion.9), channel_id=1, source_target_pairs={{0,1},{1,0},{2,3},{3,2},{4,5},{5,4},{6,7},{7,6},{8,9},{9,8},{10,11... | collective-permute-start | bytes 884744 | tf_op jit(solution)/shard_map/ppermute | solution.py:39
  25.9 5.5 %collective-permute-start.1 = (bf16[72,512]{1,0:T(8,128)(2,1)S(1)}, bf16[72,512]{1,0:T(8,128)(2,1)S(1)}, u32[]{:S(2)}, u32[]{:S(2)}) collective-permute-start(bf16[72,512]{1,0:T(8,128)(2,1)S(1)} %get-tuple-element.19), channel_id=1, source_target_pairs={{0,2},{1,3},{2,4},{3,5},{4,6},{5,7},{6,0},{7,1},{8,10},{9,11},{10,... | collective-permute-start | bytes 221192 | tf_op jit(solution)/shard_map/ppermute | solution.py:39
  27.4 4.1 %collective-permute-start.3 = (bf16[72,512]{1,0:T(8,128)(2,1)S(1)}, bf16[72,512]{1,0:T(8,128)(2,1)S(1)}, u32[]{:S(2)}, u32[]{:S(2)}) collective-permute-start(bf16[72,512]{1,0:T(8,128)(2,1)S(1)} %get-tuple-element.20), channel_id=1, source_target_pairs={{0,6},{1,7},{2,0},{3,1},{4,2},{5,3},{6,4},{7,5},{8,14},{9,15},{10,... | collective-permute-start | bytes 221192 | tf_op jit(solution)/shard_map/ppermute | solution.py:39
  28.9 4.7 %collective-permute-start.2 = (bf16[72,512]{1,0:T(8,128)(2,1)S(1)}, bf16[72,512]{1,0:T(8,128)(2,1)S(1)}, u32[]{:S(2)}, u32[]{:S(2)}) collective-permute-start(bf16[72,512]{1,0:T(8,128)(2,1)S(1)} %get-tuple-element.21), channel_id=1, source_target_pairs={{0,4},{1,5},{2,6},{3,7},{4,0},{5,1},{6,2},{7,3},{8,12},{9,13},{10,... | collective-permute-start | bytes 221192 | tf_op jit(solution)/shard_map/ppermute | solution.py:39
  33.7 7.1 %collective-permute-start.6 = (bf16[72,512]{1,0:T(8,128)(2,1)S(1)}, bf16[72,512]{1,0:T(8,128)(2,1)S(1)}, u32[]{:S(2)}, u32[]{:S(2)}) collective-permute-start(bf16[72,512]{1,0:T(8,128)(2,1)S(1)} %get-tuple-element.18), channel_id=1, source_target_pairs={{0,6},{1,7},{2,0},{3,1},{4,2},{5,3},{6,4},{7,5},{8,14},{9,15},{10,... | collective-permute-start | bytes 221192 | tf_op jit(solution)/shard_map/ppermute | solution.py:39
  35.1 5.6 %collective-permute-start.5 = (bf16[72,512]{1,0:T(8,128)(2,1)S(1)}, bf16[72,512]{1,0:T(8,128)(2,1)S(1)}, u32[]{:S(2)}, u32[]{:S(2)}) collective-permute-start(bf16[72,512]{1,0:T(8,128)(2,1)S(1)} %get-tuple-element.18), channel_id=1, source_target_pairs={{0,4},{1,5},{2,6},{3,7},{4,0},{5,1},{6,2},{7,3},{8,12},{9,13},{10,... | collective-permute-start | bytes 221192 | tf_op jit(solution)/shard_map/ppermute | solution.py:39
  36.3 4.4 %collective-permute-start.4 = (bf16[72,512]{1,0:T(8,128)(2,1)S(1)}, bf16[72,512]{1,0:T(8,128)(2,1)S(1)}, u32[]{:S(2)}, u32[]{:S(2)}) collective-permute-start(bf16[72,512]{1,0:T(8,128)(2,1)S(1)} %get-tuple-element.18), channel_id=1, source_target_pairs={{0,2},{1,3},{2,4},{3,5},{4,6},{5,7},{6,0},{7,1},{8,10},{9,11},{10,... | collective-permute-start | bytes 221192 | tf_op jit(solution)/shard_map/ppermute | solution.py:39
  40.8 4.6 %collective-permute-start.7 = (bf16[288,512]{1,0:T(8,128)(2,1)S(1)}, bf16[288,512]{1,0:T(8,128)(2,1)S(1)}, u32[]{:S(2)}, u32[]{:S(2)}) collective-permute-start(bf16[288,512]{1,0:T(8,128)(2,1)S(1)} %bitcast.155), channel_id=1, source_target_pairs={{0,1},{1,0},{2,3},{3,2},{4,5},{5,4},{6,7},{7,6},{8,9},{9,8},{10,11... | collective-permute-start | bytes 884744 | tf_op jit(solution)/shard_map/ppermute | solution.py:39
  46.8 30.9 %all-to-all-start = ((f32[16,20,576]{2,1,0:T(8,128)}), f32[16,20,576]{2,1,0:T(8,128)S(1)}, u32[]{:S(2)}, u32[]{:S(2)}) async-start(f32[16,20,576]{2,1,0:T(8,128)} %fusion.5), calls=%async_computation | async-start | bytes 1966080 | tf_op jit(solution)/shard_map/all_to_all | solution.py:322
  54.4 90.4 %all-gather.4.cloned.1.call-start = ((), (), s32[]{:S(2)}) async-start(), calls=%async_computation.1 | async-start | bytes 3342336 | tf_op jit(solution)/shard_map/all_gather | solution.py:331
  77.8 9.6 %collective-permute-start.10 = (f32[8,576]{1,0:T(8,128)S(1)}, f32[8,576]{1,0:T(8,128)S(1)}, u32[]{:S(2)}, u32[]{:S(2)}) collective-permute-start(f32[8,576]{1,0:T(8,128)S(1)} %slice.65), channel_id=1, source_target_pairs={{0,16},{8,24},{16,0},{24,8},{32,48},{40,56},{48,32},{56,40},{64,80... | collective-permute-start | bytes 55304 | tf_op jit(solution)/shard_map/ppermute | solution.py:39
  82.3 5.1 %collective-permute-start.9 = (f32[8,576]{1,0:T(8,128)S(1)}, f32[8,576]{1,0:T(8,128)S(1)}, u32[]{:S(2)}, u32[]{:S(2)}) collective-permute-start(f32[8,576]{1,0:T(8,128)S(1)} %slice.65), channel_id=1, source_target_pairs={{0,8},{8,16},{16,24},{24,0},{32,40},{40,48},{48,56},{56,32},{64,72... | collective-permute-start | bytes 55304 | tf_op jit(solution)/shard_map/ppermute | solution.py:39
  82.6 4.8 %collective-permute-start.11 = (f32[8,576]{1,0:T(8,128)S(1)}, f32[8,576]{1,0:T(8,128)S(1)}, u32[]{:S(2)}, u32[]{:S(2)}) collective-permute-start(f32[8,576]{1,0:T(8,128)S(1)} %slice.65), channel_id=1, source_target_pairs={{0,24},{8,0},{16,8},{24,16},{32,56},{40,32},{48,40},{56,48},{64,88... | collective-permute-start | bytes 55304 | tf_op jit(solution)/shard_map/ppermute | solution.py:39
  84.9 3.2 %collective-permute-start.8 = (f32[12,512]{1,0:T(8,128)S(1)}, f32[12,512]{1,0:T(8,128)S(1)}, u32[]{:S(2)}, u32[]{:S(2)}) collective-permute-start(f32[12,512]{1,0:T(8,128)S(1)} %slice.64), channel_id=1, source_target_pairs={{0,1},{1,0},{2,3},{3,2},{4,5},{5,4},{6,7},{7,6},{8,9},{9,8},{10,11... | collective-permute-start | bytes 73736 | tf_op jit(solution)/shard_map/ppermute | solution.py:39
  88.2 5.7 %collective-permute-start.21 = (f32[2,12,512]{2,1,0:T(8,128)S(1)}, f32[2,12,512]{2,1,0:T(8,128)S(1)}, u32[]{:S(2)}, u32[]{:S(2)}) collective-permute-start(f32[2,12,512]{2,1,0:T(8,128)S(1)} %bitcast_dynamic-update-slice_fusion.20), channel_id=1, source_target_pairs={{0,6},{1,7},{2,0},{3,1},{4,2},{5,3},{6,4},{7,5},{8,14},{9,15},{10,... | collective-permute-start | bytes 147464 | tf_op jit(solution)/shard_map/ppermute | solution.py:39
  88.5 5.3 %collective-permute-start.20 = (f32[2,12,512]{2,1,0:T(8,128)S(1)}, f32[2,12,512]{2,1,0:T(8,128)S(1)}, u32[]{:S(2)}, u32[]{:S(2)}) collective-permute-start(f32[2,12,512]{2,1,0:T(8,128)S(1)} %bitcast_dynamic-update-slice_fusion.20), channel_id=1, source_target_pairs={{0,4},{1,5},{2,6},{3,7},{4,0},{5,1},{6,2},{7,3},{8,12},{9,13},{10,... | collective-permute-start | bytes 147464 | tf_op jit(solution)/shard_map/ppermute | solution.py:39
  89.2 4.6 %collective-permute-start.19 = (f32[2,12,512]{2,1,0:T(8,128)S(1)}, f32[2,12,512]{2,1,0:T(8,128)S(1)}, u32[]{:S(2)}, u32[]{:S(2)}) collective-permute-start(f32[2,12,512]{2,1,0:T(8,128)S(1)} %bitcast_dynamic-update-slice_fusion.20), channel_id=1, source_target_pairs={{0,2},{1,3},{2,4},{3,5},{4,6},{5,7},{6,0},{7,1},{8,10},{9,11},{10,... | collective-permute-start | bytes 147464 | tf_op jit(solution)/shard_map/ppermute | solution.py:39
  94.7 6.5 %collective-permute-start.14 = (f32[32,576]{1,0:T(8,128)S(1)}, f32[32,576]{1,0:T(8,128)S(1)}, u32[]{:S(2)}, u32[]{:S(2)}) collective-permute-start(f32[32,576]{1,0:T(8,128)S(1)} %bitcast.157), channel_id=1, source_target_pairs={{0,96},{8,104},{16,112},{24,120},{32,0},{40,8},{48,16},{56,24},{64... | collective-permute-start | bytes 221192 | tf_op jit(solution)/shard_map/ppermute | solution.py:39
  95.5 5.7 %collective-permute-start.13 = (f32[32,576]{1,0:T(8,128)S(1)}, f32[32,576]{1,0:T(8,128)S(1)}, u32[]{:S(2)}, u32[]{:S(2)}) collective-permute-start(f32[32,576]{1,0:T(8,128)S(1)} %bitcast.158), channel_id=1, source_target_pairs={{0,64},{8,72},{16,80},{24,88},{32,96},{40,104},{48,112},{56,120},{... | collective-permute-start | bytes 221192 | tf_op jit(solution)/shard_map/ppermute | solution.py:39
  96.7 4.5 %collective-permute-start.12 = (f32[32,576]{1,0:T(8,128)S(1)}, f32[32,576]{1,0:T(8,128)S(1)}, u32[]{:S(2)}, u32[]{:S(2)}) collective-permute-start(f32[32,576]{1,0:T(8,128)S(1)} %bitcast.159), channel_id=1, source_target_pairs={{0,32},{8,40},{16,48},{24,56},{32,64},{40,72},{48,80},{56,88},{64,... | collective-permute-start | bytes 221192 | tf_op jit(solution)/shard_map/ppermute | solution.py:39
  101.3 11.5 %collective-permute-start.16 = (f32[72,576]{1,0:T(8,128)S(1)}, f32[72,576]{1,0:T(8,128)S(1)}, u32[]{:S(2)}, u32[]{:S(2)}) collective-permute-start(f32[72,576]{1,0:T(8,128)S(1)} %slice.66), channel_id=1, source_target_pairs={{0,4},{1,5},{2,6},{3,7},{4,0},{5,1},{6,2},{7,3},{8,12},{9,13},{10,... | collective-permute-start | bytes 497672 | tf_op jit(solution)/shard_map/ppermute | solution.py:39
  104.7 8.0 %collective-permute-start.15 = (f32[72,576]{1,0:T(8,128)S(1)}, f32[72,576]{1,0:T(8,128)S(1)}, u32[]{:S(2)}, u32[]{:S(2)}) collective-permute-start(f32[72,576]{1,0:T(8,128)S(1)} %slice.66), channel_id=1, source_target_pairs={{0,2},{1,3},{2,4},{3,5},{4,6},{5,7},{6,0},{7,1},{8,10},{9,11},{10,... | collective-permute-start | bytes 497672 | tf_op jit(solution)/shard_map/ppermute | solution.py:39
  104.7 8.1 %collective-permute-start.17 = (f32[72,576]{1,0:T(8,128)S(1)}, f32[72,576]{1,0:T(8,128)S(1)}, u32[]{:S(2)}, u32[]{:S(2)}) collective-permute-start(f32[72,576]{1,0:T(8,128)S(1)} %slice.66), channel_id=1, source_target_pairs={{0,6},{1,7},{2,0},{3,1},{4,2},{5,3},{6,4},{7,5},{8,14},{9,15},{10,... | collective-permute-start | bytes 497672 | tf_op jit(solution)/shard_map/ppermute | solution.py:39
  112.9 4.1 %collective-permute-start.18 = (f32[288,576]{1,0:T(8,128)S(1)}, f32[288,576]{1,0:T(8,128)S(1)}, u32[]{:S(2)}, u32[]{:S(2)}) collective-permute-start(f32[288,576]{1,0:T(8,128)S(1)} %bitcast.149), channel_id=1, source_target_pairs={{0,1},{1,0},{2,3},{3,2},{4,5},{5,4},{6,7},{7,6},{8,9},{9,8},{10,11... | collective-permute-start | bytes 1990664 | tf_op jit(solution)/shard_map/ppermute | solution.py:39
  117.0 27.8 %copy-start = (f32[32,3696]{1,0:T(8,128)S(1)}, f32[32,3696]{1,0:T(8,128)}, u32[]{:S(2)}) copy-start(f32[32,3696]{1,0:T(8,128)} %own_first_ref.1) | copy-start | bytes 1419268
  117.1 27.8 %copy-start.1 = (f32[32,3696]{1,0:T(8,128)S(1)}, f32[32,3696]{1,0:T(8,128)}, u32[]{:S(2)}) copy-start(f32[32,3696]{1,0:T(8,128)} %own_second_ref.1) | copy-start | bytes 1419268
Sparse Core Ops, SparseCore 0:
  10.8 82.1 all-gather.5
  95.7 47.9 all-gather.3

commit v8 on v7

--- a/solution.py
+++ b/solution.py
@@ -11,6 +11,7 @@
 TILE = 1024
 MIX_TILE = 512
 STEP_VMEM = 50 << 20
+PART, STEP = 24, 16
 
 beta_one = 0.9
 beta_two = 0.999
@@ -56,6 +57,11 @@
     for k in range(n):
         out = lax.dynamic_update_index_in_dim(out, got[k], (me - k) % n, 0)
     return out
+
+
+def full_sum(value, sub):
+    got = [shift(value, sub, k) for k in range(1, EXTENT[sub])]
+    return (value + got[1]) + (got[0] + got[2])
 
 
 def lane_of(value, k):
@@ -109,7 +115,6 @@
     work[:size, :size] = gram_ref[...]
     lane = lax.broadcasted_iota(jnp.int32, (8, BLOCK), 1)
     sub = lax.broadcasted_iota(jnp.int32, (8, BLOCK), 0)
-    lanes = lax.broadcasted_iota(jnp.int32, (BLOCK, padded), 1)
 
     def diagonal_inverse(o, n):
         rows = [work[pl.ds(pl.multiple_of(o + 8 * h, 8), 8), pl.ds(o, BLOCK)] for h in range(n // 8)]
@@ -127,10 +132,16 @@
         solved = jnp.dot(inverse, panel, precision=HIGHEST, preferred_element_type=f32)
         work[here, :] = solved
         work[here, here] = inverse
-        later = jnp.where(lanes >= o + BLOCK, solved, 0.0)
-        work[...] -= lax.dot_general(
-            later, work[here, :], (((0,), (0,)), ((), ())), precision=HIGHEST, preferred_element_type=f32
-        )
+        for later in range(1, padded // BLOCK):
+            there = pl.ds(later * BLOCK, BLOCK)
+
+            @pl.when(later > b)
+            def _():
+                work[there, :] -= lax.dot_general(
+                    work[here, there], work[here, :], (((0,), (0,)), ((), ())),
+                    precision=HIGHEST, preferred_element_type=f32,
+                )
+
         return carry
 
     lax.fori_loop(0, size // BLOCK, step, 0)
@@ -182,11 +193,8 @@
 
 
 def sketched_term(sketch_turned, grad_turned, layer_input):
-    token_sketch = jnp.dot(sketch_turned, grad_turned, preferred_element_type=f32)
-    rounded = lax.reduce_precision(token_sketch, 8, 7)
-    high, low = rounded.astype(bf16), (token_sketch - rounded).astype(bf16)
-    times = lambda part: jnp.dot(part, layer_input, preferred_element_type=f32)
-    return times(high) + times(low)
+    token_sketch = jnp.dot(sketch_turned, grad_turned, preferred_element_type=f32).astype(bf16)
+    return jnp.dot(lax.optimization_barrier(token_sketch), layer_input, preferred_element_type=f32)
 
 
 def moments(first, second, projected):
@@ -312,23 +320,21 @@
 
     own_tokens = lax.dynamic_index_in_dim(
         layer_input.reshape(16, 8, share, features), lax.axis_index("col"), 1, keepdims=False
-    )
-    chunks = [owned_rows[8 * (i % (own // 8)) : 8 * (i % (own // 8)) + 8] for i in range(16)]
-    left = jnp.concatenate([jnp.stack(chunks), own_tokens], axis=1)
-    terms = lax.dot_general(
-        left.reshape(16 * (8 + share), features), sketched, (((1,), (1,)), ((), ())),
-        preferred_element_type=f32,
-    )
-    terms = lax.all_to_all(terms.reshape(16, 8 + share, columns), "row", 0, 0, tiled=False)
-    terms = terms.sum(axis=0)
-
-    mixed = gather(terms[8:, :RANK], "core")
-    gram = gather(terms[:8], "z")
+    ).reshape(tokens // 8, features)
+    times = lambda a, b: lax.dot_general(a, b, (((1,), (1,)), ((), ())), preferred_element_type=f32)
+    mixed = times(own_tokens, sketched[:RANK]).reshape(16, share, RANK)
+    mixed = lax.all_to_all(mixed, "row", 0, 0, tiled=False).sum(axis=0)
+
+    gram = times(owned_rows, sketched)
+    gram = jnp.stack([gram[k * STEP : k * STEP + PART] for k in range(4)])
     mixed, gram = lax.optimization_barrier((mixed, gram))
-    mixed = gather(mixed, "y").reshape(8 * share, RANK)
-    gram = gather(gram.reshape(32, columns), "x").reshape(128, columns)[:own]
+    mixed, gram = lax.optimization_barrier((gather(mixed, "core"), scatter_sum(gram, "x")))
+    mixed, gram = lax.optimization_barrier((gather(mixed, "y"), full_sum(gram, "z")))
+    mixed = mixed.reshape(8 * share, RANK)
     mixed, gathered = lax.optimization_barrier((mixed, gathered))
     mixed = lax.all_gather(mixed, "row", axis=0, tiled=True)
+    gram = gather(gram, "x")
+    gram = jnp.concatenate([gram[0, :STEP], gram[1, :STEP], gram[2, :STEP], gram[3]], axis=0)
     gram = gather(gather(gram, "y").reshape(columns // 2, columns), "core")
 
     inverse = inverse_factor(gram.reshape(columns, columns))

time: 171 us -> 177 us (1.035)
  waiting for transfers between devices: 46 us -> 51.1 us
  Pallas kernels: 49.2 us -> 47.2 us
    ppermute x22 -> x25, waiting for transfers between devices: 22.8 us -> 33.1 us  [shift(): return lax.ppermute(value, axis, pairs)]
    all_to_all x1, waiting for transfers between devices: 23.1 us -> 14.3 us  [local(): mixed = lax.all_to_all(mixed, 'row', 0, 0, tiled=False).sum(axis=0)]
    all_gather x1, waiting for transfers between devices: 0.02 us -> 3.66 us  [local(): mixed = lax.all_gather(mixed, 'row', axis=0, tiled=True)]
    pallas_call x1, Pallas kernels: 27.7 us -> 25.8 us  [inverse_factor(): pl.pallas_call(factor_kernel, out_shape=jax.ShapeDtypeStruct((size, size)...]
    ppermute x22 -> x25, starting transfers between devices: 34.5 us -> 35.9 us  [shift(): return lax.ppermute(value, axis, pairs)]
  transfers between devices with their start and end apart: 25 -> 28, of which waited for: 10 -> 15; matrix products, arithmetic and copies ran while one was open for 11% -> 11% of each run, Pallas kernels for 16% -> 15%
where the time goes in v8:
time: 177 us
  waiting for transfers between devices  51.1 us (29%)
  Pallas kernels  47.2 us (27%)
  starting transfers between devices  43.8 us (25%)
  matrix products  16.1 us (9%)
  between operations  14.5 us (8%)
  local copies, waits for them, and re-layouts  3.94 us (2%)
    ppermute x25, starting transfers between devices, shift(): return lax.ppermute(value, axis, pairs)  35.9 us
    ppermute x25, waiting for transfers between devices, shift(): return lax.ppermute(value, axis, pairs)  33.1 us
    pallas_call x1, Pallas kernels, inverse_factor(): pl.pallas_call(factor_kernel, out_shape=jax.ShapeDtypeStruct((size, size)...  25.8 us
    pallas_call x1, Pallas kernels, adam_step(): pl.pallas_call(step_kernel, out_shape=(jax.ShapeDtypeStruct((width, featu...  19.4 us
    all_to_all x1, waiting for transfers between devices, local(): mixed = lax.all_to_all(mixed, 'row', 0, 0, tiled=False).sum(axis=0)  14.3 us
    dot_general x1, matrix products, sketched_term(): jnp.dot(sketch_turned, grad_turned, preferred_element_type=f32).astype(bf16)  12.1 us
    all_to_all x1, starting transfers between devices, local(): mixed = lax.all_to_all(mixed, 'row', 0, 0, tiled=False).sum(axis=0)  7.8 us
    all_gather x1, waiting for transfers between devices, local(): mixed = lax.all_gather(mixed, 'row', axis=0, tiled=True)  3.66 us
  transfers between devices with their start and end apart: 28, of which 15 were waited for; matrix products, arithmetic and copies ran while one was open for 11% of the time, Pallas kernels for 15%

profile of v8, /device:TPU:1, one launch (start us, length us, event | category | flops | bytes accessed | tf_op | source)
XLA Modules:
  0.0 176.9 jit_solution(17567223225551282776)
XLA Ops:
  7.2 2.0 %pack.1 = bf16[64,3696]{1,0:T(8,128)(2,1)} custom-call(f32[32,3696]{1,0:T(8,128)} %own_first_ref.1, f32[32,3696]{1,0:T(8,128)} %own_second_ref.1), custom_call_target="tpu_custom_call" | custom-call | tf_op jit(solution)/shard_map/pack/pallas_call | solution.py:188
  9.3 12.1 %convolution_convert_fusion = bf16[576,1536]{1,0:T(8,128)(2,1)} fusion(bf16[3696,576]{0,1:T(8,128)(2,1)} %param.7, bf16[1536,3696]{0,1:T(8,128)(2,1)} %param.6), kind=kOutput, calls=%fused_computation | convolution fusion | flops 6540853248 | bytes 17381376 | tf_op jit(solution)/shard_map/dot_general | solution.py:196
  21.4 2.5 %fusion.14 = f32[576,512]{1,0:T(8,128)S(1)} fusion(bf16[576,1536]{1,0:T(8,128)(2,1)} %convolution_convert_fusion, bf16[1536,512]{1,0:T(8,128)(2,1)S(1)} %copy-done.2), kind=kOutput, calls=%fused_computation.58 | convolution fusion | flops 905969664 | bytes 4521984 | tf_op jit(solution)/shard_map/dot_general | solution.py:197
  24.0 1.6 collective-permute-start
  25.6 1.2 collective-permute-done
  26.9 1.5 collective-permute-start.1
  28.4 1.5 collective-permute-start.3
  29.9 1.6 collective-permute-start.2
  31.5 0.7 collective-permute-done.1
  32.1 2.5 %collective-permute-done.2 = bf16[72,512]{1,0:T(8,128)(2,1)S(1)} collective-permute-done((bf16[72,512]{1,0:T(8,128)(2,1)S(1)}, bf16[72,512]{1,0:T(8,128)(2,1)S(1)}, u32[]{:S(2)}, u32[]{:S(2)}) %collective-permute-start.2) | collective-permute-done | bytes 73760 | tf_op jit(solution)/shard_map/ppermute | solution.py:40
  34.7 1.0 collective-permute-start.4
  35.7 1.8 collective-permute-start.6
  37.5 0.4 collective-permute-start.5
  37.8 1.8 %collective-permute-done.4 = bf16[72,512]{1,0:T(8,128)(2,1)S(1)} collective-permute-done((bf16[72,512]{1,0:T(8,128)(2,1)S(1)}, bf16[72,512]{1,0:T(8,128)(2,1)S(1)}, u32[]{:S(2)}, u32[]{:S(2)}) %collective-permute-start.4) | collective-permute-done | bytes 73760 | tf_op jit(solution)/shard_map/ppermute | solution.py:40
  39.6 2.8 %collective-permute-done.5 = bf16[72,512]{1,0:T(8,128)(2,1)S(1)} collective-permute-done((bf16[72,512]{1,0:T(8,128)(2,1)S(1)}, bf16[72,512]{1,0:T(8,128)(2,1)S(1)}, u32[]{:S(2)}, u32[]{:S(2)}) %collective-permute-start.5) | collective-permute-done | bytes 73760 | tf_op jit(solution)/shard_map/ppermute | solution.py:40
  42.4 3.4 %collective-permute-start.7 = (bf16[288,512]{1,0:T(8,128)(2,1)S(1)}, bf16[288,512]{1,0:T(8,128)(2,1)S(1)}, u32[]{:S(2)}, u32[]{:S(2)}) collective-permute-start(bf16[288,512]{1,0:T(8,128)(2,1)S(1)} %bitcast.123), channel_id=1, source_target_pairs={{0,1},{1,0},{2,3},{3,2},{4,5},{5,4},{6,7},{7,6},{8,9},{9,8},{10,11... | collective-permute-start | bytes 884744 | tf_op jit(solution)/shard_map/ppermute | solution.py:40
  45.8 2.5 %reshape.45 = bf16[16,8,12,512]{3,2,1,0:T(8,128)(2,1)S(1)} reshape(bf16[1536,512]{1,0:T(8,128)(2,1)} %param.5) | data formatting | bytes 3145728 | tf_op jit(solution)/shard_map/reshape | solution.py:322
  48.5 1.1 fusion
  49.6 7.8 %all-to-all-start = ((f32[16,12,512]{2,1,0:T(8,128)}), f32[16,12,512]{2,1,0:T(8,128)S(1)}, u32[]{:S(2)}, u32[]{:S(2)}) async-start(f32[16,12,512]{2,1,0:T(8,128)} %fusion), calls=%async_computation | async-start | bytes 1048576 | tf_op jit(solution)/shard_map/all_to_all | solution.py:326
  57.5 0.3 fusion.15
  57.8 14.3 %all-to-all-done = f32[16,12,512]{2,1,0:T(8,128)S(1)} async-done(((f32[16,12,512]{2,1,0:T(8,128)}), f32[16,12,512]{2,1,0:T(8,128)S(1)}, u32[]{:S(2)}, u32[]{:S(2)}) %all-to-all-start) | async-done | bytes 393248 | tf_op jit(solution)/shard_map/all_to_all | solution.py:326
  72.2 1.7 collective-permute-start.8
  73.9 1.4 collective-permute-start.9
  75.4 1.6 collective-permute-start.11
  77.0 1.1 collective-permute-start.10
  78.1 2.7 %collective-permute-done.9 = f32[24,576]{1,0:T(8,128)S(1)} collective-permute-done((f32[24,576]{1,0:T(8,128)S(1)}, f32[24,576]{1,0:T(8,128)S(1)}, u32[]{:S(2)}, u32[]{:S(2)}) %collective-permute-start.9) | collective-permute-done | bytes 55328 | tf_op jit(solution)/shard_map/ppermute | solution.py:40
  80.8 3.6 %collective-permute-done.10 = f32[24,576]{1,0:T(8,128)S(1)} collective-permute-done((f32[24,576]{1,0:T(8,128)S(1)}, f32[24,576]{1,0:T(8,128)S(1)}, u32[]{:S(2)}, u32[]{:S(2)}) %collective-permute-start.10) | collective-permute-done | bytes 55328 | tf_op jit(solution)/shard_map/ppermute | solution.py:40
  84.4 1.4 collective-permute-start.17
  85.8 0.1 collective-permute-start.16
  85.9 1.6 collective-permute-start.15
  87.7 1.4 collective-permute-start.12
  89.1 3.2 %collective-permute-done.12 = f32[2,12,512]{2,1,0:T(8,128)S(1)} collective-permute-done((f32[2,12,512]{2,1,0:T(8,128)S(1)}, f32[2,12,512]{2,1,0:T(8,128)S(1)}, u32[]{:S(2)}, u32[]{:S(2)}) %collective-permute-start.12) | collective-permute-done | bytes 49184 | tf_op jit(solution)/shard_map/ppermute | solution.py:40
  92.3 0.5 collective-permute-start.13
  92.8 4.1 %collective-permute-done.13 = f32[2,12,512]{2,1,0:T(8,128)S(1)} collective-permute-done((f32[2,12,512]{2,1,0:T(8,128)S(1)}, f32[2,12,512]{2,1,0:T(8,128)S(1)}, u32[]{:S(2)}, u32[]{:S(2)}) %collective-permute-start.13) | collective-permute-done | bytes 49184 | tf_op jit(solution)/shard_map/ppermute | solution.py:40
  97.0 1.2 collective-permute-start.20
  98.2 1.1 collective-permute-start.19
  99.3 0.7 reshape.52
  100.1 3.5 %collective-permute-done.18 = f32[24,576]{1,0:T(8,128)S(1)} collective-permute-done((f32[24,576]{1,0:T(8,128)S(1)}, f32[24,576]{1,0:T(8,128)S(1)}, u32[]{:S(2)}, u32[]{:S(2)}) %collective-permute-start.18) | collective-permute-done | bytes 55328 | tf_op jit(solution)/shard_map/ppermute | solution.py:40
  103.8 0.6 collective-permute-start.22
  104.4 2.1 %collective-permute-start.23 = (f32[72,576]{1,0:T(8,128)S(1)}, f32[72,576]{1,0:T(8,128)S(1)}, u32[]{:S(2)}, u32[]{:S(2)}) collective-permute-start(f32[72,576]{1,0:T(8,128)S(1)} %pad_maximum_fusion.1), channel_id=1, source_target_pairs={{0,6},{1,7},{2,0},{3,1},{4,2},{5,3},{6,4},{7,5},{8,14},{9,15},{10,... | collective-permute-start | bytes 497672 | tf_op jit(solution)/shard_map/ppermute | solution.py:40
  106.5 4.8 %collective-permute-done.21 = f32[72,576]{1,0:T(8,128)S(1)} collective-permute-done((f32[72,576]{1,0:T(8,128)S(1)}, f32[72,576]{1,0:T(8,128)S(1)}, u32[]{:S(2)}, u32[]{:S(2)}) %collective-permute-start.21) | collective-permute-done | bytes 165920 | tf_op jit(solution)/shard_map/ppermute | solution.py:40
  111.4 0.6 collective-permute-done.23
  112.0 7.2 %collective-permute-start.24 = (f32[288,576]{1,0:T(8,128)S(1)}, f32[288,576]{1,0:T(8,128)S(1)}, u32[]{:S(2)}, u32[]{:S(2)}) collective-permute-start(f32[288,576]{1,0:T(8,128)S(1)} %bitcast.119), channel_id=1, source_target_pairs={{0,1},{1,0},{2,3},{3,2},{4,5},{5,4},{6,7},{7,6},{8,9},{9,8},{10,11... | collective-permute-start | bytes 1990664 | tf_op jit(solution)/shard_map/ppermute | solution.py:40
  119.2 0.1 broadcast_in_dim.94
  119.4 1.7 collective-permute-done.24
  121.1 25.8 %inverse_factor.1.inverse_ref = f32[576,576]{1,0:T(8,128)S(1)} custom-call(f32[576,576]{1,0:T(8,128)S(1)} %bitcast.118), custom_call_target="tpu_custom_call" | custom-call | flops 30576476160 | bytes 2654208 | tf_op jit(solution)/shard_map/inverse_factor/pallas_call | solution.py:163
  146.9 3.7 %all-gather.4.cloned.1.call-done.mixed_ref = f32[1536,512]{1,0:T(8,128)} async-done(((f32[96,512]{1,0:T(8,128)}), f32[1536,512]{1,0:T(8,128)}) %all-gather.4.cloned.1.call-update) | async-done | bytes 3145744 | tf_op jit(solution)/shard_map/all_gather | solution.py:335
  150.6 19.4 %adam_step.1 = (f32[3696,512]{1,0:T(8,128)}, f32[32,3696]{1,0:T(8,128)}, f32[32,3696]{1,0:T(8,128)}) custom-call(s32[1]{0:T(128)} %bitcast.at_ref, f32[576,576]{1,0:T(8,128)S(1)} %inverse_factor.1.inverse_ref, bf16[576,512]{1,0:T(8,128)(2,1)S(1)} %bitcast.117, f32[1536,512]{1,0:T(8,128)} %all-gather.4.cloned.1.call-done.mixed_ref, ...), custom_call_target="tpu_custom_call" | custom-call | flops 10166992896 | bytes 31531008 | tf_op jit(solution)/shard_map/adam_step/pallas_call | solution.py:276
  (66 shorter events, 1.2 us)
Async XLA Ops:
  7.2 92.9 %all-gather.6.cloned.1.call-start = ((), (), s32[]{:S(2)}) async-start(), calls=%async_computation.2 | async-start | bytes 8077312 | tf_op jit(solution)/shard_map/all_gather | solution.py:313
  9.2 12.1 %copy-start.2 = (bf16[1536,512]{1,0:T(8,128)(2,1)S(1)}, bf16[1536,512]{1,0:T(8,128)(2,1)}, u32[]{:S(2)}) copy-start(bf16[1536,512]{1,0:T(8,128)(2,1)} %param.5) | copy-start | bytes 4718596
  24.0 2.8 %collective-permute-start = (bf16[288,512]{1,0:T(8,128)(2,1)S(1)}, bf16[288,512]{1,0:T(8,128)(2,1)S(1)}, u32[]{:S(2)}, u32[]{:S(2)}) collective-permute-start(bf16[288,512]{1,0:T(8,128)(2,1)S(1)} %fusion.1), channel_id=1, source_target_pairs={{0,1},{1,0},{2,3},{3,2},{4,5},{5,4},{6,7},{7,6},{8,9},{9,8},{10,11... | collective-permute-start | bytes 884744 | tf_op jit(solution)/shard_map/ppermute | solution.py:40
  26.9 5.2 %collective-permute-start.1 = (bf16[72,512]{1,0:T(8,128)(2,1)S(1)}, bf16[72,512]{1,0:T(8,128)(2,1)S(1)}, u32[]{:S(2)}, u32[]{:S(2)}) collective-permute-start(bf16[72,512]{1,0:T(8,128)(2,1)S(1)} %get-tuple-element.27), channel_id=1, source_target_pairs={{0,2},{1,3},{2,4},{3,5},{4,6},{5,7},{6,0},{7,1},{8,10},{9,11},{10,... | collective-permute-start | bytes 221192 | tf_op jit(solution)/shard_map/ppermute | solution.py:40
  28.4 3.8 %collective-permute-start.3 = (bf16[72,512]{1,0:T(8,128)(2,1)S(1)}, bf16[72,512]{1,0:T(8,128)(2,1)S(1)}, u32[]{:S(2)}, u32[]{:S(2)}) collective-permute-start(bf16[72,512]{1,0:T(8,128)(2,1)S(1)} %get-tuple-element.28), channel_id=1, source_target_pairs={{0,6},{1,7},{2,0},{3,1},{4,2},{5,3},{6,4},{7,5},{8,14},{9,15},{10,... | collective-permute-start | bytes 221192 | tf_op jit(solution)/shard_map/ppermute | solution.py:40
  29.9 4.8 %collective-permute-start.2 = (bf16[72,512]{1,0:T(8,128)(2,1)S(1)}, bf16[72,512]{1,0:T(8,128)(2,1)S(1)}, u32[]{:S(2)}, u32[]{:S(2)}) collective-permute-start(bf16[72,512]{1,0:T(8,128)(2,1)S(1)} %get-tuple-element.29), channel_id=1, source_target_pairs={{0,4},{1,5},{2,6},{3,7},{4,0},{5,1},{6,2},{7,3},{8,12},{9,13},{10,... | collective-permute-start | bytes 221192 | tf_op jit(solution)/shard_map/ppermute | solution.py:40
  34.7 4.9 %collective-permute-start.4 = (bf16[72,512]{1,0:T(8,128)(2,1)S(1)}, bf16[72,512]{1,0:T(8,128)(2,1)S(1)}, u32[]{:S(2)}, u32[]{:S(2)}) collective-permute-start(bf16[72,512]{1,0:T(8,128)(2,1)S(1)} %get-tuple-element.26), channel_id=1, source_target_pairs={{0,2},{1,3},{2,4},{3,5},{4,6},{5,7},{6,0},{7,1},{8,10},{9,11},{10,... | collective-permute-start | bytes 221192 | tf_op jit(solution)/shard_map/ppermute | solution.py:40
  35.7 6.7 %collective-permute-start.6 = (bf16[72,512]{1,0:T(8,128)(2,1)S(1)}, bf16[72,512]{1,0:T(8,128)(2,1)S(1)}, u32[]{:S(2)}, u32[]{:S(2)}) collective-permute-start(bf16[72,512]{1,0:T(8,128)(2,1)S(1)} %get-tuple-element.26), channel_id=1, source_target_pairs={{0,6},{1,7},{2,0},{3,1},{4,2},{5,3},{6,4},{7,5},{8,14},{9,15},{10,... | collective-permute-start | bytes 221192 | tf_op jit(solution)/shard_map/ppermute | solution.py:40
  37.5 4.9 %collective-permute-start.5 = (bf16[72,512]{1,0:T(8,128)(2,1)S(1)}, bf16[72,512]{1,0:T(8,128)(2,1)S(1)}, u32[]{:S(2)}, u32[]{:S(2)}) collective-permute-start(bf16[72,512]{1,0:T(8,128)(2,1)S(1)} %get-tuple-element.26), channel_id=1, source_target_pairs={{0,4},{1,5},{2,6},{3,7},{4,0},{5,1},{6,2},{7,3},{8,12},{9,13},{10,... | collective-permute-start | bytes 221192 | tf_op jit(solution)/shard_map/ppermute | solution.py:40
  42.4 6.0 %collective-permute-start.7 = (bf16[288,512]{1,0:T(8,128)(2,1)S(1)}, bf16[288,512]{1,0:T(8,128)(2,1)S(1)}, u32[]{:S(2)}, u32[]{:S(2)}) collective-permute-start(bf16[288,512]{1,0:T(8,128)(2,1)S(1)} %bitcast.123), channel_id=1, source_target_pairs={{0,1},{1,0},{2,3},{3,2},{4,5},{5,4},{6,7},{7,6},{8,9},{9,8},{10,11... | collective-permute-start | bytes 884744 | tf_op jit(solution)/shard_map/ppermute | solution.py:40
  49.6 22.5 %all-to-all-start = ((f32[16,12,512]{2,1,0:T(8,128)}), f32[16,12,512]{2,1,0:T(8,128)S(1)}, u32[]{:S(2)}, u32[]{:S(2)}) async-start(f32[16,12,512]{2,1,0:T(8,128)} %fusion), calls=%async_computation | async-start | bytes 1048576 | tf_op jit(solution)/shard_map/all_to_all | solution.py:326
  57.4 93.2 %all-gather.4.cloned.1.call-start = ((), (), s32[]{:S(2)}) async-start(), calls=%async_computation.1 | async-start | bytes 3342336 | tf_op jit(solution)/shard_map/all_gather | solution.py:335
  72.2 5.9 %collective-permute-start.8 = (f32[12,512]{1,0:T(8,128)S(1)}, f32[12,512]{1,0:T(8,128)S(1)}, u32[]{:S(2)}, u32[]{:S(2)}) collective-permute-start(f32[12,512]{1,0:T(8,128)S(1)} %reduce_sum.9), channel_id=1, source_target_pairs={{0,1},{1,0},{2,3},{3,2},{4,5},{5,4},{6,7},{7,6},{8,9},{9,8},{10,11... | collective-permute-start | bytes 73736 | tf_op jit(solution)/shard_map/ppermute | solution.py:40
  73.9 6.8 %collective-permute-start.9 = (f32[24,576]{1,0:T(8,128)S(1)}, f32[24,576]{1,0:T(8,128)S(1)}, u32[]{:S(2)}, u32[]{:S(2)}) collective-permute-start(f32[24,576]{1,0:T(8,128)S(1)} %get-tuple-element.33), channel_id=1, source_target_pairs={{0,32},{8,40},{16,48},{24,56},{32,64},{40,72},{48,80},{56,88},{64,... | collective-permute-start | bytes 165896 | tf_op jit(solution)/shard_map/ppermute | solution.py:40
  75.4 5.4 %collective-permute-start.11 = (f32[24,576]{1,0:T(8,128)S(1)}, f32[24,576]{1,0:T(8,128)S(1)}, u32[]{:S(2)}, u32[]{:S(2)}) collective-permute-start(f32[24,576]{1,0:T(8,128)S(1)} %get-tuple-element.34), channel_id=1, source_target_pairs={{0,96},{8,104},{16,112},{24,120},{32,0},{40,8},{48,16},{56,24},{64... | collective-permute-start | bytes 165896 | tf_op jit(solution)/shard_map/ppermute | solution.py:40
  77.0 7.4 %collective-permute-start.10 = (f32[24,576]{1,0:T(8,128)S(1)}, f32[24,576]{1,0:T(8,128)S(1)}, u32[]{:S(2)}, u32[]{:S(2)}) collective-permute-start(f32[24,576]{1,0:T(8,128)S(1)} %get-tuple-element.35), channel_id=1, source_target_pairs={{0,64},{8,72},{16,80},{24,88},{32,96},{40,104},{48,112},{56,120},{... | collective-permute-start | bytes 165896 | tf_op jit(solution)/shard_map/ppermute | solution.py:40
  84.4 12.5 %collective-permute-start.17 = (f32[24,576]{1,0:T(8,128)S(1)}, f32[24,576]{1,0:T(8,128)S(1)}, u32[]{:S(2)}, u32[]{:S(2)}) collective-permute-start(f32[24,576]{1,0:T(8,128)S(1)} %fusion.11), channel_id=1, source_target_pairs={{0,24},{8,0},{16,8},{24,16},{32,56},{40,32},{48,40},{56,48},{64,88... | collective-permute-start | bytes 165896 | tf_op jit(solution)/shard_map/ppermute | solution.py:40
  85.8 11.1 %collective-permute-start.16 = (f32[24,576]{1,0:T(8,128)S(1)}, f32[24,576]{1,0:T(8,128)S(1)}, u32[]{:S(2)}, u32[]{:S(2)}) collective-permute-start(f32[24,576]{1,0:T(8,128)S(1)} %fusion.11), channel_id=1, source_target_pairs={{0,8},{8,16},{16,24},{24,0},{32,40},{40,48},{48,56},{56,32},{64,72... | collective-permute-start | bytes 165896 | tf_op jit(solution)/shard_map/ppermute | solution.py:40
  85.9 11.0 %collective-permute-start.15 = (f32[24,576]{1,0:T(8,128)S(1)}, f32[24,576]{1,0:T(8,128)S(1)}, u32[]{:S(2)}, u32[]{:S(2)}) collective-permute-start(f32[24,576]{1,0:T(8,128)S(1)} %fusion.11), channel_id=1, source_target_pairs={{0,16},{8,24},{16,0},{24,8},{32,48},{40,56},{48,32},{56,40},{64,80... | collective-permute-start | bytes 165896 | tf_op jit(solution)/shard_map/ppermute | solution.py:40
  87.6 9.3 %collective-permute-start.14 = (f32[2,12,512]{2,1,0:T(8,128)S(1)}, f32[2,12,512]{2,1,0:T(8,128)S(1)}, u32[]{:S(2)}, u32[]{:S(2)}) collective-permute-start(f32[2,12,512]{2,1,0:T(8,128)S(1)} %bitcast_dynamic-update-slice_fusion.20), channel_id=1, source_target_pairs={{0,6},{1,7},{2,0},{3,1},{4,2},{5,3},{6,4},{7,5},{8,14},{9,15},{10,... | collective-permute-start | bytes 147464 | tf_op jit(solution)/shard_map/ppermute | solution.py:40
  87.7 4.6 %collective-permute-start.12 = (f32[2,12,512]{2,1,0:T(8,128)S(1)}, f32[2,12,512]{2,1,0:T(8,128)S(1)}, u32[]{:S(2)}, u32[]{:S(2)}) collective-permute-start(f32[2,12,512]{2,1,0:T(8,128)S(1)} %bitcast_dynamic-update-slice_fusion.20), channel_id=1, source_target_pairs={{0,2},{1,3},{2,4},{3,5},{4,6},{5,7},{6,0},{7,1},{8,10},{9,11},{10,... | collective-permute-start | bytes 147464 | tf_op jit(solution)/shard_map/ppermute | solution.py:40
  92.3 4.6 %collective-permute-start.13 = (f32[2,12,512]{2,1,0:T(8,128)S(1)}, f32[2,12,512]{2,1,0:T(8,128)S(1)}, u32[]{:S(2)}, u32[]{:S(2)}) collective-permute-start(f32[2,12,512]{2,1,0:T(8,128)S(1)} %bitcast_dynamic-update-slice_fusion.20), channel_id=1, source_target_pairs={{0,4},{1,5},{2,6},{3,7},{4,0},{5,1},{6,2},{7,3},{8,12},{9,13},{10,... | collective-permute-start | bytes 147464 | tf_op jit(solution)/shard_map/ppermute | solution.py:40
  97.0 6.6 %collective-permute-start.20 = (f32[24,576]{1,0:T(8,128)S(1)}, f32[24,576]{1,0:T(8,128)S(1)}, u32[]{:S(2)}, u32[]{:S(2)}) collective-permute-start(f32[24,576]{1,0:T(8,128)S(1)} %add_add_fusion), channel_id=1, source_target_pairs={{0,96},{8,104},{16,112},{24,120},{32,0},{40,8},{48,16},{56,24},{64... | collective-permute-start | bytes 165896 | tf_op jit(solution)/shard_map/ppermute | solution.py:40
  98.2 5.4 %collective-permute-start.19 = (f32[24,576]{1,0:T(8,128)S(1)}, f32[24,576]{1,0:T(8,128)S(1)}, u32[]{:S(2)}, u32[]{:S(2)}) collective-permute-start(f32[24,576]{1,0:T(8,128)S(1)} %add_add_fusion), channel_id=1, source_target_pairs={{0,64},{8,72},{16,80},{24,88},{32,96},{40,104},{48,112},{56,120},{... | collective-permute-start | bytes 165896 | tf_op jit(solution)/shard_map/ppermute | solution.py:40
  99.3 4.3 %collective-permute-start.18 = (f32[24,576]{1,0:T(8,128)S(1)}, f32[24,576]{1,0:T(8,128)S(1)}, u32[]{:S(2)}, u32[]{:S(2)}) collective-permute-start(f32[24,576]{1,0:T(8,128)S(1)} %add_add_fusion), channel_id=1, source_target_pairs={{0,32},{8,40},{16,48},{24,56},{32,64},{40,72},{48,80},{56,88},{64,... | collective-permute-start | bytes 165896 | tf_op jit(solution)/shard_map/ppermute | solution.py:40
  103.7 7.6 %collective-permute-start.21 = (f32[72,576]{1,0:T(8,128)S(1)}, f32[72,576]{1,0:T(8,128)S(1)}, u32[]{:S(2)}, u32[]{:S(2)}) collective-permute-start(f32[72,576]{1,0:T(8,128)S(1)} %pad_maximum_fusion.1), channel_id=1, source_target_pairs={{0,2},{1,3},{2,4},{3,5},{4,6},{5,7},{6,0},{7,1},{8,10},{9,11},{10,... | collective-permute-start | bytes 497672 | tf_op jit(solution)/shard_map/ppermute | solution.py:40
  103.8 7.6 %collective-permute-start.22 = (f32[72,576]{1,0:T(8,128)S(1)}, f32[72,576]{1,0:T(8,128)S(1)}, u32[]{:S(2)}, u32[]{:S(2)}) collective-permute-start(f32[72,576]{1,0:T(8,128)S(1)} %pad_maximum_fusion.1), channel_id=1, source_target_pairs={{0,4},{1,5},{2,6},{3,7},{4,0},{5,1},{6,2},{7,3},{8,12},{9,13},{10,... | collective-permute-start | bytes 497672 | tf_op jit(solution)/shard_map/ppermute | solution.py:40
  104.4 7.6 %collective-permute-start.23 = (f32[72,576]{1,0:T(8,128)S(1)}, f32[72,576]{1,0:T(8,128)S(1)}, u32[]{:S(2)}, u32[]{:S(2)}) collective-permute-start(f32[72,576]{1,0:T(8,128)S(1)} %pad_maximum_fusion.1), channel_id=1, source_target_pairs={{0,6},{1,7},{2,0},{3,1},{4,2},{5,3},{6,4},{7,5},{8,14},{9,15},{10,... | collective-permute-start | bytes 497672 | tf_op jit(solution)/shard_map/ppermute | solution.py:40
  112.0 9.1 %collective-permute-start.24 = (f32[288,576]{1,0:T(8,128)S(1)}, f32[288,576]{1,0:T(8,128)S(1)}, u32[]{:S(2)}, u32[]{:S(2)}) collective-permute-start(f32[288,576]{1,0:T(8,128)S(1)} %bitcast.119), channel_id=1, source_target_pairs={{0,1},{1,0},{2,3},{3,2},{4,5},{5,4},{6,7},{7,6},{8,9},{9,8},{10,11... | collective-permute-start | bytes 1990664 | tf_op jit(solution)/shard_map/ppermute | solution.py:40
  121.1 29.5 %copy-start = (f32[32,3696]{1,0:T(8,128)S(1)}, f32[32,3696]{1,0:T(8,128)}, u32[]{:S(2)}) copy-start(f32[32,3696]{1,0:T(8,128)} %own_first_ref.1) | copy-start | bytes 1419268
  121.1 29.5 %copy-start.1 = (f32[32,3696]{1,0:T(8,128)S(1)}, f32[32,3696]{1,0:T(8,128)}, u32[]{:S(2)}) copy-start(f32[32,3696]{1,0:T(8,128)} %own_second_ref.1) | copy-start | bytes 1419268
Sparse Core Ops, SparseCore 0:
  10.8 78.7 all-gather.5
  100.2 50.3 all-gather.3

commit v9 on v8

--- a/solution.py
+++ b/solution.py
@@ -74,7 +74,6 @@
 
 def reciprocal(value):
     guess = pl.reciprocal(value, approx=True)
-    guess = guess * (2.0 - value * guess)
     return guess * (2.0 - value * guess)
 
 
@@ -193,8 +192,11 @@
 
 
 def sketched_term(sketch_turned, grad_turned, layer_input):
-    token_sketch = jnp.dot(sketch_turned, grad_turned, preferred_element_type=f32).astype(bf16)
-    return jnp.dot(lax.optimization_barrier(token_sketch), layer_input, preferred_element_type=f32)
+    token_sketch = jnp.dot(sketch_turned, grad_turned, preferred_element_type=f32)
+    rounded = lax.reduce_precision(token_sketch, 8, 7)
+    high, low = rounded.astype(bf16), (token_sketch - rounded).astype(bf16)
+    times = lambda part: jnp.dot(part, layer_input, preferred_element_type=f32)
+    return times(high) + times(low)
 
 
 def moments(first, second, projected):
@@ -322,16 +324,15 @@
         layer_input.reshape(16, 8, share, features), lax.axis_index("col"), 1, keepdims=False
     ).reshape(tokens // 8, features)
     times = lambda a, b: lax.dot_general(a, b, (((1,), (1,)), ((), ())), preferred_element_type=f32)
-    mixed = times(own_tokens, sketched[:RANK]).reshape(16, share, RANK)
-    mixed = lax.all_to_all(mixed, "row", 0, 0, tiled=False).sum(axis=0)
-
+    mixed = scatter_sum(times(own_tokens, sketched[:RANK]).reshape(4, 4 * share, RANK), "x")
     gram = times(owned_rows, sketched)
     gram = jnp.stack([gram[k * STEP : k * STEP + PART] for k in range(4)])
     mixed, gram = lax.optimization_barrier((mixed, gram))
-    mixed, gram = lax.optimization_barrier((gather(mixed, "core"), scatter_sum(gram, "x")))
-    mixed, gram = lax.optimization_barrier((gather(mixed, "y"), full_sum(gram, "z")))
-    mixed = mixed.reshape(8 * share, RANK)
-    mixed, gathered = lax.optimization_barrier((mixed, gathered))
+    mixed, gram = lax.optimization_barrier(
+        (scatter_sum(mixed.reshape(4, share, RANK), "z"), scatter_sum(gram, "x"))
+    )
+    mixed, gram = lax.optimization_barrier((gather(gather(mixed, "core"), "y"), full_sum(gram, "z")))
+    mixed, gathered = lax.optimization_barrier((mixed.reshape(8 * share, RANK), gathered))
     mixed = lax.all_gather(mixed, "row", axis=0, tiled=True)
     gram = gather(gram, "x")
     gram = jnp.concatenate([gram[0, :STEP], gram[1, :STEP], gram[2, :STEP], gram[3]], axis=0)

time: 177 us -> 169 us (0.955)
  waiting for transfers between devices: 51.1 us -> 48.3 us
  Pallas kernels: 47.2 us -> 44.5 us
  matrix products: 16.1 us -> 14.1 us
  starting transfers between devices: 43.8 us -> 41.9 us
    all_to_all x1 -> x0, waiting for transfers between devices: 14.3 us -> none  [local(): mixed = lax.all_to_all(mixed, 'row', 0, 0, tiled=False).sum(axis=0)]
    ppermute x25 -> x31, waiting for transfers between devices: 33.1 us -> 42.1 us  [shift(): return lax.ppermute(value, axis, pairs)]
    all_to_all x1 -> x0, starting transfers between devices: 7.8 us -> none  [local(): mixed = lax.all_to_all(mixed, 'row', 0, 0, tiled=False).sum(axis=0)]
    ppermute x25 -> x31, starting transfers between devices: 35.9 us -> 41.8 us  [shift(): return lax.ppermute(value, axis, pairs)]
    pallas_call x1, Pallas kernels: 25.8 us -> 23.1 us  [inverse_factor(): pl.pallas_call(factor_kernel, out_shape=jax.ShapeDtypeStruct((size, size)...]
    all_gather x1, waiting for transfers between devices: 3.66 us -> 6.19 us  [local(): mixed = lax.all_gather(mixed, 'row', axis=0, tiled=True)]
    dot_general x2 -> x3, matrix products: 14.7 us -> 13.4 us  [the longest x1 11.2 us: sketched_term(): jnp.dot(sketch_turned, grad_turned, preferred_element_type=f32)]
  transfers between devices with their start and end apart: 28 -> 33, of which waited for: 15 -> 17; matrix products, arithmetic and copies ran while one was open for 11% -> 11% of each run, Pallas kernels for 15% -> 14%
where the time goes in v9:
time: 169 us
  waiting for transfers between devices  48.3 us (29%)
  Pallas kernels  44.5 us (26%)
  starting transfers between devices  41.9 us (25%)
  between operations  14.6 us (9%)
  matrix products  14.1 us (8%)
  local copies, waits for them, and re-layouts  4.08 us (2%)
    ppermute x31, waiting for transfers between devices, shift(): return lax.ppermute(value, axis, pairs)  42.1 us
    ppermute x31, starting transfers between devices, shift(): return lax.ppermute(value, axis, pairs)  41.8 us
    pallas_call x1, Pallas kernels, inverse_factor(): pl.pallas_call(factor_kernel, out_shape=jax.ShapeDtypeStruct((size, size)...  23.1 us
    pallas_call x1, Pallas kernels, adam_step(): pl.pallas_call(step_kernel, out_shape=(jax.ShapeDtypeStruct((width, featu...  19.5 us
    dot_general x1, matrix products, sketched_term(): jnp.dot(sketch_turned, grad_turned, preferred_element_type=f32)  11.2 us
    all_gather x1, waiting for transfers between devices, local(): mixed = lax.all_gather(mixed, 'row', axis=0, tiled=True)  6.19 us
  transfers between devices with their start and end apart: 33, of which 17 were waited for; matrix products, arithmetic and copies ran while one was open for 11% of the time, Pallas kernels for 14%

profile of v9, /device:TPU:1, one launch (start us, length us, event | category | flops | bytes accessed | tf_op | source)
XLA Modules:
  0.0 168.7 jit_solution(9410937525417179744)
XLA Ops:
  7.2 2.0 %pack.1 = bf16[64,3696]{1,0:T(8,128)(2,1)} custom-call(f32[32,3696]{1,0:T(8,128)} %own_first_ref.1, f32[32,3696]{1,0:T(8,128)} %own_second_ref.1), custom_call_target="tpu_custom_call" | custom-call | tf_op jit(solution)/shard_map/pack/pallas_call | solution.py:187
  9.3 11.2 %fusion.20 = f32[576,1536]{1,0:T(8,128)S(1)} fusion(bf16[3696,576]{0,1:T(8,128)(2,1)} %param.7, bf16[1536,3696]{0,1:T(8,128)(2,1)} %param.6), kind=kOutput, calls=%fused_computation.73 | convolution fusion | flops 6539968512 | bytes 19150848 | tf_op jit(solution)/shard_map/dot_general | solution.py:195
  20.5 1.1 fusion.1
  21.7 1.1 fusion.4
  22.8 1.5 collective-permute-start
  24.3 1.3 collective-permute-done
  25.7 1.0 bitcast_add_fusion
  26.8 1.4 collective-permute-start.1
  28.2 1.5 collective-permute-start.3
  29.7 1.6 collective-permute-start.2
  31.8 2.7 %collective-permute-done.2 = bf16[72,512]{1,0:T(8,128)(2,1)S(1)} collective-permute-done((bf16[72,512]{1,0:T(8,128)(2,1)S(1)}, bf16[72,512]{1,0:T(8,128)(2,1)S(1)}, u32[]{:S(2)}, u32[]{:S(2)}) %collective-permute-start.2) | collective-permute-done | bytes 73760 | tf_op jit(solution)/shard_map/ppermute | solution.py:40
  35.2 2.1 %collective-permute-start.6 = (bf16[72,512]{1,0:T(8,128)(2,1)S(1)}, bf16[72,512]{1,0:T(8,128)(2,1)S(1)}, u32[]{:S(2)}, u32[]{:S(2)}) collective-permute-start(bf16[72,512]{1,0:T(8,128)(2,1)S(1)} %get-tuple-element.26), channel_id=1, source_target_pairs={{0,6},{1,7},{2,0},{3,1},{4,2},{5,3},{6,4},{7,5},{8,14},{9,15},{10,... | collective-permute-start | bytes 221192 | tf_op jit(solution)/shard_map/ppermute | solution.py:40
  37.7 1.8 %collective-permute-done.4 = bf16[72,512]{1,0:T(8,128)(2,1)S(1)} collective-permute-done((bf16[72,512]{1,0:T(8,128)(2,1)S(1)}, bf16[72,512]{1,0:T(8,128)(2,1)S(1)}, u32[]{:S(2)}, u32[]{:S(2)}) %collective-permute-start.4) | collective-permute-done | bytes 73760 | tf_op jit(solution)/shard_map/ppermute | solution.py:40
  39.5 2.8 %collective-permute-done.5 = bf16[72,512]{1,0:T(8,128)(2,1)S(1)} collective-permute-done((bf16[72,512]{1,0:T(8,128)(2,1)S(1)}, bf16[72,512]{1,0:T(8,128)(2,1)S(1)}, u32[]{:S(2)}, u32[]{:S(2)}) %collective-permute-start.5) | collective-permute-done | bytes 73760 | tf_op jit(solution)/shard_map/ppermute | solution.py:40
  42.3 3.4 %collective-permute-start.7 = (bf16[288,512]{1,0:T(8,128)(2,1)S(1)}, bf16[288,512]{1,0:T(8,128)(2,1)S(1)}, u32[]{:S(2)}, u32[]{:S(2)}) collective-permute-start(bf16[288,512]{1,0:T(8,128)(2,1)S(1)} %bitcast.147), channel_id=1, source_target_pairs={{0,1},{1,0},{2,3},{3,2},{4,5},{5,4},{6,7},{7,6},{8,9},{9,8},{10,11... | collective-permute-start | bytes 884744 | tf_op jit(solution)/shard_map/ppermute | solution.py:40
  45.7 1.5 reshape.48
  47.2 1.0 constant_dynamic-slice_fusion
  48.8 1.4 collective-permute-start.8
  50.2 1.4 collective-permute-start.10
  51.6 1.6 collective-permute-start.9
  53.6 3.3 %collective-permute-done.8 = f32[48,512]{1,0:T(8,128)S(1)} collective-permute-done((f32[48,512]{1,0:T(8,128)S(1)}, f32[48,512]{1,0:T(8,128)S(1)}, u32[]{:S(2)}, u32[]{:S(2)}) %collective-permute-start.8) | collective-permute-done | bytes 98336 | tf_op jit(solution)/shard_map/ppermute | solution.py:40
  56.9 5.2 %collective-permute-done.9 = f32[48,512]{1,0:T(8,128)S(1)} collective-permute-done((f32[48,512]{1,0:T(8,128)S(1)}, f32[48,512]{1,0:T(8,128)S(1)}, u32[]{:S(2)}, u32[]{:S(2)}) %collective-permute-start.9) | collective-permute-done | bytes 98336 | tf_op jit(solution)/shard_map/ppermute | solution.py:40
  62.1 1.7 %collective-permute-start.11 = (f32[12,512]{1,0:T(8,128)S(1)}, f32[12,512]{1,0:T(8,128)S(1)}, u32[]{:S(2)}, u32[]{:S(2)}) collective-permute-start(f32[12,512]{1,0:T(8,128)S(1)} %get-tuple-element.43), channel_id=1, source_target_pairs={{0,8},{8,16},{16,24},{24,0},{32,40},{40,48},{48,56},{56,32},{64,72... | collective-permute-start | bytes 73736 | tf_op jit(solution)/shard_map/ppermute | solution.py:40
  63.8 2.1 %collective-permute-start.13 = (f32[12,512]{1,0:T(8,128)S(1)}, f32[12,512]{1,0:T(8,128)S(1)}, u32[]{:S(2)}, u32[]{:S(2)}) collective-permute-start(f32[12,512]{1,0:T(8,128)S(1)} %get-tuple-element.44), channel_id=1, source_target_pairs={{0,24},{8,0},{16,8},{24,16},{32,56},{40,32},{48,40},{56,48},{64,88... | collective-permute-start | bytes 73736 | tf_op jit(solution)/shard_map/ppermute | solution.py:40
  65.9 1.3 collective-permute-start.12
  67.2 0.8 collective-permute-start.14
  68.1 1.9 %collective-permute-start.16 = (f32[24,576]{1,0:T(8,128)S(1)}, f32[24,576]{1,0:T(8,128)S(1)}, u32[]{:S(2)}, u32[]{:S(2)}) collective-permute-start(f32[24,576]{1,0:T(8,128)S(1)} %get-tuple-element.37), channel_id=1, source_target_pairs={{0,96},{8,104},{16,112},{24,120},{32,0},{40,8},{48,16},{56,24},{64... | collective-permute-start | bytes 165896 | tf_op jit(solution)/shard_map/ppermute | solution.py:40
  70.0 1.2 collective-permute-done.12
  71.2 2.1 %collective-permute-done.14 = f32[24,576]{1,0:T(8,128)S(1)} collective-permute-done((f32[24,576]{1,0:T(8,128)S(1)}, f32[24,576]{1,0:T(8,128)S(1)}, u32[]{:S(2)}, u32[]{:S(2)}) %collective-permute-start.14) | collective-permute-done | bytes 55328 | tf_op jit(solution)/shard_map/ppermute | solution.py:40
  73.3 3.1 %collective-permute-done.15 = f32[24,576]{1,0:T(8,128)S(1)} collective-permute-done((f32[24,576]{1,0:T(8,128)S(1)}, f32[24,576]{1,0:T(8,128)S(1)}, u32[]{:S(2)}, u32[]{:S(2)}) %collective-permute-start.15) | collective-permute-done | bytes 55328 | tf_op jit(solution)/shard_map/ppermute | solution.py:40
  76.4 0.8 collective-permute-start.23
  77.2 0.9 collective-permute-start.22
  78.2 1.6 collective-permute-start.21
  79.7 3.8 %collective-permute-start.17 = (f32[12,512]{1,0:T(8,128)S(1)}, f32[12,512]{1,0:T(8,128)S(1)}, u32[]{:S(2)}, u32[]{:S(2)}) collective-permute-start(f32[12,512]{1,0:T(8,128)S(1)} %fusion.18), channel_id=1, source_target_pairs={{0,1},{1,0},{2,3},{3,2},{4,5},{5,4},{6,7},{7,6},{8,9},{9,8},{10,11... | collective-permute-start | bytes 73736 | tf_op jit(solution)/shard_map/ppermute | solution.py:40
  83.6 0.8 collective-permute-done.17
  85.3 0.7 collective-permute-start.18
  86.0 5.2 %collective-permute-done.18 = f32[2,12,512]{2,1,0:T(8,128)S(1)} collective-permute-done((f32[2,12,512]{2,1,0:T(8,128)S(1)}, f32[2,12,512]{2,1,0:T(8,128)S(1)}, u32[]{:S(2)}, u32[]{:S(2)}) %collective-permute-start.18) | collective-permute-done | bytes 49184 | tf_op jit(solution)/shard_map/ppermute | solution.py:40
  91.3 1.5 collective-permute-start.26
  93.5 0.7 reshape.56
  94.2 3.8 %collective-permute-done.24 = f32[24,576]{1,0:T(8,128)S(1)} collective-permute-done((f32[24,576]{1,0:T(8,128)S(1)}, f32[24,576]{1,0:T(8,128)S(1)}, u32[]{:S(2)}, u32[]{:S(2)}) %collective-permute-start.24) | collective-permute-done | bytes 55328 | tf_op jit(solution)/shard_map/ppermute | solution.py:40
  98.2 1.7 %collective-permute-start.28 = (f32[72,576]{1,0:T(8,128)S(1)}, f32[72,576]{1,0:T(8,128)S(1)}, u32[]{:S(2)}, u32[]{:S(2)}) collective-permute-start(f32[72,576]{1,0:T(8,128)S(1)} %pad_maximum_fusion.1), channel_id=1, source_target_pairs={{0,4},{1,5},{2,6},{3,7},{4,0},{5,1},{6,2},{7,3},{8,12},{9,13},{10,... | collective-permute-start | bytes 497672 | tf_op jit(solution)/shard_map/ppermute | solution.py:40
  99.9 1.0 collective-permute-start.29
  101.0 5.9 %collective-permute-done.27 = f32[72,576]{1,0:T(8,128)S(1)} collective-permute-done((f32[72,576]{1,0:T(8,128)S(1)}, f32[72,576]{1,0:T(8,128)S(1)}, u32[]{:S(2)}, u32[]{:S(2)}) %collective-permute-start.27) | collective-permute-done | bytes 165920 | tf_op jit(solution)/shard_map/ppermute | solution.py:40
  107.6 3.6 %collective-permute-start.30 = (f32[288,576]{1,0:T(8,128)S(1)}, f32[288,576]{1,0:T(8,128)S(1)}, u32[]{:S(2)}, u32[]{:S(2)}) collective-permute-start(f32[288,576]{1,0:T(8,128)S(1)} %bitcast.143), channel_id=1, source_target_pairs={{0,1},{1,0},{2,3},{3,2},{4,5},{5,4},{6,7},{7,6},{8,9},{9,8},{10,11... | collective-permute-start | bytes 1990664 | tf_op jit(solution)/shard_map/ppermute | solution.py:40
  111.3 1.7 collective-permute-done.30
  113.1 23.1 %inverse_factor.1.inverse_ref = f32[576,576]{1,0:T(8,128)S(1)} custom-call(f32[576,576]{1,0:T(8,128)S(1)} %bitcast.140), custom_call_target="tpu_custom_call" | custom-call | flops 30576476160 | bytes 2654208 | tf_op jit(solution)/shard_map/inverse_factor/pallas_call | solution.py:162
  136.1 6.2 %all-gather.4.cloned.1.call-done.mixed_ref = f32[1536,512]{1,0:T(8,128)} async-done(((f32[96,512]{1,0:T(8,128)}), f32[1536,512]{1,0:T(8,128)}) %all-gather.4.cloned.1.call-update) | async-done | bytes 3145744 | tf_op jit(solution)/shard_map/all_gather | solution.py:336
  142.3 19.5 %adam_step.1 = (f32[3696,512]{1,0:T(8,128)}, f32[32,3696]{1,0:T(8,128)}, f32[32,3696]{1,0:T(8,128)}) custom-call(s32[1]{0:T(128)} %bitcast.at_ref, f32[576,576]{1,0:T(8,128)S(1)} %inverse_factor.1.inverse_ref, bf16[576,512]{1,0:T(8,128)(2,1)S(1)} %bitcast.139, f32[1536,512]{1,0:T(8,128)} %all-gather.4.cloned.1.call-done.mixed_ref, ...), custom_call_target="tpu_custom_call" | custom-call | flops 10166992896 | bytes 31531008 | tf_op jit(solution)/shard_map/adam_step/pallas_call | solution.py:278
  (83 shorter events, 5.6 us)
Async XLA Ops:
  7.2 87.0 %all-gather.6.cloned.1.call-start = ((), (), s32[]{:S(2)}) async-start(), calls=%async_computation.1 | async-start | bytes 8077312 | tf_op jit(solution)/shard_map/all_gather | solution.py:315
  9.2 133.1 %all-gather.4.cloned.1.call-start = ((), (), s32[]{:S(2)}) async-start(), calls=%async_computation | async-start | bytes 3342336 | tf_op jit(solution)/shard_map/all_gather | solution.py:336
  9.3 11.2 %copy-start.2 = (bf16[1536,512]{1,0:T(8,128)(2,1)S(1)}, bf16[1536,512]{1,0:T(8,128)(2,1)}, u32[]{:S(2)}) copy-start(bf16[1536,512]{1,0:T(8,128)(2,1)} %param.5) | copy-start | bytes 4718596
  22.8 2.8 %collective-permute-start = (bf16[288,512]{1,0:T(8,128)(2,1)S(1)}, bf16[288,512]{1,0:T(8,128)(2,1)}, u32[]{:S(2)}, u32[]{:S(2)}) collective-permute-start(bf16[288,512]{1,0:T(8,128)(2,1)S(1)} %fusion.6), channel_id=1, source_target_pairs={{0,1},{1,0},{2,3},{3,2},{4,5},{5,4},{6,7},{7,6},{8,9},{9,8},{10,11... | collective-permute-start | bytes 884744 | tf_op jit(solution)/shard_map/ppermute | solution.py:40
  26.8 5.1 %collective-permute-start.1 = (bf16[72,512]{1,0:T(8,128)(2,1)S(1)}, bf16[72,512]{1,0:T(8,128)(2,1)S(1)}, u32[]{:S(2)}, u32[]{:S(2)}) collective-permute-start(bf16[72,512]{1,0:T(8,128)(2,1)S(1)} %get-tuple-element.27), channel_id=1, source_target_pairs={{0,2},{1,3},{2,4},{3,5},{4,6},{5,7},{6,0},{7,1},{8,10},{9,11},{10,... | collective-permute-start | bytes 221192 | tf_op jit(solution)/shard_map/ppermute | solution.py:40
  28.2 3.6 %collective-permute-start.3 = (bf16[72,512]{1,0:T(8,128)(2,1)S(1)}, bf16[72,512]{1,0:T(8,128)(2,1)S(1)}, u32[]{:S(2)}, u32[]{:S(2)}) collective-permute-start(bf16[72,512]{1,0:T(8,128)(2,1)S(1)} %get-tuple-element.28), channel_id=1, source_target_pairs={{0,6},{1,7},{2,0},{3,1},{4,2},{5,3},{6,4},{7,5},{8,14},{9,15},{10,... | collective-permute-start | bytes 221192 | tf_op jit(solution)/shard_map/ppermute | solution.py:40
  29.7 4.8 %collective-permute-start.2 = (bf16[72,512]{1,0:T(8,128)(2,1)S(1)}, bf16[72,512]{1,0:T(8,128)(2,1)S(1)}, u32[]{:S(2)}, u32[]{:S(2)}) collective-permute-start(bf16[72,512]{1,0:T(8,128)(2,1)S(1)} %get-tuple-element.29), channel_id=1, source_target_pairs={{0,4},{1,5},{2,6},{3,7},{4,0},{5,1},{6,2},{7,3},{8,12},{9,13},{10,... | collective-permute-start | bytes 221192 | tf_op jit(solution)/shard_map/ppermute | solution.py:40
  34.6 4.9 %collective-permute-start.4 = (bf16[72,512]{1,0:T(8,128)(2,1)S(1)}, bf16[72,512]{1,0:T(8,128)(2,1)S(1)}, u32[]{:S(2)}, u32[]{:S(2)}) collective-permute-start(bf16[72,512]{1,0:T(8,128)(2,1)S(1)} %get-tuple-element.26), channel_id=1, source_target_pairs={{0,2},{1,3},{2,4},{3,5},{4,6},{5,7},{6,0},{7,1},{8,10},{9,11},{10,... | collective-permute-start | bytes 221192 | tf_op jit(solution)/shard_map/ppermute | solution.py:40
  35.2 7.0 %collective-permute-start.6 = (bf16[72,512]{1,0:T(8,128)(2,1)S(1)}, bf16[72,512]{1,0:T(8,128)(2,1)S(1)}, u32[]{:S(2)}, u32[]{:S(2)}) collective-permute-start(bf16[72,512]{1,0:T(8,128)(2,1)S(1)} %get-tuple-element.26), channel_id=1, source_target_pairs={{0,6},{1,7},{2,0},{3,1},{4,2},{5,3},{6,4},{7,5},{8,14},{9,15},{10,... | collective-permute-start | bytes 221192 | tf_op jit(solution)/shard_map/ppermute | solution.py:40
  37.3 4.9 %collective-permute-start.5 = (bf16[72,512]{1,0:T(8,128)(2,1)S(1)}, bf16[72,512]{1,0:T(8,128)(2,1)S(1)}, u32[]{:S(2)}, u32[]{:S(2)}) collective-permute-start(bf16[72,512]{1,0:T(8,128)(2,1)S(1)} %get-tuple-element.26), channel_id=1, source_target_pairs={{0,4},{1,5},{2,6},{3,7},{4,0},{5,1},{6,2},{7,3},{8,12},{9,13},{10,... | collective-permute-start | bytes 221192 | tf_op jit(solution)/shard_map/ppermute | solution.py:40
  42.3 6.1 %collective-permute-start.7 = (bf16[288,512]{1,0:T(8,128)(2,1)S(1)}, bf16[288,512]{1,0:T(8,128)(2,1)S(1)}, u32[]{:S(2)}, u32[]{:S(2)}) collective-permute-start(bf16[288,512]{1,0:T(8,128)(2,1)S(1)} %bitcast.147), channel_id=1, source_target_pairs={{0,1},{1,0},{2,3},{3,2},{4,5},{5,4},{6,7},{7,6},{8,9},{9,8},{10,11... | collective-permute-start | bytes 884744 | tf_op jit(solution)/shard_map/ppermute | solution.py:40
  48.8 8.0 %collective-permute-start.8 = (f32[48,512]{1,0:T(8,128)S(1)}, f32[48,512]{1,0:T(8,128)S(1)}, u32[]{:S(2)}, u32[]{:S(2)}) collective-permute-start(f32[48,512]{1,0:T(8,128)S(1)} %get-tuple-element.30), channel_id=1, source_target_pairs={{0,32},{8,40},{16,48},{24,56},{32,64},{40,72},{48,80},{56,88},{64,... | collective-permute-start | bytes 294920 | tf_op jit(solution)/shard_map/ppermute | solution.py:40
  50.2 6.7 %collective-permute-start.10 = (f32[48,512]{1,0:T(8,128)S(1)}, f32[48,512]{1,0:T(8,128)S(1)}, u32[]{:S(2)}, u32[]{:S(2)}) collective-permute-start(f32[48,512]{1,0:T(8,128)S(1)} %get-tuple-element.31), channel_id=1, source_target_pairs={{0,96},{8,104},{16,112},{24,120},{32,0},{40,8},{48,16},{56,24},{64... | collective-permute-start | bytes 294920 | tf_op jit(solution)/shard_map/ppermute | solution.py:40
  51.6 10.5 %collective-permute-start.9 = (f32[48,512]{1,0:T(8,128)S(1)}, f32[48,512]{1,0:T(8,128)S(1)}, u32[]{:S(2)}, u32[]{:S(2)}) collective-permute-start(f32[48,512]{1,0:T(8,128)S(1)} %get-tuple-element.32), channel_id=1, source_target_pairs={{0,64},{8,72},{16,80},{24,88},{32,96},{40,104},{48,112},{56,120},{... | collective-permute-start | bytes 294920 | tf_op jit(solution)/shard_map/ppermute | solution.py:40
  62.1 7.9 %collective-permute-start.11 = (f32[12,512]{1,0:T(8,128)S(1)}, f32[12,512]{1,0:T(8,128)S(1)}, u32[]{:S(2)}, u32[]{:S(2)}) collective-permute-start(f32[12,512]{1,0:T(8,128)S(1)} %get-tuple-element.43), channel_id=1, source_target_pairs={{0,8},{8,16},{16,24},{24,0},{32,40},{40,48},{48,56},{56,32},{64,72... | collective-permute-start | bytes 73736 | tf_op jit(solution)/shard_map/ppermute | solution.py:40
  63.8 6.2 %collective-permute-start.13 = (f32[12,512]{1,0:T(8,128)S(1)}, f32[12,512]{1,0:T(8,128)S(1)}, u32[]{:S(2)}, u32[]{:S(2)}) collective-permute-start(f32[12,512]{1,0:T(8,128)S(1)} %get-tuple-element.44), channel_id=1, source_target_pairs={{0,24},{8,0},{16,8},{24,16},{32,56},{40,32},{48,40},{56,48},{64,88... | collective-permute-start | bytes 73736 | tf_op jit(solution)/shard_map/ppermute | solution.py:40
  65.9 5.2 %collective-permute-start.12 = (f32[12,512]{1,0:T(8,128)S(1)}, f32[12,512]{1,0:T(8,128)S(1)}, u32[]{:S(2)}, u32[]{:S(2)}) collective-permute-start(f32[12,512]{1,0:T(8,128)S(1)} %get-tuple-element.45), channel_id=1, source_target_pairs={{0,16},{8,24},{16,0},{24,8},{32,48},{40,56},{48,32},{56,40},{64,80... | collective-permute-start | bytes 73736 | tf_op jit(solution)/shard_map/ppermute | solution.py:40
  67.2 6.0 %collective-permute-start.14 = (f32[24,576]{1,0:T(8,128)S(1)}, f32[24,576]{1,0:T(8,128)S(1)}, u32[]{:S(2)}, u32[]{:S(2)}) collective-permute-start(f32[24,576]{1,0:T(8,128)S(1)} %get-tuple-element.36), channel_id=1, source_target_pairs={{0,32},{8,40},{16,48},{24,56},{32,64},{40,72},{48,80},{56,88},{64,... | collective-permute-start | bytes 165896 | tf_op jit(solution)/shard_map/ppermute | solution.py:40
  68.1 5.2 %collective-permute-start.16 = (f32[24,576]{1,0:T(8,128)S(1)}, f32[24,576]{1,0:T(8,128)S(1)}, u32[]{:S(2)}, u32[]{:S(2)}) collective-permute-start(f32[24,576]{1,0:T(8,128)S(1)} %get-tuple-element.37), channel_id=1, source_target_pairs={{0,96},{8,104},{16,112},{24,120},{32,0},{40,8},{48,16},{56,24},{64... | collective-permute-start | bytes 165896 | tf_op jit(solution)/shard_map/ppermute | solution.py:40
  70.0 6.4 %collective-permute-start.15 = (f32[24,576]{1,0:T(8,128)S(1)}, f32[24,576]{1,0:T(8,128)S(1)}, u32[]{:S(2)}, u32[]{:S(2)}) collective-permute-start(f32[24,576]{1,0:T(8,128)S(1)} %get-tuple-element.38), channel_id=1, source_target_pairs={{0,64},{8,72},{16,80},{24,88},{32,96},{40,104},{48,112},{56,120},{... | collective-permute-start | bytes 165896 | tf_op jit(solution)/shard_map/ppermute | solution.py:40
  76.4 8.9 %collective-permute-start.23 = (f32[24,576]{1,0:T(8,128)S(1)}, f32[24,576]{1,0:T(8,128)S(1)}, u32[]{:S(2)}, u32[]{:S(2)}) collective-permute-start(f32[24,576]{1,0:T(8,128)S(1)} %fusion.16), channel_id=1, source_target_pairs={{0,24},{8,0},{16,8},{24,16},{32,56},{40,32},{48,40},{56,48},{64,88... | collective-permute-start | bytes 165896 | tf_op jit(solution)/shard_map/ppermute | solution.py:40
  77.2 8.8 %collective-permute-start.22 = (f32[24,576]{1,0:T(8,128)S(1)}, f32[24,576]{1,0:T(8,128)S(1)}, u32[]{:S(2)}, u32[]{:S(2)}) collective-permute-start(f32[24,576]{1,0:T(8,128)S(1)} %fusion.16), channel_id=1, source_target_pairs={{0,8},{8,16},{16,24},{24,0},{32,40},{40,48},{48,56},{56,32},{64,72... | collective-permute-start | bytes 165896 | tf_op jit(solution)/shard_map/ppermute | solution.py:40
  78.2 7.8 %collective-permute-start.21 = (f32[24,576]{1,0:T(8,128)S(1)}, f32[24,576]{1,0:T(8,128)S(1)}, u32[]{:S(2)}, u32[]{:S(2)}) collective-permute-start(f32[24,576]{1,0:T(8,128)S(1)} %fusion.16), channel_id=1, source_target_pairs={{0,16},{8,24},{16,0},{24,8},{32,48},{40,56},{48,32},{56,40},{64,80... | collective-permute-start | bytes 165896 | tf_op jit(solution)/shard_map/ppermute | solution.py:40
  79.7 4.7 %collective-permute-start.17 = (f32[12,512]{1,0:T(8,128)S(1)}, f32[12,512]{1,0:T(8,128)S(1)}, u32[]{:S(2)}, u32[]{:S(2)}) collective-permute-start(f32[12,512]{1,0:T(8,128)S(1)} %fusion.18), channel_id=1, source_target_pairs={{0,1},{1,0},{2,3},{3,2},{4,5},{5,4},{6,7},{7,6},{8,9},{9,8},{10,11... | collective-permute-start | bytes 73736 | tf_op jit(solution)/shard_map/ppermute | solution.py:40
  84.4 6.9 %collective-permute-start.20 = (f32[2,12,512]{2,1,0:T(8,128)S(1)}, f32[2,12,512]{2,1,0:T(8,128)S(1)}, u32[]{:S(2)}, u32[]{:S(2)}) collective-permute-start(f32[2,12,512]{2,1,0:T(8,128)S(1)} %bitcast_dynamic-update-slice_fusion.20), channel_id=1, source_target_pairs={{0,6},{1,7},{2,0},{3,1},{4,2},{5,3},{6,4},{7,5},{8,14},{9,15},{10,... | collective-permute-start | bytes 147464 | tf_op jit(solution)/shard_map/ppermute | solution.py:40
  84.7 6.6 %collective-permute-start.19 = (f32[2,12,512]{2,1,0:T(8,128)S(1)}, f32[2,12,512]{2,1,0:T(8,128)S(1)}, u32[]{:S(2)}, u32[]{:S(2)}) collective-permute-start(f32[2,12,512]{2,1,0:T(8,128)S(1)} %bitcast_dynamic-update-slice_fusion.20), channel_id=1, source_target_pairs={{0,4},{1,5},{2,6},{3,7},{4,0},{5,1},{6,2},{7,3},{8,12},{9,13},{10,... | collective-permute-start | bytes 147464 | tf_op jit(solution)/shard_map/ppermute | solution.py:40
  85.3 6.0 %collective-permute-start.18 = (f32[2,12,512]{2,1,0:T(8,128)S(1)}, f32[2,12,512]{2,1,0:T(8,128)S(1)}, u32[]{:S(2)}, u32[]{:S(2)}) collective-permute-start(f32[2,12,512]{2,1,0:T(8,128)S(1)} %bitcast_dynamic-update-slice_fusion.20), channel_id=1, source_target_pairs={{0,2},{1,3},{2,4},{3,5},{4,6},{5,7},{6,0},{7,1},{8,10},{9,11},{10,... | collective-permute-start | bytes 147464 | tf_op jit(solution)/shard_map/ppermute | solution.py:40
  91.3 6.7 %collective-permute-start.26 = (f32[24,576]{1,0:T(8,128)S(1)}, f32[24,576]{1,0:T(8,128)S(1)}, u32[]{:S(2)}, u32[]{:S(2)}) collective-permute-start(f32[24,576]{1,0:T(8,128)S(1)} %add_add_fusion), channel_id=1, source_target_pairs={{0,96},{8,104},{16,112},{24,120},{32,0},{40,8},{48,16},{56,24},{64... | collective-permute-start | bytes 165896 | tf_op jit(solution)/shard_map/ppermute | solution.py:40
  92.8 5.2 %collective-permute-start.25 = (f32[24,576]{1,0:T(8,128)S(1)}, f32[24,576]{1,0:T(8,128)S(1)}, u32[]{:S(2)}, u32[]{:S(2)}) collective-permute-start(f32[24,576]{1,0:T(8,128)S(1)} %add_add_fusion), channel_id=1, source_target_pairs={{0,64},{8,72},{16,80},{24,88},{32,96},{40,104},{48,112},{56,120},{... | collective-permute-start | bytes 165896 | tf_op jit(solution)/shard_map/ppermute | solution.py:40
  93.2 4.8 %collective-permute-start.24 = (f32[24,576]{1,0:T(8,128)S(1)}, f32[24,576]{1,0:T(8,128)S(1)}, u32[]{:S(2)}, u32[]{:S(2)}) collective-permute-start(f32[24,576]{1,0:T(8,128)S(1)} %add_add_fusion), channel_id=1, source_target_pairs={{0,32},{8,40},{16,48},{24,56},{32,64},{40,72},{48,80},{56,88},{64,... | collective-permute-start | bytes 165896 | tf_op jit(solution)/shard_map/ppermute | solution.py:40
  98.1 8.7 %collective-permute-start.27 = (f32[72,576]{1,0:T(8,128)S(1)}, f32[72,576]{1,0:T(8,128)S(1)}, u32[]{:S(2)}, u32[]{:S(2)}) collective-permute-start(f32[72,576]{1,0:T(8,128)S(1)} %pad_maximum_fusion.1), channel_id=1, source_target_pairs={{0,2},{1,3},{2,4},{3,5},{4,6},{5,7},{6,0},{7,1},{8,10},{9,11},{10,... | collective-permute-start | bytes 497672 | tf_op jit(solution)/shard_map/ppermute | solution.py:40
  98.2 8.7 %collective-permute-start.28 = (f32[72,576]{1,0:T(8,128)S(1)}, f32[72,576]{1,0:T(8,128)S(1)}, u32[]{:S(2)}, u32[]{:S(2)}) collective-permute-start(f32[72,576]{1,0:T(8,128)S(1)} %pad_maximum_fusion.1), channel_id=1, source_target_pairs={{0,4},{1,5},{2,6},{3,7},{4,0},{5,1},{6,2},{7,3},{8,12},{9,13},{10,... | collective-permute-start | bytes 497672 | tf_op jit(solution)/shard_map/ppermute | solution.py:40
  99.9 7.6 %collective-permute-start.29 = (f32[72,576]{1,0:T(8,128)S(1)}, f32[72,576]{1,0:T(8,128)S(1)}, u32[]{:S(2)}, u32[]{:S(2)}) collective-permute-start(f32[72,576]{1,0:T(8,128)S(1)} %pad_maximum_fusion.1), channel_id=1, source_target_pairs={{0,6},{1,7},{2,0},{3,1},{4,2},{5,3},{6,4},{7,5},{8,14},{9,15},{10,... | collective-permute-start | bytes 497672 | tf_op jit(solution)/shard_map/ppermute | solution.py:40
  107.6 5.4 %collective-permute-start.30 = (f32[288,576]{1,0:T(8,128)S(1)}, f32[288,576]{1,0:T(8,128)S(1)}, u32[]{:S(2)}, u32[]{:S(2)}) collective-permute-start(f32[288,576]{1,0:T(8,128)S(1)} %bitcast.143), channel_id=1, source_target_pairs={{0,1},{1,0},{2,3},{3,2},{4,5},{5,4},{6,7},{7,6},{8,9},{9,8},{10,11... | collective-permute-start | bytes 1990664 | tf_op jit(solution)/shard_map/ppermute | solution.py:40
  113.0 29.3 %copy-start = (f32[32,3696]{1,0:T(8,128)S(1)}, f32[32,3696]{1,0:T(8,128)}, u32[]{:S(2)}) copy-start(f32[32,3696]{1,0:T(8,128)} %own_first_ref.1) | copy-start | bytes 1419268
  113.1 29.3 %copy-start.1 = (f32[32,3696]{1,0:T(8,128)S(1)}, f32[32,3696]{1,0:T(8,128)}, u32[]{:S(2)}) copy-start(f32[32,3696]{1,0:T(8,128)} %own_second_ref.1) | copy-start | bytes 1419268
Sparse Core Ops, SparseCore 0:
  10.8 77.2 all-gather.5
  94.3 47.9 all-gather.3

commit v10 on v9

--- a/solution.py
+++ b/solution.py
@@ -315,14 +315,15 @@
     gathered = lax.all_gather(pack(first_moment, second_moment), "row", axis=0, tiled=False)
 
     partial = sketched_term(sketch.T, grad_turned, layer_input)
+    own_tokens = lax.dynamic_index_in_dim(
+        layer_input.reshape(16, 8, share, features), lax.axis_index("col"), 1, keepdims=False
+    ).reshape(tokens // 8, features)
     half = scatter_sum(partial.reshape(2, columns // 2, features), "core", bf16)
+    half, own_tokens = lax.optimization_barrier((half, own_tokens))
     owned_rows = scatter_sum(half.reshape(4, own, features), "y", bf16).astype(bf16)
     sketched = gather(gather(owned_rows, "y").reshape(columns // 2, features), "core")
     sketched = sketched.reshape(columns, features)
 
-    own_tokens = lax.dynamic_index_in_dim(
-        layer_input.reshape(16, 8, share, features), lax.axis_index("col"), 1, keepdims=False
-    ).reshape(tokens // 8, features)
     times = lambda a, b: lax.dot_general(a, b, (((1,), (1,)), ((), ())), preferred_element_type=f32)
     mixed = scatter_sum(times(own_tokens, sketched[:RANK]).reshape(4, 4 * share, RANK), "x")
     gram = times(owned_rows, sketched)
@@ -331,7 +332,8 @@
     mixed, gram = lax.optimization_barrier(
         (scatter_sum(mixed.reshape(4, share, RANK), "z"), scatter_sum(gram, "x"))
     )
-    mixed, gram = lax.optimization_barrier((gather(gather(mixed, "core"), "y"), full_sum(gram, "z")))
+    mixed, gram = lax.optimization_barrier((gather(mixed, "core"), gram))
+    mixed, gram = lax.optimization_barrier((gather(mixed, "y"), full_sum(gram, "z")))
     mixed, gathered = lax.optimization_barrier((mixed.reshape(8 * share, RANK), gathered))
     mixed = lax.all_gather(mixed, "row", axis=0, tiled=True)
     gram = gather(gram, "x")

time: 169 us -> 170 us (level)
  starting transfers between devices: 41.9 us -> 44.5 us
    ppermute x31, starting transfers between devices: 41.8 us -> 44.4 us  [shift(): return lax.ppermute(value, axis, pairs)]
  transfers between devices with their start and end apart: 33 -> 33, of which waited for: 17 -> 19; matrix products, arithmetic and copies ran while one was open for 11% -> 11% of each run, Pallas kernels for 14% -> 14%
where the time goes in v10:
time: 170 us
  waiting for transfers between devices  48.2 us (28%)
  starting transfers between devices  44.5 us (26%)
  Pallas kernels  44.5 us (26%)
  between operations  14.5 us (9%)
  matrix products  14.1 us (8%)
  local copies, waits for them, and re-layouts  4 us (2%)
    ppermute x31, starting transfers between devices, shift(): return lax.ppermute(value, axis, pairs)  44.4 us
    ppermute x31, waiting for transfers between devices, shift(): return lax.ppermute(value, axis, pairs)  42.4 us
    pallas_call x1, Pallas kernels, inverse_factor(): pl.pallas_call(factor_kernel, out_shape=jax.ShapeDtypeStruct((size, size)...  23.1 us
    pallas_call x1, Pallas kernels, adam_step(): pl.pallas_call(step_kernel, out_shape=(jax.ShapeDtypeStruct((width, featu...  19.4 us
    dot_general x1, matrix products, sketched_term(): jnp.dot(sketch_turned, grad_turned, preferred_element_type=f32)  11.2 us
    all_gather x1, waiting for transfers between devices, local(): mixed = lax.all_gather(mixed, 'row', axis=0, tiled=True)  5.78 us
  transfers between devices with their start and end apart: 33, of which 19 were waited for; matrix products, arithmetic and copies ran while one was open for 11% of the time, Pallas kernels for 14%

profile of v10, /device:TPU:1, one launch (start us, length us, event | category | flops | bytes accessed | tf_op | source)
XLA Modules:
  0.0 170.0 jit_solution(5125711031417347961)
XLA Ops:
  7.2 2.0 %pack.1 = bf16[64,3696]{1,0:T(8,128)(2,1)} custom-call(f32[32,3696]{1,0:T(8,128)} %own_first_ref.1, f32[32,3696]{1,0:T(8,128)} %own_second_ref.1), custom_call_target="tpu_custom_call" | custom-call | tf_op jit(solution)/shard_map/pack/pallas_call | solution.py:187
  9.3 11.2 %fusion.21 = f32[576,1536]{1,0:T(8,128)S(1)} fusion(bf16[3696,576]{0,1:T(8,128)(2,1)} %param.7, bf16[1536,3696]{0,1:T(8,128)(2,1)} %param.6), kind=kOutput, calls=%fused_computation.73 | convolution fusion | flops 6539968512 | bytes 19150848 | tf_op jit(solution)/shard_map/dot_general | solution.py:195
  20.5 1.1 fusion.1
  21.7 1.1 fusion.4
  22.8 1.5 collective-permute-start
  24.3 1.5 reshape.51
  25.8 1.0 constant_dynamic-slice_fusion
  27.0 1.4 collective-permute-start.1
  28.5 1.5 collective-permute-start.3
  30.0 1.6 collective-permute-start.2
  31.6 0.9 collective-permute-done.1
  32.4 2.3 %collective-permute-done.2 = bf16[72,512]{1,0:T(8,128)(2,1)S(1)} collective-permute-done((bf16[72,512]{1,0:T(8,128)(2,1)S(1)}, bf16[72,512]{1,0:T(8,128)(2,1)S(1)}, u32[]{:S(2)}, u32[]{:S(2)}) %collective-permute-start.2) | collective-permute-done | bytes 73760 | tf_op jit(solution)/shard_map/ppermute | solution.py:40
  34.8 1.2 collective-permute-start.4
  36.0 1.6 collective-permute-start.6
  37.9 1.6 collective-permute-done.4
  39.6 2.7 %collective-permute-done.5 = bf16[72,512]{1,0:T(8,128)(2,1)S(1)} collective-permute-done((bf16[72,512]{1,0:T(8,128)(2,1)S(1)}, bf16[72,512]{1,0:T(8,128)(2,1)S(1)}, u32[]{:S(2)}, u32[]{:S(2)}) %collective-permute-start.5) | collective-permute-done | bytes 73760 | tf_op jit(solution)/shard_map/ppermute | solution.py:40
  42.3 3.4 %collective-permute-start.7 = (bf16[288,512]{1,0:T(8,128)(2,1)S(1)}, bf16[288,512]{1,0:T(8,128)(2,1)S(1)}, u32[]{:S(2)}, u32[]{:S(2)}) collective-permute-start(bf16[288,512]{1,0:T(8,128)(2,1)S(1)} %bitcast.147), channel_id=1, source_target_pairs={{0,1},{1,0},{2,3},{3,2},{4,5},{5,4},{6,7},{7,6},{8,9},{9,8},{10,11... | collective-permute-start | bytes 884744 | tf_op jit(solution)/shard_map/ppermute | solution.py:40
  45.8 1.1 collective-permute-done.7
  47.3 1.4 collective-permute-start.8
  48.7 1.4 collective-permute-start.10
  50.0 1.6 collective-permute-start.9
  52.0 2.9 %collective-permute-done.8 = f32[48,512]{1,0:T(8,128)S(1)} collective-permute-done((f32[48,512]{1,0:T(8,128)S(1)}, f32[48,512]{1,0:T(8,128)S(1)}, u32[]{:S(2)}, u32[]{:S(2)}) %collective-permute-start.8) | collective-permute-done | bytes 98336 | tf_op jit(solution)/shard_map/ppermute | solution.py:40
  55.3 5.0 %collective-permute-done.9 = f32[48,512]{1,0:T(8,128)S(1)} collective-permute-done((f32[48,512]{1,0:T(8,128)S(1)}, f32[48,512]{1,0:T(8,128)S(1)}, u32[]{:S(2)}, u32[]{:S(2)}) %collective-permute-start.9) | collective-permute-done | bytes 98336 | tf_op jit(solution)/shard_map/ppermute | solution.py:40
  60.4 1.8 %collective-permute-start.11 = (f32[12,512]{1,0:T(8,128)S(1)}, f32[12,512]{1,0:T(8,128)S(1)}, u32[]{:S(2)}, u32[]{:S(2)}) collective-permute-start(f32[12,512]{1,0:T(8,128)S(1)} %get-tuple-element.51), channel_id=1, source_target_pairs={{0,8},{8,16},{16,24},{24,0},{32,40},{40,48},{48,56},{56,32},{64,72... | collective-permute-start | bytes 73736 | tf_op jit(solution)/shard_map/ppermute | solution.py:40
  62.2 2.3 %collective-permute-start.13 = (f32[12,512]{1,0:T(8,128)S(1)}, f32[12,512]{1,0:T(8,128)S(1)}, u32[]{:S(2)}, u32[]{:S(2)}) collective-permute-start(f32[12,512]{1,0:T(8,128)S(1)} %get-tuple-element.52), channel_id=1, source_target_pairs={{0,24},{8,0},{16,8},{24,16},{32,56},{40,32},{48,40},{56,48},{64,88... | collective-permute-start | bytes 73736 | tf_op jit(solution)/shard_map/ppermute | solution.py:40
  64.5 1.2 collective-permute-start.12
  65.7 0.8 collective-permute-start.14
  66.5 1.9 %collective-permute-start.16 = (f32[24,576]{1,0:T(8,128)S(1)}, f32[24,576]{1,0:T(8,128)S(1)}, u32[]{:S(2)}, u32[]{:S(2)}) collective-permute-start(f32[24,576]{1,0:T(8,128)S(1)} %get-tuple-element.45), channel_id=1, source_target_pairs={{0,96},{8,104},{16,112},{24,120},{32,0},{40,8},{48,16},{56,24},{64... | collective-permute-start | bytes 165896 | tf_op jit(solution)/shard_map/ppermute | solution.py:40
  68.5 1.3 collective-permute-done.12
  69.7 2.0 %collective-permute-done.14 = f32[24,576]{1,0:T(8,128)S(1)} collective-permute-done((f32[24,576]{1,0:T(8,128)S(1)}, f32[24,576]{1,0:T(8,128)S(1)}, u32[]{:S(2)}, u32[]{:S(2)}) %collective-permute-start.14) | collective-permute-done | bytes 55328 | tf_op jit(solution)/shard_map/ppermute | solution.py:40
  71.7 3.1 %collective-permute-done.15 = f32[24,576]{1,0:T(8,128)S(1)} collective-permute-done((f32[24,576]{1,0:T(8,128)S(1)}, f32[24,576]{1,0:T(8,128)S(1)}, u32[]{:S(2)}, u32[]{:S(2)}) %collective-permute-start.15) | collective-permute-done | bytes 55328 | tf_op jit(solution)/shard_map/ppermute | solution.py:40
  74.9 3.3 %collective-permute-start.17 = (f32[12,512]{1,0:T(8,128)S(1)}, f32[12,512]{1,0:T(8,128)S(1)}, u32[]{:S(2)}, u32[]{:S(2)}) collective-permute-start(f32[12,512]{1,0:T(8,128)S(1)} %fusion.19), channel_id=1, source_target_pairs={{0,1},{1,0},{2,3},{3,2},{4,5},{5,4},{6,7},{7,6},{8,9},{9,8},{10,11... | collective-permute-start | bytes 73736 | tf_op jit(solution)/shard_map/ppermute | solution.py:40
  78.2 0.8 collective-permute-done.17
  79.5 1.1 collective-permute-start.22
  80.5 1.5 collective-permute-start.21
  82.0 1.4 collective-permute-start.18
  83.5 3.2 %collective-permute-done.18 = f32[2,12,512]{2,1,0:T(8,128)S(1)} collective-permute-done((f32[2,12,512]{2,1,0:T(8,128)S(1)}, f32[2,12,512]{2,1,0:T(8,128)S(1)}, u32[]{:S(2)}, u32[]{:S(2)}) %collective-permute-start.18) | collective-permute-done | bytes 49184 | tf_op jit(solution)/shard_map/ppermute | solution.py:40
  87.3 4.1 %collective-permute-done.19 = f32[2,12,512]{2,1,0:T(8,128)S(1)} collective-permute-done((f32[2,12,512]{2,1,0:T(8,128)S(1)}, f32[2,12,512]{2,1,0:T(8,128)S(1)}, u32[]{:S(2)}, u32[]{:S(2)}) %collective-permute-start.19) | collective-permute-done | bytes 49184 | tf_op jit(solution)/shard_map/ppermute | solution.py:40
  91.5 1.5 collective-permute-start.26
  93.6 0.7 reshape.60
  94.4 3.8 %collective-permute-done.24 = f32[24,576]{1,0:T(8,128)S(1)} collective-permute-done((f32[24,576]{1,0:T(8,128)S(1)}, f32[24,576]{1,0:T(8,128)S(1)}, u32[]{:S(2)}, u32[]{:S(2)}) %collective-permute-start.24) | collective-permute-done | bytes 55328 | tf_op jit(solution)/shard_map/ppermute | solution.py:40
  99.2 1.9 %collective-permute-start.29 = (f32[72,576]{1,0:T(8,128)S(1)}, f32[72,576]{1,0:T(8,128)S(1)}, u32[]{:S(2)}, u32[]{:S(2)}) collective-permute-start(f32[72,576]{1,0:T(8,128)S(1)} %pad_maximum_fusion.1), channel_id=1, source_target_pairs={{0,6},{1,7},{2,0},{3,1},{4,2},{5,3},{6,4},{7,5},{8,14},{9,15},{10,... | collective-permute-start | bytes 497672 | tf_op jit(solution)/shard_map/ppermute | solution.py:40
  101.1 4.8 %collective-permute-done.27 = f32[72,576]{1,0:T(8,128)S(1)} collective-permute-done((f32[72,576]{1,0:T(8,128)S(1)}, f32[72,576]{1,0:T(8,128)S(1)}, u32[]{:S(2)}, u32[]{:S(2)}) %collective-permute-start.27) | collective-permute-done | bytes 165920 | tf_op jit(solution)/shard_map/ppermute | solution.py:40
  106.6 6.4 %collective-permute-start.30 = (f32[288,576]{1,0:T(8,128)S(1)}, f32[288,576]{1,0:T(8,128)S(1)}, u32[]{:S(2)}, u32[]{:S(2)}) collective-permute-start(f32[288,576]{1,0:T(8,128)S(1)} %bitcast.141), channel_id=1, source_target_pairs={{0,1},{1,0},{2,3},{3,2},{4,5},{5,4},{6,7},{7,6},{8,9},{9,8},{10,11... | collective-permute-start | bytes 1990664 | tf_op jit(solution)/shard_map/ppermute | solution.py:40
  113.1 1.7 collective-permute-done.30
  114.9 23.1 %inverse_factor.1.inverse_ref = f32[576,576]{1,0:T(8,128)S(1)} custom-call(f32[576,576]{1,0:T(8,128)S(1)} %bitcast.138), custom_call_target="tpu_custom_call" | custom-call | flops 30576476160 | bytes 2654208 | tf_op jit(solution)/shard_map/inverse_factor/pallas_call | solution.py:162
  138.0 5.8 %all-gather.4.cloned.1.call-done.mixed_ref = f32[1536,512]{1,0:T(8,128)} async-done(((f32[96,512]{1,0:T(8,128)}), f32[1536,512]{1,0:T(8,128)}) %all-gather.4.cloned.1.call-update) | async-done | bytes 3145744 | tf_op jit(solution)/shard_map/all_gather | solution.py:338
  143.7 19.4 %adam_step.1 = (f32[3696,512]{1,0:T(8,128)}, f32[32,3696]{1,0:T(8,128)}, f32[32,3696]{1,0:T(8,128)}) custom-call(s32[1]{0:T(128)} %bitcast.at_ref, f32[576,576]{1,0:T(8,128)S(1)} %inverse_factor.1.inverse_ref, bf16[576,512]{1,0:T(8,128)(2,1)S(1)} %bitcast.137, f32[1536,512]{1,0:T(8,128)} %all-gather.4.cloned.1.call-done.mixed_ref, ...), custom_call_target="tpu_custom_call" | custom-call | flops 10166992896 | bytes 31531008 | tf_op jit(solution)/shard_map/adam_step/pallas_call | solution.py:278
  (83 shorter events, 5.7 us)
Async XLA Ops:
  7.2 87.2 %all-gather.6.cloned.1.call-start = ((), (), s32[]{:S(2)}) async-start(), calls=%async_computation.1 | async-start | bytes 8077312 | tf_op jit(solution)/shard_map/all_gather | solution.py:315
  9.2 134.5 %all-gather.4.cloned.1.call-start = ((), (), s32[]{:S(2)}) async-start(), calls=%async_computation | async-start | bytes 3342336 | tf_op jit(solution)/shard_map/all_gather | solution.py:338
  9.3 11.2 %copy-start.2 = (bf16[1536,512]{1,0:T(8,128)(2,1)S(1)}, bf16[1536,512]{1,0:T(8,128)(2,1)}, u32[]{:S(2)}) copy-start(bf16[1536,512]{1,0:T(8,128)(2,1)} %param.5) | copy-start | bytes 4718596
  22.8 4.0 %collective-permute-start = (bf16[288,512]{1,0:T(8,128)(2,1)S(1)}, bf16[288,512]{1,0:T(8,128)(2,1)S(1)}, u32[]{:S(2)}, u32[]{:S(2)}) collective-permute-start(bf16[288,512]{1,0:T(8,128)(2,1)S(1)} %fusion.7), channel_id=1, source_target_pairs={{0,1},{1,0},{2,3},{3,2},{4,5},{5,4},{6,7},{7,6},{8,9},{9,8},{10,11... | collective-permute-start | bytes 884744 | tf_op jit(solution)/shard_map/ppermute | solution.py:40
  27.0 5.4 %collective-permute-start.1 = (bf16[72,512]{1,0:T(8,128)(2,1)S(1)}, bf16[72,512]{1,0:T(8,128)(2,1)S(1)}, u32[]{:S(2)}, u32[]{:S(2)}) collective-permute-start(bf16[72,512]{1,0:T(8,128)(2,1)S(1)} %get-tuple-element.35), channel_id=1, source_target_pairs={{0,2},{1,3},{2,4},{3,5},{4,6},{5,7},{6,0},{7,1},{8,10},{9,11},{10,... | collective-permute-start | bytes 221192 | tf_op jit(solution)/shard_map/ppermute | solution.py:40
  28.5 4.0 %collective-permute-start.3 = (bf16[72,512]{1,0:T(8,128)(2,1)S(1)}, bf16[72,512]{1,0:T(8,128)(2,1)S(1)}, u32[]{:S(2)}, u32[]{:S(2)}) collective-permute-start(bf16[72,512]{1,0:T(8,128)(2,1)S(1)} %get-tuple-element.36), channel_id=1, source_target_pairs={{0,6},{1,7},{2,0},{3,1},{4,2},{5,3},{6,4},{7,5},{8,14},{9,15},{10,... | collective-permute-start | bytes 221192 | tf_op jit(solution)/shard_map/ppermute | solution.py:40
  30.0 4.8 %collective-permute-start.2 = (bf16[72,512]{1,0:T(8,128)(2,1)S(1)}, bf16[72,512]{1,0:T(8,128)(2,1)S(1)}, u32[]{:S(2)}, u32[]{:S(2)}) collective-permute-start(bf16[72,512]{1,0:T(8,128)(2,1)S(1)} %get-tuple-element.37), channel_id=1, source_target_pairs={{0,4},{1,5},{2,6},{3,7},{4,0},{5,1},{6,2},{7,3},{8,12},{9,13},{10,... | collective-permute-start | bytes 221192 | tf_op jit(solution)/shard_map/ppermute | solution.py:40
  34.8 4.7 %collective-permute-start.4 = (bf16[72,512]{1,0:T(8,128)(2,1)S(1)}, bf16[72,512]{1,0:T(8,128)(2,1)S(1)}, u32[]{:S(2)}, u32[]{:S(2)}) collective-permute-start(bf16[72,512]{1,0:T(8,128)(2,1)S(1)} %get-tuple-element.34), channel_id=1, source_target_pairs={{0,2},{1,3},{2,4},{3,5},{4,6},{5,7},{6,0},{7,1},{8,10},{9,11},{10,... | collective-permute-start | bytes 221192 | tf_op jit(solution)/shard_map/ppermute | solution.py:40
  36.0 6.3 %collective-permute-start.6 = (bf16[72,512]{1,0:T(8,128)(2,1)S(1)}, bf16[72,512]{1,0:T(8,128)(2,1)S(1)}, u32[]{:S(2)}, u32[]{:S(2)}) collective-permute-start(bf16[72,512]{1,0:T(8,128)(2,1)S(1)} %get-tuple-element.34), channel_id=1, source_target_pairs={{0,6},{1,7},{2,0},{3,1},{4,2},{5,3},{6,4},{7,5},{8,14},{9,15},{10,... | collective-permute-start | bytes 221192 | tf_op jit(solution)/shard_map/ppermute | solution.py:40
  37.6 4.7 %collective-permute-start.5 = (bf16[72,512]{1,0:T(8,128)(2,1)S(1)}, bf16[72,512]{1,0:T(8,128)(2,1)S(1)}, u32[]{:S(2)}, u32[]{:S(2)}) collective-permute-start(bf16[72,512]{1,0:T(8,128)(2,1)S(1)} %get-tuple-element.34), channel_id=1, source_target_pairs={{0,4},{1,5},{2,6},{3,7},{4,0},{5,1},{6,2},{7,3},{8,12},{9,13},{10,... | collective-permute-start | bytes 221192 | tf_op jit(solution)/shard_map/ppermute | solution.py:40
  42.3 4.6 %collective-permute-start.7 = (bf16[288,512]{1,0:T(8,128)(2,1)S(1)}, bf16[288,512]{1,0:T(8,128)(2,1)S(1)}, u32[]{:S(2)}, u32[]{:S(2)}) collective-permute-start(bf16[288,512]{1,0:T(8,128)(2,1)S(1)} %bitcast.147), channel_id=1, source_target_pairs={{0,1},{1,0},{2,3},{3,2},{4,5},{5,4},{6,7},{7,6},{8,9},{9,8},{10,11... | collective-permute-start | bytes 884744 | tf_op jit(solution)/shard_map/ppermute | solution.py:40
  47.3 7.6 %collective-permute-start.8 = (f32[48,512]{1,0:T(8,128)S(1)}, f32[48,512]{1,0:T(8,128)S(1)}, u32[]{:S(2)}, u32[]{:S(2)}) collective-permute-start(f32[48,512]{1,0:T(8,128)S(1)} %get-tuple-element.38), channel_id=1, source_target_pairs={{0,32},{8,40},{16,48},{24,56},{32,64},{40,72},{48,80},{56,88},{64,... | collective-permute-start | bytes 294920 | tf_op jit(solution)/shard_map/ppermute | solution.py:40
  48.7 6.6 %collective-permute-start.10 = (f32[48,512]{1,0:T(8,128)S(1)}, f32[48,512]{1,0:T(8,128)S(1)}, u32[]{:S(2)}, u32[]{:S(2)}) collective-permute-start(f32[48,512]{1,0:T(8,128)S(1)} %get-tuple-element.39), channel_id=1, source_target_pairs={{0,96},{8,104},{16,112},{24,120},{32,0},{40,8},{48,16},{56,24},{64... | collective-permute-start | bytes 294920 | tf_op jit(solution)/shard_map/ppermute | solution.py:40
  50.0 10.2 %collective-permute-start.9 = (f32[48,512]{1,0:T(8,128)S(1)}, f32[48,512]{1,0:T(8,128)S(1)}, u32[]{:S(2)}, u32[]{:S(2)}) collective-permute-start(f32[48,512]{1,0:T(8,128)S(1)} %get-tuple-element.40), channel_id=1, source_target_pairs={{0,64},{8,72},{16,80},{24,88},{32,96},{40,104},{48,112},{56,120},{... | collective-permute-start | bytes 294920 | tf_op jit(solution)/shard_map/ppermute | solution.py:40
  60.4 8.1 %collective-permute-start.11 = (f32[12,512]{1,0:T(8,128)S(1)}, f32[12,512]{1,0:T(8,128)S(1)}, u32[]{:S(2)}, u32[]{:S(2)}) collective-permute-start(f32[12,512]{1,0:T(8,128)S(1)} %get-tuple-element.51), channel_id=1, source_target_pairs={{0,8},{8,16},{16,24},{24,0},{32,40},{40,48},{48,56},{56,32},{64,72... | collective-permute-start | bytes 73736 | tf_op jit(solution)/shard_map/ppermute | solution.py:40
  62.2 6.3 %collective-permute-start.13 = (f32[12,512]{1,0:T(8,128)S(1)}, f32[12,512]{1,0:T(8,128)S(1)}, u32[]{:S(2)}, u32[]{:S(2)}) collective-permute-start(f32[12,512]{1,0:T(8,128)S(1)} %get-tuple-element.52), channel_id=1, source_target_pairs={{0,24},{8,0},{16,8},{24,16},{32,56},{40,32},{48,40},{56,48},{64,88... | collective-permute-start | bytes 73736 | tf_op jit(solution)/shard_map/ppermute | solution.py:40
  64.5 5.3 %collective-permute-start.12 = (f32[12,512]{1,0:T(8,128)S(1)}, f32[12,512]{1,0:T(8,128)S(1)}, u32[]{:S(2)}, u32[]{:S(2)}) collective-permute-start(f32[12,512]{1,0:T(8,128)S(1)} %get-tuple-element.53), channel_id=1, source_target_pairs={{0,16},{8,24},{16,0},{24,8},{32,48},{40,56},{48,32},{56,40},{64,80... | collective-permute-start | bytes 73736 | tf_op jit(solution)/shard_map/ppermute | solution.py:40
  65.7 6.0 %collective-permute-start.14 = (f32[24,576]{1,0:T(8,128)S(1)}, f32[24,576]{1,0:T(8,128)S(1)}, u32[]{:S(2)}, u32[]{:S(2)}) collective-permute-start(f32[24,576]{1,0:T(8,128)S(1)} %get-tuple-element.44), channel_id=1, source_target_pairs={{0,32},{8,40},{16,48},{24,56},{32,64},{40,72},{48,80},{56,88},{64,... | collective-permute-start | bytes 165896 | tf_op jit(solution)/shard_map/ppermute | solution.py:40
  66.5 5.2 %collective-permute-start.16 = (f32[24,576]{1,0:T(8,128)S(1)}, f32[24,576]{1,0:T(8,128)S(1)}, u32[]{:S(2)}, u32[]{:S(2)}) collective-permute-start(f32[24,576]{1,0:T(8,128)S(1)} %get-tuple-element.45), channel_id=1, source_target_pairs={{0,96},{8,104},{16,112},{24,120},{32,0},{40,8},{48,16},{56,24},{64... | collective-permute-start | bytes 165896 | tf_op jit(solution)/shard_map/ppermute | solution.py:40
  68.4 6.4 %collective-permute-start.15 = (f32[24,576]{1,0:T(8,128)S(1)}, f32[24,576]{1,0:T(8,128)S(1)}, u32[]{:S(2)}, u32[]{:S(2)}) collective-permute-start(f32[24,576]{1,0:T(8,128)S(1)} %get-tuple-element.46), channel_id=1, source_target_pairs={{0,64},{8,72},{16,80},{24,88},{32,96},{40,104},{48,112},{56,120},{... | collective-permute-start | bytes 165896 | tf_op jit(solution)/shard_map/ppermute | solution.py:40
  74.9 4.1 %collective-permute-start.17 = (f32[12,512]{1,0:T(8,128)S(1)}, f32[12,512]{1,0:T(8,128)S(1)}, u32[]{:S(2)}, u32[]{:S(2)}) collective-permute-start(f32[12,512]{1,0:T(8,128)S(1)} %fusion.19), channel_id=1, source_target_pairs={{0,1},{1,0},{2,3},{3,2},{4,5},{5,4},{6,7},{7,6},{8,9},{9,8},{10,11... | collective-permute-start | bytes 73736 | tf_op jit(solution)/shard_map/ppermute | solution.py:40
  79.1 12.4 %collective-permute-start.23 = (f32[24,576]{1,0:T(8,128)S(1)}, f32[24,576]{1,0:T(8,128)S(1)}, u32[]{:S(2)}, u32[]{:S(2)}) collective-permute-start(f32[24,576]{1,0:T(8,128)S(1)} %fusion.17), channel_id=1, source_target_pairs={{0,24},{8,0},{16,8},{24,16},{32,56},{40,32},{48,40},{56,48},{64,88... | collective-permute-start | bytes 165896 | tf_op jit(solution)/shard_map/ppermute | solution.py:40
  79.5 12.0 %collective-permute-start.22 = (f32[24,576]{1,0:T(8,128)S(1)}, f32[24,576]{1,0:T(8,128)S(1)}, u32[]{:S(2)}, u32[]{:S(2)}) collective-permute-start(f32[24,576]{1,0:T(8,128)S(1)} %fusion.17), channel_id=1, source_target_pairs={{0,8},{8,16},{16,24},{24,0},{32,40},{40,48},{48,56},{56,32},{64,72... | collective-permute-start | bytes 165896 | tf_op jit(solution)/shard_map/ppermute | solution.py:40
  80.5 10.9 %collective-permute-start.21 = (f32[24,576]{1,0:T(8,128)S(1)}, f32[24,576]{1,0:T(8,128)S(1)}, u32[]{:S(2)}, u32[]{:S(2)}) collective-permute-start(f32[24,576]{1,0:T(8,128)S(1)} %fusion.17), channel_id=1, source_target_pairs={{0,16},{8,24},{16,0},{24,8},{32,48},{40,56},{48,32},{56,40},{64,80... | collective-permute-start | bytes 165896 | tf_op jit(solution)/shard_map/ppermute | solution.py:40
  82.0 9.4 %collective-permute-start.20 = (f32[2,12,512]{2,1,0:T(8,128)S(1)}, f32[2,12,512]{2,1,0:T(8,128)S(1)}, u32[]{:S(2)}, u32[]{:S(2)}) collective-permute-start(f32[2,12,512]{2,1,0:T(8,128)S(1)} %bitcast_dynamic-update-slice_fusion.20), channel_id=1, source_target_pairs={{0,6},{1,7},{2,0},{3,1},{4,2},{5,3},{6,4},{7,5},{8,14},{9,15},{10,... | collective-permute-start | bytes 147464 | tf_op jit(solution)/shard_map/ppermute | solution.py:40
  82.0 4.7 %collective-permute-start.18 = (f32[2,12,512]{2,1,0:T(8,128)S(1)}, f32[2,12,512]{2,1,0:T(8,128)S(1)}, u32[]{:S(2)}, u32[]{:S(2)}) collective-permute-start(f32[2,12,512]{2,1,0:T(8,128)S(1)} %bitcast_dynamic-update-slice_fusion.20), channel_id=1, source_target_pairs={{0,2},{1,3},{2,4},{3,5},{4,6},{5,7},{6,0},{7,1},{8,10},{9,11},{10,... | collective-permute-start | bytes 147464 | tf_op jit(solution)/shard_map/ppermute | solution.py:40
  86.8 4.6 %collective-permute-start.19 = (f32[2,12,512]{2,1,0:T(8,128)S(1)}, f32[2,12,512]{2,1,0:T(8,128)S(1)}, u32[]{:S(2)}, u32[]{:S(2)}) collective-permute-start(f32[2,12,512]{2,1,0:T(8,128)S(1)} %bitcast_dynamic-update-slice_fusion.20), channel_id=1, source_target_pairs={{0,4},{1,5},{2,6},{3,7},{4,0},{5,1},{6,2},{7,3},{8,12},{9,13},{10,... | collective-permute-start | bytes 147464 | tf_op jit(solution)/shard_map/ppermute | solution.py:40
  91.5 6.7 %collective-permute-start.26 = (f32[24,576]{1,0:T(8,128)S(1)}, f32[24,576]{1,0:T(8,128)S(1)}, u32[]{:S(2)}, u32[]{:S(2)}) collective-permute-start(f32[24,576]{1,0:T(8,128)S(1)} %add_add_fusion), channel_id=1, source_target_pairs={{0,96},{8,104},{16,112},{24,120},{32,0},{40,8},{48,16},{56,24},{64... | collective-permute-start | bytes 165896 | tf_op jit(solution)/shard_map/ppermute | solution.py:40
  92.9 5.2 %collective-permute-start.25 = (f32[24,576]{1,0:T(8,128)S(1)}, f32[24,576]{1,0:T(8,128)S(1)}, u32[]{:S(2)}, u32[]{:S(2)}) collective-permute-start(f32[24,576]{1,0:T(8,128)S(1)} %add_add_fusion), channel_id=1, source_target_pairs={{0,64},{8,72},{16,80},{24,88},{32,96},{40,104},{48,112},{56,120},{... | collective-permute-start | bytes 165896 | tf_op jit(solution)/shard_map/ppermute | solution.py:40
  93.3 4.9 %collective-permute-start.24 = (f32[24,576]{1,0:T(8,128)S(1)}, f32[24,576]{1,0:T(8,128)S(1)}, u32[]{:S(2)}, u32[]{:S(2)}) collective-permute-start(f32[24,576]{1,0:T(8,128)S(1)} %add_add_fusion), channel_id=1, source_target_pairs={{0,32},{8,40},{16,48},{24,56},{32,64},{40,72},{48,80},{56,88},{64,... | collective-permute-start | bytes 165896 | tf_op jit(solution)/shard_map/ppermute | solution.py:40
  98.3 7.6 %collective-permute-start.27 = (f32[72,576]{1,0:T(8,128)S(1)}, f32[72,576]{1,0:T(8,128)S(1)}, u32[]{:S(2)}, u32[]{:S(2)}) collective-permute-start(f32[72,576]{1,0:T(8,128)S(1)} %pad_maximum_fusion.1), channel_id=1, source_target_pairs={{0,2},{1,3},{2,4},{3,5},{4,6},{5,7},{6,0},{7,1},{8,10},{9,11},{10,... | collective-permute-start | bytes 497672 | tf_op jit(solution)/shard_map/ppermute | solution.py:40
  98.5 7.4 %collective-permute-start.28 = (f32[72,576]{1,0:T(8,128)S(1)}, f32[72,576]{1,0:T(8,128)S(1)}, u32[]{:S(2)}, u32[]{:S(2)}) collective-permute-start(f32[72,576]{1,0:T(8,128)S(1)} %pad_maximum_fusion.1), channel_id=1, source_target_pairs={{0,4},{1,5},{2,6},{3,7},{4,0},{5,1},{6,2},{7,3},{8,12},{9,13},{10,... | collective-permute-start | bytes 497672 | tf_op jit(solution)/shard_map/ppermute | solution.py:40
  99.2 7.4 %collective-permute-start.29 = (f32[72,576]{1,0:T(8,128)S(1)}, f32[72,576]{1,0:T(8,128)S(1)}, u32[]{:S(2)}, u32[]{:S(2)}) collective-permute-start(f32[72,576]{1,0:T(8,128)S(1)} %pad_maximum_fusion.1), channel_id=1, source_target_pairs={{0,6},{1,7},{2,0},{3,1},{4,2},{5,3},{6,4},{7,5},{8,14},{9,15},{10,... | collective-permute-start | bytes 497672 | tf_op jit(solution)/shard_map/ppermute | solution.py:40
  106.6 8.2 %collective-permute-start.30 = (f32[288,576]{1,0:T(8,128)S(1)}, f32[288,576]{1,0:T(8,128)S(1)}, u32[]{:S(2)}, u32[]{:S(2)}) collective-permute-start(f32[288,576]{1,0:T(8,128)S(1)} %bitcast.141), channel_id=1, source_target_pairs={{0,1},{1,0},{2,3},{3,2},{4,5},{5,4},{6,7},{7,6},{8,9},{9,8},{10,11... | collective-permute-start | bytes 1990664 | tf_op jit(solution)/shard_map/ppermute | solution.py:40
  114.8 28.9 %copy-start = (f32[32,3696]{1,0:T(8,128)S(1)}, f32[32,3696]{1,0:T(8,128)}, u32[]{:S(2)}) copy-start(f32[32,3696]{1,0:T(8,128)} %own_first_ref.1) | copy-start | bytes 1419268
  114.9 28.9 %copy-start.1 = (f32[32,3696]{1,0:T(8,128)S(1)}, f32[32,3696]{1,0:T(8,128)}, u32[]{:S(2)}) copy-start(f32[32,3696]{1,0:T(8,128)} %own_second_ref.1) | copy-start | bytes 1419268
Sparse Core Ops, SparseCore 0:
  10.8 77.2 all-gather.5
  94.5 49.2 all-gather.3

commit v11 on v10

--- a/solution.py
+++ b/solution.py
@@ -332,8 +332,8 @@
     mixed, gram = lax.optimization_barrier(
         (scatter_sum(mixed.reshape(4, share, RANK), "z"), scatter_sum(gram, "x"))
     )
-    mixed, gram = lax.optimization_barrier((gather(mixed, "core"), gram))
-    mixed, gram = lax.optimization_barrier((gather(mixed, "y"), full_sum(gram, "z")))
+    mixed, gram = lax.optimization_barrier((gather(gather(mixed, "core"), "y"), gram))
+    gram = full_sum(gram, "z")
     mixed, gathered = lax.optimization_barrier((mixed.reshape(8 * share, RANK), gathered))
     mixed = lax.all_gather(mixed, "row", axis=0, tiled=True)
     gram = gather(gram, "x")

time: 170 us -> 171 us (level)
  waiting for transfers between devices: 48.2 us -> 50.9 us
  starting transfers between devices: 44.5 us -> 42.6 us
    ppermute x31, starting transfers between devices: 44.4 us -> 42.5 us  [shift(): return lax.ppermute(value, axis, pairs)]
  transfers between devices with their start and end apart: 33 -> 33, of which waited for: 19 -> 23; matrix products, arithmetic and copies ran while one was open for 11% -> 11% of each run, Pallas kernels for 14% -> 14%
where the time goes in v11:
time: 171 us
  waiting for transfers between devices  50.9 us (30%)
  Pallas kernels  44.5 us (26%)
  starting transfers between devices  42.6 us (25%)
  between operations  14.6 us (9%)
  matrix products  14.1 us (8%)
  local copies, waits for them, and re-layouts  3.98 us (2%)
    ppermute x31, waiting for transfers between devices, shift(): return lax.ppermute(value, axis, pairs)  43.9 us
    ppermute x31, starting transfers between devices, shift(): return lax.ppermute(value, axis, pairs)  42.5 us
    pallas_call x1, Pallas kernels, inverse_factor(): pl.pallas_call(factor_kernel, out_shape=jax.ShapeDtypeStruct((size, size)...  23.1 us
    pallas_call x1, Pallas kernels, adam_step(): pl.pallas_call(step_kernel, out_shape=(jax.ShapeDtypeStruct((width, featu...  19.4 us
    dot_general x1, matrix products, sketched_term(): jnp.dot(sketch_turned, grad_turned, preferred_element_type=f32)  11.2 us
    all_gather x1, waiting for transfers between devices, local(): mixed = lax.all_gather(mixed, 'row', axis=0, tiled=True)  6.98 us
  transfers between devices with their start and end apart: 33, of which 23 were waited for; matrix products, arithmetic and copies ran while one was open for 11% of the time, Pallas kernels for 14%

profile of v11, /device:TPU:1, one launch (start us, length us, event | category | flops | bytes accessed | tf_op | source)
XLA Modules:
  0.0 170.9 jit_solution(15327919030647021351)
XLA Ops:
  7.2 2.0 %pack.1 = bf16[64,3696]{1,0:T(8,128)(2,1)} custom-call(f32[32,3696]{1,0:T(8,128)} %own_first_ref.1, f32[32,3696]{1,0:T(8,128)} %own_second_ref.1), custom_call_target="tpu_custom_call" | custom-call | tf_op jit(solution)/shard_map/pack/pallas_call | solution.py:187
  9.3 11.2 %fusion.21 = f32[576,1536]{1,0:T(8,128)S(1)} fusion(bf16[3696,576]{0,1:T(8,128)(2,1)} %param.7, bf16[1536,3696]{0,1:T(8,128)(2,1)} %param.6), kind=kOutput, calls=%fused_computation.73 | convolution fusion | flops 6539968512 | bytes 19150848 | tf_op jit(solution)/shard_map/dot_general | solution.py:195
  20.5 1.1 fusion.1
  21.7 1.1 fusion.4
  22.8 1.5 collective-permute-start
  24.3 1.5 reshape.51
  25.8 1.0 constant_dynamic-slice_fusion
  27.0 1.4 collective-permute-start.1
  28.5 1.5 collective-permute-start.3
  30.0 1.6 collective-permute-start.2
  31.6 0.9 collective-permute-done.1
  32.4 2.3 %collective-permute-done.2 = bf16[72,512]{1,0:T(8,128)(2,1)S(1)} collective-permute-done((bf16[72,512]{1,0:T(8,128)(2,1)S(1)}, bf16[72,512]{1,0:T(8,128)(2,1)S(1)}, u32[]{:S(2)}, u32[]{:S(2)}) %collective-permute-start.2) | collective-permute-done | bytes 73760 | tf_op jit(solution)/shard_map/ppermute | solution.py:40
  34.8 1.2 collective-permute-start.4
  36.0 1.6 collective-permute-start.6
  37.9 1.6 collective-permute-done.4
  39.6 2.7 %collective-permute-done.5 = bf16[72,512]{1,0:T(8,128)(2,1)S(1)} collective-permute-done((bf16[72,512]{1,0:T(8,128)(2,1)S(1)}, bf16[72,512]{1,0:T(8,128)(2,1)S(1)}, u32[]{:S(2)}, u32[]{:S(2)}) %collective-permute-start.5) | collective-permute-done | bytes 73760 | tf_op jit(solution)/shard_map/ppermute | solution.py:40
  42.3 3.4 %collective-permute-start.7 = (bf16[288,512]{1,0:T(8,128)(2,1)S(1)}, bf16[288,512]{1,0:T(8,128)(2,1)S(1)}, u32[]{:S(2)}, u32[]{:S(2)}) collective-permute-start(bf16[288,512]{1,0:T(8,128)(2,1)S(1)} %bitcast.147), channel_id=1, source_target_pairs={{0,1},{1,0},{2,3},{3,2},{4,5},{5,4},{6,7},{7,6},{8,9},{9,8},{10,11... | collective-permute-start | bytes 884744 | tf_op jit(solution)/shard_map/ppermute | solution.py:40
  45.8 1.1 collective-permute-done.7
  47.3 1.4 collective-permute-start.8
  48.7 1.4 collective-permute-start.10
  50.0 1.6 collective-permute-start.9
  52.0 2.9 %collective-permute-done.8 = f32[48,512]{1,0:T(8,128)S(1)} collective-permute-done((f32[48,512]{1,0:T(8,128)S(1)}, f32[48,512]{1,0:T(8,128)S(1)}, u32[]{:S(2)}, u32[]{:S(2)}) %collective-permute-start.8) | collective-permute-done | bytes 98336 | tf_op jit(solution)/shard_map/ppermute | solution.py:40
  55.3 5.0 %collective-permute-done.9 = f32[48,512]{1,0:T(8,128)S(1)} collective-permute-done((f32[48,512]{1,0:T(8,128)S(1)}, f32[48,512]{1,0:T(8,128)S(1)}, u32[]{:S(2)}, u32[]{:S(2)}) %collective-permute-start.9) | collective-permute-done | bytes 98336 | tf_op jit(solution)/shard_map/ppermute | solution.py:40
  60.4 1.8 %collective-permute-start.11 = (f32[12,512]{1,0:T(8,128)S(1)}, f32[12,512]{1,0:T(8,128)S(1)}, u32[]{:S(2)}, u32[]{:S(2)}) collective-permute-start(f32[12,512]{1,0:T(8,128)S(1)} %get-tuple-element.49), channel_id=1, source_target_pairs={{0,8},{8,16},{16,24},{24,0},{32,40},{40,48},{48,56},{56,32},{64,72... | collective-permute-start | bytes 73736 | tf_op jit(solution)/shard_map/ppermute | solution.py:40
  62.2 2.3 %collective-permute-start.13 = (f32[12,512]{1,0:T(8,128)S(1)}, f32[12,512]{1,0:T(8,128)S(1)}, u32[]{:S(2)}, u32[]{:S(2)}) collective-permute-start(f32[12,512]{1,0:T(8,128)S(1)} %get-tuple-element.50), channel_id=1, source_target_pairs={{0,24},{8,0},{16,8},{24,16},{32,56},{40,32},{48,40},{56,48},{64,88... | collective-permute-start | bytes 73736 | tf_op jit(solution)/shard_map/ppermute | solution.py:40
  64.5 1.2 collective-permute-start.12
  66.5 1.9 %collective-permute-start.16 = (f32[24,576]{1,0:T(8,128)S(1)}, f32[24,576]{1,0:T(8,128)S(1)}, u32[]{:S(2)}, u32[]{:S(2)}) collective-permute-start(f32[24,576]{1,0:T(8,128)S(1)} %get-tuple-element.43), channel_id=1, source_target_pairs={{0,96},{8,104},{16,112},{24,120},{32,0},{40,8},{48,16},{56,24},{64... | collective-permute-start | bytes 165896 | tf_op jit(solution)/shard_map/ppermute | solution.py:40
  68.5 1.3 collective-permute-done.12
  69.7 2.0 %collective-permute-done.14 = f32[24,576]{1,0:T(8,128)S(1)} collective-permute-done((f32[24,576]{1,0:T(8,128)S(1)}, f32[24,576]{1,0:T(8,128)S(1)}, u32[]{:S(2)}, u32[]{:S(2)}) %collective-permute-start.14) | collective-permute-done | bytes 55328 | tf_op jit(solution)/shard_map/ppermute | solution.py:40
  71.7 3.1 %collective-permute-done.15 = f32[24,576]{1,0:T(8,128)S(1)} collective-permute-done((f32[24,576]{1,0:T(8,128)S(1)}, f32[24,576]{1,0:T(8,128)S(1)}, u32[]{:S(2)}, u32[]{:S(2)}) %collective-permute-start.15) | collective-permute-done | bytes 55328 | tf_op jit(solution)/shard_map/ppermute | solution.py:40
  74.9 3.3 %collective-permute-start.17 = (f32[12,512]{1,0:T(8,128)S(1)}, f32[12,512]{1,0:T(8,128)S(1)}, u32[]{:S(2)}, u32[]{:S(2)}) collective-permute-start(f32[12,512]{1,0:T(8,128)S(1)} %fusion.19), channel_id=1, source_target_pairs={{0,1},{1,0},{2,3},{3,2},{4,5},{5,4},{6,7},{7,6},{8,9},{9,8},{10,11... | collective-permute-start | bytes 73736 | tf_op jit(solution)/shard_map/ppermute | solution.py:40
  78.2 0.8 collective-permute-done.17
  80.6 5.4 %collective-permute-done.18 = f32[2,12,512]{2,1,0:T(8,128)S(1)} collective-permute-done((f32[2,12,512]{2,1,0:T(8,128)S(1)}, f32[2,12,512]{2,1,0:T(8,128)S(1)}, u32[]{:S(2)}, u32[]{:S(2)}) %collective-permute-start.18) | collective-permute-done | bytes 49184 | tf_op jit(solution)/shard_map/ppermute | solution.py:40
  86.5 1.1 collective-permute-start.22
  87.6 1.5 collective-permute-start.21
  89.2 1.6 collective-permute-done.22
  90.8 2.0 %collective-permute-done.21 = f32[24,576]{1,0:T(8,128)S(1)} collective-permute-done((f32[24,576]{1,0:T(8,128)S(1)}, f32[24,576]{1,0:T(8,128)S(1)}, u32[]{:S(2)}, u32[]{:S(2)}) %collective-permute-start.21) | collective-permute-done | bytes 55328 | tf_op jit(solution)/shard_map/ppermute | solution.py:40
  93.7 2.2 %collective-permute-start.25 = (f32[24,576]{1,0:T(8,128)S(1)}, f32[24,576]{1,0:T(8,128)S(1)}, u32[]{:S(2)}, u32[]{:S(2)}) collective-permute-start(f32[24,576]{1,0:T(8,128)S(1)} %get-tuple-element.30), channel_id=1, source_target_pairs={{0,64},{8,72},{16,80},{24,88},{32,96},{40,104},{48,112},{56,120},{... | collective-permute-start | bytes 165896 | tf_op jit(solution)/shard_map/ppermute | solution.py:40
  96.4 0.9 collective-permute-done.24
  97.3 1.1 collective-permute-done.25
  98.3 1.1 collective-permute-done.26
  100.3 2.0 %collective-permute-start.29 = (f32[72,576]{1,0:T(8,128)S(1)}, f32[72,576]{1,0:T(8,128)S(1)}, u32[]{:S(2)}, u32[]{:S(2)}) collective-permute-start(f32[72,576]{1,0:T(8,128)S(1)} %pad_maximum_fusion.1), channel_id=1, source_target_pairs={{0,6},{1,7},{2,0},{3,1},{4,2},{5,3},{6,4},{7,5},{8,14},{9,15},{10,... | collective-permute-start | bytes 497672 | tf_op jit(solution)/shard_map/ppermute | solution.py:40
  102.4 5.4 %collective-permute-done.27 = f32[72,576]{1,0:T(8,128)S(1)} collective-permute-done((f32[72,576]{1,0:T(8,128)S(1)}, f32[72,576]{1,0:T(8,128)S(1)}, u32[]{:S(2)}, u32[]{:S(2)}) %collective-permute-start.27) | collective-permute-done | bytes 165920 | tf_op jit(solution)/shard_map/ppermute | solution.py:40
  108.2 4.4 %collective-permute-start.30 = (f32[288,576]{1,0:T(8,128)S(1)}, f32[288,576]{1,0:T(8,128)S(1)}, u32[]{:S(2)}, u32[]{:S(2)}) collective-permute-start(f32[288,576]{1,0:T(8,128)S(1)} %bitcast.141), channel_id=1, source_target_pairs={{0,1},{1,0},{2,3},{3,2},{4,5},{5,4},{6,7},{7,6},{8,9},{9,8},{10,11... | collective-permute-start | bytes 1990664 | tf_op jit(solution)/shard_map/ppermute | solution.py:40
  112.8 1.7 collective-permute-done.30
  114.5 23.1 %inverse_factor.1.inverse_ref = f32[576,576]{1,0:T(8,128)S(1)} custom-call(f32[576,576]{1,0:T(8,128)S(1)} %bitcast.138), custom_call_target="tpu_custom_call" | custom-call | flops 30576476160 | bytes 2654208 | tf_op jit(solution)/shard_map/inverse_factor/pallas_call | solution.py:162
  137.6 7.0 %all-gather.4.cloned.1.call-done.mixed_ref = f32[1536,512]{1,0:T(8,128)} async-done(((f32[96,512]{1,0:T(8,128)}), f32[1536,512]{1,0:T(8,128)}) %all-gather.4.cloned.1.call-update) | async-done | bytes 3145744 | tf_op jit(solution)/shard_map/all_gather | solution.py:338
  144.6 19.4 %adam_step.1 = (f32[3696,512]{1,0:T(8,128)}, f32[32,3696]{1,0:T(8,128)}, f32[32,3696]{1,0:T(8,128)}) custom-call(s32[1]{0:T(128)} %bitcast.at_ref, f32[576,576]{1,0:T(8,128)S(1)} %inverse_factor.1.inverse_ref, bf16[576,512]{1,0:T(8,128)(2,1)S(1)} %bitcast.137, f32[1536,512]{1,0:T(8,128)} %all-gather.4.cloned.1.call-done.mixed_ref, ...), custom_call_target="tpu_custom_call" | custom-call | flops 10166992896 | bytes 31531008 | tf_op jit(solution)/shard_map/adam_step/pallas_call | solution.py:278
  (82 shorter events, 7.7 us)
Async XLA Ops:
  7.2 89.2 %all-gather.6.cloned.1.call-start = ((), (), s32[]{:S(2)}) async-start(), calls=%async_computation.1 | async-start | bytes 8077312 | tf_op jit(solution)/shard_map/all_gather | solution.py:315
  9.2 135.4 %all-gather.4.cloned.1.call-start = ((), (), s32[]{:S(2)}) async-start(), calls=%async_computation | async-start | bytes 3342336 | tf_op jit(solution)/shard_map/all_gather | solution.py:338
  9.3 11.2 %copy-start.2 = (bf16[1536,512]{1,0:T(8,128)(2,1)S(1)}, bf16[1536,512]{1,0:T(8,128)(2,1)}, u32[]{:S(2)}) copy-start(bf16[1536,512]{1,0:T(8,128)(2,1)} %param.5) | copy-start | bytes 4718596
  22.8 4.0 %collective-permute-start = (bf16[288,512]{1,0:T(8,128)(2,1)S(1)}, bf16[288,512]{1,0:T(8,128)(2,1)S(1)}, u32[]{:S(2)}, u32[]{:S(2)}) collective-permute-start(bf16[288,512]{1,0:T(8,128)(2,1)S(1)} %fusion.7), channel_id=1, source_target_pairs={{0,1},{1,0},{2,3},{3,2},{4,5},{5,4},{6,7},{7,6},{8,9},{9,8},{10,11... | collective-permute-start | bytes 884744 | tf_op jit(solution)/shard_map/ppermute | solution.py:40
  27.0 5.4 %collective-permute-start.1 = (bf16[72,512]{1,0:T(8,128)(2,1)S(1)}, bf16[72,512]{1,0:T(8,128)(2,1)S(1)}, u32[]{:S(2)}, u32[]{:S(2)}) collective-permute-start(bf16[72,512]{1,0:T(8,128)(2,1)S(1)} %get-tuple-element.33), channel_id=1, source_target_pairs={{0,2},{1,3},{2,4},{3,5},{4,6},{5,7},{6,0},{7,1},{8,10},{9,11},{10,... | collective-permute-start | bytes 221192 | tf_op jit(solution)/shard_map/ppermute | solution.py:40
  28.5 4.0 %collective-permute-start.3 = (bf16[72,512]{1,0:T(8,128)(2,1)S(1)}, bf16[72,512]{1,0:T(8,128)(2,1)S(1)}, u32[]{:S(2)}, u32[]{:S(2)}) collective-permute-start(bf16[72,512]{1,0:T(8,128)(2,1)S(1)} %get-tuple-element.34), channel_id=1, source_target_pairs={{0,6},{1,7},{2,0},{3,1},{4,2},{5,3},{6,4},{7,5},{8,14},{9,15},{10,... | collective-permute-start | bytes 221192 | tf_op jit(solution)/shard_map/ppermute | solution.py:40
  30.0 4.8 %collective-permute-start.2 = (bf16[72,512]{1,0:T(8,128)(2,1)S(1)}, bf16[72,512]{1,0:T(8,128)(2,1)S(1)}, u32[]{:S(2)}, u32[]{:S(2)}) collective-permute-start(bf16[72,512]{1,0:T(8,128)(2,1)S(1)} %get-tuple-element.35), channel_id=1, source_target_pairs={{0,4},{1,5},{2,6},{3,7},{4,0},{5,1},{6,2},{7,3},{8,12},{9,13},{10,... | collective-permute-start | bytes 221192 | tf_op jit(solution)/shard_map/ppermute | solution.py:40
  34.8 4.7 %collective-permute-start.4 = (bf16[72,512]{1,0:T(8,128)(2,1)S(1)}, bf16[72,512]{1,0:T(8,128)(2,1)S(1)}, u32[]{:S(2)}, u32[]{:S(2)}) collective-permute-start(bf16[72,512]{1,0:T(8,128)(2,1)S(1)} %get-tuple-element.32), channel_id=1, source_target_pairs={{0,2},{1,3},{2,4},{3,5},{4,6},{5,7},{6,0},{7,1},{8,10},{9,11},{10,... | collective-permute-start | bytes 221192 | tf_op jit(solution)/shard_map/ppermute | solution.py:40
  36.0 6.3 %collective-permute-start.6 = (bf16[72,512]{1,0:T(8,128)(2,1)S(1)}, bf16[72,512]{1,0:T(8,128)(2,1)S(1)}, u32[]{:S(2)}, u32[]{:S(2)}) collective-permute-start(bf16[72,512]{1,0:T(8,128)(2,1)S(1)} %get-tuple-element.32), channel_id=1, source_target_pairs={{0,6},{1,7},{2,0},{3,1},{4,2},{5,3},{6,4},{7,5},{8,14},{9,15},{10,... | collective-permute-start | bytes 221192 | tf_op jit(solution)/shard_map/ppermute | solution.py:40
  37.6 4.7 %collective-permute-start.5 = (bf16[72,512]{1,0:T(8,128)(2,1)S(1)}, bf16[72,512]{1,0:T(8,128)(2,1)S(1)}, u32[]{:S(2)}, u32[]{:S(2)}) collective-permute-start(bf16[72,512]{1,0:T(8,128)(2,1)S(1)} %get-tuple-element.32), channel_id=1, source_target_pairs={{0,4},{1,5},{2,6},{3,7},{4,0},{5,1},{6,2},{7,3},{8,12},{9,13},{10,... | collective-permute-start | bytes 221192 | tf_op jit(solution)/shard_map/ppermute | solution.py:40
  42.3 4.6 %collective-permute-start.7 = (bf16[288,512]{1,0:T(8,128)(2,1)S(1)}, bf16[288,512]{1,0:T(8,128)(2,1)S(1)}, u32[]{:S(2)}, u32[]{:S(2)}) collective-permute-start(bf16[288,512]{1,0:T(8,128)(2,1)S(1)} %bitcast.147), channel_id=1, source_target_pairs={{0,1},{1,0},{2,3},{3,2},{4,5},{5,4},{6,7},{7,6},{8,9},{9,8},{10,11... | collective-permute-start | bytes 884744 | tf_op jit(solution)/shard_map/ppermute | solution.py:40
  47.3 7.6 %collective-permute-start.8 = (f32[48,512]{1,0:T(8,128)S(1)}, f32[48,512]{1,0:T(8,128)S(1)}, u32[]{:S(2)}, u32[]{:S(2)}) collective-permute-start(f32[48,512]{1,0:T(8,128)S(1)} %get-tuple-element.36), channel_id=1, source_target_pairs={{0,32},{8,40},{16,48},{24,56},{32,64},{40,72},{48,80},{56,88},{64,... | collective-permute-start | bytes 294920 | tf_op jit(solution)/shard_map/ppermute | solution.py:40
  48.7 6.6 %collective-permute-start.10 = (f32[48,512]{1,0:T(8,128)S(1)}, f32[48,512]{1,0:T(8,128)S(1)}, u32[]{:S(2)}, u32[]{:S(2)}) collective-permute-start(f32[48,512]{1,0:T(8,128)S(1)} %get-tuple-element.37), channel_id=1, source_target_pairs={{0,96},{8,104},{16,112},{24,120},{32,0},{40,8},{48,16},{56,24},{64... | collective-permute-start | bytes 294920 | tf_op jit(solution)/shard_map/ppermute | solution.py:40
  50.0 10.2 %collective-permute-start.9 = (f32[48,512]{1,0:T(8,128)S(1)}, f32[48,512]{1,0:T(8,128)S(1)}, u32[]{:S(2)}, u32[]{:S(2)}) collective-permute-start(f32[48,512]{1,0:T(8,128)S(1)} %get-tuple-element.38), channel_id=1, source_target_pairs={{0,64},{8,72},{16,80},{24,88},{32,96},{40,104},{48,112},{56,120},{... | collective-permute-start | bytes 294920 | tf_op jit(solution)/shard_map/ppermute | solution.py:40
  60.4 8.1 %collective-permute-start.11 = (f32[12,512]{1,0:T(8,128)S(1)}, f32[12,512]{1,0:T(8,128)S(1)}, u32[]{:S(2)}, u32[]{:S(2)}) collective-permute-start(f32[12,512]{1,0:T(8,128)S(1)} %get-tuple-element.49), channel_id=1, source_target_pairs={{0,8},{8,16},{16,24},{24,0},{32,40},{40,48},{48,56},{56,32},{64,72... | collective-permute-start | bytes 73736 | tf_op jit(solution)/shard_map/ppermute | solution.py:40
  62.2 6.3 %collective-permute-start.13 = (f32[12,512]{1,0:T(8,128)S(1)}, f32[12,512]{1,0:T(8,128)S(1)}, u32[]{:S(2)}, u32[]{:S(2)}) collective-permute-start(f32[12,512]{1,0:T(8,128)S(1)} %get-tuple-element.50), channel_id=1, source_target_pairs={{0,24},{8,0},{16,8},{24,16},{32,56},{40,32},{48,40},{56,48},{64,88... | collective-permute-start | bytes 73736 | tf_op jit(solution)/shard_map/ppermute | solution.py:40
  64.5 5.3 %collective-permute-start.12 = (f32[12,512]{1,0:T(8,128)S(1)}, f32[12,512]{1,0:T(8,128)S(1)}, u32[]{:S(2)}, u32[]{:S(2)}) collective-permute-start(f32[12,512]{1,0:T(8,128)S(1)} %get-tuple-element.51), channel_id=1, source_target_pairs={{0,16},{8,24},{16,0},{24,8},{32,48},{40,56},{48,32},{56,40},{64,80... | collective-permute-start | bytes 73736 | tf_op jit(solution)/shard_map/ppermute | solution.py:40
  65.7 6.0 %collective-permute-start.14 = (f32[24,576]{1,0:T(8,128)S(1)}, f32[24,576]{1,0:T(8,128)S(1)}, u32[]{:S(2)}, u32[]{:S(2)}) collective-permute-start(f32[24,576]{1,0:T(8,128)S(1)} %get-tuple-element.42), channel_id=1, source_target_pairs={{0,32},{8,40},{16,48},{24,56},{32,64},{40,72},{48,80},{56,88},{64,... | collective-permute-start | bytes 165896 | tf_op jit(solution)/shard_map/ppermute | solution.py:40
  66.5 5.2 %collective-permute-start.16 = (f32[24,576]{1,0:T(8,128)S(1)}, f32[24,576]{1,0:T(8,128)S(1)}, u32[]{:S(2)}, u32[]{:S(2)}) collective-permute-start(f32[24,576]{1,0:T(8,128)S(1)} %get-tuple-element.43), channel_id=1, source_target_pairs={{0,96},{8,104},{16,112},{24,120},{32,0},{40,8},{48,16},{56,24},{64... | collective-permute-start | bytes 165896 | tf_op jit(solution)/shard_map/ppermute | solution.py:40
  68.4 6.4 %collective-permute-start.15 = (f32[24,576]{1,0:T(8,128)S(1)}, f32[24,576]{1,0:T(8,128)S(1)}, u32[]{:S(2)}, u32[]{:S(2)}) collective-permute-start(f32[24,576]{1,0:T(8,128)S(1)} %get-tuple-element.44), channel_id=1, source_target_pairs={{0,64},{8,72},{16,80},{24,88},{32,96},{40,104},{48,112},{56,120},{... | collective-permute-start | bytes 165896 | tf_op jit(solution)/shard_map/ppermute | solution.py:40
  74.9 4.1 %collective-permute-start.17 = (f32[12,512]{1,0:T(8,128)S(1)}, f32[12,512]{1,0:T(8,128)S(1)}, u32[]{:S(2)}, u32[]{:S(2)}) collective-permute-start(f32[12,512]{1,0:T(8,128)S(1)} %fusion.19), channel_id=1, source_target_pairs={{0,1},{1,0},{2,3},{3,2},{4,5},{5,4},{6,7},{7,6},{8,9},{9,8},{10,11... | collective-permute-start | bytes 73736 | tf_op jit(solution)/shard_map/ppermute | solution.py:40
  79.1 7.0 %collective-permute-start.20 = (f32[2,12,512]{2,1,0:T(8,128)S(1)}, f32[2,12,512]{2,1,0:T(8,128)S(1)}, u32[]{:S(2)}, u32[]{:S(2)}) collective-permute-start(f32[2,12,512]{2,1,0:T(8,128)S(1)} %bitcast_dynamic-update-slice_fusion.20), channel_id=1, source_target_pairs={{0,6},{1,7},{2,0},{3,1},{4,2},{5,3},{6,4},{7,5},{8,14},{9,15},{10,... | collective-permute-start | bytes 147464 | tf_op jit(solution)/shard_map/ppermute | solution.py:40
  79.1 6.9 %collective-permute-start.19 = (f32[2,12,512]{2,1,0:T(8,128)S(1)}, f32[2,12,512]{2,1,0:T(8,128)S(1)}, u32[]{:S(2)}, u32[]{:S(2)}) collective-permute-start(f32[2,12,512]{2,1,0:T(8,128)S(1)} %bitcast_dynamic-update-slice_fusion.20), channel_id=1, source_target_pairs={{0,4},{1,5},{2,6},{3,7},{4,0},{5,1},{6,2},{7,3},{8,12},{9,13},{10,... | collective-permute-start | bytes 147464 | tf_op jit(solution)/shard_map/ppermute | solution.py:40
  79.7 6.2 %collective-permute-start.18 = (f32[2,12,512]{2,1,0:T(8,128)S(1)}, f32[2,12,512]{2,1,0:T(8,128)S(1)}, u32[]{:S(2)}, u32[]{:S(2)}) collective-permute-start(f32[2,12,512]{2,1,0:T(8,128)S(1)} %bitcast_dynamic-update-slice_fusion.20), channel_id=1, source_target_pairs={{0,2},{1,3},{2,4},{3,5},{4,6},{5,7},{6,0},{7,1},{8,10},{9,11},{10,... | collective-permute-start | bytes 147464 | tf_op jit(solution)/shard_map/ppermute | solution.py:40
  86.0 3.1 %collective-permute-start.23 = (f32[24,576]{1,0:T(8,128)S(1)}, f32[24,576]{1,0:T(8,128)S(1)}, u32[]{:S(2)}, u32[]{:S(2)}) collective-permute-start(f32[24,576]{1,0:T(8,128)S(1)} %fusion.17), channel_id=1, source_target_pairs={{0,24},{8,0},{16,8},{24,16},{32,56},{40,32},{48,40},{56,48},{64,88... | collective-permute-start | bytes 165896 | tf_op jit(solution)/shard_map/ppermute | solution.py:40
  86.5 4.3 %collective-permute-start.22 = (f32[24,576]{1,0:T(8,128)S(1)}, f32[24,576]{1,0:T(8,128)S(1)}, u32[]{:S(2)}, u32[]{:S(2)}) collective-permute-start(f32[24,576]{1,0:T(8,128)S(1)} %fusion.17), channel_id=1, source_target_pairs={{0,8},{8,16},{16,24},{24,0},{32,40},{40,48},{48,56},{56,32},{64,72... | collective-permute-start | bytes 165896 | tf_op jit(solution)/shard_map/ppermute | solution.py:40
  87.6 5.3 %collective-permute-start.21 = (f32[24,576]{1,0:T(8,128)S(1)}, f32[24,576]{1,0:T(8,128)S(1)}, u32[]{:S(2)}, u32[]{:S(2)}) collective-permute-start(f32[24,576]{1,0:T(8,128)S(1)} %fusion.17), channel_id=1, source_target_pairs={{0,16},{8,24},{16,0},{24,8},{32,48},{40,56},{48,32},{56,40},{64,80... | collective-permute-start | bytes 165896 | tf_op jit(solution)/shard_map/ppermute | solution.py:40
  92.9 4.4 %collective-permute-start.24 = (f32[24,576]{1,0:T(8,128)S(1)}, f32[24,576]{1,0:T(8,128)S(1)}, u32[]{:S(2)}, u32[]{:S(2)}) collective-permute-start(f32[24,576]{1,0:T(8,128)S(1)} %get-tuple-element.30), channel_id=1, source_target_pairs={{0,32},{8,40},{16,48},{24,56},{32,64},{40,72},{48,80},{56,88},{64,... | collective-permute-start | bytes 165896 | tf_op jit(solution)/shard_map/ppermute | solution.py:40
  93.7 4.6 %collective-permute-start.25 = (f32[24,576]{1,0:T(8,128)S(1)}, f32[24,576]{1,0:T(8,128)S(1)}, u32[]{:S(2)}, u32[]{:S(2)}) collective-permute-start(f32[24,576]{1,0:T(8,128)S(1)} %get-tuple-element.30), channel_id=1, source_target_pairs={{0,64},{8,72},{16,80},{24,88},{32,96},{40,104},{48,112},{56,120},{... | collective-permute-start | bytes 165896 | tf_op jit(solution)/shard_map/ppermute | solution.py:40
  96.0 3.5 %collective-permute-start.26 = (f32[24,576]{1,0:T(8,128)S(1)}, f32[24,576]{1,0:T(8,128)S(1)}, u32[]{:S(2)}, u32[]{:S(2)}) collective-permute-start(f32[24,576]{1,0:T(8,128)S(1)} %get-tuple-element.30), channel_id=1, source_target_pairs={{0,96},{8,104},{16,112},{24,120},{32,0},{40,8},{48,16},{56,24},{64... | collective-permute-start | bytes 165896 | tf_op jit(solution)/shard_map/ppermute | solution.py:40
  99.5 8.3 %collective-permute-start.27 = (f32[72,576]{1,0:T(8,128)S(1)}, f32[72,576]{1,0:T(8,128)S(1)}, u32[]{:S(2)}, u32[]{:S(2)}) collective-permute-start(f32[72,576]{1,0:T(8,128)S(1)} %pad_maximum_fusion.1), channel_id=1, source_target_pairs={{0,2},{1,3},{2,4},{3,5},{4,6},{5,7},{6,0},{7,1},{8,10},{9,11},{10,... | collective-permute-start | bytes 497672 | tf_op jit(solution)/shard_map/ppermute | solution.py:40
  99.6 8.2 %collective-permute-start.28 = (f32[72,576]{1,0:T(8,128)S(1)}, f32[72,576]{1,0:T(8,128)S(1)}, u32[]{:S(2)}, u32[]{:S(2)}) collective-permute-start(f32[72,576]{1,0:T(8,128)S(1)} %pad_maximum_fusion.1), channel_id=1, source_target_pairs={{0,4},{1,5},{2,6},{3,7},{4,0},{5,1},{6,2},{7,3},{8,12},{9,13},{10,... | collective-permute-start | bytes 497672 | tf_op jit(solution)/shard_map/ppermute | solution.py:40
  100.3 7.9 %collective-permute-start.29 = (f32[72,576]{1,0:T(8,128)S(1)}, f32[72,576]{1,0:T(8,128)S(1)}, u32[]{:S(2)}, u32[]{:S(2)}) collective-permute-start(f32[72,576]{1,0:T(8,128)S(1)} %pad_maximum_fusion.1), channel_id=1, source_target_pairs={{0,6},{1,7},{2,0},{3,1},{4,2},{5,3},{6,4},{7,5},{8,14},{9,15},{10,... | collective-permute-start | bytes 497672 | tf_op jit(solution)/shard_map/ppermute | solution.py:40
  108.2 6.2 %collective-permute-start.30 = (f32[288,576]{1,0:T(8,128)S(1)}, f32[288,576]{1,0:T(8,128)S(1)}, u32[]{:S(2)}, u32[]{:S(2)}) collective-permute-start(f32[288,576]{1,0:T(8,128)S(1)} %bitcast.141), channel_id=1, source_target_pairs={{0,1},{1,0},{2,3},{3,2},{4,5},{5,4},{6,7},{7,6},{8,9},{9,8},{10,11... | collective-permute-start | bytes 1990664 | tf_op jit(solution)/shard_map/ppermute | solution.py:40
  114.5 30.1 %copy-start = (f32[32,3696]{1,0:T(8,128)S(1)}, f32[32,3696]{1,0:T(8,128)}, u32[]{:S(2)}) copy-start(f32[32,3696]{1,0:T(8,128)} %own_first_ref.1) | copy-start | bytes 1419268
  114.5 30.1 %copy-start.1 = (f32[32,3696]{1,0:T(8,128)S(1)}, f32[32,3696]{1,0:T(8,128)}, u32[]{:S(2)}) copy-start(f32[32,3696]{1,0:T(8,128)} %own_second_ref.1) | copy-start | bytes 1419268
Sparse Core Ops, SparseCore 0:
  10.8 77.2 all-gather.5
  96.5 48.0 all-gather.3

commit v12 on v11

--- a/solution.py
+++ b/solution.py
@@ -166,7 +166,7 @@
         out_specs=pl.BlockSpec(memory_space=pltpu.VMEM),
         scratch_shapes=[pltpu.VMEM((padded, padded), f32)],
         compiler_params=pltpu.CompilerParams(vmem_limit_bytes=16 << 20),
-        cost_estimate=pl.CostEstimate(flops=160 * size**3, bytes_accessed=8 * size**2, transcendentals=0),
+        cost_estimate=pl.CostEstimate(flops=12 * size**3, bytes_accessed=8 * size**2, transcendentals=0),
         name="inverse_factor",
     )(gram)
 
@@ -332,9 +332,10 @@
     mixed, gram = lax.optimization_barrier(
         (scatter_sum(mixed.reshape(4, share, RANK), "z"), scatter_sum(gram, "x"))
     )
-    mixed, gram = lax.optimization_barrier((gather(gather(mixed, "core"), "y"), gram))
+    mixed = gather(gather(mixed, "core"), "y").reshape(8 * share, RANK)
+    mixed, gram = lax.optimization_barrier((mixed, gram))
     gram = full_sum(gram, "z")
-    mixed, gathered = lax.optimization_barrier((mixed.reshape(8 * share, RANK), gathered))
+    mixed, gathered = lax.optimization_barrier((mixed, gathered))
     mixed = lax.all_gather(mixed, "row", axis=0, tiled=True)
     gram = gather(gram, "x")
     gram = jnp.concatenate([gram[0, :STEP], gram[1, :STEP], gram[2, :STEP], gram[3]], axis=0)

time: 171 us -> 167 us (0.977)
  waiting for transfers between devices: 50.9 us -> 41.8 us
  starting transfers between devices: 42.6 us -> 48.1 us
    all_gather x1, waiting for transfers between devices: 6.98 us -> 0.02 us  [local(): mixed = lax.all_gather(mixed, 'row', axis=0, tiled=True)]
    ppermute x31, starting transfers between devices: 42.5 us -> 48 us  [shift(): return lax.ppermute(value, axis, pairs)]
    ppermute x31, waiting for transfers between devices: 43.9 us -> 40.4 us  [shift(): return lax.ppermute(value, axis, pairs)]
  transfers between devices with their start and end apart: 33 -> 33, of which waited for: 23 -> 21; matrix products, arithmetic and copies ran while one was open for 11% -> 11% of each run, Pallas kernels for 14% -> 14%
where the time goes in v12:
time: 167 us
  starting transfers between devices  48.1 us (29%)
  Pallas kernels  44.5 us (27%)
  waiting for transfers between devices  41.8 us (25%)
  between operations  14.5 us (9%)
  matrix products  14.1 us (8%)
  local copies, waits for them, and re-layouts  3.99 us (2%)
    ppermute x31, starting transfers between devices, shift(): return lax.ppermute(value, axis, pairs)  48 us
    ppermute x31, waiting for transfers between devices, shift(): return lax.ppermute(value, axis, pairs)  40.4 us
    pallas_call x1, Pallas kernels, inverse_factor(): pl.pallas_call(factor_kernel, out_shape=jax.ShapeDtypeStruct((size, size)...  23.1 us
    pallas_call x1, Pallas kernels, adam_step(): pl.pallas_call(step_kernel, out_shape=(jax.ShapeDtypeStruct((width, featu...  19.4 us
    dot_general x1, matrix products, sketched_term(): jnp.dot(sketch_turned, grad_turned, preferred_element_type=f32)  11.2 us
  transfers between devices with their start and end apart: 33, of which 21 were waited for; matrix products, arithmetic and copies ran while one was open for 11% of the time, Pallas kernels for 14%

profile of v12, /device:TPU:1, one launch (start us, length us, event | category | flops | bytes accessed | tf_op | source)
XLA Modules:
  0.0 167.3 jit_solution(1270548518948174592)
XLA Ops:
  7.2 2.0 %pack.1 = bf16[64,3696]{1,0:T(8,128)(2,1)} custom-call(f32[32,3696]{1,0:T(8,128)} %own_first_ref.1, f32[32,3696]{1,0:T(8,128)} %own_second_ref.1), custom_call_target="tpu_custom_call" | custom-call | tf_op jit(solution)/shard_map/pack/pallas_call | solution.py:187
  9.3 11.2 %fusion.21 = f32[576,1536]{1,0:T(8,128)S(1)} fusion(bf16[3696,576]{0,1:T(8,128)(2,1)} %param.7, bf16[1536,3696]{0,1:T(8,128)(2,1)} %param.6), kind=kOutput, calls=%fused_computation.73 | convolution fusion | flops 6539968512 | bytes 19150848 | tf_op jit(solution)/shard_map/dot_general | solution.py:195
  20.5 1.1 fusion.1
  21.7 1.1 fusion.4
  22.8 1.5 collective-permute-start
  24.3 1.5 reshape.51
  25.8 1.0 constant_dynamic-slice_fusion
  27.0 1.4 collective-permute-start.1
  28.5 1.5 collective-permute-start.3
  30.0 1.6 collective-permute-start.2
  31.6 0.9 collective-permute-done.1
  32.4 2.3 %collective-permute-done.2 = bf16[72,512]{1,0:T(8,128)(2,1)S(1)} collective-permute-done((bf16[72,512]{1,0:T(8,128)(2,1)S(1)}, bf16[72,512]{1,0:T(8,128)(2,1)S(1)}, u32[]{:S(2)}, u32[]{:S(2)}) %collective-permute-start.2) | collective-permute-done | bytes 73760 | tf_op jit(solution)/shard_map/ppermute | solution.py:40
  34.8 1.2 collective-permute-start.4
  36.0 1.6 collective-permute-start.6
  37.9 1.6 collective-permute-done.4
  39.6 2.7 %collective-permute-done.5 = bf16[72,512]{1,0:T(8,128)(2,1)S(1)} collective-permute-done((bf16[72,512]{1,0:T(8,128)(2,1)S(1)}, bf16[72,512]{1,0:T(8,128)(2,1)S(1)}, u32[]{:S(2)}, u32[]{:S(2)}) %collective-permute-start.5) | collective-permute-done | bytes 73760 | tf_op jit(solution)/shard_map/ppermute | solution.py:40
  42.3 3.4 %collective-permute-start.7 = (bf16[288,512]{1,0:T(8,128)(2,1)S(1)}, bf16[288,512]{1,0:T(8,128)(2,1)S(1)}, u32[]{:S(2)}, u32[]{:S(2)}) collective-permute-start(bf16[288,512]{1,0:T(8,128)(2,1)S(1)} %bitcast.147), channel_id=1, source_target_pairs={{0,1},{1,0},{2,3},{3,2},{4,5},{5,4},{6,7},{7,6},{8,9},{9,8},{10,11... | collective-permute-start | bytes 884744 | tf_op jit(solution)/shard_map/ppermute | solution.py:40
  45.8 1.1 collective-permute-done.7
  47.3 1.4 collective-permute-start.8
  48.7 1.4 collective-permute-start.10
  50.0 1.6 collective-permute-start.9
  52.0 2.9 %collective-permute-done.8 = f32[48,512]{1,0:T(8,128)S(1)} collective-permute-done((f32[48,512]{1,0:T(8,128)S(1)}, f32[48,512]{1,0:T(8,128)S(1)}, u32[]{:S(2)}, u32[]{:S(2)}) %collective-permute-start.8) | collective-permute-done | bytes 98336 | tf_op jit(solution)/shard_map/ppermute | solution.py:40
  55.3 5.0 %collective-permute-done.9 = f32[48,512]{1,0:T(8,128)S(1)} collective-permute-done((f32[48,512]{1,0:T(8,128)S(1)}, f32[48,512]{1,0:T(8,128)S(1)}, u32[]{:S(2)}, u32[]{:S(2)}) %collective-permute-start.9) | collective-permute-done | bytes 98336 | tf_op jit(solution)/shard_map/ppermute | solution.py:40
  60.4 1.8 %collective-permute-start.11 = (f32[12,512]{1,0:T(8,128)S(1)}, f32[12,512]{1,0:T(8,128)S(1)}, u32[]{:S(2)}, u32[]{:S(2)}) collective-permute-start(f32[12,512]{1,0:T(8,128)S(1)} %get-tuple-element.49), channel_id=1, source_target_pairs={{0,8},{8,16},{16,24},{24,0},{32,40},{40,48},{48,56},{56,32},{64,72... | collective-permute-start | bytes 73736 | tf_op jit(solution)/shard_map/ppermute | solution.py:40
  62.2 2.3 %collective-permute-start.13 = (f32[12,512]{1,0:T(8,128)S(1)}, f32[12,512]{1,0:T(8,128)S(1)}, u32[]{:S(2)}, u32[]{:S(2)}) collective-permute-start(f32[12,512]{1,0:T(8,128)S(1)} %get-tuple-element.50), channel_id=1, source_target_pairs={{0,24},{8,0},{16,8},{24,16},{32,56},{40,32},{48,40},{56,48},{64,88... | collective-permute-start | bytes 73736 | tf_op jit(solution)/shard_map/ppermute | solution.py:40
  64.5 1.2 collective-permute-start.12
  66.5 1.9 %collective-permute-start.16 = (f32[24,576]{1,0:T(8,128)S(1)}, f32[24,576]{1,0:T(8,128)S(1)}, u32[]{:S(2)}, u32[]{:S(2)}) collective-permute-start(f32[24,576]{1,0:T(8,128)S(1)} %get-tuple-element.43), channel_id=1, source_target_pairs={{0,96},{8,104},{16,112},{24,120},{32,0},{40,8},{48,16},{56,24},{64... | collective-permute-start | bytes 165896 | tf_op jit(solution)/shard_map/ppermute | solution.py:40
  68.5 1.3 collective-permute-done.12
  69.7 2.0 %collective-permute-done.14 = f32[24,576]{1,0:T(8,128)S(1)} collective-permute-done((f32[24,576]{1,0:T(8,128)S(1)}, f32[24,576]{1,0:T(8,128)S(1)}, u32[]{:S(2)}, u32[]{:S(2)}) %collective-permute-start.14) | collective-permute-done | bytes 55328 | tf_op jit(solution)/shard_map/ppermute | solution.py:40
  71.7 3.1 %collective-permute-done.15 = f32[24,576]{1,0:T(8,128)S(1)} collective-permute-done((f32[24,576]{1,0:T(8,128)S(1)}, f32[24,576]{1,0:T(8,128)S(1)}, u32[]{:S(2)}, u32[]{:S(2)}) %collective-permute-start.15) | collective-permute-done | bytes 55328 | tf_op jit(solution)/shard_map/ppermute | solution.py:40
  74.9 3.3 %collective-permute-start.17 = (f32[12,512]{1,0:T(8,128)S(1)}, f32[12,512]{1,0:T(8,128)S(1)}, u32[]{:S(2)}, u32[]{:S(2)}) collective-permute-start(f32[12,512]{1,0:T(8,128)S(1)} %fusion.19), channel_id=1, source_target_pairs={{0,1},{1,0},{2,3},{3,2},{4,5},{5,4},{6,7},{7,6},{8,9},{9,8},{10,11... | collective-permute-start | bytes 73736 | tf_op jit(solution)/shard_map/ppermute | solution.py:40
  78.2 0.8 collective-permute-done.17
  80.6 5.4 %collective-permute-done.18 = f32[2,12,512]{2,1,0:T(8,128)S(1)} collective-permute-done((f32[2,12,512]{2,1,0:T(8,128)S(1)}, f32[2,12,512]{2,1,0:T(8,128)S(1)}, u32[]{:S(2)}, u32[]{:S(2)}) %collective-permute-start.18) | collective-permute-done | bytes 49184 | tf_op jit(solution)/shard_map/ppermute | solution.py:40
  86.7 1.3 all-gather.6.cloned.1.call-done
  88.1 2.6 %collective-permute-start.23 = (f32[24,576]{1,0:T(8,128)S(1)}, f32[24,576]{1,0:T(8,128)S(1)}, u32[]{:S(2)}, u32[]{:S(2)}) collective-permute-start(f32[24,576]{1,0:T(8,128)S(1)} %fusion.17), channel_id=1, source_target_pairs={{0,24},{8,0},{16,8},{24,16},{32,56},{40,32},{48,40},{56,48},{64,88... | collective-permute-start | bytes 165896 | tf_op jit(solution)/shard_map/ppermute | solution.py:40
  90.8 1.8 %collective-permute-start.21 = (f32[24,576]{1,0:T(8,128)S(1)}, f32[24,576]{1,0:T(8,128)S(1)}, u32[]{:S(2)}, u32[]{:S(2)}) collective-permute-start(f32[24,576]{1,0:T(8,128)S(1)} %fusion.17), channel_id=1, source_target_pairs={{0,16},{8,24},{16,0},{24,8},{32,48},{40,56},{48,32},{56,40},{64,80... | collective-permute-start | bytes 165896 | tf_op jit(solution)/shard_map/ppermute | solution.py:40
  92.5 3.1 %collective-permute-done.22 = f32[24,576]{1,0:T(8,128)S(1)} collective-permute-done((f32[24,576]{1,0:T(8,128)S(1)}, f32[24,576]{1,0:T(8,128)S(1)}, u32[]{:S(2)}, u32[]{:S(2)}) %collective-permute-start.22) | collective-permute-done | bytes 55328 | tf_op jit(solution)/shard_map/ppermute | solution.py:40
  96.0 1.8 %collective-permute-start.25 = (f32[24,576]{1,0:T(8,128)S(1)}, f32[24,576]{1,0:T(8,128)S(1)}, u32[]{:S(2)}, u32[]{:S(2)}) collective-permute-start(f32[24,576]{1,0:T(8,128)S(1)} %get-tuple-element.30), channel_id=1, source_target_pairs={{0,64},{8,72},{16,80},{24,88},{32,96},{40,104},{48,112},{56,120},{... | collective-permute-start | bytes 165896 | tf_op jit(solution)/shard_map/ppermute | solution.py:40
  97.8 1.4 collective-permute-start.26
  99.2 1.6 collective-permute-done.24
  101.5 1.9 %collective-permute-start.27 = (f32[72,576]{1,0:T(8,128)S(1)}, f32[72,576]{1,0:T(8,128)S(1)}, u32[]{:S(2)}, u32[]{:S(2)}) collective-permute-start(f32[72,576]{1,0:T(8,128)S(1)} %pad_maximum_fusion.1), channel_id=1, source_target_pairs={{0,2},{1,3},{2,4},{3,5},{4,6},{5,7},{6,0},{7,1},{8,10},{9,11},{10,... | collective-permute-start | bytes 497672 | tf_op jit(solution)/shard_map/ppermute | solution.py:40
  103.3 2.3 %collective-permute-start.28 = (f32[72,576]{1,0:T(8,128)S(1)}, f32[72,576]{1,0:T(8,128)S(1)}, u32[]{:S(2)}, u32[]{:S(2)}) collective-permute-start(f32[72,576]{1,0:T(8,128)S(1)} %pad_maximum_fusion.1), channel_id=1, source_target_pairs={{0,4},{1,5},{2,6},{3,7},{4,0},{5,1},{6,2},{7,3},{8,12},{9,13},{10,... | collective-permute-start | bytes 497672 | tf_op jit(solution)/shard_map/ppermute | solution.py:40
  105.6 1.1 collective-permute-start.29
  107.4 3.2 %collective-permute-done.28 = f32[72,576]{1,0:T(8,128)S(1)} collective-permute-done((f32[72,576]{1,0:T(8,128)S(1)}, f32[72,576]{1,0:T(8,128)S(1)}, u32[]{:S(2)}, u32[]{:S(2)}) %collective-permute-start.28) | collective-permute-done | bytes 165920 | tf_op jit(solution)/shard_map/ppermute | solution.py:40
  110.6 5.3 %collective-permute-start.30 = (f32[288,576]{1,0:T(8,128)S(1)}, f32[288,576]{1,0:T(8,128)S(1)}, u32[]{:S(2)}, u32[]{:S(2)}) collective-permute-start(f32[288,576]{1,0:T(8,128)S(1)} %bitcast.141), channel_id=1, source_target_pairs={{0,1},{1,0},{2,3},{3,2},{4,5},{5,4},{6,7},{7,6},{8,9},{9,8},{10,11... | collective-permute-start | bytes 1990664 | tf_op jit(solution)/shard_map/ppermute | solution.py:40
  116.1 1.7 %collective-permute-done.30 = f32[288,576]{1,0:T(8,128)S(1)} collective-permute-done((f32[288,576]{1,0:T(8,128)S(1)}, f32[288,576]{1,0:T(8,128)S(1)}, u32[]{:S(2)}, u32[]{:S(2)}) %collective-permute-start.30) | collective-permute-done | bytes 663584 | tf_op jit(solution)/shard_map/ppermute | solution.py:40
  117.9 23.1 %inverse_factor.1.inverse_ref = f32[576,576]{1,0:T(8,128)S(1)} custom-call(f32[576,576]{1,0:T(8,128)S(1)} %bitcast.138), custom_call_target="tpu_custom_call" | custom-call | flops 2293235712 | bytes 2654208 | tf_op jit(solution)/shard_map/inverse_factor/pallas_call | solution.py:162
  141.0 19.4 %adam_step.1 = (f32[3696,512]{1,0:T(8,128)}, f32[32,3696]{1,0:T(8,128)}, f32[32,3696]{1,0:T(8,128)}) custom-call(s32[1]{0:T(128)} %bitcast.at_ref, f32[576,576]{1,0:T(8,128)S(1)} %inverse_factor.1.inverse_ref, bf16[576,512]{1,0:T(8,128)(2,1)S(1)} %bitcast.137, f32[1536,512]{1,0:T(8,128)} %all-gather.4.cloned.1.call-done.mixed_ref, ...), custom_call_target="tpu_custom_call" | custom-call | flops 10166992896 | bytes 31531008 | tf_op jit(solution)/shard_map/adam_step/pallas_call | solution.py:278
  (82 shorter events, 7.1 us)
Async XLA Ops:
  7.2 80.9 %all-gather.6.cloned.1.call-start = ((), (), s32[]{:S(2)}) async-start(), calls=%async_computation.1 | async-start | bytes 8077312 | tf_op jit(solution)/shard_map/all_gather | solution.py:315
  9.2 131.7 %all-gather.4.cloned.1.call-start = ((), (), s32[]{:S(2)}) async-start(), calls=%async_computation | async-start | bytes 3342336 | tf_op jit(solution)/shard_map/all_gather | solution.py:339
  9.3 11.2 %copy-start.2 = (bf16[1536,512]{1,0:T(8,128)(2,1)S(1)}, bf16[1536,512]{1,0:T(8,128)(2,1)}, u32[]{:S(2)}) copy-start(bf16[1536,512]{1,0:T(8,128)(2,1)} %param.5) | copy-start | bytes 4718596
  22.8 4.0 %collective-permute-start = (bf16[288,512]{1,0:T(8,128)(2,1)S(1)}, bf16[288,512]{1,0:T(8,128)(2,1)S(1)}, u32[]{:S(2)}, u32[]{:S(2)}) collective-permute-start(bf16[288,512]{1,0:T(8,128)(2,1)S(1)} %fusion.7), channel_id=1, source_target_pairs={{0,1},{1,0},{2,3},{3,2},{4,5},{5,4},{6,7},{7,6},{8,9},{9,8},{10,11... | collective-permute-start | bytes 884744 | tf_op jit(solution)/shard_map/ppermute | solution.py:40
  27.0 5.4 %collective-permute-start.1 = (bf16[72,512]{1,0:T(8,128)(2,1)S(1)}, bf16[72,512]{1,0:T(8,128)(2,1)S(1)}, u32[]{:S(2)}, u32[]{:S(2)}) collective-permute-start(bf16[72,512]{1,0:T(8,128)(2,1)S(1)} %get-tuple-element.33), channel_id=1, source_target_pairs={{0,2},{1,3},{2,4},{3,5},{4,6},{5,7},{6,0},{7,1},{8,10},{9,11},{10,... | collective-permute-start | bytes 221192 | tf_op jit(solution)/shard_map/ppermute | solution.py:40
  28.5 4.0 %collective-permute-start.3 = (bf16[72,512]{1,0:T(8,128)(2,1)S(1)}, bf16[72,512]{1,0:T(8,128)(2,1)S(1)}, u32[]{:S(2)}, u32[]{:S(2)}) collective-permute-start(bf16[72,512]{1,0:T(8,128)(2,1)S(1)} %get-tuple-element.34), channel_id=1, source_target_pairs={{0,6},{1,7},{2,0},{3,1},{4,2},{5,3},{6,4},{7,5},{8,14},{9,15},{10,... | collective-permute-start | bytes 221192 | tf_op jit(solution)/shard_map/ppermute | solution.py:40
  30.0 4.8 %collective-permute-start.2 = (bf16[72,512]{1,0:T(8,128)(2,1)S(1)}, bf16[72,512]{1,0:T(8,128)(2,1)S(1)}, u32[]{:S(2)}, u32[]{:S(2)}) collective-permute-start(bf16[72,512]{1,0:T(8,128)(2,1)S(1)} %get-tuple-element.35), channel_id=1, source_target_pairs={{0,4},{1,5},{2,6},{3,7},{4,0},{5,1},{6,2},{7,3},{8,12},{9,13},{10,... | collective-permute-start | bytes 221192 | tf_op jit(solution)/shard_map/ppermute | solution.py:40
  34.8 4.7 %collective-permute-start.4 = (bf16[72,512]{1,0:T(8,128)(2,1)S(1)}, bf16[72,512]{1,0:T(8,128)(2,1)S(1)}, u32[]{:S(2)}, u32[]{:S(2)}) collective-permute-start(bf16[72,512]{1,0:T(8,128)(2,1)S(1)} %get-tuple-element.32), channel_id=1, source_target_pairs={{0,2},{1,3},{2,4},{3,5},{4,6},{5,7},{6,0},{7,1},{8,10},{9,11},{10,... | collective-permute-start | bytes 221192 | tf_op jit(solution)/shard_map/ppermute | solution.py:40
  36.0 6.3 %collective-permute-start.6 = (bf16[72,512]{1,0:T(8,128)(2,1)S(1)}, bf16[72,512]{1,0:T(8,128)(2,1)S(1)}, u32[]{:S(2)}, u32[]{:S(2)}) collective-permute-start(bf16[72,512]{1,0:T(8,128)(2,1)S(1)} %get-tuple-element.32), channel_id=1, source_target_pairs={{0,6},{1,7},{2,0},{3,1},{4,2},{5,3},{6,4},{7,5},{8,14},{9,15},{10,... | collective-permute-start | bytes 221192 | tf_op jit(solution)/shard_map/ppermute | solution.py:40
  37.6 4.7 %collective-permute-start.5 = (bf16[72,512]{1,0:T(8,128)(2,1)S(1)}, bf16[72,512]{1,0:T(8,128)(2,1)S(1)}, u32[]{:S(2)}, u32[]{:S(2)}) collective-permute-start(bf16[72,512]{1,0:T(8,128)(2,1)S(1)} %get-tuple-element.32), channel_id=1, source_target_pairs={{0,4},{1,5},{2,6},{3,7},{4,0},{5,1},{6,2},{7,3},{8,12},{9,13},{10,... | collective-permute-start | bytes 221192 | tf_op jit(solution)/shard_map/ppermute | solution.py:40
  42.3 4.6 %collective-permute-start.7 = (bf16[288,512]{1,0:T(8,128)(2,1)S(1)}, bf16[288,512]{1,0:T(8,128)(2,1)S(1)}, u32[]{:S(2)}, u32[]{:S(2)}) collective-permute-start(bf16[288,512]{1,0:T(8,128)(2,1)S(1)} %bitcast.147), channel_id=1, source_target_pairs={{0,1},{1,0},{2,3},{3,2},{4,5},{5,4},{6,7},{7,6},{8,9},{9,8},{10,11... | collective-permute-start | bytes 884744 | tf_op jit(solution)/shard_map/ppermute | solution.py:40
  47.3 7.6 %collective-permute-start.8 = (f32[48,512]{1,0:T(8,128)S(1)}, f32[48,512]{1,0:T(8,128)S(1)}, u32[]{:S(2)}, u32[]{:S(2)}) collective-permute-start(f32[48,512]{1,0:T(8,128)S(1)} %get-tuple-element.36), channel_id=1, source_target_pairs={{0,32},{8,40},{16,48},{24,56},{32,64},{40,72},{48,80},{56,88},{64,... | collective-permute-start | bytes 294920 | tf_op jit(solution)/shard_map/ppermute | solution.py:40
  48.7 6.6 %collective-permute-start.10 = (f32[48,512]{1,0:T(8,128)S(1)}, f32[48,512]{1,0:T(8,128)S(1)}, u32[]{:S(2)}, u32[]{:S(2)}) collective-permute-start(f32[48,512]{1,0:T(8,128)S(1)} %get-tuple-element.37), channel_id=1, source_target_pairs={{0,96},{8,104},{16,112},{24,120},{32,0},{40,8},{48,16},{56,24},{64... | collective-permute-start | bytes 294920 | tf_op jit(solution)/shard_map/ppermute | solution.py:40
  50.0 10.2 %collective-permute-start.9 = (f32[48,512]{1,0:T(8,128)S(1)}, f32[48,512]{1,0:T(8,128)S(1)}, u32[]{:S(2)}, u32[]{:S(2)}) collective-permute-start(f32[48,512]{1,0:T(8,128)S(1)} %get-tuple-element.38), channel_id=1, source_target_pairs={{0,64},{8,72},{16,80},{24,88},{32,96},{40,104},{48,112},{56,120},{... | collective-permute-start | bytes 294920 | tf_op jit(solution)/shard_map/ppermute | solution.py:40
  60.4 8.1 %collective-permute-start.11 = (f32[12,512]{1,0:T(8,128)S(1)}, f32[12,512]{1,0:T(8,128)S(1)}, u32[]{:S(2)}, u32[]{:S(2)}) collective-permute-start(f32[12,512]{1,0:T(8,128)S(1)} %get-tuple-element.49), channel_id=1, source_target_pairs={{0,8},{8,16},{16,24},{24,0},{32,40},{40,48},{48,56},{56,32},{64,72... | collective-permute-start | bytes 73736 | tf_op jit(solution)/shard_map/ppermute | solution.py:40
  62.2 6.3 %collective-permute-start.13 = (f32[12,512]{1,0:T(8,128)S(1)}, f32[12,512]{1,0:T(8,128)S(1)}, u32[]{:S(2)}, u32[]{:S(2)}) collective-permute-start(f32[12,512]{1,0:T(8,128)S(1)} %get-tuple-element.50), channel_id=1, source_target_pairs={{0,24},{8,0},{16,8},{24,16},{32,56},{40,32},{48,40},{56,48},{64,88... | collective-permute-start | bytes 73736 | tf_op jit(solution)/shard_map/ppermute | solution.py:40
  64.5 5.3 %collective-permute-start.12 = (f32[12,512]{1,0:T(8,128)S(1)}, f32[12,512]{1,0:T(8,128)S(1)}, u32[]{:S(2)}, u32[]{:S(2)}) collective-permute-start(f32[12,512]{1,0:T(8,128)S(1)} %get-tuple-element.51), channel_id=1, source_target_pairs={{0,16},{8,24},{16,0},{24,8},{32,48},{40,56},{48,32},{56,40},{64,80... | collective-permute-start | bytes 73736 | tf_op jit(solution)/shard_map/ppermute | solution.py:40
  65.7 6.0 %collective-permute-start.14 = (f32[24,576]{1,0:T(8,128)S(1)}, f32[24,576]{1,0:T(8,128)S(1)}, u32[]{:S(2)}, u32[]{:S(2)}) collective-permute-start(f32[24,576]{1,0:T(8,128)S(1)} %get-tuple-element.42), channel_id=1, source_target_pairs={{0,32},{8,40},{16,48},{24,56},{32,64},{40,72},{48,80},{56,88},{64,... | collective-permute-start | bytes 165896 | tf_op jit(solution)/shard_map/ppermute | solution.py:40
  66.5 5.2 %collective-permute-start.16 = (f32[24,576]{1,0:T(8,128)S(1)}, f32[24,576]{1,0:T(8,128)S(1)}, u32[]{:S(2)}, u32[]{:S(2)}) collective-permute-start(f32[24,576]{1,0:T(8,128)S(1)} %get-tuple-element.43), channel_id=1, source_target_pairs={{0,96},{8,104},{16,112},{24,120},{32,0},{40,8},{48,16},{56,24},{64... | collective-permute-start | bytes 165896 | tf_op jit(solution)/shard_map/ppermute | solution.py:40
  68.4 6.4 %collective-permute-start.15 = (f32[24,576]{1,0:T(8,128)S(1)}, f32[24,576]{1,0:T(8,128)S(1)}, u32[]{:S(2)}, u32[]{:S(2)}) collective-permute-start(f32[24,576]{1,0:T(8,128)S(1)} %get-tuple-element.44), channel_id=1, source_target_pairs={{0,64},{8,72},{16,80},{24,88},{32,96},{40,104},{48,112},{56,120},{... | collective-permute-start | bytes 165896 | tf_op jit(solution)/shard_map/ppermute | solution.py:40
  74.9 4.1 %collective-permute-start.17 = (f32[12,512]{1,0:T(8,128)S(1)}, f32[12,512]{1,0:T(8,128)S(1)}, u32[]{:S(2)}, u32[]{:S(2)}) collective-permute-start(f32[12,512]{1,0:T(8,128)S(1)} %fusion.19), channel_id=1, source_target_pairs={{0,1},{1,0},{2,3},{3,2},{4,5},{5,4},{6,7},{7,6},{8,9},{9,8},{10,11... | collective-permute-start | bytes 73736 | tf_op jit(solution)/shard_map/ppermute | solution.py:40
  79.1 7.0 %collective-permute-start.20 = (f32[2,12,512]{2,1,0:T(8,128)S(1)}, f32[2,12,512]{2,1,0:T(8,128)S(1)}, u32[]{:S(2)}, u32[]{:S(2)}) collective-permute-start(f32[2,12,512]{2,1,0:T(8,128)S(1)} %bitcast_dynamic-update-slice_fusion.20), channel_id=1, source_target_pairs={{0,6},{1,7},{2,0},{3,1},{4,2},{5,3},{6,4},{7,5},{8,14},{9,15},{10,... | collective-permute-start | bytes 147464 | tf_op jit(solution)/shard_map/ppermute | solution.py:40
  79.1 6.9 %collective-permute-start.19 = (f32[2,12,512]{2,1,0:T(8,128)S(1)}, f32[2,12,512]{2,1,0:T(8,128)S(1)}, u32[]{:S(2)}, u32[]{:S(2)}) collective-permute-start(f32[2,12,512]{2,1,0:T(8,128)S(1)} %bitcast_dynamic-update-slice_fusion.20), channel_id=1, source_target_pairs={{0,4},{1,5},{2,6},{3,7},{4,0},{5,1},{6,2},{7,3},{8,12},{9,13},{10,... | collective-permute-start | bytes 147464 | tf_op jit(solution)/shard_map/ppermute | solution.py:40
  79.7 6.2 %collective-permute-start.18 = (f32[2,12,512]{2,1,0:T(8,128)S(1)}, f32[2,12,512]{2,1,0:T(8,128)S(1)}, u32[]{:S(2)}, u32[]{:S(2)}) collective-permute-start(f32[2,12,512]{2,1,0:T(8,128)S(1)} %bitcast_dynamic-update-slice_fusion.20), channel_id=1, source_target_pairs={{0,2},{1,3},{2,4},{3,5},{4,6},{5,7},{6,0},{7,1},{8,10},{9,11},{10,... | collective-permute-start | bytes 147464 | tf_op jit(solution)/shard_map/ppermute | solution.py:40
  88.1 4.4 %collective-permute-start.23 = (f32[24,576]{1,0:T(8,128)S(1)}, f32[24,576]{1,0:T(8,128)S(1)}, u32[]{:S(2)}, u32[]{:S(2)}) collective-permute-start(f32[24,576]{1,0:T(8,128)S(1)} %fusion.17), channel_id=1, source_target_pairs={{0,24},{8,0},{16,8},{24,16},{32,56},{40,32},{48,40},{56,48},{64,88... | collective-permute-start | bytes 165896 | tf_op jit(solution)/shard_map/ppermute | solution.py:40
  90.8 4.9 %collective-permute-start.22 = (f32[24,576]{1,0:T(8,128)S(1)}, f32[24,576]{1,0:T(8,128)S(1)}, u32[]{:S(2)}, u32[]{:S(2)}) collective-permute-start(f32[24,576]{1,0:T(8,128)S(1)} %fusion.17), channel_id=1, source_target_pairs={{0,8},{8,16},{16,24},{24,0},{32,40},{40,48},{48,56},{56,32},{64,72... | collective-permute-start | bytes 165896 | tf_op jit(solution)/shard_map/ppermute | solution.py:40
  90.8 5.0 %collective-permute-start.21 = (f32[24,576]{1,0:T(8,128)S(1)}, f32[24,576]{1,0:T(8,128)S(1)}, u32[]{:S(2)}, u32[]{:S(2)}) collective-permute-start(f32[24,576]{1,0:T(8,128)S(1)} %fusion.17), channel_id=1, source_target_pairs={{0,16},{8,24},{16,0},{24,8},{32,48},{40,56},{48,32},{56,40},{64,80... | collective-permute-start | bytes 165896 | tf_op jit(solution)/shard_map/ppermute | solution.py:40
  95.8 5.0 %collective-permute-start.24 = (f32[24,576]{1,0:T(8,128)S(1)}, f32[24,576]{1,0:T(8,128)S(1)}, u32[]{:S(2)}, u32[]{:S(2)}) collective-permute-start(f32[24,576]{1,0:T(8,128)S(1)} %get-tuple-element.30), channel_id=1, source_target_pairs={{0,32},{8,40},{16,48},{24,56},{32,64},{40,72},{48,80},{56,88},{64,... | collective-permute-start | bytes 165896 | tf_op jit(solution)/shard_map/ppermute | solution.py:40
  96.0 4.8 %collective-permute-start.25 = (f32[24,576]{1,0:T(8,128)S(1)}, f32[24,576]{1,0:T(8,128)S(1)}, u32[]{:S(2)}, u32[]{:S(2)}) collective-permute-start(f32[24,576]{1,0:T(8,128)S(1)} %get-tuple-element.30), channel_id=1, source_target_pairs={{0,64},{8,72},{16,80},{24,88},{32,96},{40,104},{48,112},{56,120},{... | collective-permute-start | bytes 165896 | tf_op jit(solution)/shard_map/ppermute | solution.py:40
  97.8 3.6 %collective-permute-start.26 = (f32[24,576]{1,0:T(8,128)S(1)}, f32[24,576]{1,0:T(8,128)S(1)}, u32[]{:S(2)}, u32[]{:S(2)}) collective-permute-start(f32[24,576]{1,0:T(8,128)S(1)} %get-tuple-element.30), channel_id=1, source_target_pairs={{0,96},{8,104},{16,112},{24,120},{32,0},{40,8},{48,16},{56,24},{64... | collective-permute-start | bytes 165896 | tf_op jit(solution)/shard_map/ppermute | solution.py:40
  101.5 5.9 %collective-permute-start.27 = (f32[72,576]{1,0:T(8,128)S(1)}, f32[72,576]{1,0:T(8,128)S(1)}, u32[]{:S(2)}, u32[]{:S(2)}) collective-permute-start(f32[72,576]{1,0:T(8,128)S(1)} %pad_maximum_fusion.1), channel_id=1, source_target_pairs={{0,2},{1,3},{2,4},{3,5},{4,6},{5,7},{6,0},{7,1},{8,10},{9,11},{10,... | collective-permute-start | bytes 497672 | tf_op jit(solution)/shard_map/ppermute | solution.py:40
  103.3 7.2 %collective-permute-start.28 = (f32[72,576]{1,0:T(8,128)S(1)}, f32[72,576]{1,0:T(8,128)S(1)}, u32[]{:S(2)}, u32[]{:S(2)}) collective-permute-start(f32[72,576]{1,0:T(8,128)S(1)} %pad_maximum_fusion.1), channel_id=1, source_target_pairs={{0,4},{1,5},{2,6},{3,7},{4,0},{5,1},{6,2},{7,3},{8,12},{9,13},{10,... | collective-permute-start | bytes 497672 | tf_op jit(solution)/shard_map/ppermute | solution.py:40
  105.6 5.0 %collective-permute-start.29 = (f32[72,576]{1,0:T(8,128)S(1)}, f32[72,576]{1,0:T(8,128)S(1)}, u32[]{:S(2)}, u32[]{:S(2)}) collective-permute-start(f32[72,576]{1,0:T(8,128)S(1)} %pad_maximum_fusion.1), channel_id=1, source_target_pairs={{0,6},{1,7},{2,0},{3,1},{4,2},{5,3},{6,4},{7,5},{8,14},{9,15},{10,... | collective-permute-start | bytes 497672 | tf_op jit(solution)/shard_map/ppermute | solution.py:40
  110.6 7.2 %collective-permute-start.30 = (f32[288,576]{1,0:T(8,128)S(1)}, f32[288,576]{1,0:T(8,128)S(1)}, u32[]{:S(2)}, u32[]{:S(2)}) collective-permute-start(f32[288,576]{1,0:T(8,128)S(1)} %bitcast.141), channel_id=1, source_target_pairs={{0,1},{1,0},{2,3},{3,2},{4,5},{5,4},{6,7},{7,6},{8,9},{9,8},{10,11... | collective-permute-start | bytes 1990664 | tf_op jit(solution)/shard_map/ppermute | solution.py:40
  117.8 23.1 %copy-start = (f32[32,3696]{1,0:T(8,128)S(1)}, f32[32,3696]{1,0:T(8,128)}, u32[]{:S(2)}) copy-start(f32[32,3696]{1,0:T(8,128)} %own_first_ref.1) | copy-start | bytes 1419268
  117.8 23.1 %copy-start.1 = (f32[32,3696]{1,0:T(8,128)S(1)}, f32[32,3696]{1,0:T(8,128)}, u32[]{:S(2)}) copy-start(f32[32,3696]{1,0:T(8,128)} %own_second_ref.1) | copy-start | bytes 1419268
Sparse Core Ops, SparseCore 0:
  10.8 77.2 all-gather.5
  90.8 47.5 all-gather.3

commit v13 on v12

--- a/solution.py
+++ b/solution.py
@@ -328,11 +328,9 @@
     mixed = scatter_sum(times(own_tokens, sketched[:RANK]).reshape(4, 4 * share, RANK), "x")
     gram = times(owned_rows, sketched)
     gram = jnp.stack([gram[k * STEP : k * STEP + PART] for k in range(4)])
+    mixed = gather(scatter_sum(mixed.reshape(4, share, RANK), "z"), "core")
     mixed, gram = lax.optimization_barrier((mixed, gram))
-    mixed, gram = lax.optimization_barrier(
-        (scatter_sum(mixed.reshape(4, share, RANK), "z"), scatter_sum(gram, "x"))
-    )
-    mixed = gather(gather(mixed, "core"), "y").reshape(8 * share, RANK)
+    mixed, gram = gather(mixed, "y").reshape(8 * share, RANK), scatter_sum(gram, "x")
     mixed, gram = lax.optimization_barrier((mixed, gram))
     gram = full_sum(gram, "z")
     mixed, gathered = lax.optimization_barrier((mixed, gathered))

time: 167 us -> 167 us (level)
  no operation moved by 1% of the time
where the time goes in v13:
time: 167 us
  starting transfers between devices  47.7 us (29%)
  Pallas kernels  44.5 us (27%)
  waiting for transfers between devices  42.2 us (25%)
  between operations  14.5 us (9%)
  matrix products  14.1 us (8%)
  local copies, waits for them, and re-layouts  3.99 us (2%)
    ppermute x31, starting transfers between devices, shift(): return lax.ppermute(value, axis, pairs)  47.6 us
    ppermute x31, waiting for transfers between devices, shift(): return lax.ppermute(value, axis, pairs)  40.4 us
    pallas_call x1, Pallas kernels, inverse_factor(): pl.pallas_call(factor_kernel, out_shape=jax.ShapeDtypeStruct((size, size)...  23.1 us
    pallas_call x1, Pallas kernels, adam_step(): pl.pallas_call(step_kernel, out_shape=(jax.ShapeDtypeStruct((width, featu...  19.4 us
    dot_general x1, matrix products, sketched_term(): jnp.dot(sketch_turned, grad_turned, preferred_element_type=f32)  11.2 us
  transfers between devices with their start and end apart: 33, of which 21 were waited for; matrix products, arithmetic and copies ran while one was open for 11% of the time, Pallas kernels for 14%

profile of v13, /device:TPU:1, one launch (start us, length us, event | category | flops | bytes accessed | tf_op | source)
XLA Modules:
  0.0 167.3 jit_solution(2309658951228692949)
XLA Ops:
  7.2 2.0 %pack.1 = bf16[64,3696]{1,0:T(8,128)(2,1)} custom-call(f32[32,3696]{1,0:T(8,128)} %own_first_ref.1, f32[32,3696]{1,0:T(8,128)} %own_second_ref.1), custom_call_target="tpu_custom_call" | custom-call | tf_op jit(solution)/shard_map/pack/pallas_call | solution.py:187
  9.3 11.2 %fusion.22 = f32[576,1536]{1,0:T(8,128)S(1)} fusion(bf16[3696,576]{0,1:T(8,128)(2,1)} %param.7, bf16[1536,3696]{0,1:T(8,128)(2,1)} %param.6), kind=kOutput, calls=%fused_computation.73 | convolution fusion | flops 6539968512 | bytes 19150848 | tf_op jit(solution)/shard_map/dot_general | solution.py:195
  20.5 1.1 fusion.1
  21.7 1.1 fusion.4
  22.8 1.5 collective-permute-start
  24.3 1.5 reshape.51
  25.8 1.0 constant_dynamic-slice_fusion
  27.0 1.4 collective-permute-start.1
  28.5 1.5 collective-permute-start.3
  30.0 1.6 collective-permute-start.2
  31.6 0.9 collective-permute-done.1
  32.4 2.3 %collective-permute-done.2 = bf16[72,512]{1,0:T(8,128)(2,1)S(1)} collective-permute-done((bf16[72,512]{1,0:T(8,128)(2,1)S(1)}, bf16[72,512]{1,0:T(8,128)(2,1)S(1)}, u32[]{:S(2)}, u32[]{:S(2)}) %collective-permute-start.2) | collective-permute-done | bytes 73760 | tf_op jit(solution)/shard_map/ppermute | solution.py:40
  34.8 1.2 collective-permute-start.4
  36.0 1.6 collective-permute-start.6
  37.9 1.6 collective-permute-done.4
  39.6 2.7 %collective-permute-done.5 = bf16[72,512]{1,0:T(8,128)(2,1)S(1)} collective-permute-done((bf16[72,512]{1,0:T(8,128)(2,1)S(1)}, bf16[72,512]{1,0:T(8,128)(2,1)S(1)}, u32[]{:S(2)}, u32[]{:S(2)}) %collective-permute-start.5) | collective-permute-done | bytes 73760 | tf_op jit(solution)/shard_map/ppermute | solution.py:40
  42.3 3.4 %collective-permute-start.7 = (bf16[288,512]{1,0:T(8,128)(2,1)S(1)}, bf16[288,512]{1,0:T(8,128)(2,1)S(1)}, u32[]{:S(2)}, u32[]{:S(2)}) collective-permute-start(bf16[288,512]{1,0:T(8,128)(2,1)S(1)} %bitcast.148), channel_id=1, source_target_pairs={{0,1},{1,0},{2,3},{3,2},{4,5},{5,4},{6,7},{7,6},{8,9},{9,8},{10,11... | collective-permute-start | bytes 884744 | tf_op jit(solution)/shard_map/ppermute | solution.py:40
  45.8 1.1 collective-permute-done.7
  47.3 1.4 collective-permute-start.8
  48.7 1.4 collective-permute-start.10
  50.0 1.6 collective-permute-start.9
  52.0 2.9 %collective-permute-done.8 = f32[48,512]{1,0:T(8,128)S(1)} collective-permute-done((f32[48,512]{1,0:T(8,128)S(1)}, f32[48,512]{1,0:T(8,128)S(1)}, u32[]{:S(2)}, u32[]{:S(2)}) %collective-permute-start.8) | collective-permute-done | bytes 98336 | tf_op jit(solution)/shard_map/ppermute | solution.py:40
  55.3 5.0 %collective-permute-done.9 = f32[48,512]{1,0:T(8,128)S(1)} collective-permute-done((f32[48,512]{1,0:T(8,128)S(1)}, f32[48,512]{1,0:T(8,128)S(1)}, u32[]{:S(2)}, u32[]{:S(2)}) %collective-permute-start.9) | collective-permute-done | bytes 98336 | tf_op jit(solution)/shard_map/ppermute | solution.py:40
  60.4 1.8 %collective-permute-start.11 = (f32[12,512]{1,0:T(8,128)S(1)}, f32[12,512]{1,0:T(8,128)S(1)}, u32[]{:S(2)}, u32[]{:S(2)}) collective-permute-start(f32[12,512]{1,0:T(8,128)S(1)} %get-tuple-element.47), channel_id=1, source_target_pairs={{0,8},{8,16},{16,24},{24,0},{32,40},{40,48},{48,56},{56,32},{64,72... | collective-permute-start | bytes 73736 | tf_op jit(solution)/shard_map/ppermute | solution.py:40
  62.2 2.3 %collective-permute-start.13 = (f32[12,512]{1,0:T(8,128)S(1)}, f32[12,512]{1,0:T(8,128)S(1)}, u32[]{:S(2)}, u32[]{:S(2)}) collective-permute-start(f32[12,512]{1,0:T(8,128)S(1)} %get-tuple-element.48), channel_id=1, source_target_pairs={{0,24},{8,0},{16,8},{24,16},{32,56},{40,32},{48,40},{56,48},{64,88... | collective-permute-start | bytes 73736 | tf_op jit(solution)/shard_map/ppermute | solution.py:40
  64.5 1.2 collective-permute-start.12
  65.7 1.1 collective-permute-done.11
  66.8 3.0 %collective-permute-done.12 = f32[12,512]{1,0:T(8,128)S(1)} collective-permute-done((f32[12,512]{1,0:T(8,128)S(1)}, f32[12,512]{1,0:T(8,128)S(1)}, u32[]{:S(2)}, u32[]{:S(2)}) %collective-permute-start.12) | collective-permute-done | bytes 24608 | tf_op jit(solution)/shard_map/ppermute | solution.py:40
  69.7 2.4 %collective-permute-start.14 = (f32[12,512]{1,0:T(8,128)S(1)}, f32[12,512]{1,0:T(8,128)S(1)}, u32[]{:S(2)}, u32[]{:S(2)}) collective-permute-start(f32[12,512]{1,0:T(8,128)S(1)} %get-tuple-element.28), channel_id=1, source_target_pairs={{0,1},{1,0},{2,3},{3,2},{4,5},{5,4},{6,7},{7,6},{8,9},{9,8},{10,11... | collective-permute-start | bytes 73736 | tf_op jit(solution)/shard_map/ppermute | solution.py:40
  74.6 1.3 collective-permute-start.18
  75.9 1.6 collective-permute-start.20
  77.5 2.4 %collective-permute-done.15 = f32[2,12,512]{2,1,0:T(8,128)S(1)} collective-permute-done((f32[2,12,512]{2,1,0:T(8,128)S(1)}, f32[2,12,512]{2,1,0:T(8,128)S(1)}, u32[]{:S(2)}, u32[]{:S(2)}) %collective-permute-start.15) | collective-permute-done | bytes 49184 | tf_op jit(solution)/shard_map/ppermute | solution.py:40
  81.2 5.2 %collective-permute-done.19 = f32[24,576]{1,0:T(8,128)S(1)} collective-permute-done((f32[24,576]{1,0:T(8,128)S(1)}, f32[24,576]{1,0:T(8,128)S(1)}, u32[]{:S(2)}, u32[]{:S(2)}) %collective-permute-start.19) | collective-permute-done | bytes 55328 | tf_op jit(solution)/shard_map/ppermute | solution.py:40
  86.4 1.7 %all-gather.6.cloned.1.call-done = bf16[1024,3696]{1,0:T(8,128)(2,1)} async-done(((bf16[64,3696]{1,0:T(8,128)(2,1)}), bf16[1024,3696]{1,0:T(8,128)(2,1)}) %all-gather.6.cloned.1.call-update) | async-done | bytes 7569424 | tf_op jit(solution)/shard_map/all_gather | solution.py:315
  88.1 2.6 %collective-permute-start.23 = (f32[24,576]{1,0:T(8,128)S(1)}, f32[24,576]{1,0:T(8,128)S(1)}, u32[]{:S(2)}, u32[]{:S(2)}) collective-permute-start(f32[24,576]{1,0:T(8,128)S(1)} %fusion.17), channel_id=1, source_target_pairs={{0,24},{8,0},{16,8},{24,16},{32,56},{40,32},{48,40},{56,48},{64,88... | collective-permute-start | bytes 165896 | tf_op jit(solution)/shard_map/ppermute | solution.py:40
  90.8 1.7 %collective-permute-start.21 = (f32[24,576]{1,0:T(8,128)S(1)}, f32[24,576]{1,0:T(8,128)S(1)}, u32[]{:S(2)}, u32[]{:S(2)}) collective-permute-start(f32[24,576]{1,0:T(8,128)S(1)} %fusion.17), channel_id=1, source_target_pairs={{0,16},{8,24},{16,0},{24,8},{32,48},{40,56},{48,32},{56,40},{64,80... | collective-permute-start | bytes 165896 | tf_op jit(solution)/shard_map/ppermute | solution.py:40
  92.5 3.1 %collective-permute-done.22 = f32[24,576]{1,0:T(8,128)S(1)} collective-permute-done((f32[24,576]{1,0:T(8,128)S(1)}, f32[24,576]{1,0:T(8,128)S(1)}, u32[]{:S(2)}, u32[]{:S(2)}) %collective-permute-start.22) | collective-permute-done | bytes 55328 | tf_op jit(solution)/shard_map/ppermute | solution.py:40
  96.0 1.8 %collective-permute-start.25 = (f32[24,576]{1,0:T(8,128)S(1)}, f32[24,576]{1,0:T(8,128)S(1)}, u32[]{:S(2)}, u32[]{:S(2)}) collective-permute-start(f32[24,576]{1,0:T(8,128)S(1)} %get-tuple-element.26), channel_id=1, source_target_pairs={{0,64},{8,72},{16,80},{24,88},{32,96},{40,104},{48,112},{56,120},{... | collective-permute-start | bytes 165896 | tf_op jit(solution)/shard_map/ppermute | solution.py:40
  97.8 1.4 collective-permute-start.26
  99.2 1.7 %collective-permute-done.24 = f32[24,576]{1,0:T(8,128)S(1)} collective-permute-done((f32[24,576]{1,0:T(8,128)S(1)}, f32[24,576]{1,0:T(8,128)S(1)}, u32[]{:S(2)}, u32[]{:S(2)}) %collective-permute-start.24) | collective-permute-done | bytes 55328 | tf_op jit(solution)/shard_map/ppermute | solution.py:40
  101.5 1.8 %collective-permute-start.27 = (f32[72,576]{1,0:T(8,128)S(1)}, f32[72,576]{1,0:T(8,128)S(1)}, u32[]{:S(2)}, u32[]{:S(2)}) collective-permute-start(f32[72,576]{1,0:T(8,128)S(1)} %pad_maximum_fusion.1), channel_id=1, source_target_pairs={{0,2},{1,3},{2,4},{3,5},{4,6},{5,7},{6,0},{7,1},{8,10},{9,11},{10,... | collective-permute-start | bytes 497672 | tf_op jit(solution)/shard_map/ppermute | solution.py:40
  103.3 2.3 %collective-permute-start.28 = (f32[72,576]{1,0:T(8,128)S(1)}, f32[72,576]{1,0:T(8,128)S(1)}, u32[]{:S(2)}, u32[]{:S(2)}) collective-permute-start(f32[72,576]{1,0:T(8,128)S(1)} %pad_maximum_fusion.1), channel_id=1, source_target_pairs={{0,4},{1,5},{2,6},{3,7},{4,0},{5,1},{6,2},{7,3},{8,12},{9,13},{10,... | collective-permute-start | bytes 497672 | tf_op jit(solution)/shard_map/ppermute | solution.py:40
  105.6 1.1 collective-permute-start.29
  107.4 3.2 %collective-permute-done.28 = f32[72,576]{1,0:T(8,128)S(1)} collective-permute-done((f32[72,576]{1,0:T(8,128)S(1)}, f32[72,576]{1,0:T(8,128)S(1)}, u32[]{:S(2)}, u32[]{:S(2)}) %collective-permute-start.28) | collective-permute-done | bytes 165920 | tf_op jit(solution)/shard_map/ppermute | solution.py:40
  110.6 5.3 %collective-permute-start.30 = (f32[288,576]{1,0:T(8,128)S(1)}, f32[288,576]{1,0:T(8,128)S(1)}, u32[]{:S(2)}, u32[]{:S(2)}) collective-permute-start(f32[288,576]{1,0:T(8,128)S(1)} %bitcast.142), channel_id=1, source_target_pairs={{0,1},{1,0},{2,3},{3,2},{4,5},{5,4},{6,7},{7,6},{8,9},{9,8},{10,11... | collective-permute-start | bytes 1990664 | tf_op jit(solution)/shard_map/ppermute | solution.py:40
  116.1 1.7 %collective-permute-done.30 = f32[288,576]{1,0:T(8,128)S(1)} collective-permute-done((f32[288,576]{1,0:T(8,128)S(1)}, f32[288,576]{1,0:T(8,128)S(1)}, u32[]{:S(2)}, u32[]{:S(2)}) %collective-permute-start.30) | collective-permute-done | bytes 663584 | tf_op jit(solution)/shard_map/ppermute | solution.py:40
  117.9 23.1 %inverse_factor.1.inverse_ref = f32[576,576]{1,0:T(8,128)S(1)} custom-call(f32[576,576]{1,0:T(8,128)S(1)} %bitcast.139), custom_call_target="tpu_custom_call" | custom-call | flops 2293235712 | bytes 2654208 | tf_op jit(solution)/shard_map/inverse_factor/pallas_call | solution.py:162
  141.0 19.4 %adam_step.1 = (f32[3696,512]{1,0:T(8,128)}, f32[32,3696]{1,0:T(8,128)}, f32[32,3696]{1,0:T(8,128)}) custom-call(s32[1]{0:T(128)} %bitcast.at_ref, f32[576,576]{1,0:T(8,128)S(1)} %inverse_factor.1.inverse_ref, bf16[576,512]{1,0:T(8,128)(2,1)S(1)} %bitcast.138, f32[1536,512]{1,0:T(8,128)} %all-gather.4.cloned.1.call-done.mixed_ref, ...), custom_call_target="tpu_custom_call" | custom-call | flops 10166992896 | bytes 31531008 | tf_op jit(solution)/shard_map/adam_step/pallas_call | solution.py:278
  (81 shorter events, 7.6 us)
Async XLA Ops:
  7.2 81.0 %all-gather.6.cloned.1.call-start = ((), (), s32[]{:S(2)}) async-start(), calls=%async_computation.1 | async-start | bytes 8077312 | tf_op jit(solution)/shard_map/all_gather | solution.py:315
  9.2 131.7 %all-gather.4.cloned.1.call-start = ((), (), s32[]{:S(2)}) async-start(), calls=%async_computation | async-start | bytes 3342336 | tf_op jit(solution)/shard_map/all_gather | solution.py:337
  9.3 11.2 %copy-start.2 = (bf16[1536,512]{1,0:T(8,128)(2,1)S(1)}, bf16[1536,512]{1,0:T(8,128)(2,1)}, u32[]{:S(2)}) copy-start(bf16[1536,512]{1,0:T(8,128)(2,1)} %param.5) | copy-start | bytes 4718596
  22.8 4.0 %collective-permute-start = (bf16[288,512]{1,0:T(8,128)(2,1)S(1)}, bf16[288,512]{1,0:T(8,128)(2,1)S(1)}, u32[]{:S(2)}, u32[]{:S(2)}) collective-permute-start(bf16[288,512]{1,0:T(8,128)(2,1)S(1)} %fusion.7), channel_id=1, source_target_pairs={{0,1},{1,0},{2,3},{3,2},{4,5},{5,4},{6,7},{7,6},{8,9},{9,8},{10,11... | collective-permute-start | bytes 884744 | tf_op jit(solution)/shard_map/ppermute | solution.py:40
  27.0 5.4 %collective-permute-start.1 = (bf16[72,512]{1,0:T(8,128)(2,1)S(1)}, bf16[72,512]{1,0:T(8,128)(2,1)S(1)}, u32[]{:S(2)}, u32[]{:S(2)}) collective-permute-start(bf16[72,512]{1,0:T(8,128)(2,1)S(1)} %get-tuple-element.31), channel_id=1, source_target_pairs={{0,2},{1,3},{2,4},{3,5},{4,6},{5,7},{6,0},{7,1},{8,10},{9,11},{10,... | collective-permute-start | bytes 221192 | tf_op jit(solution)/shard_map/ppermute | solution.py:40
  28.5 4.0 %collective-permute-start.3 = (bf16[72,512]{1,0:T(8,128)(2,1)S(1)}, bf16[72,512]{1,0:T(8,128)(2,1)S(1)}, u32[]{:S(2)}, u32[]{:S(2)}) collective-permute-start(bf16[72,512]{1,0:T(8,128)(2,1)S(1)} %get-tuple-element.32), channel_id=1, source_target_pairs={{0,6},{1,7},{2,0},{3,1},{4,2},{5,3},{6,4},{7,5},{8,14},{9,15},{10,... | collective-permute-start | bytes 221192 | tf_op jit(solution)/shard_map/ppermute | solution.py:40
  30.0 4.8 %collective-permute-start.2 = (bf16[72,512]{1,0:T(8,128)(2,1)S(1)}, bf16[72,512]{1,0:T(8,128)(2,1)S(1)}, u32[]{:S(2)}, u32[]{:S(2)}) collective-permute-start(bf16[72,512]{1,0:T(8,128)(2,1)S(1)} %get-tuple-element.33), channel_id=1, source_target_pairs={{0,4},{1,5},{2,6},{3,7},{4,0},{5,1},{6,2},{7,3},{8,12},{9,13},{10,... | collective-permute-start | bytes 221192 | tf_op jit(solution)/shard_map/ppermute | solution.py:40
  34.8 4.7 %collective-permute-start.4 = (bf16[72,512]{1,0:T(8,128)(2,1)S(1)}, bf16[72,512]{1,0:T(8,128)(2,1)S(1)}, u32[]{:S(2)}, u32[]{:S(2)}) collective-permute-start(bf16[72,512]{1,0:T(8,128)(2,1)S(1)} %get-tuple-element.30), channel_id=1, source_target_pairs={{0,2},{1,3},{2,4},{3,5},{4,6},{5,7},{6,0},{7,1},{8,10},{9,11},{10,... | collective-permute-start | bytes 221192 | tf_op jit(solution)/shard_map/ppermute | solution.py:40
  36.0 6.3 %collective-permute-start.6 = (bf16[72,512]{1,0:T(8,128)(2,1)S(1)}, bf16[72,512]{1,0:T(8,128)(2,1)S(1)}, u32[]{:S(2)}, u32[]{:S(2)}) collective-permute-start(bf16[72,512]{1,0:T(8,128)(2,1)S(1)} %get-tuple-element.30), channel_id=1, source_target_pairs={{0,6},{1,7},{2,0},{3,1},{4,2},{5,3},{6,4},{7,5},{8,14},{9,15},{10,... | collective-permute-start | bytes 221192 | tf_op jit(solution)/shard_map/ppermute | solution.py:40
  37.6 4.7 %collective-permute-start.5 = (bf16[72,512]{1,0:T(8,128)(2,1)S(1)}, bf16[72,512]{1,0:T(8,128)(2,1)S(1)}, u32[]{:S(2)}, u32[]{:S(2)}) collective-permute-start(bf16[72,512]{1,0:T(8,128)(2,1)S(1)} %get-tuple-element.30), channel_id=1, source_target_pairs={{0,4},{1,5},{2,6},{3,7},{4,0},{5,1},{6,2},{7,3},{8,12},{9,13},{10,... | collective-permute-start | bytes 221192 | tf_op jit(solution)/shard_map/ppermute | solution.py:40
  42.3 4.6 %collective-permute-start.7 = (bf16[288,512]{1,0:T(8,128)(2,1)S(1)}, bf16[288,512]{1,0:T(8,128)(2,1)S(1)}, u32[]{:S(2)}, u32[]{:S(2)}) collective-permute-start(bf16[288,512]{1,0:T(8,128)(2,1)S(1)} %bitcast.148), channel_id=1, source_target_pairs={{0,1},{1,0},{2,3},{3,2},{4,5},{5,4},{6,7},{7,6},{8,9},{9,8},{10,11... | collective-permute-start | bytes 884744 | tf_op jit(solution)/shard_map/ppermute | solution.py:40
  47.3 7.6 %collective-permute-start.8 = (f32[48,512]{1,0:T(8,128)S(1)}, f32[48,512]{1,0:T(8,128)S(1)}, u32[]{:S(2)}, u32[]{:S(2)}) collective-permute-start(f32[48,512]{1,0:T(8,128)S(1)} %get-tuple-element.34), channel_id=1, source_target_pairs={{0,32},{8,40},{16,48},{24,56},{32,64},{40,72},{48,80},{56,88},{64,... | collective-permute-start | bytes 294920 | tf_op jit(solution)/shard_map/ppermute | solution.py:40
  48.7 6.6 %collective-permute-start.10 = (f32[48,512]{1,0:T(8,128)S(1)}, f32[48,512]{1,0:T(8,128)S(1)}, u32[]{:S(2)}, u32[]{:S(2)}) collective-permute-start(f32[48,512]{1,0:T(8,128)S(1)} %get-tuple-element.35), channel_id=1, source_target_pairs={{0,96},{8,104},{16,112},{24,120},{32,0},{40,8},{48,16},{56,24},{64... | collective-permute-start | bytes 294920 | tf_op jit(solution)/shard_map/ppermute | solution.py:40
  50.0 10.2 %collective-permute-start.9 = (f32[48,512]{1,0:T(8,128)S(1)}, f32[48,512]{1,0:T(8,128)S(1)}, u32[]{:S(2)}, u32[]{:S(2)}) collective-permute-start(f32[48,512]{1,0:T(8,128)S(1)} %get-tuple-element.36), channel_id=1, source_target_pairs={{0,64},{8,72},{16,80},{24,88},{32,96},{40,104},{48,112},{56,120},{... | collective-permute-start | bytes 294920 | tf_op jit(solution)/shard_map/ppermute | solution.py:40
  60.4 6.4 %collective-permute-start.11 = (f32[12,512]{1,0:T(8,128)S(1)}, f32[12,512]{1,0:T(8,128)S(1)}, u32[]{:S(2)}, u32[]{:S(2)}) collective-permute-start(f32[12,512]{1,0:T(8,128)S(1)} %get-tuple-element.47), channel_id=1, source_target_pairs={{0,8},{8,16},{16,24},{24,0},{32,40},{40,48},{48,56},{56,32},{64,72... | collective-permute-start | bytes 73736 | tf_op jit(solution)/shard_map/ppermute | solution.py:40
  62.2 4.6 %collective-permute-start.13 = (f32[12,512]{1,0:T(8,128)S(1)}, f32[12,512]{1,0:T(8,128)S(1)}, u32[]{:S(2)}, u32[]{:S(2)}) collective-permute-start(f32[12,512]{1,0:T(8,128)S(1)} %get-tuple-element.48), channel_id=1, source_target_pairs={{0,24},{8,0},{16,8},{24,16},{32,56},{40,32},{48,40},{56,48},{64,88... | collective-permute-start | bytes 73736 | tf_op jit(solution)/shard_map/ppermute | solution.py:40
  64.5 5.3 %collective-permute-start.12 = (f32[12,512]{1,0:T(8,128)S(1)}, f32[12,512]{1,0:T(8,128)S(1)}, u32[]{:S(2)}, u32[]{:S(2)}) collective-permute-start(f32[12,512]{1,0:T(8,128)S(1)} %get-tuple-element.49), channel_id=1, source_target_pairs={{0,16},{8,24},{16,0},{24,8},{32,48},{40,56},{48,32},{56,40},{64,80... | collective-permute-start | bytes 73736 | tf_op jit(solution)/shard_map/ppermute | solution.py:40
  69.7 3.3 %collective-permute-start.14 = (f32[12,512]{1,0:T(8,128)S(1)}, f32[12,512]{1,0:T(8,128)S(1)}, u32[]{:S(2)}, u32[]{:S(2)}) collective-permute-start(f32[12,512]{1,0:T(8,128)S(1)} %get-tuple-element.28), channel_id=1, source_target_pairs={{0,1},{1,0},{2,3},{3,2},{4,5},{5,4},{6,7},{7,6},{8,9},{9,8},{10,11... | collective-permute-start | bytes 73736 | tf_op jit(solution)/shard_map/ppermute | solution.py:40
  73.0 7.5 %collective-permute-start.17 = (f32[2,12,512]{2,1,0:T(8,128)S(1)}, f32[2,12,512]{2,1,0:T(8,128)S(1)}, u32[]{:S(2)}, u32[]{:S(2)}) collective-permute-start(f32[2,12,512]{2,1,0:T(8,128)S(1)} %bitcast_dynamic-update-slice_fusion.20), channel_id=1, source_target_pairs={{0,6},{1,7},{2,0},{3,1},{4,2},{5,3},{6,4},{7,5},{8,14},{9,15},{10,... | collective-permute-start | bytes 147464 | tf_op jit(solution)/shard_map/ppermute | solution.py:40
  73.1 7.4 %collective-permute-start.16 = (f32[2,12,512]{2,1,0:T(8,128)S(1)}, f32[2,12,512]{2,1,0:T(8,128)S(1)}, u32[]{:S(2)}, u32[]{:S(2)}) collective-permute-start(f32[2,12,512]{2,1,0:T(8,128)S(1)} %bitcast_dynamic-update-slice_fusion.20), channel_id=1, source_target_pairs={{0,4},{1,5},{2,6},{3,7},{4,0},{5,1},{6,2},{7,3},{8,12},{9,13},{10,... | collective-permute-start | bytes 147464 | tf_op jit(solution)/shard_map/ppermute | solution.py:40
  73.8 6.2 %collective-permute-start.15 = (f32[2,12,512]{2,1,0:T(8,128)S(1)}, f32[2,12,512]{2,1,0:T(8,128)S(1)}, u32[]{:S(2)}, u32[]{:S(2)}) collective-permute-start(f32[2,12,512]{2,1,0:T(8,128)S(1)} %bitcast_dynamic-update-slice_fusion.20), channel_id=1, source_target_pairs={{0,2},{1,3},{2,4},{3,5},{4,6},{5,7},{6,0},{7,1},{8,10},{9,11},{10,... | collective-permute-start | bytes 147464 | tf_op jit(solution)/shard_map/ppermute | solution.py:40
  74.6 6.6 %collective-permute-start.18 = (f32[24,576]{1,0:T(8,128)S(1)}, f32[24,576]{1,0:T(8,128)S(1)}, u32[]{:S(2)}, u32[]{:S(2)}) collective-permute-start(f32[24,576]{1,0:T(8,128)S(1)} %get-tuple-element.40), channel_id=1, source_target_pairs={{0,32},{8,40},{16,48},{24,56},{32,64},{40,72},{48,80},{56,88},{64,... | collective-permute-start | bytes 165896 | tf_op jit(solution)/shard_map/ppermute | solution.py:40
  75.9 5.4 %collective-permute-start.20 = (f32[24,576]{1,0:T(8,128)S(1)}, f32[24,576]{1,0:T(8,128)S(1)}, u32[]{:S(2)}, u32[]{:S(2)}) collective-permute-start(f32[24,576]{1,0:T(8,128)S(1)} %get-tuple-element.41), channel_id=1, source_target_pairs={{0,96},{8,104},{16,112},{24,120},{32,0},{40,8},{48,16},{56,24},{64... | collective-permute-start | bytes 165896 | tf_op jit(solution)/shard_map/ppermute | solution.py:40
  80.0 6.4 %collective-permute-start.19 = (f32[24,576]{1,0:T(8,128)S(1)}, f32[24,576]{1,0:T(8,128)S(1)}, u32[]{:S(2)}, u32[]{:S(2)}) collective-permute-start(f32[24,576]{1,0:T(8,128)S(1)} %get-tuple-element.42), channel_id=1, source_target_pairs={{0,64},{8,72},{16,80},{24,88},{32,96},{40,104},{48,112},{56,120},{... | collective-permute-start | bytes 165896 | tf_op jit(solution)/shard_map/ppermute | solution.py:40
  88.1 4.4 %collective-permute-start.23 = (f32[24,576]{1,0:T(8,128)S(1)}, f32[24,576]{1,0:T(8,128)S(1)}, u32[]{:S(2)}, u32[]{:S(2)}) collective-permute-start(f32[24,576]{1,0:T(8,128)S(1)} %fusion.17), channel_id=1, source_target_pairs={{0,24},{8,0},{16,8},{24,16},{32,56},{40,32},{48,40},{56,48},{64,88... | collective-permute-start | bytes 165896 | tf_op jit(solution)/shard_map/ppermute | solution.py:40
  90.8 4.8 %collective-permute-start.22 = (f32[24,576]{1,0:T(8,128)S(1)}, f32[24,576]{1,0:T(8,128)S(1)}, u32[]{:S(2)}, u32[]{:S(2)}) collective-permute-start(f32[24,576]{1,0:T(8,128)S(1)} %fusion.17), channel_id=1, source_target_pairs={{0,8},{8,16},{16,24},{24,0},{32,40},{40,48},{48,56},{56,32},{64,72... | collective-permute-start | bytes 165896 | tf_op jit(solution)/shard_map/ppermute | solution.py:40
  90.8 5.0 %collective-permute-start.21 = (f32[24,576]{1,0:T(8,128)S(1)}, f32[24,576]{1,0:T(8,128)S(1)}, u32[]{:S(2)}, u32[]{:S(2)}) collective-permute-start(f32[24,576]{1,0:T(8,128)S(1)} %fusion.17), channel_id=1, source_target_pairs={{0,16},{8,24},{16,0},{24,8},{32,48},{40,56},{48,32},{56,40},{64,80... | collective-permute-start | bytes 165896 | tf_op jit(solution)/shard_map/ppermute | solution.py:40
  95.9 5.0 %collective-permute-start.24 = (f32[24,576]{1,0:T(8,128)S(1)}, f32[24,576]{1,0:T(8,128)S(1)}, u32[]{:S(2)}, u32[]{:S(2)}) collective-permute-start(f32[24,576]{1,0:T(8,128)S(1)} %get-tuple-element.26), channel_id=1, source_target_pairs={{0,32},{8,40},{16,48},{24,56},{32,64},{40,72},{48,80},{56,88},{64,... | collective-permute-start | bytes 165896 | tf_op jit(solution)/shard_map/ppermute | solution.py:40
  96.0 4.9 %collective-permute-start.25 = (f32[24,576]{1,0:T(8,128)S(1)}, f32[24,576]{1,0:T(8,128)S(1)}, u32[]{:S(2)}, u32[]{:S(2)}) collective-permute-start(f32[24,576]{1,0:T(8,128)S(1)} %get-tuple-element.26), channel_id=1, source_target_pairs={{0,64},{8,72},{16,80},{24,88},{32,96},{40,104},{48,112},{56,120},{... | collective-permute-start | bytes 165896 | tf_op jit(solution)/shard_map/ppermute | solution.py:40
  97.8 3.7 %collective-permute-start.26 = (f32[24,576]{1,0:T(8,128)S(1)}, f32[24,576]{1,0:T(8,128)S(1)}, u32[]{:S(2)}, u32[]{:S(2)}) collective-permute-start(f32[24,576]{1,0:T(8,128)S(1)} %get-tuple-element.26), channel_id=1, source_target_pairs={{0,96},{8,104},{16,112},{24,120},{32,0},{40,8},{48,16},{56,24},{64... | collective-permute-start | bytes 165896 | tf_op jit(solution)/shard_map/ppermute | solution.py:40
  101.5 5.8 %collective-permute-start.27 = (f32[72,576]{1,0:T(8,128)S(1)}, f32[72,576]{1,0:T(8,128)S(1)}, u32[]{:S(2)}, u32[]{:S(2)}) collective-permute-start(f32[72,576]{1,0:T(8,128)S(1)} %pad_maximum_fusion.1), channel_id=1, source_target_pairs={{0,2},{1,3},{2,4},{3,5},{4,6},{5,7},{6,0},{7,1},{8,10},{9,11},{10,... | collective-permute-start | bytes 497672 | tf_op jit(solution)/shard_map/ppermute | solution.py:40
  103.3 7.2 %collective-permute-start.28 = (f32[72,576]{1,0:T(8,128)S(1)}, f32[72,576]{1,0:T(8,128)S(1)}, u32[]{:S(2)}, u32[]{:S(2)}) collective-permute-start(f32[72,576]{1,0:T(8,128)S(1)} %pad_maximum_fusion.1), channel_id=1, source_target_pairs={{0,4},{1,5},{2,6},{3,7},{4,0},{5,1},{6,2},{7,3},{8,12},{9,13},{10,... | collective-permute-start | bytes 497672 | tf_op jit(solution)/shard_map/ppermute | solution.py:40
  105.6 5.0 %collective-permute-start.29 = (f32[72,576]{1,0:T(8,128)S(1)}, f32[72,576]{1,0:T(8,128)S(1)}, u32[]{:S(2)}, u32[]{:S(2)}) collective-permute-start(f32[72,576]{1,0:T(8,128)S(1)} %pad_maximum_fusion.1), channel_id=1, source_target_pairs={{0,6},{1,7},{2,0},{3,1},{4,2},{5,3},{6,4},{7,5},{8,14},{9,15},{10,... | collective-permute-start | bytes 497672 | tf_op jit(solution)/shard_map/ppermute | solution.py:40
  110.6 7.2 %collective-permute-start.30 = (f32[288,576]{1,0:T(8,128)S(1)}, f32[288,576]{1,0:T(8,128)S(1)}, u32[]{:S(2)}, u32[]{:S(2)}) collective-permute-start(f32[288,576]{1,0:T(8,128)S(1)} %bitcast.142), channel_id=1, source_target_pairs={{0,1},{1,0},{2,3},{3,2},{4,5},{5,4},{6,7},{7,6},{8,9},{9,8},{10,11... | collective-permute-start | bytes 1990664 | tf_op jit(solution)/shard_map/ppermute | solution.py:40
  117.8 23.1 %copy-start = (f32[32,3696]{1,0:T(8,128)S(1)}, f32[32,3696]{1,0:T(8,128)}, u32[]{:S(2)}) copy-start(f32[32,3696]{1,0:T(8,128)} %own_first_ref.1) | copy-start | bytes 1419268
  117.8 23.1 %copy-start.1 = (f32[32,3696]{1,0:T(8,128)S(1)}, f32[32,3696]{1,0:T(8,128)}, u32[]{:S(2)}) copy-start(f32[32,3696]{1,0:T(8,128)} %own_second_ref.1) | copy-start | bytes 1419268
Sparse Core Ops, SparseCore 0:
  10.8 77.3 all-gather.5
  90.9 47.5 all-gather.3

commit v14 on v13

--- a/solution.py
+++ b/solution.py
@@ -212,29 +212,43 @@
 ):
     width, owned = grad_ref.shape[0], own_first_ref.shape[0]
     tiles = [(o, min(TILE, width - o)) for o in range(0, width, TILE)]
-    fetch_mixed = pltpu.make_async_copy(mixed_ref, mixed, arrived.at[0])
-    fetch_gathered = pltpu.make_async_copy(gathered_ref, gathered, arrived.at[1])
+    parts = [pl.ds(o, MIX_TILE) for o in range(0, mixed.shape[0], MIX_TILE)]
+    fetch_mixed = [
+        pltpu.make_async_copy(mixed_ref.at[here], mixed.at[here], arrived.at[1 + len(tiles) + i])
+        for i, here in enumerate(parts)
+    ]
+    fetch_gathered = pltpu.make_async_copy(gathered_ref, gathered, arrived.at[0])
     fetch_grad = [
-        pltpu.make_async_copy(grad_ref.at[pl.ds(o, n)], grad.at[pl.ds(o, n)], arrived.at[2 + i])
+        pltpu.make_async_copy(grad_ref.at[pl.ds(o, n)], grad.at[pl.ds(o, n)], arrived.at[1 + i])
         for i, (o, n) in enumerate(tiles)
     ]
-    fetch_mixed.start()
+    fetch_mixed[0].start()
+    fetch_mixed[1].start()
 
     high, low = two_parts(inverse_ref[:RANK, :RANK])
-    values = sketched_ref[:RANK, :]
-    projector[...] = (
-        jnp.dot(low, values, preferred_element_type=f32) + jnp.dot(high, values, preferred_element_type=f32)
-    ).astype(bf16)
     times = lambda a, b: lax.dot_general(a, b, (((1,), (1,)), ((), ())), preferred_element_type=f32)
-    fetch_mixed.wait()
-    fetch_grad[0].start()
-    fetch_gathered.start()
-    for o in range(0, mixed.shape[0], MIX_TILE):
-        here = pl.ds(o, MIX_TILE)
+    halves = [(pl.ds(o, RANK // 2), o, o + RANK // 2) for o in (0, RANK // 2)]
+    for rows, o, end in halves:
+        values = sketched_ref[:end, :]
+        projector[rows, :] = (
+            jnp.dot(low[o:end, :end], values, preferred_element_type=f32)
+            + jnp.dot(high[o:end, :end], values, preferred_element_type=f32)
+        ).astype(bf16)
+    after = fetch_mixed[2:] + [fetch_grad[0], fetch_gathered]
+    for i, here in enumerate(parts):
+        fetch_mixed[i].wait()
+        if i + 1 < len(parts):
+            after.pop(0).start()
+        else:
+            for copy in after:
+                copy.start()
         mixed_high, mixed_low = two_parts(mixed[here, :])
-        turned[:, here] = (
-            times(high, mixed_low) + times(low, mixed_high) + times(high, mixed_high)
-        ).astype(bf16)
+        for rows, o, end in halves:
+            turned[rows, here] = (
+                times(high[o:end, :end], mixed_low[:, :end])
+                + times(low[o:end, :end], mixed_high[:, :end])
+                + times(high[o:end, :end], mixed_high[:, :end])
+            ).astype(bf16)
 
     mine = pl.ds(pl.multiple_of(at_ref[0] * owned, owned), owned)
     send = [
@@ -293,7 +307,7 @@
             pltpu.VMEM(mixed.shape, f32),
             pltpu.VMEM(grad_turned.shape, bf16),
             pltpu.VMEM(gathered.shape, bf16),
-            pltpu.SemaphoreType.DMA((2 + pl.cdiv(width, TILE),)),
+            pltpu.SemaphoreType.DMA((1 + pl.cdiv(width, TILE) + tokens // MIX_TILE,)),
             pltpu.SemaphoreType.DMA((2,)),
         ],
         compiler_params=pltpu.CompilerParams(vmem_limit_bytes=STEP_VMEM),

time: 167 us -> 167 us (level)
  no operation moved by 1% of the time
where the time goes in v14:
time: 167 us
  starting transfers between devices  47.7 us (29%)
  Pallas kernels  44.4 us (27%)
  waiting for transfers between devices  42.2 us (25%)
  between operations  14.5 us (9%)
  matrix products  14.1 us (8%)
  local copies, waits for them, and re-layouts  3.99 us (2%)
    ppermute x31, starting transfers between devices, shift(): return lax.ppermute(value, axis, pairs)  47.6 us
    ppermute x31, waiting for transfers between devices, shift(): return lax.ppermute(value, axis, pairs)  40.4 us
    pallas_call x1, Pallas kernels, inverse_factor(): pl.pallas_call(factor_kernel, out_shape=jax.ShapeDtypeStruct((size, size)...  23.1 us
    pallas_call x1, Pallas kernels, adam_step(): pl.pallas_call(step_kernel, out_shape=(jax.ShapeDtypeStruct((width, featu...  19.3 us
    dot_general x1, matrix products, sketched_term(): jnp.dot(sketch_turned, grad_turned, preferred_element_type=f32)  11.2 us
  transfers between devices with their start and end apart: 33, of which 21 were waited for; matrix products, arithmetic and copies ran while one was open for 11% of the time, Pallas kernels for 14%

profile of v14, /device:TPU:1, one launch (start us, length us, event | category | flops | bytes accessed | tf_op | source)
XLA Modules:
  0.0 167.1 jit_solution(17899885088947910390)
XLA Ops:
  7.2 2.0 %pack.1 = bf16[64,3696]{1,0:T(8,128)(2,1)} custom-call(f32[32,3696]{1,0:T(8,128)} %own_first_ref.1, f32[32,3696]{1,0:T(8,128)} %own_second_ref.1), custom_call_target="tpu_custom_call" | custom-call | tf_op jit(solution)/shard_map/pack/pallas_call | solution.py:187
  9.3 11.2 %fusion.22 = f32[576,1536]{1,0:T(8,128)S(1)} fusion(bf16[3696,576]{0,1:T(8,128)(2,1)} %param.7, bf16[1536,3696]{0,1:T(8,128)(2,1)} %param.6), kind=kOutput, calls=%fused_computation.73 | convolution fusion | flops 6539968512 | bytes 19150848 | tf_op jit(solution)/shard_map/dot_general | solution.py:195
  20.5 1.1 fusion.1
  21.7 1.1 fusion.4
  22.8 1.5 collective-permute-start
  24.3 1.5 reshape.51
  25.8 1.0 constant_dynamic-slice_fusion
  27.0 1.4 collective-permute-start.1
  28.5 1.5 collective-permute-start.3
  30.0 1.6 collective-permute-start.2
  31.6 0.9 collective-permute-done.1
  32.4 2.3 %collective-permute-done.2 = bf16[72,512]{1,0:T(8,128)(2,1)S(1)} collective-permute-done((bf16[72,512]{1,0:T(8,128)(2,1)S(1)}, bf16[72,512]{1,0:T(8,128)(2,1)S(1)}, u32[]{:S(2)}, u32[]{:S(2)}) %collective-permute-start.2) | collective-permute-done | bytes 73760 | tf_op jit(solution)/shard_map/ppermute | solution.py:40
  34.8 1.2 collective-permute-start.4
  36.0 1.6 collective-permute-start.6
  37.9 1.6 collective-permute-done.4
  39.6 2.7 %collective-permute-done.5 = bf16[72,512]{1,0:T(8,128)(2,1)S(1)} collective-permute-done((bf16[72,512]{1,0:T(8,128)(2,1)S(1)}, bf16[72,512]{1,0:T(8,128)(2,1)S(1)}, u32[]{:S(2)}, u32[]{:S(2)}) %collective-permute-start.5) | collective-permute-done | bytes 73760 | tf_op jit(solution)/shard_map/ppermute | solution.py:40
  42.3 3.4 %collective-permute-start.7 = (bf16[288,512]{1,0:T(8,128)(2,1)S(1)}, bf16[288,512]{1,0:T(8,128)(2,1)S(1)}, u32[]{:S(2)}, u32[]{:S(2)}) collective-permute-start(bf16[288,512]{1,0:T(8,128)(2,1)S(1)} %bitcast.148), channel_id=1, source_target_pairs={{0,1},{1,0},{2,3},{3,2},{4,5},{5,4},{6,7},{7,6},{8,9},{9,8},{10,11... | collective-permute-start | bytes 884744 | tf_op jit(solution)/shard_map/ppermute | solution.py:40
  45.8 1.1 collective-permute-done.7
  47.3 1.4 collective-permute-start.8
  48.7 1.4 collective-permute-start.10
  50.0 1.6 collective-permute-start.9
  52.0 2.9 %collective-permute-done.8 = f32[48,512]{1,0:T(8,128)S(1)} collective-permute-done((f32[48,512]{1,0:T(8,128)S(1)}, f32[48,512]{1,0:T(8,128)S(1)}, u32[]{:S(2)}, u32[]{:S(2)}) %collective-permute-start.8) | collective-permute-done | bytes 98336 | tf_op jit(solution)/shard_map/ppermute | solution.py:40
  55.3 5.0 %collective-permute-done.9 = f32[48,512]{1,0:T(8,128)S(1)} collective-permute-done((f32[48,512]{1,0:T(8,128)S(1)}, f32[48,512]{1,0:T(8,128)S(1)}, u32[]{:S(2)}, u32[]{:S(2)}) %collective-permute-start.9) | collective-permute-done | bytes 98336 | tf_op jit(solution)/shard_map/ppermute | solution.py:40
  60.4 1.8 %collective-permute-start.11 = (f32[12,512]{1,0:T(8,128)S(1)}, f32[12,512]{1,0:T(8,128)S(1)}, u32[]{:S(2)}, u32[]{:S(2)}) collective-permute-start(f32[12,512]{1,0:T(8,128)S(1)} %get-tuple-element.47), channel_id=1, source_target_pairs={{0,8},{8,16},{16,24},{24,0},{32,40},{40,48},{48,56},{56,32},{64,72... | collective-permute-start | bytes 73736 | tf_op jit(solution)/shard_map/ppermute | solution.py:40
  62.2 2.3 %collective-permute-start.13 = (f32[12,512]{1,0:T(8,128)S(1)}, f32[12,512]{1,0:T(8,128)S(1)}, u32[]{:S(2)}, u32[]{:S(2)}) collective-permute-start(f32[12,512]{1,0:T(8,128)S(1)} %get-tuple-element.48), channel_id=1, source_target_pairs={{0,24},{8,0},{16,8},{24,16},{32,56},{40,32},{48,40},{56,48},{64,88... | collective-permute-start | bytes 73736 | tf_op jit(solution)/shard_map/ppermute | solution.py:40
  64.5 1.2 collective-permute-start.12
  65.7 1.1 collective-permute-done.11
  66.8 3.0 %collective-permute-done.12 = f32[12,512]{1,0:T(8,128)S(1)} collective-permute-done((f32[12,512]{1,0:T(8,128)S(1)}, f32[12,512]{1,0:T(8,128)S(1)}, u32[]{:S(2)}, u32[]{:S(2)}) %collective-permute-start.12) | collective-permute-done | bytes 24608 | tf_op jit(solution)/shard_map/ppermute | solution.py:40
  69.7 2.4 %collective-permute-start.14 = (f32[12,512]{1,0:T(8,128)S(1)}, f32[12,512]{1,0:T(8,128)S(1)}, u32[]{:S(2)}, u32[]{:S(2)}) collective-permute-start(f32[12,512]{1,0:T(8,128)S(1)} %get-tuple-element.28), channel_id=1, source_target_pairs={{0,1},{1,0},{2,3},{3,2},{4,5},{5,4},{6,7},{7,6},{8,9},{9,8},{10,11... | collective-permute-start | bytes 73736 | tf_op jit(solution)/shard_map/ppermute | solution.py:40
  74.6 1.3 collective-permute-start.18
  75.9 1.6 collective-permute-start.20
  77.5 2.4 %collective-permute-done.15 = f32[2,12,512]{2,1,0:T(8,128)S(1)} collective-permute-done((f32[2,12,512]{2,1,0:T(8,128)S(1)}, f32[2,12,512]{2,1,0:T(8,128)S(1)}, u32[]{:S(2)}, u32[]{:S(2)}) %collective-permute-start.15) | collective-permute-done | bytes 49184 | tf_op jit(solution)/shard_map/ppermute | solution.py:40
  81.2 5.2 %collective-permute-done.19 = f32[24,576]{1,0:T(8,128)S(1)} collective-permute-done((f32[24,576]{1,0:T(8,128)S(1)}, f32[24,576]{1,0:T(8,128)S(1)}, u32[]{:S(2)}, u32[]{:S(2)}) %collective-permute-start.19) | collective-permute-done | bytes 55328 | tf_op jit(solution)/shard_map/ppermute | solution.py:40
  86.4 1.7 %all-gather.6.cloned.1.call-done = bf16[1024,3696]{1,0:T(8,128)(2,1)} async-done(((bf16[64,3696]{1,0:T(8,128)(2,1)}), bf16[1024,3696]{1,0:T(8,128)(2,1)}) %all-gather.6.cloned.1.call-update) | async-done | bytes 7569424 | tf_op jit(solution)/shard_map/all_gather | solution.py:329
  88.1 2.6 %collective-permute-start.23 = (f32[24,576]{1,0:T(8,128)S(1)}, f32[24,576]{1,0:T(8,128)S(1)}, u32[]{:S(2)}, u32[]{:S(2)}) collective-permute-start(f32[24,576]{1,0:T(8,128)S(1)} %fusion.17), channel_id=1, source_target_pairs={{0,24},{8,0},{16,8},{24,16},{32,56},{40,32},{48,40},{56,48},{64,88... | collective-permute-start | bytes 165896 | tf_op jit(solution)/shard_map/ppermute | solution.py:40
  90.8 1.7 %collective-permute-start.21 = (f32[24,576]{1,0:T(8,128)S(1)}, f32[24,576]{1,0:T(8,128)S(1)}, u32[]{:S(2)}, u32[]{:S(2)}) collective-permute-start(f32[24,576]{1,0:T(8,128)S(1)} %fusion.17), channel_id=1, source_target_pairs={{0,16},{8,24},{16,0},{24,8},{32,48},{40,56},{48,32},{56,40},{64,80... | collective-permute-start | bytes 165896 | tf_op jit(solution)/shard_map/ppermute | solution.py:40
  92.5 3.1 %collective-permute-done.22 = f32[24,576]{1,0:T(8,128)S(1)} collective-permute-done((f32[24,576]{1,0:T(8,128)S(1)}, f32[24,576]{1,0:T(8,128)S(1)}, u32[]{:S(2)}, u32[]{:S(2)}) %collective-permute-start.22) | collective-permute-done | bytes 55328 | tf_op jit(solution)/shard_map/ppermute | solution.py:40
  96.0 1.8 %collective-permute-start.25 = (f32[24,576]{1,0:T(8,128)S(1)}, f32[24,576]{1,0:T(8,128)S(1)}, u32[]{:S(2)}, u32[]{:S(2)}) collective-permute-start(f32[24,576]{1,0:T(8,128)S(1)} %get-tuple-element.26), channel_id=1, source_target_pairs={{0,64},{8,72},{16,80},{24,88},{32,96},{40,104},{48,112},{56,120},{... | collective-permute-start | bytes 165896 | tf_op jit(solution)/shard_map/ppermute | solution.py:40
  97.8 1.4 collective-permute-start.26
  99.2 1.7 %collective-permute-done.24 = f32[24,576]{1,0:T(8,128)S(1)} collective-permute-done((f32[24,576]{1,0:T(8,128)S(1)}, f32[24,576]{1,0:T(8,128)S(1)}, u32[]{:S(2)}, u32[]{:S(2)}) %collective-permute-start.24) | collective-permute-done | bytes 55328 | tf_op jit(solution)/shard_map/ppermute | solution.py:40
  101.5 1.8 %collective-permute-start.27 = (f32[72,576]{1,0:T(8,128)S(1)}, f32[72,576]{1,0:T(8,128)S(1)}, u32[]{:S(2)}, u32[]{:S(2)}) collective-permute-start(f32[72,576]{1,0:T(8,128)S(1)} %pad_maximum_fusion.1), channel_id=1, source_target_pairs={{0,2},{1,3},{2,4},{3,5},{4,6},{5,7},{6,0},{7,1},{8,10},{9,11},{10,... | collective-permute-start | bytes 497672 | tf_op jit(solution)/shard_map/ppermute | solution.py:40
  103.3 2.3 %collective-permute-start.28 = (f32[72,576]{1,0:T(8,128)S(1)}, f32[72,576]{1,0:T(8,128)S(1)}, u32[]{:S(2)}, u32[]{:S(2)}) collective-permute-start(f32[72,576]{1,0:T(8,128)S(1)} %pad_maximum_fusion.1), channel_id=1, source_target_pairs={{0,4},{1,5},{2,6},{3,7},{4,0},{5,1},{6,2},{7,3},{8,12},{9,13},{10,... | collective-permute-start | bytes 497672 | tf_op jit(solution)/shard_map/ppermute | solution.py:40
  105.6 1.1 collective-permute-start.29
  107.4 3.2 %collective-permute-done.28 = f32[72,576]{1,0:T(8,128)S(1)} collective-permute-done((f32[72,576]{1,0:T(8,128)S(1)}, f32[72,576]{1,0:T(8,128)S(1)}, u32[]{:S(2)}, u32[]{:S(2)}) %collective-permute-start.28) | collective-permute-done | bytes 165920 | tf_op jit(solution)/shard_map/ppermute | solution.py:40
  110.6 5.3 %collective-permute-start.30 = (f32[288,576]{1,0:T(8,128)S(1)}, f32[288,576]{1,0:T(8,128)S(1)}, u32[]{:S(2)}, u32[]{:S(2)}) collective-permute-start(f32[288,576]{1,0:T(8,128)S(1)} %bitcast.142), channel_id=1, source_target_pairs={{0,1},{1,0},{2,3},{3,2},{4,5},{5,4},{6,7},{7,6},{8,9},{9,8},{10,11... | collective-permute-start | bytes 1990664 | tf_op jit(solution)/shard_map/ppermute | solution.py:40
  116.1 1.7 %collective-permute-done.30 = f32[288,576]{1,0:T(8,128)S(1)} collective-permute-done((f32[288,576]{1,0:T(8,128)S(1)}, f32[288,576]{1,0:T(8,128)S(1)}, u32[]{:S(2)}, u32[]{:S(2)}) %collective-permute-start.30) | collective-permute-done | bytes 663584 | tf_op jit(solution)/shard_map/ppermute | solution.py:40
  117.9 23.1 %inverse_factor.1.inverse_ref = f32[576,576]{1,0:T(8,128)S(1)} custom-call(f32[576,576]{1,0:T(8,128)S(1)} %bitcast.139), custom_call_target="tpu_custom_call" | custom-call | flops 2293235712 | bytes 2654208 | tf_op jit(solution)/shard_map/inverse_factor/pallas_call | solution.py:162
  141.0 19.3 %adam_step.1 = (f32[3696,512]{1,0:T(8,128)}, f32[32,3696]{1,0:T(8,128)}, f32[32,3696]{1,0:T(8,128)}) custom-call(s32[1]{0:T(128)} %bitcast.at_ref, f32[576,576]{1,0:T(8,128)S(1)} %inverse_factor.1.inverse_ref, bf16[576,512]{1,0:T(8,128)(2,1)S(1)} %bitcast.138, f32[1536,512]{1,0:T(8,128)} %all-gather.4.cloned.1.call-done.mixed_ref, ...), custom_call_target="tpu_custom_call" | custom-call | flops 10166992896 | bytes 31531008 | tf_op jit(solution)/shard_map/adam_step/pallas_call | solution.py:292
  (81 shorter events, 7.6 us)
Async XLA Ops:
  7.2 81.0 %all-gather.6.cloned.1.call-start = ((), (), s32[]{:S(2)}) async-start(), calls=%async_computation.1 | async-start | bytes 8077312 | tf_op jit(solution)/shard_map/all_gather | solution.py:329
  9.2 131.7 %all-gather.4.cloned.1.call-start = ((), (), s32[]{:S(2)}) async-start(), calls=%async_computation | async-start | bytes 3342336 | tf_op jit(solution)/shard_map/all_gather | solution.py:351
  9.3 11.2 %copy-start.2 = (bf16[1536,512]{1,0:T(8,128)(2,1)S(1)}, bf16[1536,512]{1,0:T(8,128)(2,1)}, u32[]{:S(2)}) copy-start(bf16[1536,512]{1,0:T(8,128)(2,1)} %param.5) | copy-start | bytes 4718596
  22.8 4.0 %collective-permute-start = (bf16[288,512]{1,0:T(8,128)(2,1)S(1)}, bf16[288,512]{1,0:T(8,128)(2,1)S(1)}, u32[]{:S(2)}, u32[]{:S(2)}) collective-permute-start(bf16[288,512]{1,0:T(8,128)(2,1)S(1)} %fusion.7), channel_id=1, source_target_pairs={{0,1},{1,0},{2,3},{3,2},{4,5},{5,4},{6,7},{7,6},{8,9},{9,8},{10,11... | collective-permute-start | bytes 884744 | tf_op jit(solution)/shard_map/ppermute | solution.py:40
  27.0 5.4 %collective-permute-start.1 = (bf16[72,512]{1,0:T(8,128)(2,1)S(1)}, bf16[72,512]{1,0:T(8,128)(2,1)S(1)}, u32[]{:S(2)}, u32[]{:S(2)}) collective-permute-start(bf16[72,512]{1,0:T(8,128)(2,1)S(1)} %get-tuple-element.31), channel_id=1, source_target_pairs={{0,2},{1,3},{2,4},{3,5},{4,6},{5,7},{6,0},{7,1},{8,10},{9,11},{10,... | collective-permute-start | bytes 221192 | tf_op jit(solution)/shard_map/ppermute | solution.py:40
  28.5 4.0 %collective-permute-start.3 = (bf16[72,512]{1,0:T(8,128)(2,1)S(1)}, bf16[72,512]{1,0:T(8,128)(2,1)S(1)}, u32[]{:S(2)}, u32[]{:S(2)}) collective-permute-start(bf16[72,512]{1,0:T(8,128)(2,1)S(1)} %get-tuple-element.32), channel_id=1, source_target_pairs={{0,6},{1,7},{2,0},{3,1},{4,2},{5,3},{6,4},{7,5},{8,14},{9,15},{10,... | collective-permute-start | bytes 221192 | tf_op jit(solution)/shard_map/ppermute | solution.py:40
  30.0 4.8 %collective-permute-start.2 = (bf16[72,512]{1,0:T(8,128)(2,1)S(1)}, bf16[72,512]{1,0:T(8,128)(2,1)S(1)}, u32[]{:S(2)}, u32[]{:S(2)}) collective-permute-start(bf16[72,512]{1,0:T(8,128)(2,1)S(1)} %get-tuple-element.33), channel_id=1, source_target_pairs={{0,4},{1,5},{2,6},{3,7},{4,0},{5,1},{6,2},{7,3},{8,12},{9,13},{10,... | collective-permute-start | bytes 221192 | tf_op jit(solution)/shard_map/ppermute | solution.py:40
  34.8 4.7 %collective-permute-start.4 = (bf16[72,512]{1,0:T(8,128)(2,1)S(1)}, bf16[72,512]{1,0:T(8,128)(2,1)S(1)}, u32[]{:S(2)}, u32[]{:S(2)}) collective-permute-start(bf16[72,512]{1,0:T(8,128)(2,1)S(1)} %get-tuple-element.30), channel_id=1, source_target_pairs={{0,2},{1,3},{2,4},{3,5},{4,6},{5,7},{6,0},{7,1},{8,10},{9,11},{10,... | collective-permute-start | bytes 221192 | tf_op jit(solution)/shard_map/ppermute | solution.py:40
  36.0 6.3 %collective-permute-start.6 = (bf16[72,512]{1,0:T(8,128)(2,1)S(1)}, bf16[72,512]{1,0:T(8,128)(2,1)S(1)}, u32[]{:S(2)}, u32[]{:S(2)}) collective-permute-start(bf16[72,512]{1,0:T(8,128)(2,1)S(1)} %get-tuple-element.30), channel_id=1, source_target_pairs={{0,6},{1,7},{2,0},{3,1},{4,2},{5,3},{6,4},{7,5},{8,14},{9,15},{10,... | collective-permute-start | bytes 221192 | tf_op jit(solution)/shard_map/ppermute | solution.py:40
  37.6 4.7 %collective-permute-start.5 = (bf16[72,512]{1,0:T(8,128)(2,1)S(1)}, bf16[72,512]{1,0:T(8,128)(2,1)S(1)}, u32[]{:S(2)}, u32[]{:S(2)}) collective-permute-start(bf16[72,512]{1,0:T(8,128)(2,1)S(1)} %get-tuple-element.30), channel_id=1, source_target_pairs={{0,4},{1,5},{2,6},{3,7},{4,0},{5,1},{6,2},{7,3},{8,12},{9,13},{10,... | collective-permute-start | bytes 221192 | tf_op jit(solution)/shard_map/ppermute | solution.py:40
  42.3 4.6 %collective-permute-start.7 = (bf16[288,512]{1,0:T(8,128)(2,1)S(1)}, bf16[288,512]{1,0:T(8,128)(2,1)S(1)}, u32[]{:S(2)}, u32[]{:S(2)}) collective-permute-start(bf16[288,512]{1,0:T(8,128)(2,1)S(1)} %bitcast.148), channel_id=1, source_target_pairs={{0,1},{1,0},{2,3},{3,2},{4,5},{5,4},{6,7},{7,6},{8,9},{9,8},{10,11... | collective-permute-start | bytes 884744 | tf_op jit(solution)/shard_map/ppermute | solution.py:40
  47.3 7.6 %collective-permute-start.8 = (f32[48,512]{1,0:T(8,128)S(1)}, f32[48,512]{1,0:T(8,128)S(1)}, u32[]{:S(2)}, u32[]{:S(2)}) collective-permute-start(f32[48,512]{1,0:T(8,128)S(1)} %get-tuple-element.34), channel_id=1, source_target_pairs={{0,32},{8,40},{16,48},{24,56},{32,64},{40,72},{48,80},{56,88},{64,... | collective-permute-start | bytes 294920 | tf_op jit(solution)/shard_map/ppermute | solution.py:40
  48.7 6.6 %collective-permute-start.10 = (f32[48,512]{1,0:T(8,128)S(1)}, f32[48,512]{1,0:T(8,128)S(1)}, u32[]{:S(2)}, u32[]{:S(2)}) collective-permute-start(f32[48,512]{1,0:T(8,128)S(1)} %get-tuple-element.35), channel_id=1, source_target_pairs={{0,96},{8,104},{16,112},{24,120},{32,0},{40,8},{48,16},{56,24},{64... | collective-permute-start | bytes 294920 | tf_op jit(solution)/shard_map/ppermute | solution.py:40
  50.0 10.2 %collective-permute-start.9 = (f32[48,512]{1,0:T(8,128)S(1)}, f32[48,512]{1,0:T(8,128)S(1)}, u32[]{:S(2)}, u32[]{:S(2)}) collective-permute-start(f32[48,512]{1,0:T(8,128)S(1)} %get-tuple-element.36), channel_id=1, source_target_pairs={{0,64},{8,72},{16,80},{24,88},{32,96},{40,104},{48,112},{56,120},{... | collective-permute-start | bytes 294920 | tf_op jit(solution)/shard_map/ppermute | solution.py:40
  60.4 6.4 %collective-permute-start.11 = (f32[12,512]{1,0:T(8,128)S(1)}, f32[12,512]{1,0:T(8,128)S(1)}, u32[]{:S(2)}, u32[]{:S(2)}) collective-permute-start(f32[12,512]{1,0:T(8,128)S(1)} %get-tuple-element.47), channel_id=1, source_target_pairs={{0,8},{8,16},{16,24},{24,0},{32,40},{40,48},{48,56},{56,32},{64,72... | collective-permute-start | bytes 73736 | tf_op jit(solution)/shard_map/ppermute | solution.py:40
  62.2 4.6 %collective-permute-start.13 = (f32[12,512]{1,0:T(8,128)S(1)}, f32[12,512]{1,0:T(8,128)S(1)}, u32[]{:S(2)}, u32[]{:S(2)}) collective-permute-start(f32[12,512]{1,0:T(8,128)S(1)} %get-tuple-element.48), channel_id=1, source_target_pairs={{0,24},{8,0},{16,8},{24,16},{32,56},{40,32},{48,40},{56,48},{64,88... | collective-permute-start | bytes 73736 | tf_op jit(solution)/shard_map/ppermute | solution.py:40
  64.5 5.3 %collective-permute-start.12 = (f32[12,512]{1,0:T(8,128)S(1)}, f32[12,512]{1,0:T(8,128)S(1)}, u32[]{:S(2)}, u32[]{:S(2)}) collective-permute-start(f32[12,512]{1,0:T(8,128)S(1)} %get-tuple-element.49), channel_id=1, source_target_pairs={{0,16},{8,24},{16,0},{24,8},{32,48},{40,56},{48,32},{56,40},{64,80... | collective-permute-start | bytes 73736 | tf_op jit(solution)/shard_map/ppermute | solution.py:40
  69.7 3.3 %collective-permute-start.14 = (f32[12,512]{1,0:T(8,128)S(1)}, f32[12,512]{1,0:T(8,128)S(1)}, u32[]{:S(2)}, u32[]{:S(2)}) collective-permute-start(f32[12,512]{1,0:T(8,128)S(1)} %get-tuple-element.28), channel_id=1, source_target_pairs={{0,1},{1,0},{2,3},{3,2},{4,5},{5,4},{6,7},{7,6},{8,9},{9,8},{10,11... | collective-permute-start | bytes 73736 | tf_op jit(solution)/shard_map/ppermute | solution.py:40
  73.0 7.5 %collective-permute-start.17 = (f32[2,12,512]{2,1,0:T(8,128)S(1)}, f32[2,12,512]{2,1,0:T(8,128)S(1)}, u32[]{:S(2)}, u32[]{:S(2)}) collective-permute-start(f32[2,12,512]{2,1,0:T(8,128)S(1)} %bitcast_dynamic-update-slice_fusion.20), channel_id=1, source_target_pairs={{0,6},{1,7},{2,0},{3,1},{4,2},{5,3},{6,4},{7,5},{8,14},{9,15},{10,... | collective-permute-start | bytes 147464 | tf_op jit(solution)/shard_map/ppermute | solution.py:40
  73.1 7.4 %collective-permute-start.16 = (f32[2,12,512]{2,1,0:T(8,128)S(1)}, f32[2,12,512]{2,1,0:T(8,128)S(1)}, u32[]{:S(2)}, u32[]{:S(2)}) collective-permute-start(f32[2,12,512]{2,1,0:T(8,128)S(1)} %bitcast_dynamic-update-slice_fusion.20), channel_id=1, source_target_pairs={{0,4},{1,5},{2,6},{3,7},{4,0},{5,1},{6,2},{7,3},{8,12},{9,13},{10,... | collective-permute-start | bytes 147464 | tf_op jit(solution)/shard_map/ppermute | solution.py:40
  73.8 6.2 %collective-permute-start.15 = (f32[2,12,512]{2,1,0:T(8,128)S(1)}, f32[2,12,512]{2,1,0:T(8,128)S(1)}, u32[]{:S(2)}, u32[]{:S(2)}) collective-permute-start(f32[2,12,512]{2,1,0:T(8,128)S(1)} %bitcast_dynamic-update-slice_fusion.20), channel_id=1, source_target_pairs={{0,2},{1,3},{2,4},{3,5},{4,6},{5,7},{6,0},{7,1},{8,10},{9,11},{10,... | collective-permute-start | bytes 147464 | tf_op jit(solution)/shard_map/ppermute | solution.py:40
  74.6 6.6 %collective-permute-start.18 = (f32[24,576]{1,0:T(8,128)S(1)}, f32[24,576]{1,0:T(8,128)S(1)}, u32[]{:S(2)}, u32[]{:S(2)}) collective-permute-start(f32[24,576]{1,0:T(8,128)S(1)} %get-tuple-element.40), channel_id=1, source_target_pairs={{0,32},{8,40},{16,48},{24,56},{32,64},{40,72},{48,80},{56,88},{64,... | collective-permute-start | bytes 165896 | tf_op jit(solution)/shard_map/ppermute | solution.py:40
  75.9 5.4 %collective-permute-start.20 = (f32[24,576]{1,0:T(8,128)S(1)}, f32[24,576]{1,0:T(8,128)S(1)}, u32[]{:S(2)}, u32[]{:S(2)}) collective-permute-start(f32[24,576]{1,0:T(8,128)S(1)} %get-tuple-element.41), channel_id=1, source_target_pairs={{0,96},{8,104},{16,112},{24,120},{32,0},{40,8},{48,16},{56,24},{64... | collective-permute-start | bytes 165896 | tf_op jit(solution)/shard_map/ppermute | solution.py:40
  80.0 6.4 %collective-permute-start.19 = (f32[24,576]{1,0:T(8,128)S(1)}, f32[24,576]{1,0:T(8,128)S(1)}, u32[]{:S(2)}, u32[]{:S(2)}) collective-permute-start(f32[24,576]{1,0:T(8,128)S(1)} %get-tuple-element.42), channel_id=1, source_target_pairs={{0,64},{8,72},{16,80},{24,88},{32,96},{40,104},{48,112},{56,120},{... | collective-permute-start | bytes 165896 | tf_op jit(solution)/shard_map/ppermute | solution.py:40
  88.1 4.4 %collective-permute-start.23 = (f32[24,576]{1,0:T(8,128)S(1)}, f32[24,576]{1,0:T(8,128)S(1)}, u32[]{:S(2)}, u32[]{:S(2)}) collective-permute-start(f32[24,576]{1,0:T(8,128)S(1)} %fusion.17), channel_id=1, source_target_pairs={{0,24},{8,0},{16,8},{24,16},{32,56},{40,32},{48,40},{56,48},{64,88... | collective-permute-start | bytes 165896 | tf_op jit(solution)/shard_map/ppermute | solution.py:40
  90.8 4.8 %collective-permute-start.22 = (f32[24,576]{1,0:T(8,128)S(1)}, f32[24,576]{1,0:T(8,128)S(1)}, u32[]{:S(2)}, u32[]{:S(2)}) collective-permute-start(f32[24,576]{1,0:T(8,128)S(1)} %fusion.17), channel_id=1, source_target_pairs={{0,8},{8,16},{16,24},{24,0},{32,40},{40,48},{48,56},{56,32},{64,72... | collective-permute-start | bytes 165896 | tf_op jit(solution)/shard_map/ppermute | solution.py:40
  90.8 5.0 %collective-permute-start.21 = (f32[24,576]{1,0:T(8,128)S(1)}, f32[24,576]{1,0:T(8,128)S(1)}, u32[]{:S(2)}, u32[]{:S(2)}) collective-permute-start(f32[24,576]{1,0:T(8,128)S(1)} %fusion.17), channel_id=1, source_target_pairs={{0,16},{8,24},{16,0},{24,8},{32,48},{40,56},{48,32},{56,40},{64,80... | collective-permute-start | bytes 165896 | tf_op jit(solution)/shard_map/ppermute | solution.py:40
  95.9 5.0 %collective-permute-start.24 = (f32[24,576]{1,0:T(8,128)S(1)}, f32[24,576]{1,0:T(8,128)S(1)}, u32[]{:S(2)}, u32[]{:S(2)}) collective-permute-start(f32[24,576]{1,0:T(8,128)S(1)} %get-tuple-element.26), channel_id=1, source_target_pairs={{0,32},{8,40},{16,48},{24,56},{32,64},{40,72},{48,80},{56,88},{64,... | collective-permute-start | bytes 165896 | tf_op jit(solution)/shard_map/ppermute | solution.py:40
  96.0 4.9 %collective-permute-start.25 = (f32[24,576]{1,0:T(8,128)S(1)}, f32[24,576]{1,0:T(8,128)S(1)}, u32[]{:S(2)}, u32[]{:S(2)}) collective-permute-start(f32[24,576]{1,0:T(8,128)S(1)} %get-tuple-element.26), channel_id=1, source_target_pairs={{0,64},{8,72},{16,80},{24,88},{32,96},{40,104},{48,112},{56,120},{... | collective-permute-start | bytes 165896 | tf_op jit(solution)/shard_map/ppermute | solution.py:40
  97.8 3.7 %collective-permute-start.26 = (f32[24,576]{1,0:T(8,128)S(1)}, f32[24,576]{1,0:T(8,128)S(1)}, u32[]{:S(2)}, u32[]{:S(2)}) collective-permute-start(f32[24,576]{1,0:T(8,128)S(1)} %get-tuple-element.26), channel_id=1, source_target_pairs={{0,96},{8,104},{16,112},{24,120},{32,0},{40,8},{48,16},{56,24},{64... | collective-permute-start | bytes 165896 | tf_op jit(solution)/shard_map/ppermute | solution.py:40
  101.5 5.8 %collective-permute-start.27 = (f32[72,576]{1,0:T(8,128)S(1)}, f32[72,576]{1,0:T(8,128)S(1)}, u32[]{:S(2)}, u32[]{:S(2)}) collective-permute-start(f32[72,576]{1,0:T(8,128)S(1)} %pad_maximum_fusion.1), channel_id=1, source_target_pairs={{0,2},{1,3},{2,4},{3,5},{4,6},{5,7},{6,0},{7,1},{8,10},{9,11},{10,... | collective-permute-start | bytes 497672 | tf_op jit(solution)/shard_map/ppermute | solution.py:40
  103.3 7.2 %collective-permute-start.28 = (f32[72,576]{1,0:T(8,128)S(1)}, f32[72,576]{1,0:T(8,128)S(1)}, u32[]{:S(2)}, u32[]{:S(2)}) collective-permute-start(f32[72,576]{1,0:T(8,128)S(1)} %pad_maximum_fusion.1), channel_id=1, source_target_pairs={{0,4},{1,5},{2,6},{3,7},{4,0},{5,1},{6,2},{7,3},{8,12},{9,13},{10,... | collective-permute-start | bytes 497672 | tf_op jit(solution)/shard_map/ppermute | solution.py:40
  105.6 5.0 %collective-permute-start.29 = (f32[72,576]{1,0:T(8,128)S(1)}, f32[72,576]{1,0:T(8,128)S(1)}, u32[]{:S(2)}, u32[]{:S(2)}) collective-permute-start(f32[72,576]{1,0:T(8,128)S(1)} %pad_maximum_fusion.1), channel_id=1, source_target_pairs={{0,6},{1,7},{2,0},{3,1},{4,2},{5,3},{6,4},{7,5},{8,14},{9,15},{10,... | collective-permute-start | bytes 497672 | tf_op jit(solution)/shard_map/ppermute | solution.py:40
  110.6 7.2 %collective-permute-start.30 = (f32[288,576]{1,0:T(8,128)S(1)}, f32[288,576]{1,0:T(8,128)S(1)}, u32[]{:S(2)}, u32[]{:S(2)}) collective-permute-start(f32[288,576]{1,0:T(8,128)S(1)} %bitcast.142), channel_id=1, source_target_pairs={{0,1},{1,0},{2,3},{3,2},{4,5},{5,4},{6,7},{7,6},{8,9},{9,8},{10,11... | collective-permute-start | bytes 1990664 | tf_op jit(solution)/shard_map/ppermute | solution.py:40
  117.8 23.1 %copy-start = (f32[32,3696]{1,0:T(8,128)S(1)}, f32[32,3696]{1,0:T(8,128)}, u32[]{:S(2)}) copy-start(f32[32,3696]{1,0:T(8,128)} %own_first_ref.1) | copy-start | bytes 1419268
  117.8 23.1 %copy-start.1 = (f32[32,3696]{1,0:T(8,128)S(1)}, f32[32,3696]{1,0:T(8,128)}, u32[]{:S(2)}) copy-start(f32[32,3696]{1,0:T(8,128)} %own_second_ref.1) | copy-start | bytes 1419268
Sparse Core Ops, SparseCore 0:
  10.8 77.3 all-gather.5
  90.9 47.5 all-gather.3
